TPU v7x, 32 devices: a whole 2x2x4 slice. The times are simulated.
32 devices in a mesh: seg: 4 (over z), lines: 8 (over y, x, core).
Axes of the slice: x: 2, y: 2, z: 4, core: 2. Of those that a mesh axis runs over, the one named last changes fastest.
Arguments:
- left_features: bfloat16 [32, 4096, 128], P('lines', 'seg'), may hold values from -400 to 400
- right_features: bfloat16 [32, 4096, 128], P('lines', 'seg'), may hold values from -6 to 6
- conv_weight: bfloat16 [3, 3, 3, 128, 128], replicated, may hold values from -0.1875 to 0.1875
- conv_bias: float32 [3, 128], replicated, may hold values from -3 to 3
Outputs:
- refined: bfloat16 [32, 4096, 128], P('lines', 'seg')
- disparity: float32 [32, 4096], P('lines', 'seg')
All inputs are finite; a program needn't handle non-finite values.
Results may differ from a plain program's by a relative error of at most 0.006.
Values may be sent and summed in bfloat16 or wider, within the bound.
No kernel may reach another device: no remote copies, remote signals or barrier semaphores. Data moves between devices by JAX's collectives and lax.ppermute only.
A program may use at most 128 MiB of HBM per device.

v0:
```python
import functools
import math

import jax
import jax.numpy as jnp
from jax import lax
from jax.experimental import pallas as pl
from jax.experimental.pallas import tpu as pltpu
from jax.sharding import PartitionSpec as P

DISP = 1024
NEG = -1e30
EDGE = 16
VMEM_BYTES = 56 * 1024 * 1024


def shifted(block, axis, step):
    count = lax.axis_size(axis)
    route = [(i, i + step) for i in range(count) if 0 <= i + step < count]
    return lax.ppermute(block, axis, route)


def whole(shape):
    return pl.BlockSpec(shape, lambda l: (0,) * len(shape))


def per_line(shape):
    return pl.BlockSpec((1,) + shape, lambda l: (l,) + (0,) * len(shape))


def params():
    return pltpu.CompilerParams(vmem_limit_bytes=VMEM_BYTES)


def scores_of(left, right):
    return lax.dot_general(
        left, right, (((1,), (1,)), ((), ())), preferred_element_type=jnp.float32
    )


def log2_scale(channels):
    return math.log2(math.e) / math.sqrt(channels)


def column_kernel(own, block, left_ref, right_ref, out_ref):
    line = pl.program_id(0)
    lines_here = out_ref.shape[0] // 2
    seg_len, channels = left_ref.shape[1:]
    scale = log2_scale(channels)
    row_ids = lax.broadcasted_iota(jnp.int32, (block, block), 0)
    col_ids = lax.broadcasted_iota(jnp.int32, (block, block), 1)
    for first in range(0, seg_len, block):
        cols = slice(first, first + block)
        rows = slice(first, seg_len) if own else slice(0, first + block)
        raw = scores_of(left_ref[0, rows], right_ref[0, cols])
        if own:
            edge = jnp.where(col_ids <= row_ids, raw[:block], NEG)
            rest = raw[block:]
        else:
            edge = jnp.where(col_ids > row_ids, raw[first:], NEG)
            rest = raw[:first]
        peak = jnp.max(edge, axis=0, keepdims=True)
        if rest.shape[0]:
            peak = jnp.maximum(peak, jnp.max(rest, axis=0, keepdims=True))
        total = jnp.sum(jnp.exp2((edge - peak) * scale), axis=0, keepdims=True)
        if rest.shape[0]:
            total += jnp.sum(jnp.exp2((rest - peak) * scale), axis=0, keepdims=True)
        out_ref[pl.ds(line, 1), cols] = peak * scale
        out_ref[pl.ds(lines_here + line, 1), cols] = total


def column_partials(own, left, right):
    lines_here, seg_len, channels = left.shape
    block = min(256, seg_len)
    return pl.pallas_call(
        functools.partial(column_kernel, own, block),
        grid=(lines_here,),
        in_specs=[per_line((seg_len, channels))] * 2,
        out_specs=whole((2 * lines_here, seg_len)),
        out_shape=jax.ShapeDtypeStruct((2 * lines_here, seg_len), jnp.float32),
        compiler_params=params(),
        cost_estimate=pl.CostEstimate(
            flops=lines_here * seg_len * seg_len * channels,
            bytes_accessed=4 * lines_here * seg_len * channels,
            transcendentals=lines_here * seg_len * seg_len // 2,
        ),
        name="column_own" if own else "column_prev",
    )(left, right)


def merged_potential(first, second, lines_here):
    first_max = jnp.where(first[lines_here:] > 0, first[:lines_here], NEG)
    second_max = jnp.where(second[lines_here:] > 0, second[:lines_here], NEG)
    peak = jnp.maximum(first_max, second_max)
    total = first[lines_here:] * jnp.exp2(first_max - peak) + second[
        lines_here:
    ] * jnp.exp2(second_max - peak)
    return -(peak + jnp.log2(total))


def row_kernel(
    block,
    left_ref,
    right_ref,
    prev_ref,
    own_ref,
    next_ref,
    before_ref,
    back_ref,
    plan_ref,
    own_out,
    prev_out,
    ext,
    pot,
    sums,
):
    line = pl.program_id(0)
    lines_here = own_out.shape[0]
    seg_len, channels = left_ref.shape[1:]
    scale = log2_scale(channels)

    @pl.when(line == 0)
    def _():
        pot[:, seg_len:] = merged_potential(own_ref[...], next_ref[...], lines_here)
        before = before_ref[...]
        pot[:, :seg_len] = jnp.where(
            before[lines_here:] > 0,
            merged_potential(before, back_ref[...], lines_here),
            NEG,
        )

    ext[:seg_len] = prev_ref[0]
    ext[seg_len:] = right_ref[0]
    sums[...] = jnp.zeros_like(sums)
    row_ids = lax.broadcasted_iota(jnp.int32, (block, block), 0)
    col_ids = lax.broadcasted_iota(jnp.int32, (block, block), 1)
    window = seg_len + block
    col_pot = pot[pl.ds(line, 1), :]
    for index in range(seg_len // block):
        first = index * block
        raw = scores_of(left_ref[0, first : first + block], ext[first : first + window])
        logits = raw * scale + col_pot[:, first : first + window]
        logits = jnp.concatenate(
            [
                jnp.where(col_ids > row_ids, logits[:, :block], NEG),
                logits[:, block:seg_len],
                jnp.where(col_ids <= row_ids, logits[:, seg_len:], NEG),
            ],
            axis=1,
        )
        peak = jnp.max(logits, axis=1, keepdims=True)
        terms = jnp.exp2(logits - peak)
        plan_ref[0, index] = terms.astype(plan_ref.dtype)
        plan = terms * (1.0 / jnp.sum(terms, axis=1, keepdims=True))
        sums[:, first : first + window] += jnp.sum(
            plan.reshape(block // 8, 8, window), axis=0
        )
    totals = jnp.sum(sums[...], axis=0, keepdims=True)
    prev_out[pl.ds(line, 1), :] = totals[:, :seg_len]
    own_out[pl.ds(line, 1), :] = totals[:, seg_len:]


def row_pass(left, right, prev, own, following, before, back, block):
    lines_here, seg_len, channels = left.shape
    window = seg_len + block
    part = (2 * lines_here, seg_len)
    marginal = jax.ShapeDtypeStruct((lines_here, seg_len), jnp.float32)
    return pl.pallas_call(
        functools.partial(row_kernel, block),
        grid=(lines_here,),
        in_specs=[per_line((seg_len, channels))] * 3 + [whole(part)] * 4,
        out_specs=[
            per_line((seg_len // block, block, window)),
            whole((lines_here, seg_len)),
            whole((lines_here, seg_len)),
        ],
        out_shape=[
            jax.ShapeDtypeStruct(
                (lines_here, seg_len // block, block, window), jnp.bfloat16
            ),
            marginal,
            marginal,
        ],
        scratch_shapes=[
            pltpu.VMEM((2 * seg_len, channels), jnp.bfloat16),
            pltpu.VMEM((lines_here, 2 * seg_len), jnp.float32),
            pltpu.VMEM((8, 2 * seg_len), jnp.float32),
        ],
        compiler_params=params(),
        name="row_pass",
    )(left, right, prev, own, following, before, back)


def transport_kernel(
    block,
    plan_ref,
    left_ref,
    right_ref,
    prev_ref,
    own_ref,
    next_ref,
    before_ref,
    back_ref,
    state_ref,
    disp_ref,
    ext,
    gain,
    marks,
):
    line = pl.program_id(0)
    seg_len, channels = left_ref.shape[1:]
    window = seg_len + block

    @pl.when(line == 0)
    def _():
        gain[:, seg_len:] = 1.0 / (own_ref[...] + next_ref[...])
        total = before_ref[...] + back_ref[...]
        gain[:, :seg_len] = jnp.where(
            total > 0, 1.0 / jnp.where(total > 0, total, 1.0), 0.0
        )
        lane = lax.broadcasted_iota(jnp.int32, (window, channels), 1)
        distance = seg_len - lax.broadcasted_iota(jnp.int32, (window, channels), 0)
        low = jnp.bitwise_and(distance, 15)
        values = jnp.where(
            lane == 0,
            1,
            jnp.where(lane == 1, distance - low, jnp.where(lane == 2, low, 0)),
        )
        marks[...] = values.astype(jnp.float32).astype(jnp.bfloat16)

    ext[:seg_len] = prev_ref[0]
    ext[seg_len:] = right_ref[0]
    line_gain = gain[pl.ds(line, 1), :]
    offsets = lax.broadcasted_iota(jnp.int32, (1, block), 1).astype(jnp.float32)
    disparity = []
    for index in range(seg_len // block):
        first = index * block
        rows = slice(first, first + block)
        weights = (
            plan_ref[0, index].astype(jnp.float32)
            * line_gain[:, first : first + window]
        ).astype(jnp.bfloat16)
        table = jnp.concatenate([ext[first : first + window], marks[...]], axis=1)
        result = jnp.dot(weights, table, preferred_element_type=jnp.float32)
        total = result[:, channels : channels + 1]
        matched = result[:, :channels] * (1.0 / total)
        state_ref[0, rows] = (matched - left_ref[0, rows].astype(jnp.float32)).astype(
            state_ref.dtype
        )
        moments = result[:, channels:].T
        disparity.append(offsets + (moments[1:2] + moments[2:3]) / moments[0:1])
    disp_ref[pl.ds(line, 1), :] = jnp.concatenate(disparity, axis=1)


def transport(plan, left, right, prev, own, following, before, back, block):
    lines_here, seg_len, channels = left.shape
    window = seg_len + block
    return pl.pallas_call(
        functools.partial(transport_kernel, block),
        grid=(lines_here,),
        in_specs=[per_line((seg_len // block, block, window))]
        + [per_line((seg_len, channels))] * 3
        + [whole((lines_here, seg_len))] * 4,
        out_specs=[per_line((seg_len, channels)), whole((lines_here, seg_len))],
        out_shape=[
            jax.ShapeDtypeStruct(left.shape, jnp.bfloat16),
            jax.ShapeDtypeStruct((lines_here, seg_len), jnp.float32),
        ],
        scratch_shapes=[
            pltpu.VMEM((2 * seg_len, channels), jnp.bfloat16),
            pltpu.VMEM((lines_here, 2 * seg_len), jnp.float32),
            pltpu.VMEM((window, channels), jnp.bfloat16),
        ],
        compiler_params=params(),
        name="transport",
    )(plan, left, right, prev, own, following, before, back)


def conv_layers(state, top, bottom, left_px, right_px, corners_top, corners_bottom, weight, bias):
    layers = weight.shape[0]
    lines_here, seg_len, channels = state.shape
    middle = jnp.concatenate([top, state, bottom], axis=0)
    before = jnp.concatenate(
        [corners_top[:, EDGE - layers : EDGE], left_px[:, EDGE - layers :], corners_bottom[:, EDGE - layers : EDGE]], axis=0
    )
    after = jnp.concatenate(
        [corners_top[:, EDGE : EDGE + layers], right_px[:, :layers], corners_bottom[:, EDGE : EDGE + layers]], axis=0
    )
    image = jnp.concatenate([before, middle, after], axis=1)
    line0 = lax.axis_index("lines") * lines_here
    px0 = lax.axis_index("seg") * seg_len
    all_lines = lax.axis_size("lines") * lines_here
    all_px = lax.axis_size("seg") * seg_len
    for layer in range(layers):
        reach = layers - 1 - layer
        total = lax.conv_general_dilated(
            image[None],
            weight[layer],
            (1, 1),
            "VALID",
            dimension_numbers=("NHWC", "HWIO", "NHWC"),
            preferred_element_type=jnp.float32,
        )[0]
        updated = image[1:-1, 1:-1].astype(jnp.float32) + jax.nn.relu(total + bias[layer])
        if reach:
            line_ids = line0 - reach + lax.broadcasted_iota(jnp.int32, updated.shape, 0)
            px_ids = px0 - reach + lax.broadcasted_iota(jnp.int32, updated.shape, 1)
            inside = (line_ids >= 0) & (line_ids < all_lines) & (px_ids >= 0) & (px_ids < all_px)
            updated = jnp.where(inside, updated, 0.0)
        image = updated.astype(jnp.bfloat16)
    return image


def shards(left_features, right_features, conv_weight, conv_bias):
    seg_len = left_features.shape[1]
    block = min(128, seg_len)
    layers = conv_weight.shape[0]
    prev = shifted(right_features, "seg", 1)
    own = column_partials(True, left_features, right_features)
    before = shifted(own, "seg", 1)
    back = column_partials(False, left_features, prev)
    following = shifted(back, "seg", -1)
    plan, own, back = row_pass(
        left_features, right_features, prev, own, following, before, back, block
    )
    before = shifted(own, "seg", 1)
    following = shifted(back, "seg", -1)
    state, disparity = transport(
        plan, left_features, right_features, prev, own, following, before, back, block
    )
    bottom = shifted(state[:layers], "lines", -1)
    top = shifted(state[-layers:], "lines", 1)
    left_px = shifted(state[:, -EDGE:], "seg", 1)
    right_px = shifted(state[:, :EDGE], "seg", -1)
    edges = jnp.concatenate([left_px, right_px], axis=1)
    corners_bottom = shifted(edges[:layers], "lines", -1)
    corners_top = shifted(edges[-layers:], "lines", 1)
    refined = conv_layers(
        state, top, bottom, left_px, right_px, corners_top, corners_bottom, conv_weight, conv_bias
    )
    return (refined, disparity)


def solution(mesh):
    return jax.shard_map(
        shards,
        mesh=mesh,
        in_specs=(P("lines", "seg", None), P("lines", "seg", None), P(), P()),
        out_specs=(P("lines", "seg", None), P("lines", "seg")),
        check_vma=False,
    )
```

profile of v0, /device:TPU:19, one launch (start us, length us, event | category | flops | bytes accessed | tf_op | source)
XLA Modules:
  0.0 161.6 jit_solution(4643883335416252768)
XLA Ops:
  0.6 3.2 %collective-permute-start = (bf16[4,1024,128]{2,1,0:T(8,128)(2,1)}, bf16[4,1024,128]{2,1,0:T(8,128)(2,1)S(1)}, u32[]{:S(2)}, u32[]{:S(2)}) collective-permute-start(bf16[4,1024,128]{2,1,0:T(8,128)(2,1)} %right_ref.5), channel_id=1, source_target_pairs={{0,8},{8,16},{16,24},{1,9},{9,17},{17,25},{2,10},{10,18},{18,26},{... | collective-permute-start | bytes 3145736 | tf_op jit(solution)/shard_map/ppermute | solution.py:20
  3.9 5.3 %column_own.1.own_ref = f32[8,1024]{1,0:T(8,128)} custom-call(bf16[4,1024,128]{2,1,0:T(8,128)(2,1)} %left_ref.7, bf16[4,1024,128]{2,1,0:T(8,128)(2,1)} %right_ref.5), custom_call_target="tpu_custom_call" | custom-call | flops 536870912 | bytes 2097152 | tf_op jit(solution)/shard_map/column_own/pallas_call | solution.py:75
  9.2 1.9 %collective-permute-start.2 = (f32[8,1024]{1,0:T(8,128)}, f32[8,1024]{1,0:T(8,128)S(1)}, u32[]{:S(2)}, u32[]{:S(2)}) collective-permute-start(f32[8,1024]{1,0:T(8,128)} %column_own.1.own_ref), channel_id=1, source_target_pairs={{0,8},{8,16},{16,24},{1,9},{9,17},{17,25},{2,10},{10,18},{18,26},{... | collective-permute-start | bytes 98312 | tf_op jit(solution)/shard_map/ppermute | solution.py:20
  11.2 15.6 %collective-permute-done.right_ref.prev_ref = bf16[4,1024,128]{2,1,0:T(8,128)(2,1)S(1)} collective-permute-done((bf16[4,1024,128]{2,1,0:T(8,128)(2,1)}, bf16[4,1024,128]{2,1,0:T(8,128)(2,1)S(1)}, u32[]{:S(2)}, u32[]{:S(2)}) %collective-permute-start) | collective-permute-done | bytes 1048608 | tf_op jit(solution)/shard_map/ppermute | solution.py:20
  27.7 5.1 %column_prev.1.back_ref = f32[8,1024]{1,0:T(8,128)} custom-call(bf16[4,1024,128]{2,1,0:T(8,128)(2,1)} %left_ref.7, bf16[4,1024,128]{2,1,0:T(8,128)(2,1)} %copy-done.5), custom_call_target="tpu_custom_call" | custom-call | flops 536870912 | bytes 2097152 | tf_op jit(solution)/shard_map/column_prev/pallas_call | solution.py:75
  32.9 2.1 %collective-permute-start.1 = (f32[8,1024]{1,0:T(8,128)}, f32[8,1024]{1,0:T(8,128)S(1)}, u32[]{:S(2)}, u32[]{:S(2)}) collective-permute-start(f32[8,1024]{1,0:T(8,128)} %column_prev.1.back_ref), channel_id=1, source_target_pairs={{8,0},{16,8},{24,16},{9,1},{17,9},{25,17},{10,2},{18,10},{26,18},{... | collective-permute-start | bytes 98312 | tf_op jit(solution)/shard_map/ppermute | solution.py:20
  35.0 2.7 %collective-permute-done.1.next_ref = f32[8,1024]{1,0:T(8,128)S(1)} collective-permute-done((f32[8,1024]{1,0:T(8,128)}, f32[8,1024]{1,0:T(8,128)S(1)}, u32[]{:S(2)}, u32[]{:S(2)}) %collective-permute-start.1) | collective-permute-done | bytes 32800 | tf_op jit(solution)/shard_map/ppermute | solution.py:20
  38.3 10.9 %row_pass.1 = (bf16[4,8,128,1152]{3,2,1,0:T(8,128)(2,1)}, f32[4,1024]{1,0:T(4,128)}, f32[4,1024]{1,0:T(4,128)}) custom-call(bf16[4,1024,128]{2,1,0:T(8,128)(2,1)} %left_ref.7, bf16[4,1024,128]{2,1,0:T(8,128)(2,1)} %right_ref.5, bf16[4,1024,128]{2,1,0:T(8,128)(2,1)} %copy-done.5, f32[8,1024]{1,0:T(8,128)} %column_own.1.own_ref, f32[8,1024]{1,0:T(8,128)} %copy-done.7, ...), custom_call_target="tpu_custom_call" | custom-call | tf_op jit(solution)/shard_map/row_pass/pallas_call | solution.py:168
  49.2 2.1 %collective-permute-start.3 = (f32[4,1024]{1,0:T(4,128)}, f32[4,1024]{1,0:T(4,128)S(1)}, u32[]{:S(2)}, u32[]{:S(2)}) collective-permute-start(f32[4,1024]{1,0:T(4,128)} %get-tuple-element.9.back_ref), channel_id=1, source_target_pairs={{8,0},{16,8},{24,16},{9,1},{17,9},{25,17},{10,2},{18,10},{26,18},{... | collective-permute-start | bytes 49160 | tf_op jit(solution)/shard_map/ppermute | solution.py:20
  51.3 3.2 %collective-permute-start.4 = (f32[4,1024]{1,0:T(4,128)}, f32[4,1024]{1,0:T(4,128)S(1)}, u32[]{:S(2)}, u32[]{:S(2)}) collective-permute-start(f32[4,1024]{1,0:T(4,128)} %get-tuple-element.8.own_ref), channel_id=1, source_target_pairs={{0,8},{8,16},{16,24},{1,9},{9,17},{17,25},{2,10},{10,18},{18,26},{... | collective-permute-start | bytes 49160 | tf_op jit(solution)/shard_map/ppermute | solution.py:20
  56.6 7.9 %transport.1 = (bf16[4,1024,128]{2,1,0:T(8,128)(2,1)}, f32[4,1024]{1,0:T(4,128)}) custom-call(bf16[4,8,128,1152]{3,2,1,0:T(8,128)(2,1)} %get-tuple-element.7.plan_ref, bf16[4,1024,128]{2,1,0:T(8,128)(2,1)} %left_ref.7, bf16[4,1024,128]{2,1,0:T(8,128)(2,1)} %right_ref.5, bf16[4,1024,128]{2,1,0:T(8,128)(2,1)} %copy-done.5, ...), custom_call_target="tpu_custom_call" | custom-call | tf_op jit(solution)/shard_map/transport/pallas_call | solution.py:258
  65.3 3.2 %collective-permute-start.5 = (bf16[4,16,128]{2,1,0:T(8,128)(2,1)S(1)}, bf16[4,16,128]{2,1,0:T(8,128)(2,1)S(1)}, u32[]{:S(2)}, u32[]{:S(2)}) collective-permute-start(bf16[4,16,128]{2,1,0:T(8,128)(2,1)S(1)} %get-tuple-element.15), channel_id=1, source_target_pairs={{0,8},{8,16},{16,24},{1,9},{9,17},{17,25},{2,10},{10,18},{18,26},{... | collective-permute-start | bytes 49160 | tf_op jit(solution)/shard_map/ppermute | solution.py:20
  69.9 6.7 %collective-permute-start.10 = (bf16[3,1024,128]{2,1,0:T(8,128)(2,1)S(1)}, bf16[3,1024,128]{2,1,0:T(8,128)(2,1)S(1)}, u32[]{:S(2)}, u32[]{:S(2)}) collective-permute-start(bf16[3,1024,128]{2,1,0:T(8,128)(2,1)S(1)} %get-tuple-element.13), channel_id=1, source_target_pairs={{1,0},{2,1},{3,2},{4,3},{5,4},{6,5},{7,6},{9,8},{10,9},{11,10},{12... | collective-permute-start | bytes 2359304 | tf_op jit(solution)/shard_map/ppermute | solution.py:20
  76.6 3.0 %collective-permute-start.9 = (bf16[3,1024,128]{2,1,0:T(8,128)(2,1)S(1)}, bf16[3,1024,128]{2,1,0:T(8,128)(2,1)S(1)}, u32[]{:S(2)}, u32[]{:S(2)}) collective-permute-start(bf16[3,1024,128]{2,1,0:T(8,128)(2,1)S(1)} %get-tuple-element.12), channel_id=1, source_target_pairs={{0,1},{1,2},{2,3},{3,4},{4,5},{5,6},{6,7},{8,9},{9,10},{10,11},{11... | collective-permute-start | bytes 2359304 | tf_op jit(solution)/shard_map/ppermute | solution.py:20
  79.6 2.1 %collective-permute-start.6 = (bf16[4,16,128]{2,1,0:T(8,128)(2,1)S(1)}, bf16[4,16,128]{2,1,0:T(8,128)(2,1)S(1)}, u32[]{:S(2)}, u32[]{:S(2)}) collective-permute-start(bf16[4,16,128]{2,1,0:T(8,128)(2,1)S(1)} %get-tuple-element.14), channel_id=1, source_target_pairs={{8,0},{16,8},{24,16},{9,1},{17,9},{25,17},{10,2},{18,10},{26,18},{... | collective-permute-start | bytes 49160 | tf_op jit(solution)/shard_map/ppermute | solution.py:20
  81.8 2.7 %collective-permute-done.6 = bf16[4,16,128]{2,1,0:T(8,128)(2,1)S(1)} collective-permute-done((bf16[4,16,128]{2,1,0:T(8,128)(2,1)S(1)}, bf16[4,16,128]{2,1,0:T(8,128)(2,1)S(1)}, u32[]{:S(2)}, u32[]{:S(2)}) %collective-permute-start.6) | collective-permute-done | bytes 16416 | tf_op jit(solution)/shard_map/ppermute | solution.py:20
  84.5 3.3 %collective-permute-start.7 = (bf16[3,32,128]{2,1,0:T(8,128)(2,1)S(1)}, bf16[3,32,128]{2,1,0:T(8,128)(2,1)S(1)}, u32[]{:S(2)}, u32[]{:S(2)}) collective-permute-start(bf16[3,32,128]{2,1,0:T(8,128)(2,1)S(1)} %get-tuple-element.16), channel_id=1, source_target_pairs={{0,1},{1,2},{2,3},{3,4},{4,5},{5,6},{6,7},{8,9},{9,10},{10,11},{11... | collective-permute-start | bytes 73736 | tf_op jit(solution)/shard_map/ppermute | solution.py:20
  87.8 2.1 %collective-permute-start.8 = (bf16[3,32,128]{2,1,0:T(8,128)(2,1)S(1)}, bf16[3,32,128]{2,1,0:T(8,128)(2,1)S(1)}, u32[]{:S(2)}, u32[]{:S(2)}) collective-permute-start(bf16[3,32,128]{2,1,0:T(8,128)(2,1)S(1)} %get-tuple-element.17), channel_id=1, source_target_pairs={{1,0},{2,1},{3,2},{4,3},{5,4},{6,5},{7,6},{9,8},{10,9},{11,10},{12... | collective-permute-start | bytes 73736 | tf_op jit(solution)/shard_map/ppermute | solution.py:20
  89.9 4.8 %collective-permute-done.7 = bf16[3,32,128]{2,1,0:T(8,128)(2,1)S(1)} collective-permute-done((bf16[3,32,128]{2,1,0:T(8,128)(2,1)S(1)}, bf16[3,32,128]{2,1,0:T(8,128)(2,1)S(1)}, u32[]{:S(2)}, u32[]{:S(2)}) %collective-permute-start.7) | collective-permute-done | bytes 24608 | tf_op jit(solution)/shard_map/ppermute | solution.py:20
  96.5 14.7 %concatenate.19 = bf16[10,1030,128]{2,1,0:T(8,128)(2,1)S(1)} concatenate(bf16[10,3,128]{2,1,0:T(4,128)(2,1)S(1)} %get-tuple-element.25, bf16[10,1024,128]{2,1,0:T(8,128)(2,1)} %pad_maximum_fusion, bf16[10,3,128]{2,1,0:T(4,128)(2,1)S(1)} %get-tuple-element.26), dimensions={1} | concatenate | bytes 5273600 | tf_op jit(solution)/shard_map/concatenate | solution.py:289
  112.9 5.1 %reshape.9 = bf16[10,1,8,129,128]{4,3,2,0,1:T(8,128)(2,1)} reshape(bf16[10,1,1032,128]{3,2,0,1:T(8,128)(2,1)} %pad) | data formatting | bytes 5283840 | tf_op jit(solution)/shard_map/conv_general_dilated | solution.py:296
  118.0 2.2 %copy.16 = bf16[10,1,8,129,128]{4,2,3,0,1:T(8,128)(2,1)S(1)} copy(bf16[10,1,8,129,128]{4,3,2,0,1:T(8,128)(2,1)} %reshape.9) | data formatting | bytes 5283840 | tf_op jit(solution)/shard_map/conv_general_dilated | solution.py:296
  120.3 5.1 %broadcast_select_fusion = f32[8,8,129,128]{3,1,2,0:T(8,128)S(1)} fusion(pred[8,129]{0,1:T(8,128)(4,1)S(1)} %copy-done.14, bf16[10,1,7,2,128]{4,2,3,0,1:T(8,128)(2,1)S(1)} %slice.99, bf16[10,1,8,129,128]{4,2,3,0,1:T(8,128)(2,1)S(1)} %copy.16, bf16[3,3,3,128,128]{4,3,2,1,0:T(8,128)(2,1)S(1)} %copy-done.11), kind=kOutput, calls=%fused_computation.31 | convolution fusion | flops 2443898880 | bytes 7222272 | tf_op jit(solution)/shard_map/conv_general_dilated | solution.py:296
  126.5 2.6 %fusion.6 = bf16[8,1028,128]{2,1,0:T(8,128)(2,1)S(1)} fusion(f32[8,1,1028,128]{3,0,2,1:T(8,128)S(1)} %slice.100, bf16[10,1030,128]{2,1,0:T(8,128)(2,1)S(1)} %concatenate.19, f32[128]{0:T(128)S(1)} %get-tuple-element.23, pred[1028]{0:T(1024)(128)(4,1)S(1)} %get-tuple-element.27, pred[8]{0:T(512)(128)(4,1)S(1)} %compare_and_fusion, ...), kind=kLoop, calls=%fused_computation.9 | loop fusion | flops 8421376 | bytes 8423952 | tf_op jit(solution)/shard_map/convert_element_type | solution.py:310
  129.1 3.8 %copy.27 = bf16[8,1,1028,128]{3,0,2,1:T(8,128)(2,1)S(1)} copy(bf16[8,1,1028,128]{3,2,0,1:T(8,128)(2,1)S(1)} %bitcast.79) | data formatting | bytes 4210688
  134.1 4.1 %broadcast_select_fusion.1 = f32[6,8,129,128]{3,1,2,0:T(8,128)S(1)} fusion(pred[8,129]{0,1:T(8,128)(4,1)S(1)} %copy-done.13, bf16[8,1,7,2,128]{4,2,3,0,1:T(8,128)(2,1)S(1)} %slice.102, bf16[8,1,8,129,128]{4,2,3,0,1:T(8,128)(2,1)S(1)} %copy.21, bf16[3,3,3,128,128]{4,3,2,1,0:T(8,128)(2,1)S(1)} %copy-done.11), kind=kOutput, calls=%fused_computation.43 | convolution fusion | flops 1833326592 | bytes 5628928 | tf_op jit(solution)/shard_map/conv_general_dilated | solution.py:296
  138.2 2.3 %copy.22 = f32[6,8,129,128]{3,2,1,0:T(8,128)} copy(f32[6,8,129,128]{3,1,2,0:T(8,128)S(1)} %broadcast_select_fusion.1) | data formatting | bytes 6340608 | tf_op jit(solution)/shard_map/conv_general_dilated | solution.py:296
  140.5 4.6 %reshape.20 = f32[6,1,1032,128]{3,2,0,1:T(8,128)} reshape(f32[6,8,129,128]{3,2,1,0:T(8,128)} %copy.22) | data formatting | bytes 6340608 | tf_op jit(solution)/shard_map/conv_general_dilated | solution.py:296
  145.1 3.1 %fusion.12 = bf16[6,1026,128]{2,1,0:T(8,128)(2,1)S(1)} fusion(f32[6,1,1032,128]{3,2,0,1:T(8,128)} %reshape.20, bf16[8,1028,128]{2,1,0:T(8,128)(2,1)S(1)} %copy-done.1, f32[128]{0:T(128)S(1)} %get-tuple-element.24, pred[1026]{0:T(1024)(128)(4,1)S(1)} %get-tuple-element.29, pred[6]{0:T(512)(128)(4,1)S(1)} %compare_and_fusion.1, ...), kind=kLoop, calls=%fused_computation.17 | loop fusion | flops 6303744 | bytes 6306314 | tf_op jit(solution)/shard_map/convert_element_type | solution.py:310
  150.3 3.7 %fusion.42 = f32[4,8,129,128]{3,1,2,0:T(8,128)S(1)} fusion(bf16[6,1,7,2,128]{4,2,3,0,1:T(8,128)(2,1)S(1)} %slice.105, bf16[6,1,8,129,128]{4,2,3,0,1:T(8,128)(2,1)S(1)} %copy.24, pred[8,129]{0,1:T(8,128)(4,1)S(1)} %copy-done.12, bf16[3,3,3,128,128]{4,3,2,1,0:T(8,128)(2,1)} %param.6), kind=kOutput, calls=%fused_computation.44 | convolution fusion | flops 1222754304 | bytes 4016136 | tf_op jit(solution)/shard_map/conv_general_dilated | solution.py:296
  155.8 2.8 %reshape.27 = f32[4,1,1032,128]{3,2,0,1:T(8,128)} reshape(f32[4,8,129,128]{3,2,1,0:T(8,128)} %copy.25) | data formatting | bytes 4227072 | tf_op jit(solution)/shard_map/conv_general_dilated | solution.py:296
  158.6 3.0 %fusion.30 = bf16[4,1024,128]{2,1,0:T(8,128)(2,1)} fusion(f32[4,1,1032,128]{3,2,0,1:T(8,128)} %reshape.27, bf16[6,1026,128]{2,1,0:T(8,128)(2,1)S(1)} %copy-done.3, f32[128]{0:T(128)S(1)} %get-tuple-element.22), kind=kLoop, calls=%fused_computation.36 | loop fusion | flops 2621440 | bytes 4194816 | tf_op jit(solution)/shard_map/convert_element_type | solution.py:310
  (65 shorter events, 15.7 us)
Async XLA Ops:
  0.6 10.5 %copy-start.10 = (f32[3,128]{1,0:T(4,128)S(1)}, f32[3,128]{1,0:T(4,128)}, u32[]{:S(2)}) copy-start(f32[3,128]{1,0:T(4,128)} %param.7) | copy-start | bytes 4612
  0.6 26.1 %collective-permute-start = (bf16[4,1024,128]{2,1,0:T(8,128)(2,1)}, bf16[4,1024,128]{2,1,0:T(8,128)(2,1)S(1)}, u32[]{:S(2)}, u32[]{:S(2)}) collective-permute-start(bf16[4,1024,128]{2,1,0:T(8,128)(2,1)} %right_ref.5), channel_id=1, source_target_pairs={{0,8},{8,16},{16,24},{1,9},{9,17},{17,25},{2,10},{10,18},{18,26},{... | collective-permute-start | bytes 3145736 | tf_op jit(solution)/shard_map/ppermute | solution.py:20
  9.2 25.8 %collective-permute-start.2 = (f32[8,1024]{1,0:T(8,128)}, f32[8,1024]{1,0:T(8,128)S(1)}, u32[]{:S(2)}, u32[]{:S(2)}) collective-permute-start(f32[8,1024]{1,0:T(8,128)} %column_own.1.own_ref), channel_id=1, source_target_pairs={{0,8},{8,16},{16,24},{1,9},{9,17},{17,25},{2,10},{10,18},{18,26},{... | collective-permute-start | bytes 98312 | tf_op jit(solution)/shard_map/ppermute | solution.py:20
  26.8 1.0 copy-start.5
  32.9 4.9 %collective-permute-start.1 = (f32[8,1024]{1,0:T(8,128)}, f32[8,1024]{1,0:T(8,128)S(1)}, u32[]{:S(2)}, u32[]{:S(2)}) collective-permute-start(f32[8,1024]{1,0:T(8,128)} %column_prev.1.back_ref), channel_id=1, source_target_pairs={{8,0},{16,8},{24,16},{9,1},{17,9},{25,17},{10,2},{18,10},{26,18},{... | collective-permute-start | bytes 98312 | tf_op jit(solution)/shard_map/ppermute | solution.py:20
  35.0 2.8 %copy-start.6 = (f32[8,1024]{1,0:T(8,128)}, f32[8,1024]{1,0:T(8,128)S(1)}, u32[]{:S(2)}) copy-start(f32[8,1024]{1,0:T(8,128)S(1)} %collective-permute-done.2.before_ref) | copy-start | bytes 98308
  37.7 0.6 copy-start.7
  49.2 5.3 %collective-permute-start.3 = (f32[4,1024]{1,0:T(4,128)}, f32[4,1024]{1,0:T(4,128)S(1)}, u32[]{:S(2)}, u32[]{:S(2)}) collective-permute-start(f32[4,1024]{1,0:T(4,128)} %get-tuple-element.9.back_ref), channel_id=1, source_target_pairs={{8,0},{16,8},{24,16},{9,1},{17,9},{25,17},{10,2},{18,10},{26,18},{... | collective-permute-start | bytes 49160 | tf_op jit(solution)/shard_map/ppermute | solution.py:20
  51.3 4.7 %collective-permute-start.4 = (f32[4,1024]{1,0:T(4,128)}, f32[4,1024]{1,0:T(4,128)S(1)}, u32[]{:S(2)}, u32[]{:S(2)}) collective-permute-start(f32[4,1024]{1,0:T(4,128)} %get-tuple-element.8.own_ref), channel_id=1, source_target_pairs={{0,8},{8,16},{16,24},{1,9},{9,17},{17,25},{2,10},{10,18},{18,26},{... | collective-permute-start | bytes 49160 | tf_op jit(solution)/shard_map/ppermute | solution.py:20
  54.5 1.5 copy-start.8
  56.0 0.6 copy-start.9
  64.4 30.3 %copy-start.4 = (bf16[4,1024,128]{2,1,0:T(8,128)(2,1)S(1)}, bf16[4,1024,128]{2,1,0:T(8,128)(2,1)}, u32[]{:S(2)}) copy-start(bf16[4,1024,128]{2,1,0:T(8,128)(2,1)} %get-tuple-element.10) | copy-start | bytes 3145732
  65.3 16.5 %collective-permute-start.5 = (bf16[4,16,128]{2,1,0:T(8,128)(2,1)S(1)}, bf16[4,16,128]{2,1,0:T(8,128)(2,1)S(1)}, u32[]{:S(2)}, u32[]{:S(2)}) collective-permute-start(bf16[4,16,128]{2,1,0:T(8,128)(2,1)S(1)} %get-tuple-element.15), channel_id=1, source_target_pairs={{0,8},{8,16},{16,24},{1,9},{9,17},{17,25},{2,10},{10,18},{18,26},{... | collective-permute-start | bytes 49160 | tf_op jit(solution)/shard_map/ppermute | solution.py:20
  69.9 24.8 %collective-permute-start.10 = (bf16[3,1024,128]{2,1,0:T(8,128)(2,1)S(1)}, bf16[3,1024,128]{2,1,0:T(8,128)(2,1)S(1)}, u32[]{:S(2)}, u32[]{:S(2)}) collective-permute-start(bf16[3,1024,128]{2,1,0:T(8,128)(2,1)S(1)} %get-tuple-element.13), channel_id=1, source_target_pairs={{1,0},{2,1},{3,2},{4,3},{5,4},{6,5},{7,6},{9,8},{10,9},{11,10},{12... | collective-permute-start | bytes 2359304 | tf_op jit(solution)/shard_map/ppermute | solution.py:20
  76.6 18.1 %collective-permute-start.9 = (bf16[3,1024,128]{2,1,0:T(8,128)(2,1)S(1)}, bf16[3,1024,128]{2,1,0:T(8,128)(2,1)S(1)}, u32[]{:S(2)}, u32[]{:S(2)}) collective-permute-start(bf16[3,1024,128]{2,1,0:T(8,128)(2,1)S(1)} %get-tuple-element.12), channel_id=1, source_target_pairs={{0,1},{1,2},{2,3},{3,4},{4,5},{5,6},{6,7},{8,9},{9,10},{10,11},{11... | collective-permute-start | bytes 2359304 | tf_op jit(solution)/shard_map/ppermute | solution.py:20
  79.6 4.8 %collective-permute-start.6 = (bf16[4,16,128]{2,1,0:T(8,128)(2,1)S(1)}, bf16[4,16,128]{2,1,0:T(8,128)(2,1)S(1)}, u32[]{:S(2)}, u32[]{:S(2)}) collective-permute-start(bf16[4,16,128]{2,1,0:T(8,128)(2,1)S(1)} %get-tuple-element.14), channel_id=1, source_target_pairs={{8,0},{16,8},{24,16},{9,1},{17,9},{25,17},{10,2},{18,10},{26,18},{... | collective-permute-start | bytes 49160 | tf_op jit(solution)/shard_map/ppermute | solution.py:20
  84.5 10.2 %collective-permute-start.7 = (bf16[3,32,128]{2,1,0:T(8,128)(2,1)S(1)}, bf16[3,32,128]{2,1,0:T(8,128)(2,1)S(1)}, u32[]{:S(2)}, u32[]{:S(2)}) collective-permute-start(bf16[3,32,128]{2,1,0:T(8,128)(2,1)S(1)} %get-tuple-element.16), channel_id=1, source_target_pairs={{0,1},{1,2},{2,3},{3,4},{4,5},{5,6},{6,7},{8,9},{9,10},{10,11},{11... | collective-permute-start | bytes 73736 | tf_op jit(solution)/shard_map/ppermute | solution.py:20
  87.8 6.9 %collective-permute-start.8 = (bf16[3,32,128]{2,1,0:T(8,128)(2,1)S(1)}, bf16[3,32,128]{2,1,0:T(8,128)(2,1)S(1)}, u32[]{:S(2)}, u32[]{:S(2)}) collective-permute-start(bf16[3,32,128]{2,1,0:T(8,128)(2,1)S(1)} %get-tuple-element.17), channel_id=1, source_target_pairs={{1,0},{2,1},{3,2},{4,3},{5,4},{6,5},{7,6},{9,8},{10,9},{11,10},{12... | collective-permute-start | bytes 73736 | tf_op jit(solution)/shard_map/ppermute | solution.py:20
  118.0 2.2 %copy-start.11 = (bf16[3,3,3,128,128]{4,3,2,1,0:T(8,128)(2,1)S(1)}, bf16[3,3,3,128,128]{4,3,2,1,0:T(8,128)(2,1)}, u32[]{:S(2)}) copy-start(bf16[3,3,3,128,128]{4,3,2,1,0:T(8,128)(2,1)} %param.6) | copy-start | bytes 2654212
  118.0 2.2 %copy-start.14 = (pred[8,129]{0,1:T(8,128)(4,1)S(1)}, pred[8,129]{0,1:T(8,128)(4,1)}, u32[]{:S(2)}) copy-start(pred[8,129]{0,1:T(8,128)(4,1)} %constant.51) | copy-start | bytes 3100
  129.1 4.3 %copy-start = (bf16[8,1028,128]{2,1,0:T(8,128)(2,1)}, bf16[8,1028,128]{2,1,0:T(8,128)(2,1)S(1)}, u32[]{:S(2)}) copy-start(bf16[8,1028,128]{2,1,0:T(8,128)(2,1)S(1)} %fusion.6) | copy-start | bytes 6316036
  133.4 0.7 copy-start.13
  140.5 4.6 %copy-start.1 = (bf16[8,1028,128]{2,1,0:T(8,128)(2,1)S(1)}, bf16[8,1028,128]{2,1,0:T(8,128)(2,1)}, u32[]{:S(2)}) copy-start(bf16[8,1028,128]{2,1,0:T(8,128)(2,1)} %copy-done) | copy-start | bytes 6316036
  148.2 1.2 copy-start.2
  149.5 0.8 copy-start.12
  155.8 2.8 %copy-start.3 = (bf16[6,1026,128]{2,1,0:T(8,128)(2,1)S(1)}, bf16[6,1026,128]{2,1,0:T(8,128)(2,1)}, u32[]{:S(2)}) copy-start(bf16[6,1026,128]{2,1,0:T(8,128)(2,1)} %copy-done.2) | copy-start | bytes 4727812
where the time goes:
time: 165 us; the launch traced here: 162 us
  local copies, waits for them, and re-layouts  47.8 us (29%)
  starting transfers between devices  32.8 us (20%)
  Pallas kernels  29.2 us (18%)
  waiting for transfers between devices  27.3 us (17%)
  matrix products  12.8 us (8%)
  other arithmetic  10.6 us (6%)
    ppermute x11, starting transfers between devices, shifted(): return lax.ppermute(block, axis, route)  32.8 us
    ppermute x11, waiting for transfers between devices, shifted(): return lax.ppermute(block, axis, route)  27.3 us
    conv_general_dilated x14, local copies, waits for them, and re-layouts, conv_layers(): lax.conv_general_dilated(image[None], weight[layer], (1, 1), 'VALID', dim...  20.9 us
    concatenate x1, local copies, waits for them, and re-layouts, conv_layers(): image = jnp.concatenate([before, middle, after], axis=1)  14.7 us
    conv_general_dilated x3, matrix products, conv_layers(): lax.conv_general_dilated(image[None], weight[layer], (1, 1), 'VALID', dim...  12.8 us
    pallas_call x1, Pallas kernels, row_pass(): pl.pallas_call(functools.partial(row_kernel, block), grid=(lines_here,),...  10.9 us
    pallas_call x2, Pallas kernels, column_partials(): pl.pallas_call(functools.partial(column_kernel, own, block), grid=(lines_...  10.5 us
    convert_element_type x3, other arithmetic, conv_layers(): image = updated.astype(jnp.bfloat16)  8.75 us
  transfers between devices with their start and end apart: 11, of which 5 were waited for; matrix products, arithmetic and copies ran while one was open for 1% of the time, Pallas kernels for 6%

commit v1 on v0

--- a/solution.py
+++ b/solution.py
@@ -42,8 +42,16 @@
     return math.log2(math.e) / math.sqrt(channels)
 
 
-def column_kernel(own, block, left_ref, right_ref, out_ref):
+def column_kernel(own, block, left_ref, right_ref, *refs):
     line = pl.program_id(0)
+    out_ref = refs[-1]
+    if own:
+        weight_ref, stacked_ref, out_ref = refs
+
+        @pl.when(line == 0)
+        def _():
+            stack_weights(weight_ref, stacked_ref)
+
     lines_here = out_ref.shape[0] // 2
     seg_len, channels = left_ref.shape[1:]
     scale = log2_scale(channels)
@@ -69,15 +77,26 @@
         out_ref[pl.ds(lines_here + line, 1), cols] = total
 
 
-def column_partials(own, left, right):
+def column_partials(left, right, weight=None):
     lines_here, seg_len, channels = left.shape
     block = min(256, seg_len)
+    own = weight is not None
+    in_specs = [per_line((seg_len, channels))] * 2
+    out_specs = [whole((2 * lines_here, seg_len))]
+    out_shape = [jax.ShapeDtypeStruct((2 * lines_here, seg_len), jnp.float32)]
+    operands = [left, right]
+    if own:
+        stacked = (weight.shape[0], 12 * channels, 2 * channels)
+        in_specs.append(whole(weight.shape))
+        out_specs.insert(0, whole(stacked))
+        out_shape.insert(0, jax.ShapeDtypeStruct(stacked, weight.dtype))
+        operands.append(weight)
     return pl.pallas_call(
         functools.partial(column_kernel, own, block),
         grid=(lines_here,),
-        in_specs=[per_line((seg_len, channels))] * 2,
-        out_specs=whole((2 * lines_here, seg_len)),
-        out_shape=jax.ShapeDtypeStruct((2 * lines_here, seg_len), jnp.float32),
+        in_specs=in_specs,
+        out_specs=out_specs,
+        out_shape=out_shape,
         compiler_params=params(),
         cost_estimate=pl.CostEstimate(
             flops=lines_here * seg_len * seg_len * channels,
@@ -85,7 +104,7 @@
             transcendentals=lines_here * seg_len * seg_len // 2,
         ),
         name="column_own" if own else "column_prev",
-    )(left, right)
+    )(*operands)
 
 
 def merged_potential(first, second, lines_here):
@@ -193,6 +212,7 @@
 
 def transport_kernel(
     block,
+    edge_lines,
     plan_ref,
     left_ref,
     right_ref,
@@ -203,11 +223,16 @@
     back_ref,
     state_ref,
     disp_ref,
+    first_ref,
+    last_ref,
+    low_ref,
+    high_ref,
     ext,
     gain,
     marks,
 ):
     line = pl.program_id(0)
+    layers, lines_here = edge_lines, gain.shape[0]
     seg_len, channels = left_ref.shape[1:]
     window = seg_len + block
 
@@ -250,21 +275,45 @@
         moments = result[:, channels:].T
         disparity.append(offsets + (moments[1:2] + moments[2:3]) / moments[0:1])
     disp_ref[pl.ds(line, 1), :] = jnp.concatenate(disparity, axis=1)
-
-
-def transport(plan, left, right, prev, own, following, before, back, block):
+    low_ref[...] = state_ref[:, :EDGE]
+    high_ref[...] = state_ref[:, seg_len - EDGE :]
+
+    @pl.when(line < layers)
+    def _():
+        first_ref[...] = state_ref[...]
+
+    @pl.when(line >= lines_here - layers)
+    def _():
+        last_ref[...] = state_ref[...]
+
+
+def transport(plan, left, right, prev, own, following, before, back, block, layers):
     lines_here, seg_len, channels = left.shape
     window = seg_len + block
     return pl.pallas_call(
-        functools.partial(transport_kernel, block),
+        functools.partial(transport_kernel, block, layers),
         grid=(lines_here,),
         in_specs=[per_line((seg_len // block, block, window))]
         + [per_line((seg_len, channels))] * 3
         + [whole((lines_here, seg_len))] * 4,
-        out_specs=[per_line((seg_len, channels)), whole((lines_here, seg_len))],
+        out_specs=[
+            per_line((seg_len, channels)),
+            whole((lines_here, seg_len)),
+            pl.BlockSpec((1, seg_len, channels), lambda l: (jnp.minimum(l, layers - 1), 0, 0)),
+            pl.BlockSpec(
+                (1, seg_len, channels),
+                lambda l: (jnp.maximum(l - (lines_here - layers), 0), 0, 0),
+            ),
+            per_line((EDGE, channels)),
+            per_line((EDGE, channels)),
+        ],
         out_shape=[
             jax.ShapeDtypeStruct(left.shape, jnp.bfloat16),
             jax.ShapeDtypeStruct((lines_here, seg_len), jnp.float32),
+            jax.ShapeDtypeStruct((layers, seg_len, channels), jnp.bfloat16),
+            jax.ShapeDtypeStruct((layers, seg_len, channels), jnp.bfloat16),
+            jax.ShapeDtypeStruct((lines_here, EDGE, channels), jnp.bfloat16),
+            jax.ShapeDtypeStruct((lines_here, EDGE, channels), jnp.bfloat16),
         ],
         scratch_shapes=[
             pltpu.VMEM((2 * seg_len, channels), jnp.bfloat16),
@@ -276,39 +325,103 @@
     )(plan, left, right, prev, own, following, before, back)
 
 
+def stack_weights(weight_ref, stacked_ref):
+    layers, taps, _, channels, _ = weight_ref.shape
+    zeros = jnp.zeros((channels, channels), stacked_ref.dtype)
+    for layer in range(layers):
+        for col_tap in range(taps):
+            for line in range(taps + 1):
+                row = (col_tap * (taps + 1) + line) * channels
+                for out in range(2):
+                    row_tap = line - out
+                    stacked_ref[
+                        layer, row : row + channels, out * channels : (out + 1) * channels
+                    ] = weight_ref[layer, row_tap, col_tap] if 0 <= row_tap < taps else zeros
+
+
+def conv_kernel(
+    state_ref,
+    top_ref,
+    bottom_ref,
+    left_ref,
+    right_ref,
+    corner_top_ref,
+    corner_bottom_ref,
+    weight_ref,
+    bias_ref,
+    out_ref,
+    first_image,
+    second_image,
+):
+    lines_here, seg_len, channels = state_ref.shape
+    layers = weight_ref.shape[0]
+    after = layers + lines_here
+    right = EDGE + seg_len
+    f32 = jnp.float32
+    first_image[:layers, EDGE:right] = top_ref[...].astype(f32)
+    first_image[layers:after, EDGE:right] = state_ref[...].astype(f32)
+    first_image[after:, EDGE:right] = bottom_ref[...].astype(f32)
+    first_image[layers:after, :EDGE] = left_ref[...].astype(f32)
+    first_image[layers:after, right:] = right_ref[...].astype(f32)
+    for rows, corner_ref in ((slice(0, layers), corner_top_ref), (slice(after, None), corner_bottom_ref)):
+        first_image[rows, :EDGE] = corner_ref[:, :EDGE].astype(f32)
+        first_image[rows, right:] = corner_ref[:, EDGE:].astype(f32)
+    line0 = lax.axis_index("lines") * lines_here - layers
+    all_lines = lax.axis_size("lines") * lines_here
+    px0 = lax.axis_index("seg") * seg_len - EDGE
+    all_px = lax.axis_size("seg") * seg_len
+    source, target = first_image, second_image
+    for layer in range(layers):
+        reach = layers - 1 - layer
+        begin, end = (EDGE // 2, right + EDGE // 2) if reach else (EDGE, right)
+        pieces = 5 if reach else 4
+        size = (end - begin) // pieces
+
+        def pair(index, carry, layer=layer, reach=reach, begin=begin, pieces=pieces, size=size, source=source, target=target):
+            base = layer + 2 * index
+            for piece in range(pieces):
+                start = begin + piece * size
+                taps = [
+                    source[base + line, start + col_tap - 1 : start + col_tap - 1 + size].astype(jnp.bfloat16)
+                    for col_tap in range(3)
+                    for line in range(4)
+                ]
+                total = jnp.dot(
+                    jnp.concatenate(taps, axis=1), weight_ref[layer], preferred_element_type=f32
+                )
+                for out in range(2):
+                    line = base + 1 + out
+                    part = total[:, out * channels : (out + 1) * channels] + bias_ref[layer : layer + 1]
+                    updated = source[line, start : start + size] + jnp.maximum(part, 0.0)
+                    if not reach:
+                        out_ref[line - layers, start - EDGE : start - EDGE + size] = updated.astype(out_ref.dtype)
+                        continue
+                    image_line = line0 + line
+                    inside = (image_line >= 0) & (image_line < all_lines)
+                    if piece in (0, pieces - 1):
+                        px = px0 + start + lax.broadcasted_iota(jnp.int32, updated.shape, 0)
+                        inside = inside & (px >= 0) & (px < all_px)
+                    updated = jnp.where(inside, updated, 0.0)
+                    target[line, start : start + size] = updated.astype(jnp.bfloat16).astype(f32)
+            return carry
+
+        lax.fori_loop(0, (lines_here + 2 * reach) // 2, pair, 0)
+        source, target = target, source
+
+
 def conv_layers(state, top, bottom, left_px, right_px, corners_top, corners_bottom, weight, bias):
     layers = weight.shape[0]
     lines_here, seg_len, channels = state.shape
-    middle = jnp.concatenate([top, state, bottom], axis=0)
-    before = jnp.concatenate(
-        [corners_top[:, EDGE - layers : EDGE], left_px[:, EDGE - layers :], corners_bottom[:, EDGE - layers : EDGE]], axis=0
-    )
-    after = jnp.concatenate(
-        [corners_top[:, EDGE : EDGE + layers], right_px[:, :layers], corners_bottom[:, EDGE : EDGE + layers]], axis=0
-    )
-    image = jnp.concatenate([before, middle, after], axis=1)
-    line0 = lax.axis_index("lines") * lines_here
-    px0 = lax.axis_index("seg") * seg_len
-    all_lines = lax.axis_size("lines") * lines_here
-    all_px = lax.axis_size("seg") * seg_len
-    for layer in range(layers):
-        reach = layers - 1 - layer
-        total = lax.conv_general_dilated(
-            image[None],
-            weight[layer],
-            (1, 1),
-            "VALID",
-            dimension_numbers=("NHWC", "HWIO", "NHWC"),
-            preferred_element_type=jnp.float32,
-        )[0]
-        updated = image[1:-1, 1:-1].astype(jnp.float32) + jax.nn.relu(total + bias[layer])
-        if reach:
-            line_ids = line0 - reach + lax.broadcasted_iota(jnp.int32, updated.shape, 0)
-            px_ids = px0 - reach + lax.broadcasted_iota(jnp.int32, updated.shape, 1)
-            inside = (line_ids >= 0) & (line_ids < all_lines) & (px_ids >= 0) & (px_ids < all_px)
-            updated = jnp.where(inside, updated, 0.0)
-        image = updated.astype(jnp.bfloat16)
-    return image
+    image = pltpu.VMEM((lines_here + 2 * layers, seg_len + 2 * EDGE, channels), jnp.float32)
+    return pl.pallas_call(
+        conv_kernel,
+        in_specs=[pl.BlockSpec(memory_space=pltpu.VMEM)] * 9,
+        out_specs=pl.BlockSpec(memory_space=pltpu.VMEM),
+        out_shape=jax.ShapeDtypeStruct(state.shape, state.dtype),
+        scratch_shapes=[image, image],
+        compiler_params=params(),
+        name="conv_layers",
+    )(state, top, bottom, left_px, right_px, corners_top, corners_bottom, weight, bias)
 
 
 def shards(left_features, right_features, conv_weight, conv_bias):
@@ -316,27 +429,27 @@
     block = min(128, seg_len)
     layers = conv_weight.shape[0]
     prev = shifted(right_features, "seg", 1)
-    own = column_partials(True, left_features, right_features)
+    stacked, own = column_partials(left_features, right_features, conv_weight)
     before = shifted(own, "seg", 1)
-    back = column_partials(False, left_features, prev)
+    (back,) = column_partials(left_features, prev)
     following = shifted(back, "seg", -1)
     plan, own, back = row_pass(
         left_features, right_features, prev, own, following, before, back, block
     )
     before = shifted(own, "seg", 1)
     following = shifted(back, "seg", -1)
-    state, disparity = transport(
-        plan, left_features, right_features, prev, own, following, before, back, block
+    state, disparity, first, last, low, high = transport(
+        plan, left_features, right_features, prev, own, following, before, back, block, layers
     )
-    bottom = shifted(state[:layers], "lines", -1)
-    top = shifted(state[-layers:], "lines", 1)
-    left_px = shifted(state[:, -EDGE:], "seg", 1)
-    right_px = shifted(state[:, :EDGE], "seg", -1)
+    bottom = shifted(first, "lines", -1)
+    top = shifted(last, "lines", 1)
+    left_px = shifted(high, "seg", 1)
+    right_px = shifted(low, "seg", -1)
     edges = jnp.concatenate([left_px, right_px], axis=1)
     corners_bottom = shifted(edges[:layers], "lines", -1)
     corners_top = shifted(edges[-layers:], "lines", 1)
     refined = conv_layers(
-        state, top, bottom, left_px, right_px, corners_top, corners_bottom, conv_weight, conv_bias
+        state, top, bottom, left_px, right_px, corners_top, corners_bottom, stacked, conv_bias
     )
     return (refined, disparity)
 

time: 165 us -> 109 us (0.66)
  the two profiles are of different devices: /device:TPU:19 before, /device:TPU:1 now
where the time goes in v1:
time: 109 us
  Pallas kernels  43.8 us (40%)
  starting transfers between devices  34 us (31%)
  waiting for transfers between devices  26.5 us (24%)
  local copies, waits for them, and re-layouts  3.33 us (3%)
    ppermute x11, starting transfers between devices, shifted(): return lax.ppermute(block, axis, route)  34 us
    ppermute x11, waiting for transfers between devices, shifted(): return lax.ppermute(block, axis, route)  26.5 us
    pallas_call x1, Pallas kernels, conv_layers(): pl.pallas_call(conv_kernel, in_specs=[pl.BlockSpec(memory_space=pltpu.VME...  13.4 us
    pallas_call x2, Pallas kernels, column_partials(): pl.pallas_call(functools.partial(column_kernel, own, block), grid=(lines_...  11.1 us
    pallas_call x1, Pallas kernels, row_pass(): pl.pallas_call(functools.partial(row_kernel, block), grid=(lines_here,),...  10.9 us
    pallas_call x1, Pallas kernels, transport(): pl.pallas_call(functools.partial(transport_kernel, block, layers), grid=(...  8.4 us
    unnamed x23, local copies, waits for them, and re-layouts  3.31 us
  transfers between devices with their start and end apart: 11, of which 5 were waited for; matrix products, arithmetic and copies ran while one was open for 0% of the time, Pallas kernels for 10%

profile of v1, /device:TPU:1, one launch (start us, length us, event | category | flops | bytes accessed | tf_op | source)
XLA Modules:
  0.0 108.5 jit_solution(8953204906560897316)
XLA Ops:
  0.6 4.1 %collective-permute-start = (bf16[4,1024,128]{2,1,0:T(8,128)(2,1)}, bf16[4,1024,128]{2,1,0:T(8,128)(2,1)S(1)}, u32[]{:S(2)}, u32[]{:S(2)}) collective-permute-start(bf16[4,1024,128]{2,1,0:T(8,128)(2,1)} %right_ref.5), channel_id=1, source_target_pairs={{0,8},{8,16},{16,24},{1,9},{9,17},{17,25},{2,10},{10,18},{18,26},{... | collective-permute-start | bytes 3145736 | tf_op jit(solution)/shard_map/ppermute | solution.py:20
  4.7 6.0 %column_own.1 = (bf16[3,1536,256]{2,1,0:T(8,128)(2,1)}, f32[8,1024]{1,0:T(8,128)}) custom-call(bf16[4,1024,128]{2,1,0:T(8,128)(2,1)} %left_ref.7, bf16[4,1024,128]{2,1,0:T(8,128)(2,1)} %right_ref.5, bf16[3,3,3,128,128]{4,3,2,1,0:T(8,128)(2,1)} %refs_0_.1), custom_call_target="tpu_custom_call" | custom-call | flops 536870912 | bytes 2097152 | tf_op jit(solution)/shard_map/column_own/pallas_call | solution.py:94
  10.7 3.1 %collective-permute-start.2 = (f32[8,1024]{1,0:T(8,128)}, f32[8,1024]{1,0:T(8,128)S(1)}, u32[]{:S(2)}, u32[]{:S(2)}) collective-permute-start(f32[8,1024]{1,0:T(8,128)} %get-tuple-element.13.own_ref), channel_id=1, source_target_pairs={{0,8},{8,16},{16,24},{1,9},{9,17},{17,25},{2,10},{10,18},{18,26},{... | collective-permute-start | bytes 98312 | tf_op jit(solution)/shard_map/ppermute | solution.py:20
  13.8 13.0 %collective-permute-done.right_ref.prev_ref = bf16[4,1024,128]{2,1,0:T(8,128)(2,1)S(1)} collective-permute-done((bf16[4,1024,128]{2,1,0:T(8,128)(2,1)}, bf16[4,1024,128]{2,1,0:T(8,128)(2,1)S(1)}, u32[]{:S(2)}, u32[]{:S(2)}) %collective-permute-start) | collective-permute-done | bytes 1048608 | tf_op jit(solution)/shard_map/ppermute | solution.py:20
  26.8 1.0 copy-done
  27.8 5.1 %column_prev.1.back_ref = f32[8,1024]{1,0:T(8,128)} custom-call(bf16[4,1024,128]{2,1,0:T(8,128)(2,1)} %left_ref.7, bf16[4,1024,128]{2,1,0:T(8,128)(2,1)} %copy-done), custom_call_target="tpu_custom_call" | custom-call | flops 536870912 | bytes 2097152 | tf_op jit(solution)/shard_map/column_prev/pallas_call | solution.py:94
  32.9 1.3 %collective-permute-start.1 = (f32[8,1024]{1,0:T(8,128)}, f32[8,1024]{1,0:T(8,128)S(1)}, u32[]{:S(2)}, u32[]{:S(2)}) collective-permute-start(f32[8,1024]{1,0:T(8,128)} %column_prev.1.back_ref), channel_id=1, source_target_pairs={{8,0},{16,8},{24,16},{9,1},{17,9},{25,17},{10,2},{18,10},{26,18},{... | collective-permute-start | bytes 98312 | tf_op jit(solution)/shard_map/ppermute | solution.py:20
  34.2 4.2 %collective-permute-done.1.next_ref = f32[8,1024]{1,0:T(8,128)S(1)} collective-permute-done((f32[8,1024]{1,0:T(8,128)}, f32[8,1024]{1,0:T(8,128)S(1)}, u32[]{:S(2)}, u32[]{:S(2)}) %collective-permute-start.1) | collective-permute-done | bytes 32800 | tf_op jit(solution)/shard_map/ppermute | solution.py:20
  38.4 0.6 copy-done.6
  39.0 10.9 %row_pass.1 = (bf16[4,8,128,1152]{3,2,1,0:T(8,128)(2,1)}, f32[4,1024]{1,0:T(4,128)}, f32[4,1024]{1,0:T(4,128)}) custom-call(bf16[4,1024,128]{2,1,0:T(8,128)(2,1)} %left_ref.7, bf16[4,1024,128]{2,1,0:T(8,128)(2,1)} %right_ref.5, bf16[4,1024,128]{2,1,0:T(8,128)(2,1)} %copy-done, f32[8,1024]{1,0:T(8,128)} %get-tuple-element.13.own_ref, f32[8,1024]{1,0:T(8,128)} %copy-done.6, ...), custom_call_target="tpu_custom_call" | custom-call | tf_op jit(solution)/shard_map/row_pass/pallas_call | solution.py:187
  49.9 3.3 %collective-permute-start.4 = (f32[4,1024]{1,0:T(4,128)}, f32[4,1024]{1,0:T(4,128)S(1)}, u32[]{:S(2)}, u32[]{:S(2)}) collective-permute-start(f32[4,1024]{1,0:T(4,128)} %get-tuple-element.15.own_ref), channel_id=1, source_target_pairs={{0,8},{8,16},{16,24},{1,9},{9,17},{17,25},{2,10},{10,18},{18,26},{... | collective-permute-start | bytes 49160 | tf_op jit(solution)/shard_map/ppermute | solution.py:20
  53.2 1.3 %collective-permute-start.3 = (f32[4,1024]{1,0:T(4,128)}, f32[4,1024]{1,0:T(4,128)S(1)}, u32[]{:S(2)}, u32[]{:S(2)}) collective-permute-start(f32[4,1024]{1,0:T(4,128)} %get-tuple-element.16.back_ref), channel_id=1, source_target_pairs={{8,0},{16,8},{24,16},{9,1},{17,9},{25,17},{10,2},{18,10},{26,18},{... | collective-permute-start | bytes 49160 | tf_op jit(solution)/shard_map/ppermute | solution.py:20
  54.5 0.0 collective-permute-done.4.before_ref
  54.5 3.4 %collective-permute-done.3.next_ref = f32[4,1024]{1,0:T(4,128)S(1)} collective-permute-done((f32[4,1024]{1,0:T(4,128)}, f32[4,1024]{1,0:T(4,128)S(1)}, u32[]{:S(2)}, u32[]{:S(2)}) %collective-permute-start.3) | collective-permute-done | bytes 16416 | tf_op jit(solution)/shard_map/ppermute | solution.py:20
  57.9 0.6 copy-done.10
  58.5 8.4 %transport.1 = (bf16[4,1024,128]{2,1,0:T(8,128)(2,1)}, f32[4,1024]{1,0:T(4,128)}, bf16[3,1024,128]{2,1,0:T(8,128)(2,1)}, bf16[3,1024,128]{2,1,0:T(8,128)(2,1)}, ...) custom-call(bf16[4,8,128,1152]{3,2,1,0:T(8,128)(2,1)} %get-tuple-element.14.plan_ref, ...), custom_call_target="tpu_custom_call" | custom-call | tf_op jit(solution)/shard_map/transport/pallas_call | solution.py:293
  66.9 7.5 %collective-permute-start.5 = (bf16[3,1024,128]{2,1,0:T(8,128)(2,1)}, bf16[3,1024,128]{2,1,0:T(8,128)(2,1)S(1)}, u32[]{:S(2)}, u32[]{:S(2)}) collective-permute-start(bf16[3,1024,128]{2,1,0:T(8,128)(2,1)} %get-tuple-element.18), channel_id=1, source_target_pairs={{0,1},{1,2},{2,3},{3,4},{4,5},{5,6},{6,7},{8,9},{9,10},{10,11},{11... | collective-permute-start | bytes 2359304 | tf_op jit(solution)/shard_map/ppermute | solution.py:20
  74.4 1.9 %collective-permute-start.6 = (bf16[3,1024,128]{2,1,0:T(8,128)(2,1)}, bf16[3,1024,128]{2,1,0:T(8,128)(2,1)S(1)}, u32[]{:S(2)}, u32[]{:S(2)}) collective-permute-start(bf16[3,1024,128]{2,1,0:T(8,128)(2,1)} %get-tuple-element.19), channel_id=1, source_target_pairs={{1,0},{2,1},{3,2},{4,3},{5,4},{6,5},{7,6},{9,8},{10,9},{11,10},{12... | collective-permute-start | bytes 2359304 | tf_op jit(solution)/shard_map/ppermute | solution.py:20
  76.3 3.2 %collective-permute-start.7 = (bf16[4,16,128]{2,1,0:T(8,128)(2,1)}, bf16[4,16,128]{2,1,0:T(8,128)(2,1)S(1)}, u32[]{:S(2)}, u32[]{:S(2)}) collective-permute-start(bf16[4,16,128]{2,1,0:T(8,128)(2,1)} %get-tuple-element.20), channel_id=1, source_target_pairs={{0,8},{8,16},{16,24},{1,9},{9,17},{17,25},{2,10},{10,18},{18,26},{... | collective-permute-start | bytes 49160 | tf_op jit(solution)/shard_map/ppermute | solution.py:20
  79.6 1.3 %collective-permute-start.8 = (bf16[4,16,128]{2,1,0:T(8,128)(2,1)}, bf16[4,16,128]{2,1,0:T(8,128)(2,1)S(1)}, u32[]{:S(2)}, u32[]{:S(2)}) collective-permute-start(bf16[4,16,128]{2,1,0:T(8,128)(2,1)} %get-tuple-element.21), channel_id=1, source_target_pairs={{8,0},{16,8},{24,16},{9,1},{17,9},{25,17},{10,2},{18,10},{26,18},{... | collective-permute-start | bytes 49160 | tf_op jit(solution)/shard_map/ppermute | solution.py:20
  80.9 0.0 collective-permute-done.7.left_ref
  80.9 3.4 %collective-permute-done.8.right_ref = bf16[4,16,128]{2,1,0:T(8,128)(2,1)S(1)} collective-permute-done((bf16[4,16,128]{2,1,0:T(8,128)(2,1)}, bf16[4,16,128]{2,1,0:T(8,128)(2,1)S(1)}, u32[]{:S(2)}, u32[]{:S(2)}) %collective-permute-start.8) | collective-permute-done | bytes 16416 | tf_op jit(solution)/shard_map/ppermute | solution.py:20
  84.3 1.9 %collective-permute-start.10 = (bf16[3,32,128]{2,1,0:T(8,128)(2,1)S(1)}, bf16[3,32,128]{2,1,0:T(8,128)(2,1)S(1)}, u32[]{:S(2)}, u32[]{:S(2)}) collective-permute-start(bf16[3,32,128]{2,1,0:T(8,128)(2,1)S(1)} %get-tuple-element.24), channel_id=1, source_target_pairs={{1,0},{2,1},{3,2},{4,3},{5,4},{6,5},{7,6},{9,8},{10,9},{11,10},{12... | collective-permute-start | bytes 73736 | tf_op jit(solution)/shard_map/ppermute | solution.py:20
  86.2 5.1 %collective-permute-start.9 = (bf16[3,32,128]{2,1,0:T(8,128)(2,1)S(1)}, bf16[3,32,128]{2,1,0:T(8,128)(2,1)S(1)}, u32[]{:S(2)}, u32[]{:S(2)}) collective-permute-start(bf16[3,32,128]{2,1,0:T(8,128)(2,1)S(1)} %get-tuple-element.25), channel_id=1, source_target_pairs={{0,1},{1,2},{2,3},{3,4},{4,5},{5,6},{6,7},{8,9},{9,10},{10,11},{11... | collective-permute-start | bytes 73736 | tf_op jit(solution)/shard_map/ppermute | solution.py:20
  91.3 2.6 %collective-permute-done.10.corner_bottom_ref = bf16[3,32,128]{2,1,0:T(8,128)(2,1)S(1)} collective-permute-done((bf16[3,32,128]{2,1,0:T(8,128)(2,1)S(1)}, bf16[3,32,128]{2,1,0:T(8,128)(2,1)S(1)}, u32[]{:S(2)}, u32[]{:S(2)}) %collective-permute-start.10) | collective-permute-done | bytes 24608 | tf_op jit(solution)/shard_map/ppermute | solution.py:20
  93.9 0.0 collective-permute-done.9.corner_top_ref
  93.9 0.0 collective-permute-done.5.top_ref
  93.9 0.5 copy-done.7
  94.5 0.0 copy-done.8
  94.5 0.3 copy-done.1
  94.8 0.3 copy-done.2
  95.1 13.4 %conv_layers.1 = bf16[4,1024,128]{2,1,0:T(8,128)(2,1)} custom-call(bf16[4,1024,128]{2,1,0:T(8,128)(2,1)} %get-tuple-element.17.state_ref, bf16[3,1024,128]{2,1,0:T(8,128)(2,1)} %copy-done.1, bf16[3,1024,128]{2,1,0:T(8,128)(2,1)} %copy-done.2, bf16[4,16,128]{2,1,0:T(8,128)(2,1)} %copy-done.3, bf16[4,16,128]{2,1,0:T(8,128)(2,1)} %copy-done.4, ...), custom_call_target="tpu_custom_call" | custom-call | tf_op jit(solution)/shard_map/conv_layers/pallas_call | solution.py:416
  (20 shorter events, 0.1 us)
Async XLA Ops:
  0.6 26.2 %collective-permute-start = (bf16[4,1024,128]{2,1,0:T(8,128)(2,1)}, bf16[4,1024,128]{2,1,0:T(8,128)(2,1)S(1)}, u32[]{:S(2)}, u32[]{:S(2)}) collective-permute-start(bf16[4,1024,128]{2,1,0:T(8,128)(2,1)} %right_ref.5), channel_id=1, source_target_pairs={{0,8},{8,16},{16,24},{1,9},{9,17},{17,25},{2,10},{10,18},{18,26},{... | collective-permute-start | bytes 3145736 | tf_op jit(solution)/shard_map/ppermute | solution.py:20
  10.7 23.5 %collective-permute-start.2 = (f32[8,1024]{1,0:T(8,128)}, f32[8,1024]{1,0:T(8,128)S(1)}, u32[]{:S(2)}, u32[]{:S(2)}) collective-permute-start(f32[8,1024]{1,0:T(8,128)} %get-tuple-element.13.own_ref), channel_id=1, source_target_pairs={{0,8},{8,16},{16,24},{1,9},{9,17},{17,25},{2,10},{10,18},{18,26},{... | collective-permute-start | bytes 98312 | tf_op jit(solution)/shard_map/ppermute | solution.py:20
  26.8 1.0 copy-start
  32.9 5.5 %collective-permute-start.1 = (f32[8,1024]{1,0:T(8,128)}, f32[8,1024]{1,0:T(8,128)S(1)}, u32[]{:S(2)}, u32[]{:S(2)}) collective-permute-start(f32[8,1024]{1,0:T(8,128)} %column_prev.1.back_ref), channel_id=1, source_target_pairs={{8,0},{16,8},{24,16},{9,1},{17,9},{25,17},{10,2},{18,10},{26,18},{... | collective-permute-start | bytes 98312 | tf_op jit(solution)/shard_map/ppermute | solution.py:20
  34.2 4.2 %copy-start.5 = (f32[8,1024]{1,0:T(8,128)}, f32[8,1024]{1,0:T(8,128)S(1)}, u32[]{:S(2)}) copy-start(f32[8,1024]{1,0:T(8,128)S(1)} %collective-permute-done.2.before_ref) | copy-start | bytes 98308
  38.4 0.6 copy-start.6
  49.9 4.7 %collective-permute-start.4 = (f32[4,1024]{1,0:T(4,128)}, f32[4,1024]{1,0:T(4,128)S(1)}, u32[]{:S(2)}, u32[]{:S(2)}) collective-permute-start(f32[4,1024]{1,0:T(4,128)} %get-tuple-element.15.own_ref), channel_id=1, source_target_pairs={{0,8},{8,16},{16,24},{1,9},{9,17},{17,25},{2,10},{10,18},{18,26},{... | collective-permute-start | bytes 49160 | tf_op jit(solution)/shard_map/ppermute | solution.py:20
  53.2 4.7 %collective-permute-start.3 = (f32[4,1024]{1,0:T(4,128)}, f32[4,1024]{1,0:T(4,128)S(1)}, u32[]{:S(2)}, u32[]{:S(2)}) collective-permute-start(f32[4,1024]{1,0:T(4,128)} %get-tuple-element.16.back_ref), channel_id=1, source_target_pairs={{8,0},{16,8},{24,16},{9,1},{17,9},{25,17},{10,2},{18,10},{26,18},{... | collective-permute-start | bytes 49160 | tf_op jit(solution)/shard_map/ppermute | solution.py:20
  54.5 3.4 %copy-start.9 = (f32[4,1024]{1,0:T(4,128)}, f32[4,1024]{1,0:T(4,128)S(1)}, u32[]{:S(2)}) copy-start(f32[4,1024]{1,0:T(4,128)S(1)} %collective-permute-done.4.before_ref) | copy-start | bytes 49156
  57.9 0.6 copy-start.10
  66.9 27.0 %collective-permute-start.5 = (bf16[3,1024,128]{2,1,0:T(8,128)(2,1)}, bf16[3,1024,128]{2,1,0:T(8,128)(2,1)S(1)}, u32[]{:S(2)}, u32[]{:S(2)}) collective-permute-start(bf16[3,1024,128]{2,1,0:T(8,128)(2,1)} %get-tuple-element.18), channel_id=1, source_target_pairs={{0,1},{1,2},{2,3},{3,4},{4,5},{5,6},{6,7},{8,9},{9,10},{10,11},{11... | collective-permute-start | bytes 2359304 | tf_op jit(solution)/shard_map/ppermute | solution.py:20
  74.4 19.5 %collective-permute-start.6 = (bf16[3,1024,128]{2,1,0:T(8,128)(2,1)}, bf16[3,1024,128]{2,1,0:T(8,128)(2,1)S(1)}, u32[]{:S(2)}, u32[]{:S(2)}) collective-permute-start(bf16[3,1024,128]{2,1,0:T(8,128)(2,1)} %get-tuple-element.19), channel_id=1, source_target_pairs={{1,0},{2,1},{3,2},{4,3},{5,4},{6,5},{7,6},{9,8},{10,9},{11,10},{12... | collective-permute-start | bytes 2359304 | tf_op jit(solution)/shard_map/ppermute | solution.py:20
  76.3 4.5 %collective-permute-start.7 = (bf16[4,16,128]{2,1,0:T(8,128)(2,1)}, bf16[4,16,128]{2,1,0:T(8,128)(2,1)S(1)}, u32[]{:S(2)}, u32[]{:S(2)}) collective-permute-start(bf16[4,16,128]{2,1,0:T(8,128)(2,1)} %get-tuple-element.20), channel_id=1, source_target_pairs={{0,8},{8,16},{16,24},{1,9},{9,17},{17,25},{2,10},{10,18},{18,26},{... | collective-permute-start | bytes 49160 | tf_op jit(solution)/shard_map/ppermute | solution.py:20
  79.6 4.7 %collective-permute-start.8 = (bf16[4,16,128]{2,1,0:T(8,128)(2,1)}, bf16[4,16,128]{2,1,0:T(8,128)(2,1)S(1)}, u32[]{:S(2)}, u32[]{:S(2)}) collective-permute-start(bf16[4,16,128]{2,1,0:T(8,128)(2,1)} %get-tuple-element.21), channel_id=1, source_target_pairs={{8,0},{16,8},{24,16},{9,1},{17,9},{25,17},{10,2},{18,10},{26,18},{... | collective-permute-start | bytes 49160 | tf_op jit(solution)/shard_map/ppermute | solution.py:20
  80.9 13.1 %copy-start.3 = (bf16[4,16,128]{2,1,0:T(8,128)(2,1)}, bf16[4,16,128]{2,1,0:T(8,128)(2,1)S(1)}, u32[]{:S(2)}) copy-start(bf16[4,16,128]{2,1,0:T(8,128)(2,1)S(1)} %collective-permute-done.7.left_ref) | copy-start | bytes 49156
  84.3 9.7 %copy-start.4 = (bf16[4,16,128]{2,1,0:T(8,128)(2,1)}, bf16[4,16,128]{2,1,0:T(8,128)(2,1)S(1)}, u32[]{:S(2)}) copy-start(bf16[4,16,128]{2,1,0:T(8,128)(2,1)S(1)} %collective-permute-done.8.right_ref) | copy-start | bytes 49156
  84.3 9.6 %collective-permute-start.10 = (bf16[3,32,128]{2,1,0:T(8,128)(2,1)S(1)}, bf16[3,32,128]{2,1,0:T(8,128)(2,1)S(1)}, u32[]{:S(2)}, u32[]{:S(2)}) collective-permute-start(bf16[3,32,128]{2,1,0:T(8,128)(2,1)S(1)} %get-tuple-element.24), channel_id=1, source_target_pairs={{1,0},{2,1},{3,2},{4,3},{5,4},{6,5},{7,6},{9,8},{10,9},{11,10},{12... | collective-permute-start | bytes 73736 | tf_op jit(solution)/shard_map/ppermute | solution.py:20
  86.2 7.7 %collective-permute-start.9 = (bf16[3,32,128]{2,1,0:T(8,128)(2,1)S(1)}, bf16[3,32,128]{2,1,0:T(8,128)(2,1)S(1)}, u32[]{:S(2)}, u32[]{:S(2)}) collective-permute-start(bf16[3,32,128]{2,1,0:T(8,128)(2,1)S(1)} %get-tuple-element.25), channel_id=1, source_target_pairs={{0,1},{1,2},{2,3},{3,4},{4,5},{5,6},{6,7},{8,9},{9,10},{10,11},{11... | collective-permute-start | bytes 73736 | tf_op jit(solution)/shard_map/ppermute | solution.py:20
  93.9 0.6 copy-start.7
  93.9 0.6 copy-start.8
  93.9 0.9 copy-start.1
  93.9 1.1 %copy-start.2 = (bf16[3,1024,128]{2,1,0:T(8,128)(2,1)}, bf16[3,1024,128]{2,1,0:T(8,128)(2,1)S(1)}, u32[]{:S(2)}) copy-start(bf16[3,1024,128]{2,1,0:T(8,128)(2,1)S(1)} %collective-permute-done.6.bottom_ref) | copy-start | bytes 2359300

commit v2 on v1

--- a/solution.py
+++ b/solution.py
@@ -42,86 +42,144 @@
     return math.log2(math.e) / math.sqrt(channels)
 
 
-def column_kernel(own, block, left_ref, right_ref, *refs):
-    line = pl.program_id(0)
-    out_ref = refs[-1]
-    if own:
-        weight_ref, stacked_ref, out_ref = refs
-
-        @pl.when(line == 0)
-        def _():
-            stack_weights(weight_ref, stacked_ref)
-
-    lines_here = out_ref.shape[0] // 2
-    seg_len, channels = left_ref.shape[1:]
+def over_rows(reduce, values, chains=64):
+    count, width = values.shape
+    while count > chains >= 8 and count % chains == 0:
+        values = reduce(values.reshape(count // chains, chains, width), axis=0)
+        count, chains = chains, chains // 8
+    return reduce(values, axis=0, keepdims=True)
+
+
+def column_block(left, right, diagonal_first):
+    block, channels = right.shape
     scale = log2_scale(channels)
+    raw = scores_of(left, right)
     row_ids = lax.broadcasted_iota(jnp.int32, (block, block), 0)
     col_ids = lax.broadcasted_iota(jnp.int32, (block, block), 1)
+    if diagonal_first:
+        parts = [jnp.where(col_ids <= row_ids, raw[:block], NEG), raw[block:]]
+    else:
+        parts = [raw[:-block], jnp.where(col_ids > row_ids, raw[-block:], NEG)]
+    parts = [part for part in parts if part.shape[0]]
+    peak = functools.reduce(jnp.maximum, [over_rows(jnp.max, part) for part in parts])
+    total = sum(over_rows(jnp.sum, jnp.exp2((part - peak) * scale)) for part in parts)
+    return (peak * scale, total)
+
+
+def own_kernel(block, left_ref, right_ref, weight_ref, stacked_ref, out_ref):
+    line = pl.program_id(0)
+    lines_here = out_ref.shape[0] // 2
+    seg_len = left_ref.shape[1]
+
+    @pl.when(line == 0)
+    def _():
+        stack_weights(weight_ref, stacked_ref)
+
     for first in range(0, seg_len, block):
         cols = slice(first, first + block)
-        rows = slice(first, seg_len) if own else slice(0, first + block)
-        raw = scores_of(left_ref[0, rows], right_ref[0, cols])
-        if own:
-            edge = jnp.where(col_ids <= row_ids, raw[:block], NEG)
-            rest = raw[block:]
-        else:
-            edge = jnp.where(col_ids > row_ids, raw[first:], NEG)
-            rest = raw[:first]
-        peak = jnp.max(edge, axis=0, keepdims=True)
-        if rest.shape[0]:
-            peak = jnp.maximum(peak, jnp.max(rest, axis=0, keepdims=True))
-        total = jnp.sum(jnp.exp2((edge - peak) * scale), axis=0, keepdims=True)
-        if rest.shape[0]:
-            total += jnp.sum(jnp.exp2((rest - peak) * scale), axis=0, keepdims=True)
-        out_ref[pl.ds(line, 1), cols] = peak * scale
+        peak, total = column_block(left_ref[0, first:], right_ref[0, cols], True)
+        out_ref[pl.ds(line, 1), cols] = peak
         out_ref[pl.ds(lines_here + line, 1), cols] = total
 
 
-def column_partials(left, right, weight=None):
+def own_partials(left, right, weight):
     lines_here, seg_len, channels = left.shape
-    block = min(256, seg_len)
-    own = weight is not None
-    in_specs = [per_line((seg_len, channels))] * 2
-    out_specs = [whole((2 * lines_here, seg_len))]
-    out_shape = [jax.ShapeDtypeStruct((2 * lines_here, seg_len), jnp.float32)]
-    operands = [left, right]
-    if own:
-        stacked = (weight.shape[0], 12 * channels, 2 * channels)
-        in_specs.append(whole(weight.shape))
-        out_specs.insert(0, whole(stacked))
-        out_shape.insert(0, jax.ShapeDtypeStruct(stacked, weight.dtype))
-        operands.append(weight)
+    stacked = (weight.shape[0], 12 * channels, 2 * channels)
+    part = (2 * lines_here, seg_len)
     return pl.pallas_call(
-        functools.partial(column_kernel, own, block),
+        functools.partial(own_kernel, min(256, seg_len)),
         grid=(lines_here,),
-        in_specs=in_specs,
-        out_specs=out_specs,
-        out_shape=out_shape,
+        in_specs=[per_line((seg_len, channels))] * 2 + [whole(weight.shape)],
+        out_specs=[whole(stacked), whole(part)],
+        out_shape=[
+            jax.ShapeDtypeStruct(stacked, weight.dtype),
+            jax.ShapeDtypeStruct(part, jnp.float32),
+        ],
         compiler_params=params(),
         cost_estimate=pl.CostEstimate(
-            flops=lines_here * seg_len * seg_len * channels,
-            bytes_accessed=4 * lines_here * seg_len * channels,
+            flops=2 * lines_here * seg_len * seg_len * channels,
+            bytes_accessed=8 * lines_here * seg_len * channels,
             transcendentals=lines_here * seg_len * seg_len // 2,
         ),
-        name="column_own" if own else "column_prev",
-    )(*operands)
-
-
-def merged_potential(first, second, lines_here):
-    first_max = jnp.where(first[lines_here:] > 0, first[:lines_here], NEG)
-    second_max = jnp.where(second[lines_here:] > 0, second[:lines_here], NEG)
+        name="column_own",
+    )(left, right, weight)
+
+
+def cross_kernel(block, left_ref, prev_ref, next_ref, right_ref, own_ref, merged_ref, back_ref):
+    line = pl.program_id(0)
+    lines_here = own_ref.shape[0] // 2
+    half = next_ref.shape[1]
+    last = lax.axis_index("seg") == lax.axis_size("seg") - 1
+    top, bottom = pl.ds(line, 1), pl.ds(lines_here + line, 1)
+    for first in range(0, prev_ref.shape[1], block):
+        cols = slice(first, first + block)
+        peak, total = column_block(
+            left_ref[0, : half + first + block], prev_ref[0, cols], False
+        )
+        back_ref[top, cols] = peak
+        back_ref[bottom, cols] = total
+    for first in range(0, half, block):
+        cols = slice(first, first + block)
+        peak, total = column_block(next_ref[0, : first + block], right_ref[0, cols], False)
+        peak = jnp.where(last, NEG, peak)
+        total = jnp.where(last, 0.0, total)
+        own_peak = own_ref[top, cols]
+        merged = jnp.maximum(own_peak, peak)
+        merged_ref[top, cols] = merged
+        merged_ref[bottom, cols] = own_ref[bottom, cols] * jnp.exp2(
+            own_peak - merged
+        ) + total * jnp.exp2(peak - merged)
+    merged_ref[top, half:] = own_ref[top, half:]
+    merged_ref[bottom, half:] = own_ref[bottom, half:]
+
+
+def cross_partials(left, prev_high, next_low, right, own):
+    lines_here, seg_len, channels = left.shape
+    half = next_low.shape[1]
+    back = (2 * lines_here, seg_len - half)
+    return pl.pallas_call(
+        functools.partial(cross_kernel, min(256, half)),
+        grid=(lines_here,),
+        in_specs=[
+            per_line((seg_len, channels)),
+            per_line((seg_len - half, channels)),
+            per_line((half, channels)),
+            per_line((seg_len, channels)),
+            whole(own.shape),
+        ],
+        out_specs=[whole(own.shape), whole(back)],
+        out_shape=[
+            jax.ShapeDtypeStruct(own.shape, jnp.float32),
+            jax.ShapeDtypeStruct(back, jnp.float32),
+        ],
+        compiler_params=params(),
+        cost_estimate=pl.CostEstimate(
+            flops=2 * lines_here * seg_len * seg_len * channels,
+            bytes_accessed=8 * lines_here * seg_len * channels,
+            transcendentals=lines_here * seg_len * seg_len // 2,
+        ),
+        name="column_cross",
+    )(left, prev_high, next_low, right, own)
+
+
+def potential(peak, total):
+    return -(peak + jnp.log2(total))
+
+
+def merged_potential(first, second):
+    first_max = jnp.where(first[1] > 0, first[0], NEG)
+    second_max = jnp.where(second[1] > 0, second[0], NEG)
     peak = jnp.maximum(first_max, second_max)
-    total = first[lines_here:] * jnp.exp2(first_max - peak) + second[
-        lines_here:
-    ] * jnp.exp2(second_max - peak)
-    return -(peak + jnp.log2(total))
+    total = first[1] * jnp.exp2(first_max - peak) + second[1] * jnp.exp2(second_max - peak)
+    return potential(peak, total)
 
 
 def row_kernel(
     block,
     left_ref,
     right_ref,
-    prev_ref,
+    prev_low_ref,
+    prev_high_ref,
     own_ref,
     next_ref,
     before_ref,
@@ -132,71 +190,99 @@
     ext,
     pot,
     sums,
+    raw,
 ):
     line = pl.program_id(0)
     lines_here = own_out.shape[0]
     seg_len, channels = left_ref.shape[1:]
+    half = prev_low_ref.shape[1]
     scale = log2_scale(channels)
 
     @pl.when(line == 0)
     def _():
-        pot[:, seg_len:] = merged_potential(own_ref[...], next_ref[...], lines_here)
-        before = before_ref[...]
-        pot[:, :seg_len] = jnp.where(
-            before[lines_here:] > 0,
-            merged_potential(before, back_ref[...], lines_here),
-            NEG,
-        )
-
-    ext[:seg_len] = prev_ref[0]
+        def parts(ref, start, stop):
+            return ref[:lines_here, start:stop], ref[lines_here:, start:stop]
+
+        rest = seg_len - half
+        pot[:, seg_len : seg_len + half] = potential(*parts(own_ref, 0, half))
+        pot[:, seg_len + half :] = merged_potential(
+            parts(own_ref, half, seg_len), parts(next_ref, 0, rest)
+        )
+        low = parts(before_ref, 0, half)
+        high = parts(before_ref, half, seg_len)
+        pot[:, :half] = jnp.where(low[1] > 0, potential(*low), NEG)
+        pot[:, half:seg_len] = jnp.where(
+            high[1] > 0, merged_potential(high, parts(back_ref, 0, rest)), NEG
+        )
+
+    ext[:half] = prev_low_ref[0]
+    ext[half:seg_len] = prev_high_ref[0]
     ext[seg_len:] = right_ref[0]
     sums[...] = jnp.zeros_like(sums)
-    row_ids = lax.broadcasted_iota(jnp.int32, (block, block), 0)
-    col_ids = lax.broadcasted_iota(jnp.int32, (block, block), 1)
     window = seg_len + block
+    big = 2 * block
+    strip = 16
+    col_ids = lax.broadcasted_iota(jnp.int32, (strip, block), 1)
+    row_ids = lax.broadcasted_iota(jnp.int32, (strip, block), 0)
     col_pot = pot[pl.ds(line, 1), :]
-    for index in range(seg_len // block):
-        first = index * block
-        raw = scores_of(left_ref[0, first : first + block], ext[first : first + window])
-        logits = raw * scale + col_pot[:, first : first + window]
-        logits = jnp.concatenate(
-            [
-                jnp.where(col_ids > row_ids, logits[:, :block], NEG),
-                logits[:, block:seg_len],
-                jnp.where(col_ids <= row_ids, logits[:, seg_len:], NEG),
-            ],
-            axis=1,
-        )
-        peak = jnp.max(logits, axis=1, keepdims=True)
-        terms = jnp.exp2(logits - peak)
-        plan_ref[0, index] = terms.astype(plan_ref.dtype)
-        plan = terms * (1.0 / jnp.sum(terms, axis=1, keepdims=True))
-        sums[:, first : first + window] += jnp.sum(
-            plan.reshape(block // 8, 8, window), axis=0
-        )
+    corner = jnp.zeros((block, block), plan_ref.dtype)
+    for index in range(seg_len // big):
+        start = index * big
+        slot = index % 2
+        raw[slot] = scores_of(
+            left_ref[0, start : start + big], ext[start : start + seg_len + big]
+        )
+        plan_ref[0, index, :block, window:] = corner
+        plan_ref[0, index, block:, :block] = corner
+        for side in range(2):
+            shift = side * block
+            first = start + shift
+            window_pot = col_pot[:, first : first + window]
+            column_sum = jnp.zeros((8, window), jnp.float32)
+            for row in range(0, block, strip):
+                rows = slice(shift + row, shift + row + strip)
+                logits = raw[slot, rows, shift : shift + window] * scale + window_pot
+                logits = jnp.concatenate(
+                    [
+                        jnp.where(col_ids > row_ids + row, logits[:, :block], NEG),
+                        logits[:, block:seg_len],
+                        jnp.where(col_ids <= row_ids + row, logits[:, seg_len:], NEG),
+                    ],
+                    axis=1,
+                )
+                peak = jnp.max(logits, axis=1, keepdims=True)
+                terms = jnp.exp2(logits - peak)
+                plan_ref[0, index, rows, shift : shift + window] = terms.astype(plan_ref.dtype)
+                plan = terms * (1.0 / jnp.sum(terms, axis=1, keepdims=True))
+                column_sum += plan[:8] + plan[8:]
+            sums[:, first : first + window] += column_sum
     totals = jnp.sum(sums[...], axis=0, keepdims=True)
     prev_out[pl.ds(line, 1), :] = totals[:, :seg_len]
     own_out[pl.ds(line, 1), :] = totals[:, seg_len:]
 
 
-def row_pass(left, right, prev, own, following, before, back, block):
+def plan_shape(seg_len, block):
+    return (seg_len // (2 * block), 2 * block, seg_len + 2 * block)
+
+
+def row_pass(left, right, prev_low, prev_high, own, following, before, back, block):
     lines_here, seg_len, channels = left.shape
-    window = seg_len + block
-    part = (2 * lines_here, seg_len)
+    half = prev_low.shape[1]
     marginal = jax.ShapeDtypeStruct((lines_here, seg_len), jnp.float32)
+    plan = plan_shape(seg_len, block)
     return pl.pallas_call(
         functools.partial(row_kernel, block),
         grid=(lines_here,),
-        in_specs=[per_line((seg_len, channels))] * 3 + [whole(part)] * 4,
+        in_specs=[per_line((seg_len, channels))] * 2
+        + [per_line((half, channels)), per_line((seg_len - half, channels))]
+        + [whole(part.shape) for part in (own, following, before, back)],
         out_specs=[
-            per_line((seg_len // block, block, window)),
+            per_line(plan),
             whole((lines_here, seg_len)),
             whole((lines_here, seg_len)),
         ],
         out_shape=[
-            jax.ShapeDtypeStruct(
-                (lines_here, seg_len // block, block, window), jnp.bfloat16
-            ),
+            jax.ShapeDtypeStruct((lines_here,) + plan, jnp.bfloat16),
             marginal,
             marginal,
         ],
@@ -204,19 +290,21 @@
             pltpu.VMEM((2 * seg_len, channels), jnp.bfloat16),
             pltpu.VMEM((lines_here, 2 * seg_len), jnp.float32),
             pltpu.VMEM((8, 2 * seg_len), jnp.float32),
+            pltpu.VMEM((2, 2 * block, seg_len + 2 * block), jnp.float32),
         ],
         compiler_params=params(),
         name="row_pass",
-    )(left, right, prev, own, following, before, back)
+    )(left, right, prev_low, prev_high, own, following, before, back)
 
 
 def transport_kernel(
     block,
-    edge_lines,
+    layers,
     plan_ref,
     left_ref,
     right_ref,
-    prev_ref,
+    prev_low_ref,
+    prev_high_ref,
     own_ref,
     next_ref,
     before_ref,
@@ -232,8 +320,9 @@
     marks,
 ):
     line = pl.program_id(0)
-    layers, lines_here = edge_lines, gain.shape[0]
+    lines_here = gain.shape[0]
     seg_len, channels = left_ref.shape[1:]
+    half = prev_low_ref.shape[1]
     window = seg_len + block
 
     @pl.when(line == 0)
@@ -253,7 +342,8 @@
         )
         marks[...] = values.astype(jnp.float32).astype(jnp.bfloat16)
 
-    ext[:seg_len] = prev_ref[0]
+    ext[:half] = prev_low_ref[0]
+    ext[half:seg_len] = prev_high_ref[0]
     ext[seg_len:] = right_ref[0]
     line_gain = gain[pl.ds(line, 1), :]
     offsets = lax.broadcasted_iota(jnp.int32, (1, block), 1).astype(jnp.float32)
@@ -267,8 +357,7 @@
         ).astype(jnp.bfloat16)
         table = jnp.concatenate([ext[first : first + window], marks[...]], axis=1)
         result = jnp.dot(weights, table, preferred_element_type=jnp.float32)
-        total = result[:, channels : channels + 1]
-        matched = result[:, :channels] * (1.0 / total)
+        matched = result[:, :channels] * (1.0 / result[:, channels : channels + 1])
         state_ref[0, rows] = (matched - left_ref[0, rows].astype(jnp.float32)).astype(
             state_ref.dtype
         )
@@ -287,14 +376,18 @@
         last_ref[...] = state_ref[...]
 
 
-def transport(plan, left, right, prev, own, following, before, back, block, layers):
+def transport(plan, left, right, prev_low, prev_high, own, following, before, back, layers):
     lines_here, seg_len, channels = left.shape
-    window = seg_len + block
+    half = prev_low.shape[1]
+    block = plan.shape[2]
+    edge = jax.ShapeDtypeStruct((layers, seg_len, channels), jnp.bfloat16)
+    side = jax.ShapeDtypeStruct((lines_here, EDGE, channels), jnp.bfloat16)
     return pl.pallas_call(
         functools.partial(transport_kernel, block, layers),
         grid=(lines_here,),
-        in_specs=[per_line((seg_len // block, block, window))]
-        + [per_line((seg_len, channels))] * 3
+        in_specs=[per_line(plan.shape[1:])]
+        + [per_line((seg_len, channels))] * 2
+        + [per_line((half, channels)), per_line((seg_len - half, channels))]
         + [whole((lines_here, seg_len))] * 4,
         out_specs=[
             per_line((seg_len, channels)),
@@ -310,19 +403,19 @@
         out_shape=[
             jax.ShapeDtypeStruct(left.shape, jnp.bfloat16),
             jax.ShapeDtypeStruct((lines_here, seg_len), jnp.float32),
-            jax.ShapeDtypeStruct((layers, seg_len, channels), jnp.bfloat16),
-            jax.ShapeDtypeStruct((layers, seg_len, channels), jnp.bfloat16),
-            jax.ShapeDtypeStruct((lines_here, EDGE, channels), jnp.bfloat16),
-            jax.ShapeDtypeStruct((lines_here, EDGE, channels), jnp.bfloat16),
+            edge,
+            edge,
+            side,
+            side,
         ],
         scratch_shapes=[
             pltpu.VMEM((2 * seg_len, channels), jnp.bfloat16),
             pltpu.VMEM((lines_here, 2 * seg_len), jnp.float32),
-            pltpu.VMEM((window, channels), jnp.bfloat16),
+            pltpu.VMEM((seg_len + block, channels), jnp.bfloat16),
         ],
         compiler_params=params(),
         name="transport",
-    )(plan, left, right, prev, own, following, before, back)
+    )(plan, left, right, prev_low, prev_high, own, following, before, back)
 
 
 def stack_weights(weight_ref, stacked_ref):
@@ -426,20 +519,22 @@
 
 def shards(left_features, right_features, conv_weight, conv_bias):
     seg_len = left_features.shape[1]
-    block = min(128, seg_len)
+    half = seg_len // 2
     layers = conv_weight.shape[0]
-    prev = shifted(right_features, "seg", 1)
-    stacked, own = column_partials(left_features, right_features, conv_weight)
+    prev_high = shifted(right_features[:, half:], "seg", 1)
+    next_low = shifted(left_features[:, :half], "seg", -1)
+    prev_low = shifted(right_features[:, :half], "seg", 1)
+    stacked, own = own_partials(left_features, right_features, conv_weight)
+    own, back = cross_partials(left_features, prev_high, next_low, right_features, own)
     before = shifted(own, "seg", 1)
-    (back,) = column_partials(left_features, prev)
     following = shifted(back, "seg", -1)
     plan, own, back = row_pass(
-        left_features, right_features, prev, own, following, before, back, block
+        left_features, right_features, prev_low, prev_high, own, following, before, back, min(128, half)
     )
     before = shifted(own, "seg", 1)
     following = shifted(back, "seg", -1)
     state, disparity, first, last, low, high = transport(
-        plan, left_features, right_features, prev, own, following, before, back, block, layers
+        plan, left_features, right_features, prev_low, prev_high, own, following, before, back, layers
     )
     bottom = shifted(first, "lines", -1)
     top = shifted(last, "lines", 1)

time: 109 us -> 108 us (level)
  waiting for transfers between devices: 26.5 us -> 13.9 us
  starting transfers between devices: 34 us -> 41.7 us
  local copies, waits for them, and re-layouts: 3.33 us -> 6.16 us
    ppermute x11 -> x13, waiting for transfers between devices: 26.5 us -> 13.9 us  [shifted(): return lax.ppermute(block, axis, route)]
    ppermute x11 -> x13, starting transfers between devices: 34 us -> 41.7 us  [shifted(): return lax.ppermute(block, axis, route)]
    slice x0 -> x2, local copies, waits for them, and re-layouts: none -> 2.36 us  [the longest x1 1.28 us: shards(): prev_high = shifted(right_features[:, half:], 'seg', 1)]
    unnamed x23 -> x27, local copies, waits for them, and re-layouts: 3.31 us -> 3.78 us
  transfers between devices with their start and end apart: 11 -> 13, of which waited for: 5 -> 5; matrix products, arithmetic and copies ran while one was open for 0% -> 1% of each run, Pallas kernels for 10% -> 11%
where the time goes in v2:
time: 108 us; the launch traced here: 107 us
  Pallas kernels  44.5 us (41%)
  starting transfers between devices  41.7 us (39%)
  waiting for transfers between devices  13.9 us (13%)
  local copies, waits for them, and re-layouts  6.16 us (6%)
    ppermute x13, starting transfers between devices, shifted(): return lax.ppermute(block, axis, route)  41.7 us
    ppermute x13, waiting for transfers between devices, shifted(): return lax.ppermute(block, axis, route)  13.9 us
    pallas_call x1, Pallas kernels, conv_layers(): pl.pallas_call(conv_kernel, in_specs=[pl.BlockSpec(memory_space=pltpu.VME...  13.4 us
    pallas_call x1, Pallas kernels, row_pass(): pl.pallas_call(functools.partial(row_kernel, block), grid=(lines_here,),...  10.6 us
    pallas_call x1, Pallas kernels, transport(): pl.pallas_call(functools.partial(transport_kernel, block, layers), grid=(...  8.91 us
    pallas_call x1, Pallas kernels, own_partials(): pl.pallas_call(functools.partial(own_kernel, min(256, seg_len)), grid=(li...  5.99 us
    pallas_call x1, Pallas kernels, cross_partials(): pl.pallas_call(functools.partial(cross_kernel, min(256, half)), grid=(lin...  5.51 us
    unnamed x27, local copies, waits for them, and re-layouts  3.78 us
  transfers between devices with their start and end apart: 13, of which 5 were waited for; matrix products, arithmetic and copies ran while one was open for 1% of the time, Pallas kernels for 11%

profile of v2, /device:TPU:1, one launch (start us, length us, event | category | flops | bytes accessed | tf_op | source)
XLA Modules:
  0.0 107.1 jit_solution(9443490779194053256)
XLA Ops:
  0.6 1.1 %slice.17 = bf16[4,512,128]{2,1,0:T(8,128)(2,1)S(1)} slice(bf16[4,1024,128]{2,1,0:T(8,128)(2,1)} %left_ref.7), slice={[0:4], [0:512], [0:128]} | slice | bytes 1048576 | tf_op jit(solution)/shard_map/slice | solution.py:525
  1.7 1.3 %collective-permute-start.2 = (bf16[4,512,128]{2,1,0:T(8,128)(2,1)S(1)}, bf16[4,512,128]{2,1,0:T(8,128)(2,1)S(1)}, u32[]{:S(2)}, u32[]{:S(2)}) collective-permute-start(bf16[4,512,128]{2,1,0:T(8,128)(2,1)S(1)} %slice.17), channel_id=1, source_target_pairs={{8,0},{16,8},{24,16},{9,1},{17,9},{25,17},{10,2},{18,10},{26,18},{... | collective-permute-start | bytes 1572872 | tf_op jit(solution)/shard_map/ppermute | solution.py:20
  3.0 1.3 %fusion = (bf16[4,512,128]{2,1,0:T(8,128)(2,1)S(1)}, bf16[4,512,128]{2,1,0:T(8,128)(2,1)S(1)}) fusion(bf16[4,1024,128]{2,1,0:T(8,128)(2,1)} %right_ref.7), kind=kLoop, calls=%fused_computation.2 | loop fusion | bytes 2097152 | tf_op jit(solution)/shard_map/slice | solution.py:524
  4.3 4.7 %collective-permute-start.1 = (bf16[4,512,128]{2,1,0:T(8,128)(2,1)S(1)}, bf16[4,512,128]{2,1,0:T(8,128)(2,1)S(1)}, u32[]{:S(2)}, u32[]{:S(2)}) collective-permute-start(bf16[4,512,128]{2,1,0:T(8,128)(2,1)S(1)} %get-tuple-element.28), channel_id=1, source_target_pairs={{0,8},{8,16},{16,24},{1,9},{9,17},{17,25},{2,10},{10,18},{18,26},{... | collective-permute-start | bytes 1572872 | tf_op jit(solution)/shard_map/ppermute | solution.py:20
  9.0 3.4 %collective-permute-start = (bf16[4,512,128]{2,1,0:T(8,128)(2,1)S(1)}, bf16[4,512,128]{2,1,0:T(8,128)(2,1)S(1)}, u32[]{:S(2)}, u32[]{:S(2)}) collective-permute-start(bf16[4,512,128]{2,1,0:T(8,128)(2,1)S(1)} %get-tuple-element.29), channel_id=1, source_target_pairs={{0,8},{8,16},{16,24},{1,9},{9,17},{17,25},{2,10},{10,18},{18,26},{... | collective-permute-start | bytes 1572872 | tf_op jit(solution)/shard_map/ppermute | solution.py:20
  12.4 6.0 %column_own.1 = (bf16[3,1536,256]{2,1,0:T(8,128)(2,1)}, f32[8,1024]{1,0:T(8,128)}) custom-call(bf16[4,1024,128]{2,1,0:T(8,128)(2,1)} %left_ref.7, bf16[4,1024,128]{2,1,0:T(8,128)(2,1)} %right_ref.7, bf16[3,3,3,128,128]{4,3,2,1,0:T(8,128)(2,1)} %weight_ref.1), custom_call_target="tpu_custom_call" | custom-call | flops 1073741824 | bytes 4194304 | tf_op jit(solution)/shard_map/column_own/pallas_call | solution.py:89
  18.4 1.2 %collective-permute-done.1.prev_ref.prev_high_ref = bf16[4,512,128]{2,1,0:T(8,128)(2,1)S(1)} collective-permute-done((bf16[4,512,128]{2,1,0:T(8,128)(2,1)S(1)}, bf16[4,512,128]{2,1,0:T(8,128)(2,1)S(1)}, u32[]{:S(2)}, u32[]{:S(2)}) %collective-permute-start.1) | collective-permute-done | bytes 524320 | tf_op jit(solution)/shard_map/ppermute | solution.py:20
  19.5 0.8 copy-done
  20.4 5.5 %column_cross.1 = (f32[8,1024]{1,0:T(8,128)}, f32[8,512]{1,0:T(8,128)}) custom-call(bf16[4,1024,128]{2,1,0:T(8,128)(2,1)} %left_ref.7, bf16[4,512,128]{2,1,0:T(8,128)(2,1)} %copy-done, bf16[4,512,128]{2,1,0:T(8,128)(2,1)} %copy-done.12, bf16[4,1024,128]{2,1,0:T(8,128)(2,1)} %right_ref.7, f32[8,1024]{1,0:T(8,128)} %get-tuple-element.15.own_ref), custom_call_target="tpu_custom_call" | custom-call | flops 1073741824 | bytes 4194304 | tf_op jit(solution)/shard_map/column_cross/pallas_call | solution.py:140
  25.9 4.1 %collective-permute-start.4 = (f32[8,1024]{1,0:T(8,128)}, f32[8,1024]{1,0:T(8,128)S(1)}, u32[]{:S(2)}, u32[]{:S(2)}) collective-permute-start(f32[8,1024]{1,0:T(8,128)} %get-tuple-element.16.own_ref), channel_id=1, source_target_pairs={{0,8},{8,16},{16,24},{1,9},{9,17},{17,25},{2,10},{10,18},{18,26},{... | collective-permute-start | bytes 98312 | tf_op jit(solution)/shard_map/ppermute | solution.py:20
  30.0 1.3 %collective-permute-start.3 = (f32[8,512]{1,0:T(8,128)}, f32[8,512]{1,0:T(8,128)S(1)}, u32[]{:S(2)}, u32[]{:S(2)}) collective-permute-start(f32[8,512]{1,0:T(8,128)} %get-tuple-element.17.back_ref), channel_id=1, source_target_pairs={{8,0},{16,8},{24,16},{9,1},{17,9},{25,17},{10,2},{18,10},{26,18},{... | collective-permute-start | bytes 49160 | tf_op jit(solution)/shard_map/ppermute | solution.py:20
  31.3 3.4 %collective-permute-done.3.next_ref = f32[8,512]{1,0:T(8,128)S(1)} collective-permute-done((f32[8,512]{1,0:T(8,128)}, f32[8,512]{1,0:T(8,128)S(1)}, u32[]{:S(2)}, u32[]{:S(2)}) %collective-permute-start.3) | collective-permute-done | bytes 16416 | tf_op jit(solution)/shard_map/ppermute | solution.py:20
  34.7 0.6 copy-done.11
  35.3 0.6 copy-done.6
  35.9 10.6 %row_pass.1 = (bf16[4,4,256,1280]{3,2,1,0:T(8,128)(2,1)}, f32[4,1024]{1,0:T(4,128)}, f32[4,1024]{1,0:T(4,128)}) custom-call(bf16[4,1024,128]{2,1,0:T(8,128)(2,1)} %left_ref.7, bf16[4,1024,128]{2,1,0:T(8,128)(2,1)} %right_ref.7, bf16[4,512,128]{2,1,0:T(8,128)(2,1)} %copy-done.1, bf16[4,512,128]{2,1,0:T(8,128)(2,1)} %copy-done, ...), custom_call_target="tpu_custom_call" | custom-call | tf_op jit(solution)/shard_map/row_pass/pallas_call | solution.py:273
  46.5 3.3 %collective-permute-start.6 = (f32[4,1024]{1,0:T(4,128)}, f32[4,1024]{1,0:T(4,128)S(1)}, u32[]{:S(2)}, u32[]{:S(2)}) collective-permute-start(f32[4,1024]{1,0:T(4,128)} %get-tuple-element.19.own_ref), channel_id=1, source_target_pairs={{0,8},{8,16},{16,24},{1,9},{9,17},{17,25},{2,10},{10,18},{18,26},{... | collective-permute-start | bytes 49160 | tf_op jit(solution)/shard_map/ppermute | solution.py:20
  49.8 1.3 %collective-permute-start.5 = (f32[4,1024]{1,0:T(4,128)}, f32[4,1024]{1,0:T(4,128)S(1)}, u32[]{:S(2)}, u32[]{:S(2)}) collective-permute-start(f32[4,1024]{1,0:T(4,128)} %get-tuple-element.20.back_ref), channel_id=1, source_target_pairs={{8,0},{16,8},{24,16},{9,1},{17,9},{25,17},{10,2},{18,10},{26,18},{... | collective-permute-start | bytes 49160 | tf_op jit(solution)/shard_map/ppermute | solution.py:20
  51.1 3.4 %collective-permute-done.5.next_ref = f32[4,1024]{1,0:T(4,128)S(1)} collective-permute-done((f32[4,1024]{1,0:T(4,128)}, f32[4,1024]{1,0:T(4,128)S(1)}, u32[]{:S(2)}, u32[]{:S(2)}) %collective-permute-start.5) | collective-permute-done | bytes 16416 | tf_op jit(solution)/shard_map/ppermute | solution.py:20
  54.5 0.6 copy-done.10
  55.1 8.9 %transport.1 = (bf16[4,1024,128]{2,1,0:T(8,128)(2,1)}, f32[4,1024]{1,0:T(4,128)}, bf16[3,1024,128]{2,1,0:T(8,128)(2,1)}, bf16[3,1024,128]{2,1,0:T(8,128)(2,1)}, ...) custom-call(bf16[4,4,256,1280]{3,2,1,0:T(8,128)(2,1)} %get-tuple-element.18.plan_ref, ...), custom_call_target="tpu_custom_call" | custom-call | tf_op jit(solution)/shard_map/transport/pallas_call | solution.py:385
  64.0 8.9 %collective-permute-start.7 = (bf16[3,1024,128]{2,1,0:T(8,128)(2,1)}, bf16[3,1024,128]{2,1,0:T(8,128)(2,1)S(1)}, u32[]{:S(2)}, u32[]{:S(2)}) collective-permute-start(bf16[3,1024,128]{2,1,0:T(8,128)(2,1)} %get-tuple-element.22), channel_id=1, source_target_pairs={{0,1},{1,2},{2,3},{3,4},{4,5},{5,6},{6,7},{8,9},{9,10},{10,11},{11... | collective-permute-start | bytes 2359304 | tf_op jit(solution)/shard_map/ppermute | solution.py:20
  72.9 1.9 %collective-permute-start.8 = (bf16[3,1024,128]{2,1,0:T(8,128)(2,1)}, bf16[3,1024,128]{2,1,0:T(8,128)(2,1)S(1)}, u32[]{:S(2)}, u32[]{:S(2)}) collective-permute-start(bf16[3,1024,128]{2,1,0:T(8,128)(2,1)} %get-tuple-element.23), channel_id=1, source_target_pairs={{1,0},{2,1},{3,2},{4,3},{5,4},{6,5},{7,6},{9,8},{10,9},{11,10},{12... | collective-permute-start | bytes 2359304 | tf_op jit(solution)/shard_map/ppermute | solution.py:20
  74.9 3.2 %collective-permute-start.9 = (bf16[4,16,128]{2,1,0:T(8,128)(2,1)}, bf16[4,16,128]{2,1,0:T(8,128)(2,1)S(1)}, u32[]{:S(2)}, u32[]{:S(2)}) collective-permute-start(bf16[4,16,128]{2,1,0:T(8,128)(2,1)} %get-tuple-element.24), channel_id=1, source_target_pairs={{0,8},{8,16},{16,24},{1,9},{9,17},{17,25},{2,10},{10,18},{18,26},{... | collective-permute-start | bytes 49160 | tf_op jit(solution)/shard_map/ppermute | solution.py:20
  78.1 1.3 %collective-permute-start.10 = (bf16[4,16,128]{2,1,0:T(8,128)(2,1)}, bf16[4,16,128]{2,1,0:T(8,128)(2,1)S(1)}, u32[]{:S(2)}, u32[]{:S(2)}) collective-permute-start(bf16[4,16,128]{2,1,0:T(8,128)(2,1)} %get-tuple-element.25), channel_id=1, source_target_pairs={{8,0},{16,8},{24,16},{9,1},{17,9},{25,17},{10,2},{18,10},{26,18},{... | collective-permute-start | bytes 49160 | tf_op jit(solution)/shard_map/ppermute | solution.py:20
  79.4 3.4 %collective-permute-done.10.right_ref = bf16[4,16,128]{2,1,0:T(8,128)(2,1)S(1)} collective-permute-done((bf16[4,16,128]{2,1,0:T(8,128)(2,1)}, bf16[4,16,128]{2,1,0:T(8,128)(2,1)S(1)}, u32[]{:S(2)}, u32[]{:S(2)}) %collective-permute-start.10) | collective-permute-done | bytes 16416 | tf_op jit(solution)/shard_map/ppermute | solution.py:20
  82.8 1.9 %collective-permute-start.12 = (bf16[3,32,128]{2,1,0:T(8,128)(2,1)S(1)}, bf16[3,32,128]{2,1,0:T(8,128)(2,1)S(1)}, u32[]{:S(2)}, u32[]{:S(2)}) collective-permute-start(bf16[3,32,128]{2,1,0:T(8,128)(2,1)S(1)} %get-tuple-element.30), channel_id=1, source_target_pairs={{1,0},{2,1},{3,2},{4,3},{5,4},{6,5},{7,6},{9,8},{10,9},{11,10},{12... | collective-permute-start | bytes 73736 | tf_op jit(solution)/shard_map/ppermute | solution.py:20
  84.7 5.1 %collective-permute-start.11 = (bf16[3,32,128]{2,1,0:T(8,128)(2,1)S(1)}, bf16[3,32,128]{2,1,0:T(8,128)(2,1)S(1)}, u32[]{:S(2)}, u32[]{:S(2)}) collective-permute-start(bf16[3,32,128]{2,1,0:T(8,128)(2,1)S(1)} %get-tuple-element.31), channel_id=1, source_target_pairs={{0,1},{1,2},{2,3},{3,4},{4,5},{5,6},{6,7},{8,9},{9,10},{10,11},{11... | collective-permute-start | bytes 73736 | tf_op jit(solution)/shard_map/ppermute | solution.py:20
  89.8 2.6 %collective-permute-done.12.corner_bottom_ref = bf16[3,32,128]{2,1,0:T(8,128)(2,1)S(1)} collective-permute-done((bf16[3,32,128]{2,1,0:T(8,128)(2,1)S(1)}, bf16[3,32,128]{2,1,0:T(8,128)(2,1)S(1)}, u32[]{:S(2)}, u32[]{:S(2)}) %collective-permute-start.12) | collective-permute-done | bytes 24608 | tf_op jit(solution)/shard_map/ppermute | solution.py:20
  92.5 0.5 copy-done.7
  93.0 0.3 copy-done.2
  93.3 0.3 copy-done.3
  93.6 13.4 %conv_layers.1 = bf16[4,1024,128]{2,1,0:T(8,128)(2,1)} custom-call(bf16[4,1024,128]{2,1,0:T(8,128)(2,1)} %get-tuple-element.21.state_ref, bf16[3,1024,128]{2,1,0:T(8,128)(2,1)} %copy-done.2, bf16[3,1024,128]{2,1,0:T(8,128)(2,1)} %copy-done.3, bf16[4,16,128]{2,1,0:T(8,128)(2,1)} %copy-done.4, bf16[4,16,128]{2,1,0:T(8,128)(2,1)} %copy-done.5, ...), custom_call_target="tpu_custom_call" | custom-call | tf_op jit(solution)/shard_map/conv_layers/pallas_call | solution.py:509
  (30 shorter events, 0.1 us)
Async XLA Ops:
  1.7 16.6 %collective-permute-start.2 = (bf16[4,512,128]{2,1,0:T(8,128)(2,1)S(1)}, bf16[4,512,128]{2,1,0:T(8,128)(2,1)S(1)}, u32[]{:S(2)}, u32[]{:S(2)}) collective-permute-start(bf16[4,512,128]{2,1,0:T(8,128)(2,1)S(1)} %slice.17), channel_id=1, source_target_pairs={{8,0},{16,8},{24,16},{9,1},{17,9},{25,17},{10,2},{18,10},{26,18},{... | collective-permute-start | bytes 1572872 | tf_op jit(solution)/shard_map/ppermute | solution.py:20
  4.3 15.2 %collective-permute-start.1 = (bf16[4,512,128]{2,1,0:T(8,128)(2,1)S(1)}, bf16[4,512,128]{2,1,0:T(8,128)(2,1)S(1)}, u32[]{:S(2)}, u32[]{:S(2)}) collective-permute-start(bf16[4,512,128]{2,1,0:T(8,128)(2,1)S(1)} %get-tuple-element.28), channel_id=1, source_target_pairs={{0,8},{8,16},{16,24},{1,9},{9,17},{17,25},{2,10},{10,18},{18,26},{... | collective-permute-start | bytes 1572872 | tf_op jit(solution)/shard_map/ppermute | solution.py:20
  9.0 22.3 %collective-permute-start = (bf16[4,512,128]{2,1,0:T(8,128)(2,1)S(1)}, bf16[4,512,128]{2,1,0:T(8,128)(2,1)S(1)}, u32[]{:S(2)}, u32[]{:S(2)}) collective-permute-start(bf16[4,512,128]{2,1,0:T(8,128)(2,1)S(1)} %get-tuple-element.29), channel_id=1, source_target_pairs={{0,8},{8,16},{16,24},{1,9},{9,17},{17,25},{2,10},{10,18},{18,26},{... | collective-permute-start | bytes 1572872 | tf_op jit(solution)/shard_map/ppermute | solution.py:20
  18.4 1.2 %copy-start.12 = (bf16[4,512,128]{2,1,0:T(8,128)(2,1)}, bf16[4,512,128]{2,1,0:T(8,128)(2,1)S(1)}, u32[]{:S(2)}) copy-start(bf16[4,512,128]{2,1,0:T(8,128)(2,1)S(1)} %collective-permute-done.2.next_ref) | copy-start | bytes 1572868
  19.5 0.8 copy-start
  25.9 8.8 %collective-permute-start.4 = (f32[8,1024]{1,0:T(8,128)}, f32[8,1024]{1,0:T(8,128)S(1)}, u32[]{:S(2)}, u32[]{:S(2)}) collective-permute-start(f32[8,1024]{1,0:T(8,128)} %get-tuple-element.16.own_ref), channel_id=1, source_target_pairs={{0,8},{8,16},{16,24},{1,9},{9,17},{17,25},{2,10},{10,18},{18,26},{... | collective-permute-start | bytes 98312 | tf_op jit(solution)/shard_map/ppermute | solution.py:20
  30.0 4.7 %collective-permute-start.3 = (f32[8,512]{1,0:T(8,128)}, f32[8,512]{1,0:T(8,128)S(1)}, u32[]{:S(2)}, u32[]{:S(2)}) collective-permute-start(f32[8,512]{1,0:T(8,128)} %get-tuple-element.17.back_ref), channel_id=1, source_target_pairs={{8,0},{16,8},{24,16},{9,1},{17,9},{25,17},{10,2},{18,10},{26,18},{... | collective-permute-start | bytes 49160 | tf_op jit(solution)/shard_map/ppermute | solution.py:20
  31.3 3.4 %copy-start.1 = (bf16[4,512,128]{2,1,0:T(8,128)(2,1)}, bf16[4,512,128]{2,1,0:T(8,128)(2,1)S(1)}, u32[]{:S(2)}) copy-start(bf16[4,512,128]{2,1,0:T(8,128)(2,1)S(1)} %collective-permute-done.prev_low_ref) | copy-start | bytes 1572868
  34.7 0.6 copy-start.11
  35.3 0.6 copy-start.6
  46.5 4.6 %collective-permute-start.6 = (f32[4,1024]{1,0:T(4,128)}, f32[4,1024]{1,0:T(4,128)S(1)}, u32[]{:S(2)}, u32[]{:S(2)}) collective-permute-start(f32[4,1024]{1,0:T(4,128)} %get-tuple-element.19.own_ref), channel_id=1, source_target_pairs={{0,8},{8,16},{16,24},{1,9},{9,17},{17,25},{2,10},{10,18},{18,26},{... | collective-permute-start | bytes 49160 | tf_op jit(solution)/shard_map/ppermute | solution.py:20
  49.8 4.7 %collective-permute-start.5 = (f32[4,1024]{1,0:T(4,128)}, f32[4,1024]{1,0:T(4,128)S(1)}, u32[]{:S(2)}, u32[]{:S(2)}) collective-permute-start(f32[4,1024]{1,0:T(4,128)} %get-tuple-element.20.back_ref), channel_id=1, source_target_pairs={{8,0},{16,8},{24,16},{9,1},{17,9},{25,17},{10,2},{18,10},{26,18},{... | collective-permute-start | bytes 49160 | tf_op jit(solution)/shard_map/ppermute | solution.py:20
  51.1 3.4 %copy-start.9 = (f32[4,1024]{1,0:T(4,128)}, f32[4,1024]{1,0:T(4,128)S(1)}, u32[]{:S(2)}) copy-start(f32[4,1024]{1,0:T(4,128)S(1)} %collective-permute-done.6.before_ref) | copy-start | bytes 49156
  54.5 0.6 copy-start.10
  64.0 28.4 %collective-permute-start.7 = (bf16[3,1024,128]{2,1,0:T(8,128)(2,1)}, bf16[3,1024,128]{2,1,0:T(8,128)(2,1)S(1)}, u32[]{:S(2)}, u32[]{:S(2)}) collective-permute-start(bf16[3,1024,128]{2,1,0:T(8,128)(2,1)} %get-tuple-element.22), channel_id=1, source_target_pairs={{0,1},{1,2},{2,3},{3,4},{4,5},{5,6},{6,7},{8,9},{9,10},{10,11},{11... | collective-permute-start | bytes 2359304 | tf_op jit(solution)/shard_map/ppermute | solution.py:20
  72.9 19.5 %collective-permute-start.8 = (bf16[3,1024,128]{2,1,0:T(8,128)(2,1)}, bf16[3,1024,128]{2,1,0:T(8,128)(2,1)S(1)}, u32[]{:S(2)}, u32[]{:S(2)}) collective-permute-start(bf16[3,1024,128]{2,1,0:T(8,128)(2,1)} %get-tuple-element.23), channel_id=1, source_target_pairs={{1,0},{2,1},{3,2},{4,3},{5,4},{6,5},{7,6},{9,8},{10,9},{11,10},{12... | collective-permute-start | bytes 2359304 | tf_op jit(solution)/shard_map/ppermute | solution.py:20
  74.9 4.6 %collective-permute-start.9 = (bf16[4,16,128]{2,1,0:T(8,128)(2,1)}, bf16[4,16,128]{2,1,0:T(8,128)(2,1)S(1)}, u32[]{:S(2)}, u32[]{:S(2)}) collective-permute-start(bf16[4,16,128]{2,1,0:T(8,128)(2,1)} %get-tuple-element.24), channel_id=1, source_target_pairs={{0,8},{8,16},{16,24},{1,9},{9,17},{17,25},{2,10},{10,18},{18,26},{... | collective-permute-start | bytes 49160 | tf_op jit(solution)/shard_map/ppermute | solution.py:20
  78.1 4.7 %collective-permute-start.10 = (bf16[4,16,128]{2,1,0:T(8,128)(2,1)}, bf16[4,16,128]{2,1,0:T(8,128)(2,1)S(1)}, u32[]{:S(2)}, u32[]{:S(2)}) collective-permute-start(bf16[4,16,128]{2,1,0:T(8,128)(2,1)} %get-tuple-element.25), channel_id=1, source_target_pairs={{8,0},{16,8},{24,16},{9,1},{17,9},{25,17},{10,2},{18,10},{26,18},{... | collective-permute-start | bytes 49160 | tf_op jit(solution)/shard_map/ppermute | solution.py:20
  79.4 13.0 %copy-start.4 = (bf16[4,16,128]{2,1,0:T(8,128)(2,1)}, bf16[4,16,128]{2,1,0:T(8,128)(2,1)S(1)}, u32[]{:S(2)}) copy-start(bf16[4,16,128]{2,1,0:T(8,128)(2,1)S(1)} %collective-permute-done.9.left_ref) | copy-start | bytes 49156
  82.8 9.7 %copy-start.5 = (bf16[4,16,128]{2,1,0:T(8,128)(2,1)}, bf16[4,16,128]{2,1,0:T(8,128)(2,1)S(1)}, u32[]{:S(2)}) copy-start(bf16[4,16,128]{2,1,0:T(8,128)(2,1)S(1)} %collective-permute-done.10.right_ref) | copy-start | bytes 49156
  82.8 9.6 %collective-permute-start.12 = (bf16[3,32,128]{2,1,0:T(8,128)(2,1)S(1)}, bf16[3,32,128]{2,1,0:T(8,128)(2,1)S(1)}, u32[]{:S(2)}, u32[]{:S(2)}) collective-permute-start(bf16[3,32,128]{2,1,0:T(8,128)(2,1)S(1)} %get-tuple-element.30), channel_id=1, source_target_pairs={{1,0},{2,1},{3,2},{4,3},{5,4},{6,5},{7,6},{9,8},{10,9},{11,10},{12... | collective-permute-start | bytes 73736 | tf_op jit(solution)/shard_map/ppermute | solution.py:20
  84.7 7.7 %collective-permute-start.11 = (bf16[3,32,128]{2,1,0:T(8,128)(2,1)S(1)}, bf16[3,32,128]{2,1,0:T(8,128)(2,1)S(1)}, u32[]{:S(2)}, u32[]{:S(2)}) collective-permute-start(bf16[3,32,128]{2,1,0:T(8,128)(2,1)S(1)} %get-tuple-element.31), channel_id=1, source_target_pairs={{0,1},{1,2},{2,3},{3,4},{4,5},{5,6},{6,7},{8,9},{9,10},{10,11},{11... | collective-permute-start | bytes 73736 | tf_op jit(solution)/shard_map/ppermute | solution.py:20
  92.4 0.6 copy-start.7
  92.4 0.6 copy-start.8
  92.4 0.9 copy-start.2
  92.4 1.2 %copy-start.3 = (bf16[3,1024,128]{2,1,0:T(8,128)(2,1)}, bf16[3,1024,128]{2,1,0:T(8,128)(2,1)S(1)}, u32[]{:S(2)}) copy-start(bf16[3,1024,128]{2,1,0:T(8,128)(2,1)S(1)} %collective-permute-done.8.bottom_ref) | copy-start | bytes 2359300

commit v3 on v2

--- a/solution.py
+++ b/solution.py
@@ -174,6 +174,49 @@
     return potential(peak, total)
 
 
+def split(values, parts):
+    pieces = []
+    for _ in range(parts):
+        piece = values.astype(jnp.bfloat16).astype(jnp.float32)
+        pieces.append(piece)
+        values = values - piece
+    return pieces
+
+
+SHIFT = 2
+
+
+def potential_lanes(pot, channels):
+    lines_here, count = pot.shape
+    parts = split(pot, 3)
+    filler = jnp.zeros((channels - 3 * lines_here, count), jnp.float32)
+    lanes = jnp.concatenate(parts + [filler], axis=0).T
+    lane = lax.broadcasted_iota(jnp.int32, lanes.shape, 1)
+    return jnp.where(lane >= channels - SHIFT, -1.0, lanes).astype(jnp.bfloat16)
+
+
+def line_lanes(line, lines_here, shape):
+    lane = lax.broadcasted_iota(jnp.int32, shape, 1)
+    mine = jnp.zeros(shape, jnp.float32)
+    for part in range(3):
+        mine = jnp.where(lane == part * lines_here + line, 1.0, mine)
+    return mine
+
+
+def banded(values, row, block):
+    rows, window = values.shape
+    col_ids = lax.broadcasted_iota(jnp.int32, (rows, block), 1)
+    row_ids = lax.broadcasted_iota(jnp.int32, (rows, block), 0) + row
+    return jnp.concatenate(
+        [
+            jnp.where(col_ids > row_ids, values[:, :block], NEG),
+            values[:, block : window - block],
+            jnp.where(col_ids <= row_ids, values[:, window - block :], NEG),
+        ],
+        axis=1,
+    )
+
+
 def row_kernel(
     block,
     left_ref,
@@ -184,11 +227,11 @@
     next_ref,
     before_ref,
     back_ref,
-    plan_ref,
+    pot,
+    lanes_ref,
     own_out,
     prev_out,
     ext,
-    pot,
     sums,
     raw,
 ):
@@ -214,62 +257,50 @@
         pot[:, half:seg_len] = jnp.where(
             high[1] > 0, merged_potential(high, parts(back_ref, 0, rest)), NEG
         )
-
-    ext[:half] = prev_low_ref[0]
-    ext[half:seg_len] = prev_high_ref[0]
-    ext[seg_len:] = right_ref[0]
+        ext[:, channels:] = potential_lanes(pot[...] * (1.0 / scale), channels)
+
+    ext[:half, :channels] = prev_low_ref[0]
+    ext[half:seg_len, :channels] = prev_high_ref[0]
+    ext[seg_len:, :channels] = right_ref[0]
     sums[...] = jnp.zeros_like(sums)
     window = seg_len + block
     big = 2 * block
     strip = 16
-    col_ids = lax.broadcasted_iota(jnp.int32, (strip, block), 1)
-    row_ids = lax.broadcasted_iota(jnp.int32, (strip, block), 0)
-    col_pot = pot[pl.ds(line, 1), :]
-    corner = jnp.zeros((block, block), plan_ref.dtype)
+    mine = line_lanes(line, lines_here, (big, channels)).astype(jnp.bfloat16)
+    strip_lanes = line_lanes(line, lines_here, (strip, channels))
+    lane = lax.broadcasted_iota(jnp.int32, (strip, channels), 1)
     for index in range(seg_len // big):
         start = index * big
         slot = index % 2
         raw[slot] = scores_of(
-            left_ref[0, start : start + big], ext[start : start + seg_len + big]
-        )
-        plan_ref[0, index, :block, window:] = corner
-        plan_ref[0, index, block:, :block] = corner
+            jnp.concatenate([left_ref[0, start : start + big], mine], axis=1),
+            ext[start : start + seg_len + big],
+        )
         for side in range(2):
             shift = side * block
             first = start + shift
-            window_pot = col_pot[:, first : first + window]
             column_sum = jnp.zeros((8, window), jnp.float32)
             for row in range(0, block, strip):
                 rows = slice(shift + row, shift + row + strip)
-                logits = raw[slot, rows, shift : shift + window] * scale + window_pot
-                logits = jnp.concatenate(
-                    [
-                        jnp.where(col_ids > row_ids + row, logits[:, :block], NEG),
-                        logits[:, block:seg_len],
-                        jnp.where(col_ids <= row_ids + row, logits[:, seg_len:], NEG),
-                    ],
-                    axis=1,
-                )
+                logits = banded(raw[slot, rows, shift : shift + window], row, block)
                 peak = jnp.max(logits, axis=1, keepdims=True)
-                terms = jnp.exp2(logits - peak)
-                plan_ref[0, index, rows, shift : shift + window] = terms.astype(plan_ref.dtype)
+                terms = jnp.exp2((logits - peak) * scale)
                 plan = terms * (1.0 / jnp.sum(terms, axis=1, keepdims=True))
                 column_sum += plan[:8] + plan[8:]
+                lanes = strip_lanes
+                for part, piece in enumerate(split(peak, SHIFT)):
+                    lanes = jnp.where(lane == channels - SHIFT + part, piece, lanes)
+                lanes_ref[0, first + row : first + row + strip] = lanes.astype(jnp.bfloat16)
             sums[:, first : first + window] += column_sum
     totals = jnp.sum(sums[...], axis=0, keepdims=True)
     prev_out[pl.ds(line, 1), :] = totals[:, :seg_len]
     own_out[pl.ds(line, 1), :] = totals[:, seg_len:]
 
 
-def plan_shape(seg_len, block):
-    return (seg_len // (2 * block), 2 * block, seg_len + 2 * block)
-
-
 def row_pass(left, right, prev_low, prev_high, own, following, before, back, block):
     lines_here, seg_len, channels = left.shape
     half = prev_low.shape[1]
     marginal = jax.ShapeDtypeStruct((lines_here, seg_len), jnp.float32)
-    plan = plan_shape(seg_len, block)
     return pl.pallas_call(
         functools.partial(row_kernel, block),
         grid=(lines_here,),
@@ -277,18 +308,19 @@
         + [per_line((half, channels)), per_line((seg_len - half, channels))]
         + [whole(part.shape) for part in (own, following, before, back)],
         out_specs=[
-            per_line(plan),
+            whole((lines_here, 2 * seg_len)),
+            per_line((seg_len, channels)),
             whole((lines_here, seg_len)),
             whole((lines_here, seg_len)),
         ],
         out_shape=[
-            jax.ShapeDtypeStruct((lines_here,) + plan, jnp.bfloat16),
+            jax.ShapeDtypeStruct((lines_here, 2 * seg_len), jnp.float32),
+            jax.ShapeDtypeStruct(left.shape, jnp.bfloat16),
             marginal,
             marginal,
         ],
         scratch_shapes=[
-            pltpu.VMEM((2 * seg_len, channels), jnp.bfloat16),
-            pltpu.VMEM((lines_here, 2 * seg_len), jnp.float32),
+            pltpu.VMEM((2 * seg_len, 2 * channels), jnp.bfloat16),
             pltpu.VMEM((8, 2 * seg_len), jnp.float32),
             pltpu.VMEM((2, 2 * block, seg_len + 2 * block), jnp.float32),
         ],
@@ -300,7 +332,8 @@
 def transport_kernel(
     block,
     layers,
-    plan_ref,
+    pot_ref,
+    lanes_ref,
     left_ref,
     right_ref,
     prev_low_ref,
@@ -316,22 +349,24 @@
     low_ref,
     high_ref,
     ext,
-    gain,
     marks,
+    raw,
 ):
     line = pl.program_id(0)
-    lines_here = gain.shape[0]
+    lines_here = pot_ref.shape[0]
     seg_len, channels = left_ref.shape[1:]
     half = prev_low_ref.shape[1]
-    window = seg_len + block
+    scale = log2_scale(channels)
+    big = 2 * block
+    window = seg_len + big
 
     @pl.when(line == 0)
     def _():
-        gain[:, seg_len:] = 1.0 / (own_ref[...] + next_ref[...])
-        total = before_ref[...] + back_ref[...]
-        gain[:, :seg_len] = jnp.where(
-            total > 0, 1.0 / jnp.where(total > 0, total, 1.0), 0.0
-        )
+        total = jnp.concatenate(
+            [before_ref[...] + back_ref[...], own_ref[...] + next_ref[...]], axis=1
+        )
+        pot = jnp.where(total > 0, pot_ref[...] - jnp.log2(total), NEG)
+        ext[:, channels:] = potential_lanes(pot * (1.0 / scale), channels)
         lane = lax.broadcasted_iota(jnp.int32, (window, channels), 1)
         distance = seg_len - lax.broadcasted_iota(jnp.int32, (window, channels), 0)
         low = jnp.bitwise_and(distance, 15)
@@ -342,20 +377,30 @@
         )
         marks[...] = values.astype(jnp.float32).astype(jnp.bfloat16)
 
-    ext[:half] = prev_low_ref[0]
-    ext[half:seg_len] = prev_high_ref[0]
-    ext[seg_len:] = right_ref[0]
-    line_gain = gain[pl.ds(line, 1), :]
-    offsets = lax.broadcasted_iota(jnp.int32, (1, block), 1).astype(jnp.float32)
+    ext[:half, :channels] = prev_low_ref[0]
+    ext[half:seg_len, :channels] = prev_high_ref[0]
+    ext[seg_len:, :channels] = right_ref[0]
+    offsets = lax.broadcasted_iota(jnp.int32, (1, big), 1).astype(jnp.float32)
+    corner = jnp.zeros((block, block), jnp.bfloat16)
     disparity = []
-    for index in range(seg_len // block):
-        first = index * block
-        rows = slice(first, first + block)
-        weights = (
-            plan_ref[0, index].astype(jnp.float32)
-            * line_gain[:, first : first + window]
-        ).astype(jnp.bfloat16)
-        table = jnp.concatenate([ext[first : first + window], marks[...]], axis=1)
+    for index in range(seg_len // big):
+        first = index * big
+        slot = index % 2
+        rows = slice(first, first + big)
+        raw[slot] = scores_of(
+            jnp.concatenate([left_ref[0, rows], lanes_ref[0, rows]], axis=1),
+            ext[first : first + window],
+        )
+        upper = jnp.exp2(banded(raw[slot, :block, : window - block], 0, block) * scale)
+        lower = jnp.exp2(banded(raw[slot, block:, block:], 0, block) * scale)
+        weights = jnp.concatenate(
+            [
+                jnp.concatenate([upper.astype(jnp.bfloat16), corner], axis=1),
+                jnp.concatenate([corner, lower.astype(jnp.bfloat16)], axis=1),
+            ],
+            axis=0,
+        )
+        table = jnp.concatenate([ext[first : first + window, :channels], marks[...]], axis=1)
         result = jnp.dot(weights, table, preferred_element_type=jnp.float32)
         matched = result[:, :channels] * (1.0 / result[:, channels : channels + 1])
         state_ref[0, rows] = (matched - left_ref[0, rows].astype(jnp.float32)).astype(
@@ -376,17 +421,16 @@
         last_ref[...] = state_ref[...]
 
 
-def transport(plan, left, right, prev_low, prev_high, own, following, before, back, layers):
+def transport(pot, lanes, left, right, prev_low, prev_high, own, following, before, back, block, layers):
     lines_here, seg_len, channels = left.shape
     half = prev_low.shape[1]
-    block = plan.shape[2]
     edge = jax.ShapeDtypeStruct((layers, seg_len, channels), jnp.bfloat16)
     side = jax.ShapeDtypeStruct((lines_here, EDGE, channels), jnp.bfloat16)
     return pl.pallas_call(
         functools.partial(transport_kernel, block, layers),
         grid=(lines_here,),
-        in_specs=[per_line(plan.shape[1:])]
-        + [per_line((seg_len, channels))] * 2
+        in_specs=[whole(pot.shape)]
+        + [per_line((seg_len, channels))] * 3
         + [per_line((half, channels)), per_line((seg_len - half, channels))]
         + [whole((lines_here, seg_len))] * 4,
         out_specs=[
@@ -409,13 +453,13 @@
             side,
         ],
         scratch_shapes=[
-            pltpu.VMEM((2 * seg_len, channels), jnp.bfloat16),
-            pltpu.VMEM((lines_here, 2 * seg_len), jnp.float32),
-            pltpu.VMEM((seg_len + block, channels), jnp.bfloat16),
+            pltpu.VMEM((2 * seg_len, 2 * channels), jnp.bfloat16),
+            pltpu.VMEM((seg_len + 2 * block, channels), jnp.bfloat16),
+            pltpu.VMEM((2, 2 * block, seg_len + 2 * block), jnp.float32),
         ],
         compiler_params=params(),
         name="transport",
-    )(plan, left, right, prev_low, prev_high, own, following, before, back)
+    )(pot, lanes, left, right, prev_low, prev_high, own, following, before, back)
 
 
 def stack_weights(weight_ref, stacked_ref):
@@ -528,13 +572,14 @@
     own, back = cross_partials(left_features, prev_high, next_low, right_features, own)
     before = shifted(own, "seg", 1)
     following = shifted(back, "seg", -1)
-    plan, own, back = row_pass(
-        left_features, right_features, prev_low, prev_high, own, following, before, back, min(128, half)
+    block = min(128, half)
+    pot, lanes, own, back = row_pass(
+        left_features, right_features, prev_low, prev_high, own, following, before, back, block
     )
     before = shifted(own, "seg", 1)
     following = shifted(back, "seg", -1)
     state, disparity, first, last, low, high = transport(
-        plan, left_features, right_features, prev_low, prev_high, own, following, before, back, layers
+        pot, lanes, left_features, right_features, prev_low, prev_high, own, following, before, back, block, layers
     )
     bottom = shifted(first, "lines", -1)
     top = shifted(last, "lines", 1)

time: 108 us -> 108 us (level)
    pallas_call x1, Pallas kernels: 10.6 us -> 9.25 us  [row_pass(): pl.pallas_call(functools.partial(row_kernel, block), grid=(lines_here,),...]
    pallas_call x1, Pallas kernels: 8.91 us -> 10.2 us  [transport(): pl.pallas_call(functools.partial(transport_kernel, block, layers), grid=(...]
where the time goes in v3:
time: 108 us; the launch traced here: 107 us
  Pallas kernels  44.4 us (41%)
  starting transfers between devices  41.7 us (39%)
  waiting for transfers between devices  13.9 us (13%)
  local copies, waits for them, and re-layouts  6.12 us (6%)
    ppermute x13, starting transfers between devices, shifted(): return lax.ppermute(block, axis, route)  41.7 us
    ppermute x13, waiting for transfers between devices, shifted(): return lax.ppermute(block, axis, route)  13.9 us
    pallas_call x1, Pallas kernels, conv_layers(): pl.pallas_call(conv_kernel, in_specs=[pl.BlockSpec(memory_space=pltpu.VME...  13.5 us
    pallas_call x1, Pallas kernels, transport(): pl.pallas_call(functools.partial(transport_kernel, block, layers), grid=(...  10.2 us
    pallas_call x1, Pallas kernels, row_pass(): pl.pallas_call(functools.partial(row_kernel, block), grid=(lines_here,),...  9.25 us
    pallas_call x1, Pallas kernels, own_partials(): pl.pallas_call(functools.partial(own_kernel, min(256, seg_len)), grid=(li...  5.95 us
    pallas_call x1, Pallas kernels, cross_partials(): pl.pallas_call(functools.partial(cross_kernel, min(256, half)), grid=(lin...  5.51 us
    unnamed x27, local copies, waits for them, and re-layouts  3.74 us
  transfers between devices with their start and end apart: 13, of which 5 were waited for; matrix products, arithmetic and copies ran while one was open for 1% of the time, Pallas kernels for 11%

profile of v3, /device:TPU:1, one launch (start us, length us, event | category | flops | bytes accessed | tf_op | source)
XLA Modules:
  0.0 107.0 jit_solution(13337699266553038322)
XLA Ops:
  0.6 1.1 %slice.17 = bf16[4,512,128]{2,1,0:T(8,128)(2,1)S(1)} slice(bf16[4,1024,128]{2,1,0:T(8,128)(2,1)} %left_ref.7), slice={[0:4], [0:512], [0:128]} | slice | bytes 1048576 | tf_op jit(solution)/shard_map/slice | solution.py:569
  1.7 1.3 %collective-permute-start.2 = (bf16[4,512,128]{2,1,0:T(8,128)(2,1)S(1)}, bf16[4,512,128]{2,1,0:T(8,128)(2,1)S(1)}, u32[]{:S(2)}, u32[]{:S(2)}) collective-permute-start(bf16[4,512,128]{2,1,0:T(8,128)(2,1)S(1)} %slice.17), channel_id=1, source_target_pairs={{8,0},{16,8},{24,16},{9,1},{17,9},{25,17},{10,2},{18,10},{26,18},{... | collective-permute-start | bytes 1572872 | tf_op jit(solution)/shard_map/ppermute | solution.py:20
  3.0 1.3 %fusion = (bf16[4,512,128]{2,1,0:T(8,128)(2,1)S(1)}, bf16[4,512,128]{2,1,0:T(8,128)(2,1)S(1)}) fusion(bf16[4,1024,128]{2,1,0:T(8,128)(2,1)} %right_ref.7), kind=kLoop, calls=%fused_computation.2 | loop fusion | bytes 2097152 | tf_op jit(solution)/shard_map/slice | solution.py:568
  4.3 4.7 %collective-permute-start.1 = (bf16[4,512,128]{2,1,0:T(8,128)(2,1)S(1)}, bf16[4,512,128]{2,1,0:T(8,128)(2,1)S(1)}, u32[]{:S(2)}, u32[]{:S(2)}) collective-permute-start(bf16[4,512,128]{2,1,0:T(8,128)(2,1)S(1)} %get-tuple-element.30), channel_id=1, source_target_pairs={{0,8},{8,16},{16,24},{1,9},{9,17},{17,25},{2,10},{10,18},{18,26},{... | collective-permute-start | bytes 1572872 | tf_op jit(solution)/shard_map/ppermute | solution.py:20
  9.0 3.4 %collective-permute-start = (bf16[4,512,128]{2,1,0:T(8,128)(2,1)S(1)}, bf16[4,512,128]{2,1,0:T(8,128)(2,1)S(1)}, u32[]{:S(2)}, u32[]{:S(2)}) collective-permute-start(bf16[4,512,128]{2,1,0:T(8,128)(2,1)S(1)} %get-tuple-element.31), channel_id=1, source_target_pairs={{0,8},{8,16},{16,24},{1,9},{9,17},{17,25},{2,10},{10,18},{18,26},{... | collective-permute-start | bytes 1572872 | tf_op jit(solution)/shard_map/ppermute | solution.py:20
  12.4 5.9 %column_own.1 = (bf16[3,1536,256]{2,1,0:T(8,128)(2,1)}, f32[8,1024]{1,0:T(8,128)}) custom-call(bf16[4,1024,128]{2,1,0:T(8,128)(2,1)} %left_ref.7, bf16[4,1024,128]{2,1,0:T(8,128)(2,1)} %right_ref.7, bf16[3,3,3,128,128]{4,3,2,1,0:T(8,128)(2,1)} %weight_ref.1), custom_call_target="tpu_custom_call" | custom-call | flops 1073741824 | bytes 4194304 | tf_op jit(solution)/shard_map/column_own/pallas_call | solution.py:89
  18.3 1.2 %collective-permute-done.1.prev_ref.prev_high_ref = bf16[4,512,128]{2,1,0:T(8,128)(2,1)S(1)} collective-permute-done((bf16[4,512,128]{2,1,0:T(8,128)(2,1)S(1)}, bf16[4,512,128]{2,1,0:T(8,128)(2,1)S(1)}, u32[]{:S(2)}, u32[]{:S(2)}) %collective-permute-start.1) | collective-permute-done | bytes 524320 | tf_op jit(solution)/shard_map/ppermute | solution.py:20
  19.5 0.8 copy-done
  20.4 5.5 %column_cross.1 = (f32[8,1024]{1,0:T(8,128)}, f32[8,512]{1,0:T(8,128)}) custom-call(bf16[4,1024,128]{2,1,0:T(8,128)(2,1)} %left_ref.7, bf16[4,512,128]{2,1,0:T(8,128)(2,1)} %copy-done, bf16[4,512,128]{2,1,0:T(8,128)(2,1)} %copy-done.12, bf16[4,1024,128]{2,1,0:T(8,128)(2,1)} %right_ref.7, f32[8,1024]{1,0:T(8,128)} %get-tuple-element.16.own_ref), custom_call_target="tpu_custom_call" | custom-call | flops 1073741824 | bytes 4194304 | tf_op jit(solution)/shard_map/column_cross/pallas_call | solution.py:140
  25.9 4.1 %collective-permute-start.4 = (f32[8,1024]{1,0:T(8,128)}, f32[8,1024]{1,0:T(8,128)S(1)}, u32[]{:S(2)}, u32[]{:S(2)}) collective-permute-start(f32[8,1024]{1,0:T(8,128)} %get-tuple-element.17.own_ref), channel_id=1, source_target_pairs={{0,8},{8,16},{16,24},{1,9},{9,17},{17,25},{2,10},{10,18},{18,26},{... | collective-permute-start | bytes 98312 | tf_op jit(solution)/shard_map/ppermute | solution.py:20
  30.0 1.3 %collective-permute-start.3 = (f32[8,512]{1,0:T(8,128)}, f32[8,512]{1,0:T(8,128)S(1)}, u32[]{:S(2)}, u32[]{:S(2)}) collective-permute-start(f32[8,512]{1,0:T(8,128)} %get-tuple-element.18.back_ref), channel_id=1, source_target_pairs={{8,0},{16,8},{24,16},{9,1},{17,9},{25,17},{10,2},{18,10},{26,18},{... | collective-permute-start | bytes 49160 | tf_op jit(solution)/shard_map/ppermute | solution.py:20
  31.3 3.4 %collective-permute-done.3.next_ref = f32[8,512]{1,0:T(8,128)S(1)} collective-permute-done((f32[8,512]{1,0:T(8,128)}, f32[8,512]{1,0:T(8,128)S(1)}, u32[]{:S(2)}, u32[]{:S(2)}) %collective-permute-start.3) | collective-permute-done | bytes 16416 | tf_op jit(solution)/shard_map/ppermute | solution.py:20
  34.7 0.6 copy-done.11
  35.3 0.6 copy-done.6
  35.9 9.3 %row_pass.1 = (f32[4,2048]{1,0:T(4,128)}, bf16[4,1024,128]{2,1,0:T(8,128)(2,1)}, f32[4,1024]{1,0:T(4,128)}, f32[4,1024]{1,0:T(4,128)}) custom-call(bf16[4,1024,128]{2,1,0:T(8,128)(2,1)} %left_ref.7, bf16[4,1024,128]{2,1,0:T(8,128)(2,1)} %right_ref.7, bf16[4,512,128]{2,1,0:T(8,128)(2,1)} %copy-done.1, bf16[4,512,128]{2,1,0:T(8,128)(2,1)} %copy-done, ...), custom_call_target="tpu_custom_call" | custom-call | tf_op jit(solution)/shard_map/row_pass/pallas_call | solution.py:304
  45.1 3.3 %collective-permute-start.6 = (f32[4,1024]{1,0:T(4,128)}, f32[4,1024]{1,0:T(4,128)S(1)}, u32[]{:S(2)}, u32[]{:S(2)}) collective-permute-start(f32[4,1024]{1,0:T(4,128)} %get-tuple-element.21.own_ref), channel_id=1, source_target_pairs={{0,8},{8,16},{16,24},{1,9},{9,17},{17,25},{2,10},{10,18},{18,26},{... | collective-permute-start | bytes 49160 | tf_op jit(solution)/shard_map/ppermute | solution.py:20
  48.5 1.3 %collective-permute-start.5 = (f32[4,1024]{1,0:T(4,128)}, f32[4,1024]{1,0:T(4,128)S(1)}, u32[]{:S(2)}, u32[]{:S(2)}) collective-permute-start(f32[4,1024]{1,0:T(4,128)} %get-tuple-element.22.back_ref), channel_id=1, source_target_pairs={{8,0},{16,8},{24,16},{9,1},{17,9},{25,17},{10,2},{18,10},{26,18},{... | collective-permute-start | bytes 49160 | tf_op jit(solution)/shard_map/ppermute | solution.py:20
  49.8 3.4 %collective-permute-done.5.next_ref = f32[4,1024]{1,0:T(4,128)S(1)} collective-permute-done((f32[4,1024]{1,0:T(4,128)}, f32[4,1024]{1,0:T(4,128)S(1)}, u32[]{:S(2)}, u32[]{:S(2)}) %collective-permute-start.5) | collective-permute-done | bytes 16416 | tf_op jit(solution)/shard_map/ppermute | solution.py:20
  53.2 0.6 copy-done.10
  53.8 10.2 %transport.1 = (bf16[4,1024,128]{2,1,0:T(8,128)(2,1)}, f32[4,1024]{1,0:T(4,128)}, bf16[3,1024,128]{2,1,0:T(8,128)(2,1)}, bf16[3,1024,128]{2,1,0:T(8,128)(2,1)}, ...) custom-call(f32[4,2048]{1,0:T(4,128)} %get-tuple-element.19.pot_ref, ...), custom_call_target="tpu_custom_call" | custom-call | tf_op jit(solution)/shard_map/transport/pallas_call | solution.py:429
  64.0 8.9 %collective-permute-start.7 = (bf16[3,1024,128]{2,1,0:T(8,128)(2,1)}, bf16[3,1024,128]{2,1,0:T(8,128)(2,1)S(1)}, u32[]{:S(2)}, u32[]{:S(2)}) collective-permute-start(bf16[3,1024,128]{2,1,0:T(8,128)(2,1)} %get-tuple-element.24), channel_id=1, source_target_pairs={{0,1},{1,2},{2,3},{3,4},{4,5},{5,6},{6,7},{8,9},{9,10},{10,11},{11... | collective-permute-start | bytes 2359304 | tf_op jit(solution)/shard_map/ppermute | solution.py:20
  72.9 1.9 %collective-permute-start.8 = (bf16[3,1024,128]{2,1,0:T(8,128)(2,1)}, bf16[3,1024,128]{2,1,0:T(8,128)(2,1)S(1)}, u32[]{:S(2)}, u32[]{:S(2)}) collective-permute-start(bf16[3,1024,128]{2,1,0:T(8,128)(2,1)} %get-tuple-element.25), channel_id=1, source_target_pairs={{1,0},{2,1},{3,2},{4,3},{5,4},{6,5},{7,6},{9,8},{10,9},{11,10},{12... | collective-permute-start | bytes 2359304 | tf_op jit(solution)/shard_map/ppermute | solution.py:20
  74.8 3.2 %collective-permute-start.9 = (bf16[4,16,128]{2,1,0:T(8,128)(2,1)}, bf16[4,16,128]{2,1,0:T(8,128)(2,1)S(1)}, u32[]{:S(2)}, u32[]{:S(2)}) collective-permute-start(bf16[4,16,128]{2,1,0:T(8,128)(2,1)} %get-tuple-element.26), channel_id=1, source_target_pairs={{0,8},{8,16},{16,24},{1,9},{9,17},{17,25},{2,10},{10,18},{18,26},{... | collective-permute-start | bytes 49160 | tf_op jit(solution)/shard_map/ppermute | solution.py:20
  78.1 1.3 %collective-permute-start.10 = (bf16[4,16,128]{2,1,0:T(8,128)(2,1)}, bf16[4,16,128]{2,1,0:T(8,128)(2,1)S(1)}, u32[]{:S(2)}, u32[]{:S(2)}) collective-permute-start(bf16[4,16,128]{2,1,0:T(8,128)(2,1)} %get-tuple-element.27), channel_id=1, source_target_pairs={{8,0},{16,8},{24,16},{9,1},{17,9},{25,17},{10,2},{18,10},{26,18},{... | collective-permute-start | bytes 49160 | tf_op jit(solution)/shard_map/ppermute | solution.py:20
  79.4 3.4 %collective-permute-done.10.right_ref = bf16[4,16,128]{2,1,0:T(8,128)(2,1)S(1)} collective-permute-done((bf16[4,16,128]{2,1,0:T(8,128)(2,1)}, bf16[4,16,128]{2,1,0:T(8,128)(2,1)S(1)}, u32[]{:S(2)}, u32[]{:S(2)}) %collective-permute-start.10) | collective-permute-done | bytes 16416 | tf_op jit(solution)/shard_map/ppermute | solution.py:20
  82.8 1.9 %collective-permute-start.12 = (bf16[3,32,128]{2,1,0:T(8,128)(2,1)S(1)}, bf16[3,32,128]{2,1,0:T(8,128)(2,1)S(1)}, u32[]{:S(2)}, u32[]{:S(2)}) collective-permute-start(bf16[3,32,128]{2,1,0:T(8,128)(2,1)S(1)} %get-tuple-element.32), channel_id=1, source_target_pairs={{1,0},{2,1},{3,2},{4,3},{5,4},{6,5},{7,6},{9,8},{10,9},{11,10},{12... | collective-permute-start | bytes 73736 | tf_op jit(solution)/shard_map/ppermute | solution.py:20
  84.7 5.1 %collective-permute-start.11 = (bf16[3,32,128]{2,1,0:T(8,128)(2,1)S(1)}, bf16[3,32,128]{2,1,0:T(8,128)(2,1)S(1)}, u32[]{:S(2)}, u32[]{:S(2)}) collective-permute-start(bf16[3,32,128]{2,1,0:T(8,128)(2,1)S(1)} %get-tuple-element.33), channel_id=1, source_target_pairs={{0,1},{1,2},{2,3},{3,4},{4,5},{5,6},{6,7},{8,9},{9,10},{10,11},{11... | collective-permute-start | bytes 73736 | tf_op jit(solution)/shard_map/ppermute | solution.py:20
  89.8 2.6 %collective-permute-done.12.corner_bottom_ref = bf16[3,32,128]{2,1,0:T(8,128)(2,1)S(1)} collective-permute-done((bf16[3,32,128]{2,1,0:T(8,128)(2,1)S(1)}, bf16[3,32,128]{2,1,0:T(8,128)(2,1)S(1)}, u32[]{:S(2)}, u32[]{:S(2)}) %collective-permute-start.12) | collective-permute-done | bytes 24608 | tf_op jit(solution)/shard_map/ppermute | solution.py:20
  92.4 0.5 copy-done.7
  93.0 0.3 copy-done.2
  93.3 0.3 copy-done.3
  93.5 13.5 %conv_layers.1 = bf16[4,1024,128]{2,1,0:T(8,128)(2,1)} custom-call(bf16[4,1024,128]{2,1,0:T(8,128)(2,1)} %get-tuple-element.23.state_ref, bf16[3,1024,128]{2,1,0:T(8,128)(2,1)} %copy-done.2, bf16[3,1024,128]{2,1,0:T(8,128)(2,1)} %copy-done.3, bf16[4,16,128]{2,1,0:T(8,128)(2,1)} %copy-done.4, bf16[4,16,128]{2,1,0:T(8,128)(2,1)} %copy-done.5, ...), custom_call_target="tpu_custom_call" | custom-call | tf_op jit(solution)/shard_map/conv_layers/pallas_call | solution.py:553
  (30 shorter events, 0.1 us)
Async XLA Ops:
  1.7 16.6 %collective-permute-start.2 = (bf16[4,512,128]{2,1,0:T(8,128)(2,1)S(1)}, bf16[4,512,128]{2,1,0:T(8,128)(2,1)S(1)}, u32[]{:S(2)}, u32[]{:S(2)}) collective-permute-start(bf16[4,512,128]{2,1,0:T(8,128)(2,1)S(1)} %slice.17), channel_id=1, source_target_pairs={{8,0},{16,8},{24,16},{9,1},{17,9},{25,17},{10,2},{18,10},{26,18},{... | collective-permute-start | bytes 1572872 | tf_op jit(solution)/shard_map/ppermute | solution.py:20
  4.3 15.2 %collective-permute-start.1 = (bf16[4,512,128]{2,1,0:T(8,128)(2,1)S(1)}, bf16[4,512,128]{2,1,0:T(8,128)(2,1)S(1)}, u32[]{:S(2)}, u32[]{:S(2)}) collective-permute-start(bf16[4,512,128]{2,1,0:T(8,128)(2,1)S(1)} %get-tuple-element.30), channel_id=1, source_target_pairs={{0,8},{8,16},{16,24},{1,9},{9,17},{17,25},{2,10},{10,18},{18,26},{... | collective-permute-start | bytes 1572872 | tf_op jit(solution)/shard_map/ppermute | solution.py:20
  9.0 22.3 %collective-permute-start = (bf16[4,512,128]{2,1,0:T(8,128)(2,1)S(1)}, bf16[4,512,128]{2,1,0:T(8,128)(2,1)S(1)}, u32[]{:S(2)}, u32[]{:S(2)}) collective-permute-start(bf16[4,512,128]{2,1,0:T(8,128)(2,1)S(1)} %get-tuple-element.31), channel_id=1, source_target_pairs={{0,8},{8,16},{16,24},{1,9},{9,17},{17,25},{2,10},{10,18},{18,26},{... | collective-permute-start | bytes 1572872 | tf_op jit(solution)/shard_map/ppermute | solution.py:20
  18.3 1.2 %copy-start.12 = (bf16[4,512,128]{2,1,0:T(8,128)(2,1)}, bf16[4,512,128]{2,1,0:T(8,128)(2,1)S(1)}, u32[]{:S(2)}) copy-start(bf16[4,512,128]{2,1,0:T(8,128)(2,1)S(1)} %collective-permute-done.2.next_ref) | copy-start | bytes 1572868
  19.5 0.8 copy-start
  25.9 8.8 %collective-permute-start.4 = (f32[8,1024]{1,0:T(8,128)}, f32[8,1024]{1,0:T(8,128)S(1)}, u32[]{:S(2)}, u32[]{:S(2)}) collective-permute-start(f32[8,1024]{1,0:T(8,128)} %get-tuple-element.17.own_ref), channel_id=1, source_target_pairs={{0,8},{8,16},{16,24},{1,9},{9,17},{17,25},{2,10},{10,18},{18,26},{... | collective-permute-start | bytes 98312 | tf_op jit(solution)/shard_map/ppermute | solution.py:20
  30.0 4.7 %collective-permute-start.3 = (f32[8,512]{1,0:T(8,128)}, f32[8,512]{1,0:T(8,128)S(1)}, u32[]{:S(2)}, u32[]{:S(2)}) collective-permute-start(f32[8,512]{1,0:T(8,128)} %get-tuple-element.18.back_ref), channel_id=1, source_target_pairs={{8,0},{16,8},{24,16},{9,1},{17,9},{25,17},{10,2},{18,10},{26,18},{... | collective-permute-start | bytes 49160 | tf_op jit(solution)/shard_map/ppermute | solution.py:20
  31.3 3.4 %copy-start.1 = (bf16[4,512,128]{2,1,0:T(8,128)(2,1)}, bf16[4,512,128]{2,1,0:T(8,128)(2,1)S(1)}, u32[]{:S(2)}) copy-start(bf16[4,512,128]{2,1,0:T(8,128)(2,1)S(1)} %collective-permute-done.prev_low_ref) | copy-start | bytes 1572868
  34.7 0.6 copy-start.11
  35.3 0.6 copy-start.6
  45.1 4.7 %collective-permute-start.6 = (f32[4,1024]{1,0:T(4,128)}, f32[4,1024]{1,0:T(4,128)S(1)}, u32[]{:S(2)}, u32[]{:S(2)}) collective-permute-start(f32[4,1024]{1,0:T(4,128)} %get-tuple-element.21.own_ref), channel_id=1, source_target_pairs={{0,8},{8,16},{16,24},{1,9},{9,17},{17,25},{2,10},{10,18},{18,26},{... | collective-permute-start | bytes 49160 | tf_op jit(solution)/shard_map/ppermute | solution.py:20
  48.5 4.7 %collective-permute-start.5 = (f32[4,1024]{1,0:T(4,128)}, f32[4,1024]{1,0:T(4,128)S(1)}, u32[]{:S(2)}, u32[]{:S(2)}) collective-permute-start(f32[4,1024]{1,0:T(4,128)} %get-tuple-element.22.back_ref), channel_id=1, source_target_pairs={{8,0},{16,8},{24,16},{9,1},{17,9},{25,17},{10,2},{18,10},{26,18},{... | collective-permute-start | bytes 49160 | tf_op jit(solution)/shard_map/ppermute | solution.py:20
  49.8 3.4 %copy-start.9 = (f32[4,1024]{1,0:T(4,128)}, f32[4,1024]{1,0:T(4,128)S(1)}, u32[]{:S(2)}) copy-start(f32[4,1024]{1,0:T(4,128)S(1)} %collective-permute-done.6.before_ref) | copy-start | bytes 49156
  53.2 0.6 copy-start.10
  64.0 28.4 %collective-permute-start.7 = (bf16[3,1024,128]{2,1,0:T(8,128)(2,1)}, bf16[3,1024,128]{2,1,0:T(8,128)(2,1)S(1)}, u32[]{:S(2)}, u32[]{:S(2)}) collective-permute-start(bf16[3,1024,128]{2,1,0:T(8,128)(2,1)} %get-tuple-element.24), channel_id=1, source_target_pairs={{0,1},{1,2},{2,3},{3,4},{4,5},{5,6},{6,7},{8,9},{9,10},{10,11},{11... | collective-permute-start | bytes 2359304 | tf_op jit(solution)/shard_map/ppermute | solution.py:20
  72.9 19.5 %collective-permute-start.8 = (bf16[3,1024,128]{2,1,0:T(8,128)(2,1)}, bf16[3,1024,128]{2,1,0:T(8,128)(2,1)S(1)}, u32[]{:S(2)}, u32[]{:S(2)}) collective-permute-start(bf16[3,1024,128]{2,1,0:T(8,128)(2,1)} %get-tuple-element.25), channel_id=1, source_target_pairs={{1,0},{2,1},{3,2},{4,3},{5,4},{6,5},{7,6},{9,8},{10,9},{11,10},{12... | collective-permute-start | bytes 2359304 | tf_op jit(solution)/shard_map/ppermute | solution.py:20
  74.8 4.6 %collective-permute-start.9 = (bf16[4,16,128]{2,1,0:T(8,128)(2,1)}, bf16[4,16,128]{2,1,0:T(8,128)(2,1)S(1)}, u32[]{:S(2)}, u32[]{:S(2)}) collective-permute-start(bf16[4,16,128]{2,1,0:T(8,128)(2,1)} %get-tuple-element.26), channel_id=1, source_target_pairs={{0,8},{8,16},{16,24},{1,9},{9,17},{17,25},{2,10},{10,18},{18,26},{... | collective-permute-start | bytes 49160 | tf_op jit(solution)/shard_map/ppermute | solution.py:20
  78.1 4.7 %collective-permute-start.10 = (bf16[4,16,128]{2,1,0:T(8,128)(2,1)}, bf16[4,16,128]{2,1,0:T(8,128)(2,1)S(1)}, u32[]{:S(2)}, u32[]{:S(2)}) collective-permute-start(bf16[4,16,128]{2,1,0:T(8,128)(2,1)} %get-tuple-element.27), channel_id=1, source_target_pairs={{8,0},{16,8},{24,16},{9,1},{17,9},{25,17},{10,2},{18,10},{26,18},{... | collective-permute-start | bytes 49160 | tf_op jit(solution)/shard_map/ppermute | solution.py:20
  79.4 13.0 %copy-start.4 = (bf16[4,16,128]{2,1,0:T(8,128)(2,1)}, bf16[4,16,128]{2,1,0:T(8,128)(2,1)S(1)}, u32[]{:S(2)}) copy-start(bf16[4,16,128]{2,1,0:T(8,128)(2,1)S(1)} %collective-permute-done.9.left_ref) | copy-start | bytes 49156
  82.8 9.6 %copy-start.5 = (bf16[4,16,128]{2,1,0:T(8,128)(2,1)}, bf16[4,16,128]{2,1,0:T(8,128)(2,1)S(1)}, u32[]{:S(2)}) copy-start(bf16[4,16,128]{2,1,0:T(8,128)(2,1)S(1)} %collective-permute-done.10.right_ref) | copy-start | bytes 49156
  82.8 9.6 %collective-permute-start.12 = (bf16[3,32,128]{2,1,0:T(8,128)(2,1)S(1)}, bf16[3,32,128]{2,1,0:T(8,128)(2,1)S(1)}, u32[]{:S(2)}, u32[]{:S(2)}) collective-permute-start(bf16[3,32,128]{2,1,0:T(8,128)(2,1)S(1)} %get-tuple-element.32), channel_id=1, source_target_pairs={{1,0},{2,1},{3,2},{4,3},{5,4},{6,5},{7,6},{9,8},{10,9},{11,10},{12... | collective-permute-start | bytes 73736 | tf_op jit(solution)/shard_map/ppermute | solution.py:20
  84.7 7.6 %collective-permute-start.11 = (bf16[3,32,128]{2,1,0:T(8,128)(2,1)S(1)}, bf16[3,32,128]{2,1,0:T(8,128)(2,1)S(1)}, u32[]{:S(2)}, u32[]{:S(2)}) collective-permute-start(bf16[3,32,128]{2,1,0:T(8,128)(2,1)S(1)} %get-tuple-element.33), channel_id=1, source_target_pairs={{0,1},{1,2},{2,3},{3,4},{4,5},{5,6},{6,7},{8,9},{9,10},{10,11},{11... | collective-permute-start | bytes 73736 | tf_op jit(solution)/shard_map/ppermute | solution.py:20
  92.4 0.6 copy-start.7
  92.4 0.6 copy-start.8
  92.4 0.9 copy-start.2
  92.4 1.1 %copy-start.3 = (bf16[3,1024,128]{2,1,0:T(8,128)(2,1)}, bf16[3,1024,128]{2,1,0:T(8,128)(2,1)S(1)}, u32[]{:S(2)}) copy-start(bf16[3,1024,128]{2,1,0:T(8,128)(2,1)S(1)} %collective-permute-done.8.bottom_ref) | copy-start | bytes 2359300

commit v4 on v3

v4 whole, which is shorter than its diff:
```python
import functools
import math

import jax
import jax.numpy as jnp
from jax import lax
from jax.experimental import pallas as pl
from jax.experimental.pallas import tpu as pltpu
from jax.sharding import PartitionSpec as P

DISP = 1024
NEG = -1e30
EDGE = 16
VMEM_BYTES = 32 * 1024 * 1024


def shifted(block, axis, step):
    count = lax.axis_size(axis)
    route = [(i, i + step) for i in range(count) if 0 <= i + step < count]
    return lax.ppermute(block, axis, route)


def params():
    return pltpu.CompilerParams(vmem_limit_bytes=VMEM_BYTES)


ANYWHERE = pl.BlockSpec(memory_space=pl.ANY)


def kernel_call(kernel, operands, results, scratch, copies, name, cost=None):
    return pl.pallas_call(
        kernel,
        in_specs=[ANYWHERE] * len(operands),
        out_specs=[ANYWHERE] * len(results),
        out_shape=[jax.ShapeDtypeStruct(shape, dtype) for shape, dtype in results],
        scratch_shapes=[pltpu.VMEM(shape, dtype) for shape, dtype in scratch]
        + [pltpu.SemaphoreType.DMA((count,)) for count in copies],
        compiler_params=params(),
        cost_estimate=cost,
        name=name,
    )(*operands)


def copies_of(pairs, sems):
    return [
        pltpu.make_async_copy(source, target, sems.at[index])
        for index, (source, target) in enumerate(pairs)
    ]


def line_copies(pairs, sems, line, lines_here):
    return [
        pltpu.make_async_copy(source.at[line], target.at[line], sems.at[index * lines_here + line])
        for index, (source, target) in enumerate(pairs)
    ]


def begin_copies(copies):
    for copy in copies:
        copy.start()


def wait(copies):
    for copy in copies:
        copy.wait()


def scores_of(left, right):
    return lax.dot_general(
        left, right, (((1,), (1,)), ((), ())), preferred_element_type=jnp.float32
    )


def log2_scale(channels):
    return math.log2(math.e) / math.sqrt(channels)


def over_rows(reduce, values, chains=64):
    count, width = values.shape
    while count > chains >= 8 and count % chains == 0:
        values = reduce(values.reshape(count // chains, chains, width), axis=0)
        count, chains = chains, chains // 8
    return reduce(values, axis=0, keepdims=True)


def column_block(left, right, diagonal_first):
    block, channels = right.shape
    scale = log2_scale(channels)
    raw = scores_of(left, right)
    row_ids = lax.broadcasted_iota(jnp.int32, (block, block), 0)
    col_ids = lax.broadcasted_iota(jnp.int32, (block, block), 1)
    if diagonal_first:
        parts = [jnp.where(col_ids <= row_ids, raw[:block], NEG), raw[block:]]
    else:
        parts = [raw[:-block], jnp.where(col_ids > row_ids, raw[-block:], NEG)]
    parts = [part for part in parts if part.shape[0]]
    peak = functools.reduce(jnp.maximum, [over_rows(jnp.max, part) for part in parts])
    total = sum(over_rows(jnp.sum, jnp.exp2((part - peak) * scale)) for part in parts)
    return (peak * scale, total)


def own_kernel(
    block,
    left_in,
    right_in,
    weight_in,
    stacked_out,
    part_out,
    left,
    right,
    weight,
    stacked,
    part,
    line_sems,
    sems,
):
    lines_here, seg_len = left.shape[:2]
    pairs = ((left_in, left), (right_in, right))
    for line in range(lines_here):
        begin_copies(line_copies(pairs, line_sems, line, lines_here))
    fetch, send_stacked, send_part = copies_of(
        ((weight_in, weight), (stacked, stacked_out), (part, part_out)), sems
    )
    fetch.start()

    def one_line(line, carry):
        wait(line_copies(pairs, line_sems, line, lines_here))
        for first in range(0, seg_len, block):
            cols = slice(first, first + block)
            peak, total = column_block(left[line, first:], right[line, cols], True)
            part[pl.ds(line, 1), cols] = peak
            part[pl.ds(lines_here + line, 1), cols] = total
        return carry

    lax.fori_loop(0, lines_here, one_line, 0)
    send_part.start()
    fetch.wait()
    stack_weights(weight, stacked)
    send_stacked.start()
    send_part.wait()
    send_stacked.wait()


def column_cost(lines_here, seg_len, channels):
    return pl.CostEstimate(
        flops=2 * lines_here * seg_len * seg_len * channels,
        bytes_accessed=8 * lines_here * seg_len * channels,
        transcendentals=lines_here * seg_len * seg_len // 2,
    )


def own_partials(left, right, weight):
    lines_here, seg_len, channels = left.shape
    bf16, f32 = jnp.bfloat16, jnp.float32
    stacked = ((weight.shape[0], 12 * channels, 2 * channels), bf16)
    part = ((2 * lines_here, seg_len), f32)
    return kernel_call(
        functools.partial(own_kernel, min(256, seg_len)),
        (left, right, weight),
        (stacked, part),
        ((left.shape, bf16), (right.shape, bf16), (weight.shape, bf16), stacked, part),
        (2 * lines_here, 3),
        "column_own",
        column_cost(*left.shape),
    )


def cross_kernel(
    block,
    left_in,
    prev_in,
    next_in,
    right_in,
    own_in,
    merged_out,
    back_out,
    left,
    prev,
    following,
    right,
    own,
    merged,
    back,
    line_sems,
    sems,
):
    lines_here, half = following.shape[:2]
    pairs = (
        (left_in, left),
        (prev_in, prev),
        (next_in, following),
        (right_in.at[:, pl.ds(0, half)], right),
    )
    fetch, send_merged, send_back = copies_of(
        ((own_in, own), (merged, merged_out), (back, back_out)), sems
    )
    fetch.start()
    for line in range(lines_here):
        begin_copies(line_copies(pairs, line_sems, line, lines_here))
    fetch.wait()
    last = lax.axis_index("seg") == lax.axis_size("seg") - 1
    merged[:, half:] = own[:, half:]

    def one_line(line, carry):
        wait(line_copies(pairs, line_sems, line, lines_here))
        top, bottom = pl.ds(line, 1), pl.ds(lines_here + line, 1)
        for first in range(0, prev.shape[1], block):
            cols = slice(first, first + block)
            peak, total = column_block(
                left[line, : half + first + block], prev[line, cols], False
            )
            back[top, cols] = peak
            back[bottom, cols] = total
        for first in range(0, half, block):
            cols = slice(first, first + block)
            peak, total = column_block(following[line, : first + block], right[line, cols], False)
            peak = jnp.where(last, NEG, peak)
            total = jnp.where(last, 0.0, total)
            own_peak = own[top, cols]
            joint = jnp.maximum(own_peak, peak)
            merged[top, cols] = joint
            merged[bottom, cols] = own[bottom, cols] * jnp.exp2(
                own_peak - joint
            ) + total * jnp.exp2(peak - joint)
        return carry

    lax.fori_loop(0, lines_here, one_line, 0)
    begin_copies((send_merged, send_back))
    wait((send_merged, send_back))


def cross_partials(left, prev_high, next_low, right, own):
    lines_here, seg_len, channels = left.shape
    half = next_low.shape[1]
    bf16, f32 = jnp.bfloat16, jnp.float32
    back = ((2 * lines_here, seg_len - half), f32)
    merged = (own.shape, f32)
    return kernel_call(
        functools.partial(cross_kernel, min(256, half)),
        (left, prev_high, next_low, right, own),
        (merged, back),
        (
            (left.shape, bf16),
            (prev_high.shape, bf16),
            (next_low.shape, bf16),
            (next_low.shape, bf16),
            merged,
            merged,
            back,
        ),
        (4 * lines_here, 3),
        "column_cross",
        column_cost(*left.shape),
    )


def potential(peak, total):
    return -(peak + jnp.log2(total))


def merged_potential(first, second):
    first_max = jnp.where(first[1] > 0, first[0], NEG)
    second_max = jnp.where(second[1] > 0, second[0], NEG)
    peak = jnp.maximum(first_max, second_max)
    total = first[1] * jnp.exp2(first_max - peak) + second[1] * jnp.exp2(second_max - peak)
    return potential(peak, total)


def split(values, parts):
    pieces = []
    for _ in range(parts):
        piece = values.astype(jnp.bfloat16).astype(jnp.float32)
        pieces.append(piece)
        values = values - piece
    return pieces


SHIFT = 2


def potential_lanes(pot, channels):
    lines_here, count = pot.shape
    parts = split(pot, 3)
    filler = jnp.zeros((channels - 3 * lines_here, count), jnp.float32)
    lanes = jnp.concatenate(parts + [filler], axis=0).T
    lane = lax.broadcasted_iota(jnp.int32, lanes.shape, 1)
    return jnp.where(lane >= channels - SHIFT, -1.0, lanes).astype(jnp.bfloat16)


def line_lanes(line, lines_here, shape):
    lane = lax.broadcasted_iota(jnp.int32, shape, 1)
    mine = jnp.zeros(shape, jnp.float32)
    for part in range(3):
        mine = jnp.where(lane == part * lines_here + line, 1.0, mine)
    return mine


def banded(values, row, block):
    rows, window = values.shape
    col_ids = lax.broadcasted_iota(jnp.int32, (rows, block), 1)
    row_ids = lax.broadcasted_iota(jnp.int32, (rows, block), 0) + row
    return jnp.concatenate(
        [
            jnp.where(col_ids > row_ids, values[:, :block], NEG),
            values[:, block : window - block],
            jnp.where(col_ids <= row_ids, values[:, window - block :], NEG),
        ],
        axis=1,
    )


def feature_pairs(left_in, right_in, prev_low_in, prev_high_in, left, ext):
    seg_len, half = left.shape[1], prev_low_in.shape[1]
    return (
        (left_in, left),
        (prev_low_in, ext.at[:, pl.ds(0, half)]),
        (prev_high_in, ext.at[:, pl.ds(half, seg_len - half)]),
        (right_in, ext.at[:, pl.ds(seg_len, seg_len)]),
    )


def row_kernel(
    block,
    left_in,
    right_in,
    prev_low_in,
    prev_high_in,
    own_in,
    next_in,
    before_in,
    back_in,
    pot_out,
    lanes_out,
    own_out,
    prev_out,
    left,
    ext,
    own,
    following,
    before,
    back,
    pot,
    lanes,
    own_sum,
    prev_sum,
    pot_lanes,
    sums,
    raw,
    line_sems,
    sems,
):
    lines_here, seg_len, channels = left.shape
    half = prev_low_in.shape[1]
    scale = log2_scale(channels)
    fetches = copies_of(
        ((own_in, own), (next_in, following), (before_in, before), (back_in, back)), sems
    )
    begin_copies(fetches)
    pairs = feature_pairs(left_in, right_in, prev_low_in, prev_high_in, left, ext)
    for line in range(lines_here):
        begin_copies(line_copies(pairs, line_sems, line, lines_here))
    wait(fetches)

    def parts(ref, first, stop):
        return ref[:lines_here, first:stop], ref[lines_here:, first:stop]

    rest = seg_len - half
    pot[:, seg_len : seg_len + half] = potential(*parts(own, 0, half))
    pot[:, seg_len + half :] = merged_potential(
        parts(own, half, seg_len), parts(following, 0, rest)
    )
    low = parts(before, 0, half)
    high = parts(before, half, seg_len)
    pot[:, :half] = jnp.where(low[1] > 0, potential(*low), NEG)
    pot[:, half:seg_len] = jnp.where(
        high[1] > 0, merged_potential(high, parts(back, 0, rest)), NEG
    )
    pot_lanes[...] = potential_lanes(pot[...] * (1.0 / scale), channels)
    window = seg_len + block
    big = 2 * block
    steps = seg_len // big
    strip = 16
    lane = lax.broadcasted_iota(jnp.int32, (strip, channels), 1)

    def one_line(line, carry):
        wait(line_copies(pairs, line_sems, line, lines_here))
        sums[...] = jnp.zeros_like(sums)
        mine = line_lanes(line, lines_here, (big, channels)).astype(jnp.bfloat16)
        strip_lanes = line_lanes(line, lines_here, (strip, channels))

        def score(index):
            first = index * big
            reach = slice(first, first + seg_len + big)
            raw[index % 2] = scores_of(
                jnp.concatenate([left[line, first : first + big], mine], axis=1),
                jnp.concatenate([ext[line, reach], pot_lanes[reach]], axis=1),
            )

        score(0)
        for index in range(steps):
            slot = index % 2
            if index + 1 < steps:
                score(index + 1)
            for side in range(2):
                shift = side * block
                first = index * big + shift
                column_sum = jnp.zeros((8, window), jnp.float32)
                for row in range(0, block, strip):
                    rows = slice(shift + row, shift + row + strip)
                    logits = banded(raw[slot, rows, shift : shift + window], row, block)
                    peak = jnp.max(logits, axis=1, keepdims=True)
                    terms = jnp.exp2((logits - peak) * scale)
                    plan = terms * (1.0 / jnp.sum(terms, axis=1, keepdims=True))
                    column_sum += plan[:8] + plan[8:]
                    marked = strip_lanes
                    for part, piece in enumerate(split(peak, SHIFT)):
                        marked = jnp.where(lane == channels - SHIFT + part, piece, marked)
                    lanes[line, first + row : first + row + strip] = marked.astype(jnp.bfloat16)
                sums[:, first : first + window] += column_sum
        totals = jnp.sum(sums[...], axis=0, keepdims=True)
        prev_sum[pl.ds(line, 1), :] = totals[:, :seg_len]
        own_sum[pl.ds(line, 1), :] = totals[:, seg_len:]
        return carry

    lax.fori_loop(0, lines_here, one_line, 0)
    sends = copies_of(
        ((own_sum, own_out), (prev_sum, prev_out), (pot, pot_out), (lanes, lanes_out)), sems
    )
    begin_copies(sends)
    wait(sends)


def row_pass(left, right, prev_low, prev_high, own, following, before, back, block):
    lines_here, seg_len, channels = left.shape
    bf16, f32 = jnp.bfloat16, jnp.float32
    marginal = ((lines_here, seg_len), f32)
    pot = ((lines_here, 2 * seg_len), f32)
    lanes = (left.shape, bf16)
    return kernel_call(
        functools.partial(row_kernel, block),
        (left, right, prev_low, prev_high, own, following, before, back),
        (pot, lanes, marginal, marginal),
        (
            (left.shape, bf16),
            ((lines_here, 2 * seg_len, channels), bf16),
            (own.shape, f32),
            (following.shape, f32),
            (before.shape, f32),
            (back.shape, f32),
            pot,
            lanes,
            marginal,
            marginal,
            ((2 * seg_len, channels), bf16),
            ((8, 2 * seg_len), f32),
            ((2, 2 * block, seg_len + 2 * block), f32),
        ),
        (4 * lines_here, 4),
        "row_pass",
    )


def transport_kernel(
    block,
    pot_in,
    lanes_in,
    left_in,
    right_in,
    prev_low_in,
    prev_high_in,
    own_in,
    next_in,
    before_in,
    back_in,
    state_out,
    disp_out,
    first_out,
    last_out,
    low_out,
    high_out,
    pot,
    lanes,
    left,
    ext,
    own,
    following,
    before,
    back,
    state,
    disp,
    pot_lanes,
    marks,
    raw,
    weights,
    line_sems,
    sems,
    send_sems,
):
    lines_here, seg_len, channels = left.shape
    layers = first_out.shape[0]
    scale = log2_scale(channels)
    big = 2 * block
    window = seg_len + big
    fetches = copies_of(
        ((pot_in, pot), (own_in, own), (next_in, following), (before_in, before), (back_in, back)),
        sems,
    )
    begin_copies(fetches)
    pairs = feature_pairs(left_in, right_in, prev_low_in, prev_high_in, left, ext) + (
        (lanes_in, lanes),
    )
    for line in range(lines_here):
        begin_copies(line_copies(pairs, line_sems, line, lines_here))
    lane = lax.broadcasted_iota(jnp.int32, (window, channels), 1)
    distance = seg_len - lax.broadcasted_iota(jnp.int32, (window, channels), 0)
    fine = jnp.bitwise_and(distance, 15)
    values = jnp.where(
        lane == 0,
        1,
        jnp.where(lane == 1, distance - fine, jnp.where(lane == 2, fine, 0)),
    )
    marks[...] = values.astype(jnp.float32).astype(jnp.bfloat16)
    wait(fetches)
    total = jnp.concatenate([before[...] + back[...], own[...] + following[...]], axis=1)
    final = jnp.where(total > 0, pot[...] - jnp.log2(total), NEG)
    pot_lanes[...] = potential_lanes(final * (1.0 / scale), channels)
    offsets = lax.broadcasted_iota(jnp.int32, (1, big), 1).astype(jnp.float32)
    corner = jnp.zeros((block, block), jnp.bfloat16)
    steps = seg_len // big
    edges = ((state.at[:, pl.ds(0, EDGE)], low_out), (state.at[:, pl.ds(seg_len - EDGE, EDGE)], high_out))

    def one_line(line, carry):
        wait(line_copies(pairs, line_sems, line, lines_here))

        def score(index):
            first = index * big
            rows, reach = slice(first, first + big), slice(first, first + window)
            raw[index % 2] = scores_of(
                jnp.concatenate([left[line, rows], lanes[line, rows]], axis=1),
                jnp.concatenate([ext[line, reach], pot_lanes[reach]], axis=1),
            )

        def weigh(index):
            slot = index % 2
            upper = jnp.exp2(banded(raw[slot, :block, : window - block], 0, block) * scale)
            lower = jnp.exp2(banded(raw[slot, block:, block:], 0, block) * scale)
            weights[slot, :block, : window - block] = upper.astype(jnp.bfloat16)
            weights[slot, :block, window - block :] = corner
            weights[slot, block:, block:] = lower.astype(jnp.bfloat16)
            weights[slot, block:, :block] = corner

        def gather(index):
            first = index * big
            rows = slice(first, first + big)
            table = jnp.concatenate([ext[line, first : first + window], marks[...]], axis=1)
            result = jnp.dot(weights[index % 2], table, preferred_element_type=jnp.float32)
            matched = result[:, :channels] * (1.0 / result[:, channels : channels + 1])
            state[line, rows] = (matched - left[line, rows].astype(jnp.float32)).astype(
                state.dtype
            )
            moments = result[:, channels:].T
            return offsets + (moments[1:2] + moments[2:3]) / moments[0:1]

        disparity = []
        for index in range(steps + 2):
            if index < steps:
                score(index)
            if index >= 2:
                disparity.append(gather(index - 2))
            if 1 <= index <= steps:
                weigh(index - 1)
        disp[pl.ds(line, 1), :] = jnp.concatenate(disparity, axis=1)
        begin_copies(line_copies(((state, state_out),) + edges, send_sems, line, lines_here))

        @pl.when(line < layers)
        def _():
            pltpu.make_async_copy(state.at[line], first_out.at[line], sems.at[line]).start()

        @pl.when(line >= lines_here - layers)
        def _():
            target = line - (lines_here - layers)
            pltpu.make_async_copy(
                state.at[line], last_out.at[target], sems.at[layers + target]
            ).start()

        return carry

    lax.fori_loop(0, lines_here, one_line, 0)
    send = pltpu.make_async_copy(disp, disp_out, sems.at[2 * layers])
    send.start()
    for line in range(layers):
        pltpu.make_async_copy(state.at[line], first_out.at[line], sems.at[line]).wait()
        source = line + lines_here - layers
        pltpu.make_async_copy(state.at[source], last_out.at[line], sems.at[layers + line]).wait()
    for line in range(lines_here):
        wait(line_copies(((state, state_out),) + edges, send_sems, line, lines_here))
    send.wait()


def transport(pot, lanes, left, right, prev_low, prev_high, own, following, before, back, block, layers):
    lines_here, seg_len, channels = left.shape
    bf16, f32 = jnp.bfloat16, jnp.float32
    edge = ((layers, seg_len, channels), bf16)
    side = ((lines_here, EDGE, channels), bf16)
    state = (left.shape, bf16)
    marginal = ((lines_here, seg_len), f32)
    window = seg_len + 2 * block
    return kernel_call(
        functools.partial(transport_kernel, block),
        (pot, lanes, left, right, prev_low, prev_high, own, following, before, back),
        (state, marginal, edge, edge, side, side),
        (
            (pot.shape, f32),
            (lanes.shape, bf16),
            state,
            ((lines_here, 2 * seg_len, channels), bf16),
            marginal,
            marginal,
            marginal,
            marginal,
            state,
            marginal,
            ((2 * seg_len, channels), bf16),
            ((window, channels), bf16),
            ((2, 2 * block, window), f32),
            ((2, 2 * block, window), bf16),
        ),
        (5 * lines_here, max(5, 2 * layers + 1), 3 * lines_here),
        "transport",
    )


def stack_weights(weight_ref, stacked_ref):
    layers, taps, _, channels, _ = weight_ref.shape
    zeros = jnp.zeros((channels, channels), stacked_ref.dtype)
    for layer in range(layers):
        for col_tap in range(taps):
            for line in range(taps + 1):
                row = (col_tap * (taps + 1) + line) * channels
                for out in range(2):
                    row_tap = line - out
                    stacked_ref[
                        layer, row : row + channels, out * channels : (out + 1) * channels
                    ] = weight_ref[layer, row_tap, col_tap] if 0 <= row_tap < taps else zeros


def conv_kernel(
    state_in,
    top_in,
    bottom_in,
    left_in,
    right_in,
    corner_top_in,
    corner_bottom_in,
    weight_in,
    bias_in,
    result_out,
    state_ref,
    top_ref,
    bottom_ref,
    left_ref,
    right_ref,
    corner_top_ref,
    corner_bottom_ref,
    weight_ref,
    bias_ref,
    out_ref,
    first_image,
    second_image,
    sems,
    send_sems,
):
    fetches = copies_of(
        (
            (state_in, state_ref),
            (left_in, left_ref),
            (right_in, right_ref),
            (corner_top_in, corner_top_ref),
            (corner_bottom_in, corner_bottom_ref),
            (top_in, top_ref),
            (bottom_in, bottom_ref),
            (weight_in, weight_ref),
            (bias_in, bias_ref),
        ),
        sems,
    )
    begin_copies(fetches)
    lines_here, seg_len, channels = state_ref.shape
    layers = weight_ref.shape[0]
    after = layers + lines_here
    right = EDGE + seg_len
    f32 = jnp.float32
    wait(fetches[:1])
    first_image[layers:after, EDGE:right] = state_ref[...].astype(f32)
    wait(fetches[1:])
    first_image[:layers, EDGE:right] = top_ref[...].astype(f32)
    first_image[after:, EDGE:right] = bottom_ref[...].astype(f32)
    first_image[layers:after, :EDGE] = left_ref[...].astype(f32)
    first_image[layers:after, right:] = right_ref[...].astype(f32)
    for rows, corner_ref in ((slice(0, layers), corner_top_ref), (slice(after, None), corner_bottom_ref)):
        first_image[rows, :EDGE] = corner_ref[:, :EDGE].astype(f32)
        first_image[rows, right:] = corner_ref[:, EDGE:].astype(f32)
    line0 = lax.axis_index("lines") * lines_here - layers
    all_lines = lax.axis_size("lines") * lines_here
    px0 = lax.axis_index("seg") * seg_len - EDGE
    all_px = lax.axis_size("seg") * seg_len
    source, target = first_image, second_image
    for layer in range(layers):
        reach = layers - 1 - layer
        begin, end = (EDGE // 2, right + EDGE // 2) if reach else (EDGE, right)
        pieces = 5 if reach else 4
        size = (end - begin) // pieces

        def pair(index, carry, layer=layer, reach=reach, begin=begin, pieces=pieces, size=size, source=source, target=target):
            base = layer + 2 * index
            for piece in range(pieces):
                start = begin + piece * size
                taps = [
                    source[base + line, start + col_tap - 1 : start + col_tap - 1 + size].astype(jnp.bfloat16)
                    for col_tap in range(3)
                    for line in range(4)
                ]
                total = jnp.dot(
                    jnp.concatenate(taps, axis=1), weight_ref[layer], preferred_element_type=f32
                )
                for out in range(2):
                    line = base + 1 + out
                    part = total[:, out * channels : (out + 1) * channels] + bias_ref[layer : layer + 1]
                    updated = source[line, start : start + size] + jnp.maximum(part, 0.0)
                    if not reach:
                        out_ref[line - layers, start - EDGE : start - EDGE + size] = updated.astype(out_ref.dtype)
                        continue
                    image_line = line0 + line
                    inside = (image_line >= 0) & (image_line < all_lines)
                    if piece in (0, pieces - 1):
                        px = px0 + start + lax.broadcasted_iota(jnp.int32, updated.shape, 0)
                        inside = inside & (px >= 0) & (px < all_px)
                    updated = jnp.where(inside, updated, 0.0)
                    target[line, start : start + size] = updated.astype(jnp.bfloat16).astype(f32)
            if not reach:
                for line in (base + 1, base + 2):
                    begin_copies(line_copies(((out_ref, result_out),), send_sems, line - layers, lines_here))
            return carry

        lax.fori_loop(0, (lines_here + 2 * reach) // 2, pair, 0)
        source, target = target, source
    for line in range(lines_here):
        wait(line_copies(((out_ref, result_out),), send_sems, line, lines_here))


def conv_layers(state, top, bottom, left_px, right_px, corners_top, corners_bottom, weight, bias):
    layers = weight.shape[0]
    lines_here, seg_len, channels = state.shape
    image = ((lines_here + 2 * layers, seg_len + 2 * EDGE, channels), jnp.float32)
    operands = (state, top, bottom, left_px, right_px, corners_top, corners_bottom, weight, bias)
    result = (state.shape, state.dtype)
    return kernel_call(
        conv_kernel,
        operands,
        (result,),
        tuple((operand.shape, operand.dtype) for operand in operands) + (result, image, image),
        (len(operands), lines_here),
        "conv_layers",
    )[0]


def shards(left_features, right_features, conv_weight, conv_bias):
    seg_len = left_features.shape[1]
    half = seg_len // 2
    layers = conv_weight.shape[0]
    prev_high = shifted(right_features[:, half:], "seg", 1)
    next_low = shifted(left_features[:, :half], "seg", -1)
    prev_low = shifted(right_features[:, :half], "seg", 1)
    stacked, own = own_partials(left_features, right_features, conv_weight)
    own, back = cross_partials(left_features, prev_high, next_low, right_features, own)
    before = shifted(own, "seg", 1)
    following = shifted(back, "seg", -1)
    block = min(128, half)
    pot, lanes, own, back = row_pass(
        left_features, right_features, prev_low, prev_high, own, following, before, back, block
    )
    before = shifted(own, "seg", 1)
    following = shifted(back, "seg", -1)
    state, disparity, first, last, low, high = transport(
        pot, lanes, left_features, right_features, prev_low, prev_high, own, following, before, back, block, layers
    )
    bottom = shifted(first, "lines", -1)
    top = shifted(last, "lines", 1)
    left_px = shifted(high, "seg", 1)
    right_px = shifted(low, "seg", -1)
    edges = jnp.concatenate([left_px, right_px], axis=1)
    corners_bottom = shifted(edges[:layers], "lines", -1)
    corners_top = shifted(edges[-layers:], "lines", 1)
    refined = conv_layers(
        state, top, bottom, left_px, right_px, corners_top, corners_bottom, stacked, conv_bias
    )
    return (refined, disparity)


def solution(mesh):
    return jax.shard_map(
        shards,
        mesh=mesh,
        in_specs=(P("lines", "seg", None), P("lines", "seg", None), P(), P()),
        out_specs=(P("lines", "seg", None), P("lines", "seg")),
        check_vma=False,
    )
```

time: 108 us -> 102 us (0.944)
  local copies, waits for them, and re-layouts: 6.12 us -> 2.55 us
  Pallas kernels: 44.4 us -> 41.4 us
    unnamed x27 -> x9, local copies, waits for them, and re-layouts: 3.74 us -> 0.02 us
    pallas_call x5, Pallas kernels: 44.4 us -> 41.4 us  [kernel_call(): pl.pallas_call(kernel, in_specs=[ANYWHERE] * len(operands), out_specs=[AN...]
  transfers between devices with their start and end apart: 13 -> 13, of which waited for: 5 -> 7; matrix products, arithmetic and copies ran while one was open for 1% -> 1% of each run, Pallas kernels for 11% -> 10%
where the time goes in v4:
time: 102 us; the launch traced here: 101 us
  starting transfers between devices  41.7 us (41%)
  Pallas kernels  41.4 us (41%)
  waiting for transfers between devices  14.8 us (15%)
  local copies, waits for them, and re-layouts  2.55 us (2%)
    ppermute x13, starting transfers between devices, shifted(): return lax.ppermute(block, axis, route)  41.7 us
    pallas_call x5, Pallas kernels, kernel_call(): pl.pallas_call(kernel, in_specs=[ANYWHERE] * len(operands), out_specs=[AN...  41.4 us
    ppermute x13, waiting for transfers between devices, shifted(): return lax.ppermute(block, axis, route)  14.8 us
  transfers between devices with their start and end apart: 13, of which 7 were waited for; matrix products, arithmetic and copies ran while one was open for 1% of the time, Pallas kernels for 10%

profile of v4, /device:TPU:1, one launch (start us, length us, event | category | flops | bytes accessed | tf_op | source)
XLA Modules:
  0.0 101.3 jit_solution(16117323976539956385)
XLA Ops:
  0.6 0.0 copy-start
  0.7 1.2 %slice.17 = bf16[4,512,128]{2,1,0:T(8,128)(2,1)S(1)} slice(bf16[4,1024,128]{2,1,0:T(8,128)(2,1)} %left_in.7), slice={[0:4], [0:512], [0:128]} | slice | bytes 1048576 | tf_op jit(solution)/shard_map/slice | solution.py:772
  1.9 1.3 %collective-permute-start.2 = (bf16[4,512,128]{2,1,0:T(8,128)(2,1)S(1)}, bf16[4,512,128]{2,1,0:T(8,128)(2,1)S(1)}, u32[]{:S(2)}, u32[]{:S(2)}) collective-permute-start(bf16[4,512,128]{2,1,0:T(8,128)(2,1)S(1)} %slice.17), channel_id=1, source_target_pairs={{8,0},{16,8},{24,16},{9,1},{17,9},{25,17},{10,2},{18,10},{26,18},{... | collective-permute-start | bytes 1572872 | tf_op jit(solution)/shard_map/ppermute | solution.py:20
  3.2 1.3 %fusion = (bf16[4,512,128]{2,1,0:T(8,128)(2,1)S(1)}, bf16[4,512,128]{2,1,0:T(8,128)(2,1)S(1)}) fusion(bf16[4,1024,128]{2,1,0:T(8,128)(2,1)} %right_in.7), kind=kLoop, calls=%fused_computation.2 | loop fusion | bytes 2097152 | tf_op jit(solution)/shard_map/slice | solution.py:771
  4.5 4.7 %collective-permute-start.1 = (bf16[4,512,128]{2,1,0:T(8,128)(2,1)S(1)}, bf16[4,512,128]{2,1,0:T(8,128)(2,1)S(1)}, u32[]{:S(2)}, u32[]{:S(2)}) collective-permute-start(bf16[4,512,128]{2,1,0:T(8,128)(2,1)S(1)} %get-tuple-element.30), channel_id=1, source_target_pairs={{0,8},{8,16},{16,24},{1,9},{9,17},{17,25},{2,10},{10,18},{18,26},{... | collective-permute-start | bytes 1572872 | tf_op jit(solution)/shard_map/ppermute | solution.py:20
  9.2 3.4 %collective-permute-start = (bf16[4,512,128]{2,1,0:T(8,128)(2,1)S(1)}, bf16[4,512,128]{2,1,0:T(8,128)(2,1)S(1)}, u32[]{:S(2)}, u32[]{:S(2)}) collective-permute-start(bf16[4,512,128]{2,1,0:T(8,128)(2,1)S(1)} %get-tuple-element.31), channel_id=1, source_target_pairs={{0,8},{8,16},{16,24},{1,9},{9,17},{17,25},{2,10},{10,18},{18,26},{... | collective-permute-start | bytes 1572872 | tf_op jit(solution)/shard_map/ppermute | solution.py:20
  12.6 4.4 %column_own.1 = (bf16[3,1536,256]{2,1,0:T(8,128)(2,1)S(1)}, f32[8,1024]{1,0:T(8,128)S(1)}) custom-call(bf16[4,1024,128]{2,1,0:T(8,128)(2,1)S(1)} %copy-done.1, bf16[4,1024,128]{2,1,0:T(8,128)(2,1)S(1)} %copy-done, bf16[3,3,3,128,128]{4,3,2,1,0:T(8,128)(2,1)S(1)} %copy-done.3), custom_call_target="tpu_custom_call" | custom-call | flops 1073741824 | bytes 4194304 | tf_op jit(solution)/shard_map/column_own/pallas_call | solution.py:31
  17.0 0.5 collective-permute-done.2.next_in
  17.6 2.2 %collective-permute-done.1.prev_in.prev_high_in = bf16[4,512,128]{2,1,0:T(8,128)(2,1)S(1)} collective-permute-done((bf16[4,512,128]{2,1,0:T(8,128)(2,1)S(1)}, bf16[4,512,128]{2,1,0:T(8,128)(2,1)S(1)}, u32[]{:S(2)}, u32[]{:S(2)}) %collective-permute-start.1) | collective-permute-done | bytes 524320 | tf_op jit(solution)/shard_map/ppermute | solution.py:20
  19.7 5.7 %column_cross.1 = (f32[8,1024]{1,0:T(8,128)S(1)}, f32[8,512]{1,0:T(8,128)S(1)}) custom-call(bf16[4,1024,128]{2,1,0:T(8,128)(2,1)S(1)} %copy-done.1, bf16[4,512,128]{2,1,0:T(8,128)(2,1)S(1)} %collective-permute-done.1.prev_in.prev_high_in, bf16[4,512,128]{2,1,0:T(8,128)(2,1)S(1)} %collective-permute-done.2.next_in, bf16[4,1024,128]{2,1,0:T(8,128)(2,1)S(1)} %copy-done, ...), custom_call_target="tpu_custom_call" | custom-call | flops 1073741824 | bytes 4194304 | tf_op jit(solution)/shard_map/column_cross/pallas_call | solution.py:31
  25.4 4.1 %collective-permute-start.4 = (f32[8,1024]{1,0:T(8,128)S(1)}, f32[8,1024]{1,0:T(8,128)S(1)}, u32[]{:S(2)}, u32[]{:S(2)}) collective-permute-start(f32[8,1024]{1,0:T(8,128)S(1)} %get-tuple-element.17.own_in), channel_id=1, source_target_pairs={{0,8},{8,16},{16,24},{1,9},{9,17},{17,25},{2,10},{10,18},{18,26},{... | collective-permute-start | bytes 98312 | tf_op jit(solution)/shard_map/ppermute | solution.py:20
  29.5 1.3 %collective-permute-start.3 = (f32[8,512]{1,0:T(8,128)S(1)}, f32[8,512]{1,0:T(8,128)S(1)}, u32[]{:S(2)}, u32[]{:S(2)}) collective-permute-start(f32[8,512]{1,0:T(8,128)S(1)} %get-tuple-element.18.back_in), channel_id=1, source_target_pairs={{8,0},{16,8},{24,16},{9,1},{17,9},{25,17},{10,2},{18,10},{26,18},{... | collective-permute-start | bytes 49160 | tf_op jit(solution)/shard_map/ppermute | solution.py:20
  30.8 0.1 collective-permute-done.prev_low_in
  31.0 3.1 %collective-permute-done.3.next_in = f32[8,512]{1,0:T(8,128)S(1)} collective-permute-done((f32[8,512]{1,0:T(8,128)S(1)}, f32[8,512]{1,0:T(8,128)S(1)}, u32[]{:S(2)}, u32[]{:S(2)}) %collective-permute-start.3) | collective-permute-done | bytes 16416 | tf_op jit(solution)/shard_map/ppermute | solution.py:20
  34.0 9.3 %row_pass.1 = (f32[4,2048]{1,0:T(4,128)S(1)}, bf16[4,1024,128]{2,1,0:T(8,128)(2,1)S(1)}, f32[4,1024]{1,0:T(4,128)S(1)}, f32[4,1024]{1,0:T(4,128)S(1)}) custom-call(bf16[4,1024,128]{2,1,0:T(8,128)(2,1)S(1)} %copy-done.1, bf16[4,1024,128]{2,1,0:T(8,128)(2,1)S(1)} %copy-done, bf16[4,512,128]{2,1,0:T(8,128)(2,1)S(1)} %collective-permute-done.prev_low_in, ...), custom_call_target="tpu_custom_call" | custom-call | tf_op jit(solution)/shard_map/row_pass/pallas_call | solution.py:31
  43.3 0.0 copy-start.2
  43.4 3.3 %collective-permute-start.6 = (f32[4,1024]{1,0:T(4,128)S(1)}, f32[4,1024]{1,0:T(4,128)S(1)}, u32[]{:S(2)}, u32[]{:S(2)}) collective-permute-start(f32[4,1024]{1,0:T(4,128)S(1)} %get-tuple-element.21.own_in), channel_id=1, source_target_pairs={{0,8},{8,16},{16,24},{1,9},{9,17},{17,25},{2,10},{10,18},{18,26},{... | collective-permute-start | bytes 49160 | tf_op jit(solution)/shard_map/ppermute | solution.py:20
  46.7 1.3 %collective-permute-start.5 = (f32[4,1024]{1,0:T(4,128)S(1)}, f32[4,1024]{1,0:T(4,128)S(1)}, u32[]{:S(2)}, u32[]{:S(2)}) collective-permute-start(f32[4,1024]{1,0:T(4,128)S(1)} %get-tuple-element.22.back_in), channel_id=1, source_target_pairs={{8,0},{16,8},{24,16},{9,1},{17,9},{25,17},{10,2},{18,10},{26,18},{... | collective-permute-start | bytes 49160 | tf_op jit(solution)/shard_map/ppermute | solution.py:20
  48.0 0.0 collective-permute-done.6.before_in
  48.0 3.2 %collective-permute-done.5.next_in = f32[4,1024]{1,0:T(4,128)S(1)} collective-permute-done((f32[4,1024]{1,0:T(4,128)S(1)}, f32[4,1024]{1,0:T(4,128)S(1)}, u32[]{:S(2)}, u32[]{:S(2)}) %collective-permute-start.5) | collective-permute-done | bytes 16416 | tf_op jit(solution)/shard_map/ppermute | solution.py:20
  51.2 10.3 %transport.1 = (bf16[4,1024,128]{2,1,0:T(8,128)(2,1)S(1)}, f32[4,1024]{1,0:T(4,128)}, bf16[3,1024,128]{2,1,0:T(8,128)(2,1)S(1)}, bf16[3,1024,128]{2,1,0:T(8,128)...) custom-call(f32[4,2048]{1,0:T(4,128)S(1)} %get-tuple-element.19.pot_in, ...), custom_call_target="tpu_custom_call" | custom-call | tf_op jit(solution)/shard_map/transport/pallas_call | solution.py:31
  61.5 8.9 %collective-permute-start.7 = (bf16[3,1024,128]{2,1,0:T(8,128)(2,1)S(1)}, bf16[3,1024,128]{2,1,0:T(8,128)(2,1)S(1)}, u32[]{:S(2)}, u32[]{:S(2)}) collective-permute-start(bf16[3,1024,128]{2,1,0:T(8,128)(2,1)S(1)} %get-tuple-element.24), channel_id=1, source_target_pairs={{0,1},{1,2},{2,3},{3,4},{4,5},{5,6},{6,7},{8,9},{9,10},{10,11},{11... | collective-permute-start | bytes 2359304 | tf_op jit(solution)/shard_map/ppermute | solution.py:20
  70.4 1.9 %collective-permute-start.8 = (bf16[3,1024,128]{2,1,0:T(8,128)(2,1)S(1)}, bf16[3,1024,128]{2,1,0:T(8,128)(2,1)S(1)}, u32[]{:S(2)}, u32[]{:S(2)}) collective-permute-start(bf16[3,1024,128]{2,1,0:T(8,128)(2,1)S(1)} %get-tuple-element.25), channel_id=1, source_target_pairs={{1,0},{2,1},{3,2},{4,3},{5,4},{6,5},{7,6},{9,8},{10,9},{11,10},{12... | collective-permute-start | bytes 2359304 | tf_op jit(solution)/shard_map/ppermute | solution.py:20
  72.3 3.2 %collective-permute-start.9 = (bf16[4,16,128]{2,1,0:T(8,128)(2,1)S(1)}, bf16[4,16,128]{2,1,0:T(8,128)(2,1)S(1)}, u32[]{:S(2)}, u32[]{:S(2)}) collective-permute-start(bf16[4,16,128]{2,1,0:T(8,128)(2,1)S(1)} %get-tuple-element.26), channel_id=1, source_target_pairs={{0,8},{8,16},{16,24},{1,9},{9,17},{17,25},{2,10},{10,18},{18,26},{... | collective-permute-start | bytes 49160 | tf_op jit(solution)/shard_map/ppermute | solution.py:20
  75.6 1.3 %collective-permute-start.10 = (bf16[4,16,128]{2,1,0:T(8,128)(2,1)S(1)}, bf16[4,16,128]{2,1,0:T(8,128)(2,1)S(1)}, u32[]{:S(2)}, u32[]{:S(2)}) collective-permute-start(bf16[4,16,128]{2,1,0:T(8,128)(2,1)S(1)} %get-tuple-element.27), channel_id=1, source_target_pairs={{8,0},{16,8},{24,16},{9,1},{17,9},{25,17},{10,2},{18,10},{26,18},{... | collective-permute-start | bytes 49160 | tf_op jit(solution)/shard_map/ppermute | solution.py:20
  76.9 0.0 collective-permute-done.9.left_in
  76.9 3.2 %collective-permute-done.10.right_in = bf16[4,16,128]{2,1,0:T(8,128)(2,1)S(1)} collective-permute-done((bf16[4,16,128]{2,1,0:T(8,128)(2,1)S(1)}, bf16[4,16,128]{2,1,0:T(8,128)(2,1)S(1)}, u32[]{:S(2)}, u32[]{:S(2)}) %collective-permute-start.10) | collective-permute-done | bytes 16416 | tf_op jit(solution)/shard_map/ppermute | solution.py:20
  80.1 1.9 %collective-permute-start.12 = (bf16[3,32,128]{2,1,0:T(8,128)(2,1)S(1)}, bf16[3,32,128]{2,1,0:T(8,128)(2,1)S(1)}, u32[]{:S(2)}, u32[]{:S(2)}) collective-permute-start(bf16[3,32,128]{2,1,0:T(8,128)(2,1)S(1)} %get-tuple-element.32), channel_id=1, source_target_pairs={{1,0},{2,1},{3,2},{4,3},{5,4},{6,5},{7,6},{9,8},{10,9},{11,10},{12... | collective-permute-start | bytes 73736 | tf_op jit(solution)/shard_map/ppermute | solution.py:20
  82.0 5.1 %collective-permute-start.11 = (bf16[3,32,128]{2,1,0:T(8,128)(2,1)S(1)}, bf16[3,32,128]{2,1,0:T(8,128)(2,1)S(1)}, u32[]{:S(2)}, u32[]{:S(2)}) collective-permute-start(bf16[3,32,128]{2,1,0:T(8,128)(2,1)S(1)} %get-tuple-element.33), channel_id=1, source_target_pairs={{0,1},{1,2},{2,3},{3,4},{4,5},{5,6},{6,7},{8,9},{9,10},{10,11},{11... | collective-permute-start | bytes 73736 | tf_op jit(solution)/shard_map/ppermute | solution.py:20
  87.1 2.6 %collective-permute-done.12.corner_bottom_in = bf16[3,32,128]{2,1,0:T(8,128)(2,1)S(1)} collective-permute-done((bf16[3,32,128]{2,1,0:T(8,128)(2,1)S(1)}, bf16[3,32,128]{2,1,0:T(8,128)(2,1)S(1)}, u32[]{:S(2)}, u32[]{:S(2)}) %collective-permute-start.12) | collective-permute-done | bytes 24608 | tf_op jit(solution)/shard_map/ppermute | solution.py:20
  89.7 0.0 collective-permute-done.11.corner_top_in
  89.7 11.6 %conv_layers.1 = bf16[4,1024,128]{2,1,0:T(8,128)(2,1)} custom-call(bf16[4,1024,128]{2,1,0:T(8,128)(2,1)S(1)} %get-tuple-element.23.state_in, bf16[3,1024,128]{2,1,0:T(8,128)(2,1)S(1)} %collective-permute-done.7.top_in, bf16[3,1024,128]{2,1,0:T(8,128)(2,1)S(1)} %collective-permute-done.8.bottom_in, bf16[4,16,128]{2,1,0:T(8,128)(2,1)S(1)} %collective-permute-done.9.left_in, ...), custom_call_target="tpu_custom_call" | custom-call | tf_op jit(solution)/shard_map/conv_layers/pallas_call | solution.py:31
  (12 shorter events, 0.0 us)
Async XLA Ops:
  0.6 11.9 %copy-start.1 = (bf16[4,1024,128]{2,1,0:T(8,128)(2,1)S(1)}, bf16[4,1024,128]{2,1,0:T(8,128)(2,1)}, u32[]{:S(2)}) copy-start(bf16[4,1024,128]{2,1,0:T(8,128)(2,1)} %left_in.7) | copy-start | bytes 3145732
  0.6 11.9 %copy-start = (bf16[4,1024,128]{2,1,0:T(8,128)(2,1)S(1)}, bf16[4,1024,128]{2,1,0:T(8,128)(2,1)}, u32[]{:S(2)}) copy-start(bf16[4,1024,128]{2,1,0:T(8,128)(2,1)} %right_in.7) | copy-start | bytes 3145732
  0.7 11.9 %copy-start.3 = (bf16[3,3,3,128,128]{4,3,2,1,0:T(8,128)(2,1)S(1)}, bf16[3,3,3,128,128]{4,3,2,1,0:T(8,128)(2,1)}, u32[]{:S(2)}) copy-start(bf16[3,3,3,128,128]{4,3,2,1,0:T(8,128)(2,1)} %weight_in.1) | copy-start | bytes 2654212
  1.9 15.7 %collective-permute-start.2 = (bf16[4,512,128]{2,1,0:T(8,128)(2,1)S(1)}, bf16[4,512,128]{2,1,0:T(8,128)(2,1)S(1)}, u32[]{:S(2)}, u32[]{:S(2)}) collective-permute-start(bf16[4,512,128]{2,1,0:T(8,128)(2,1)S(1)} %slice.17), channel_id=1, source_target_pairs={{8,0},{16,8},{24,16},{9,1},{17,9},{25,17},{10,2},{18,10},{26,18},{... | collective-permute-start | bytes 1572872 | tf_op jit(solution)/shard_map/ppermute | solution.py:20
  4.5 15.2 %collective-permute-start.1 = (bf16[4,512,128]{2,1,0:T(8,128)(2,1)S(1)}, bf16[4,512,128]{2,1,0:T(8,128)(2,1)S(1)}, u32[]{:S(2)}, u32[]{:S(2)}) collective-permute-start(bf16[4,512,128]{2,1,0:T(8,128)(2,1)S(1)} %get-tuple-element.30), channel_id=1, source_target_pairs={{0,8},{8,16},{16,24},{1,9},{9,17},{17,25},{2,10},{10,18},{18,26},{... | collective-permute-start | bytes 1572872 | tf_op jit(solution)/shard_map/ppermute | solution.py:20
  9.2 21.8 %collective-permute-start = (bf16[4,512,128]{2,1,0:T(8,128)(2,1)S(1)}, bf16[4,512,128]{2,1,0:T(8,128)(2,1)S(1)}, u32[]{:S(2)}, u32[]{:S(2)}) collective-permute-start(bf16[4,512,128]{2,1,0:T(8,128)(2,1)S(1)} %get-tuple-element.31), channel_id=1, source_target_pairs={{0,8},{8,16},{16,24},{1,9},{9,17},{17,25},{2,10},{10,18},{18,26},{... | collective-permute-start | bytes 1572872 | tf_op jit(solution)/shard_map/ppermute | solution.py:20
  25.4 8.6 %collective-permute-start.4 = (f32[8,1024]{1,0:T(8,128)S(1)}, f32[8,1024]{1,0:T(8,128)S(1)}, u32[]{:S(2)}, u32[]{:S(2)}) collective-permute-start(f32[8,1024]{1,0:T(8,128)S(1)} %get-tuple-element.17.own_in), channel_id=1, source_target_pairs={{0,8},{8,16},{16,24},{1,9},{9,17},{17,25},{2,10},{10,18},{18,26},{... | collective-permute-start | bytes 98312 | tf_op jit(solution)/shard_map/ppermute | solution.py:20
  29.5 4.5 %collective-permute-start.3 = (f32[8,512]{1,0:T(8,128)S(1)}, f32[8,512]{1,0:T(8,128)S(1)}, u32[]{:S(2)}, u32[]{:S(2)}) collective-permute-start(f32[8,512]{1,0:T(8,128)S(1)} %get-tuple-element.18.back_in), channel_id=1, source_target_pairs={{8,0},{16,8},{24,16},{9,1},{17,9},{25,17},{10,2},{18,10},{26,18},{... | collective-permute-start | bytes 49160 | tf_op jit(solution)/shard_map/ppermute | solution.py:20
  43.3 46.4 %copy-start.2 = (f32[3,128]{1,0:T(4,128)S(1)}, f32[3,128]{1,0:T(4,128)}, u32[]{:S(2)}) copy-start(f32[3,128]{1,0:T(4,128)} %bias_in.1) | copy-start | bytes 4612
  43.4 4.6 %collective-permute-start.6 = (f32[4,1024]{1,0:T(4,128)S(1)}, f32[4,1024]{1,0:T(4,128)S(1)}, u32[]{:S(2)}, u32[]{:S(2)}) collective-permute-start(f32[4,1024]{1,0:T(4,128)S(1)} %get-tuple-element.21.own_in), channel_id=1, source_target_pairs={{0,8},{8,16},{16,24},{1,9},{9,17},{17,25},{2,10},{10,18},{18,26},{... | collective-permute-start | bytes 49160 | tf_op jit(solution)/shard_map/ppermute | solution.py:20
  46.7 4.5 %collective-permute-start.5 = (f32[4,1024]{1,0:T(4,128)S(1)}, f32[4,1024]{1,0:T(4,128)S(1)}, u32[]{:S(2)}, u32[]{:S(2)}) collective-permute-start(f32[4,1024]{1,0:T(4,128)S(1)} %get-tuple-element.22.back_in), channel_id=1, source_target_pairs={{8,0},{16,8},{24,16},{9,1},{17,9},{25,17},{10,2},{18,10},{26,18},{... | collective-permute-start | bytes 49160 | tf_op jit(solution)/shard_map/ppermute | solution.py:20
  61.5 28.2 %collective-permute-start.7 = (bf16[3,1024,128]{2,1,0:T(8,128)(2,1)S(1)}, bf16[3,1024,128]{2,1,0:T(8,128)(2,1)S(1)}, u32[]{:S(2)}, u32[]{:S(2)}) collective-permute-start(bf16[3,1024,128]{2,1,0:T(8,128)(2,1)S(1)} %get-tuple-element.24), channel_id=1, source_target_pairs={{0,1},{1,2},{2,3},{3,4},{4,5},{5,6},{6,7},{8,9},{9,10},{10,11},{11... | collective-permute-start | bytes 2359304 | tf_op jit(solution)/shard_map/ppermute | solution.py:20
  70.4 19.3 %collective-permute-start.8 = (bf16[3,1024,128]{2,1,0:T(8,128)(2,1)S(1)}, bf16[3,1024,128]{2,1,0:T(8,128)(2,1)S(1)}, u32[]{:S(2)}, u32[]{:S(2)}) collective-permute-start(bf16[3,1024,128]{2,1,0:T(8,128)(2,1)S(1)} %get-tuple-element.25), channel_id=1, source_target_pairs={{1,0},{2,1},{3,2},{4,3},{5,4},{6,5},{7,6},{9,8},{10,9},{11,10},{12... | collective-permute-start | bytes 2359304 | tf_op jit(solution)/shard_map/ppermute | solution.py:20
  72.3 4.5 %collective-permute-start.9 = (bf16[4,16,128]{2,1,0:T(8,128)(2,1)S(1)}, bf16[4,16,128]{2,1,0:T(8,128)(2,1)S(1)}, u32[]{:S(2)}, u32[]{:S(2)}) collective-permute-start(bf16[4,16,128]{2,1,0:T(8,128)(2,1)S(1)} %get-tuple-element.26), channel_id=1, source_target_pairs={{0,8},{8,16},{16,24},{1,9},{9,17},{17,25},{2,10},{10,18},{18,26},{... | collective-permute-start | bytes 49160 | tf_op jit(solution)/shard_map/ppermute | solution.py:20
  75.6 4.5 %collective-permute-start.10 = (bf16[4,16,128]{2,1,0:T(8,128)(2,1)S(1)}, bf16[4,16,128]{2,1,0:T(8,128)(2,1)S(1)}, u32[]{:S(2)}, u32[]{:S(2)}) collective-permute-start(bf16[4,16,128]{2,1,0:T(8,128)(2,1)S(1)} %get-tuple-element.27), channel_id=1, source_target_pairs={{8,0},{16,8},{24,16},{9,1},{17,9},{25,17},{10,2},{18,10},{26,18},{... | collective-permute-start | bytes 49160 | tf_op jit(solution)/shard_map/ppermute | solution.py:20
  80.1 9.6 %collective-permute-start.12 = (bf16[3,32,128]{2,1,0:T(8,128)(2,1)S(1)}, bf16[3,32,128]{2,1,0:T(8,128)(2,1)S(1)}, u32[]{:S(2)}, u32[]{:S(2)}) collective-permute-start(bf16[3,32,128]{2,1,0:T(8,128)(2,1)S(1)} %get-tuple-element.32), channel_id=1, source_target_pairs={{1,0},{2,1},{3,2},{4,3},{5,4},{6,5},{7,6},{9,8},{10,9},{11,10},{12... | collective-permute-start | bytes 73736 | tf_op jit(solution)/shard_map/ppermute | solution.py:20
  82.0 7.7 %collective-permute-start.11 = (bf16[3,32,128]{2,1,0:T(8,128)(2,1)S(1)}, bf16[3,32,128]{2,1,0:T(8,128)(2,1)S(1)}, u32[]{:S(2)}, u32[]{:S(2)}) collective-permute-start(bf16[3,32,128]{2,1,0:T(8,128)(2,1)S(1)} %get-tuple-element.33), channel_id=1, source_target_pairs={{0,1},{1,2},{2,3},{3,4},{4,5},{5,6},{6,7},{8,9},{9,10},{10,11},{11... | collective-permute-start | bytes 73736 | tf_op jit(solution)/shard_map/ppermute | solution.py:20

commit v5 on v4

--- a/solution.py
+++ b/solution.py
@@ -18,6 +18,22 @@
     count = lax.axis_size(axis)
     route = [(i, i + step) for i in range(count) if 0 <= i + step < count]
     return lax.ppermute(block, axis, route)
+
+
+def exchanged(block, axis, odd):
+    route = []
+    for low in range(odd, lax.axis_size(axis) - 1, 2):
+        route += [(low, low + 1), (low + 1, low)]
+    return lax.ppermute(block, axis, route)
+
+
+def even_segment():
+    return lax.rem(lax.axis_index("seg"), 2) == 0
+
+
+def by_parity(following, previous):
+    even = even_segment()
+    return jnp.where(even, following, previous), jnp.where(even, previous, following)
 
 
 def params():
@@ -165,41 +181,82 @@
     )
 
 
-def cross_kernel(
-    block,
-    left_in,
-    prev_in,
-    next_in,
-    right_in,
-    own_in,
-    merged_out,
-    back_out,
-    left,
-    prev,
-    following,
-    right,
-    own,
-    merged,
-    back,
-    line_sems,
-    sems,
+def next_kernel(
+    block, next_in, right_in, own_in, merged_out, following, right, merged, line_sems, sems
 ):
     lines_here, half = following.shape[:2]
-    pairs = (
-        (left_in, left),
-        (prev_in, prev),
-        (next_in, following),
-        (right_in.at[:, pl.ds(0, half)], right),
-    )
-    fetch, send_merged, send_back = copies_of(
-        ((own_in, own), (merged, merged_out), (back, back_out)), sems
-    )
+    pairs = ((next_in, following), (right_in.at[:, pl.ds(0, half)], right))
+    fetch, send = copies_of(((own_in, merged), (merged, merged_out)), sems)
     fetch.start()
     for line in range(lines_here):
         begin_copies(line_copies(pairs, line_sems, line, lines_here))
     fetch.wait()
     last = lax.axis_index("seg") == lax.axis_size("seg") - 1
-    merged[:, half:] = own[:, half:]
+
+    def one_line(line, carry):
+        wait(line_copies(pairs, line_sems, line, lines_here))
+        top, bottom = pl.ds(line, 1), pl.ds(lines_here + line, 1)
+        for first in range(0, half, block):
+            cols = slice(first, first + block)
+            peak, total = column_block(following[line, : first + block], right[line, cols], False)
+            peak = jnp.where(last, NEG, peak)
+            total = jnp.where(last, 0.0, total)
+            own_peak = merged[top, cols]
+            joint = jnp.maximum(own_peak, peak)
+            merged[bottom, cols] = merged[bottom, cols] * jnp.exp2(
+                own_peak - joint
+            ) + total * jnp.exp2(peak - joint)
+            merged[top, cols] = joint
+        return carry
+
+    lax.fori_loop(0, lines_here, one_line, 0)
+    send.start()
+    send.wait()
+
+
+def next_partials(next_low, right, own):
+    lines_here, half, channels = next_low.shape
+    merged = (own.shape, jnp.float32)
+    features = (next_low.shape, jnp.bfloat16)
+    return kernel_call(
+        functools.partial(next_kernel, min(256, half)),
+        (next_low, right, own),
+        (merged,),
+        (features, features, merged),
+        (2 * lines_here, 2),
+        "column_next",
+        column_cost(lines_here, half, channels),
+    )[0]
+
+
+def cross_kernel(
+    block,
+    left_in,
+    prev_in,
+    own_in,
+    back_out,
+    first_out,
+    second_out,
+    left,
+    prev,
+    own,
+    back,
+    first_part,
+    second_part,
+    line_sems,
+    sems,
+):
+    lines_here, seg_len = left.shape[:2]
+    half = seg_len - prev.shape[1]
+    pairs = ((left_in, left), (prev_in, prev))
+    fetch, *sends = copies_of(
+        ((own_in, own), (back, back_out), (first_part, first_out), (second_part, second_out)), sems
+    )
+    fetch.start()
+    for line in range(lines_here):
+        begin_copies(line_copies(pairs, line_sems, line, lines_here))
+    fetch.wait()
+    back[...] = jnp.zeros_like(back)
 
     def one_line(line, carry):
         wait(line_copies(pairs, line_sems, line, lines_here))
@@ -211,44 +268,23 @@
             )
             back[top, cols] = peak
             back[bottom, cols] = total
-        for first in range(0, half, block):
-            cols = slice(first, first + block)
-            peak, total = column_block(following[line, : first + block], right[line, cols], False)
-            peak = jnp.where(last, NEG, peak)
-            total = jnp.where(last, 0.0, total)
-            own_peak = own[top, cols]
-            joint = jnp.maximum(own_peak, peak)
-            merged[top, cols] = joint
-            merged[bottom, cols] = own[bottom, cols] * jnp.exp2(
-                own_peak - joint
-            ) + total * jnp.exp2(peak - joint)
         return carry
 
     lax.fori_loop(0, lines_here, one_line, 0)
-    begin_copies((send_merged, send_back))
-    wait((send_merged, send_back))
-
-
-def cross_partials(left, prev_high, next_low, right, own):
+    first_part[...], second_part[...] = by_parity(own[...], back[...])
+    begin_copies(sends)
+    wait(sends)
+
+
+def cross_partials(left, prev_high, own):
     lines_here, seg_len, channels = left.shape
-    half = next_low.shape[1]
-    bf16, f32 = jnp.bfloat16, jnp.float32
-    back = ((2 * lines_here, seg_len - half), f32)
-    merged = (own.shape, f32)
+    part = (own.shape, jnp.float32)
     return kernel_call(
-        functools.partial(cross_kernel, min(256, half)),
-        (left, prev_high, next_low, right, own),
-        (merged, back),
-        (
-            (left.shape, bf16),
-            (prev_high.shape, bf16),
-            (next_low.shape, bf16),
-            (next_low.shape, bf16),
-            merged,
-            merged,
-            back,
-        ),
-        (4 * lines_here, 3),
+        functools.partial(cross_kernel, min(256, prev_high.shape[1])),
+        (left, prev_high, own),
+        (part,) * 3,
+        ((left.shape, jnp.bfloat16), (prev_high.shape, jnp.bfloat16)) + (part,) * 4,
+        (2 * lines_here, 4),
         "column_cross",
         column_cost(*left.shape),
     )
@@ -326,23 +362,27 @@
     prev_low_in,
     prev_high_in,
     own_in,
-    next_in,
-    before_in,
     back_in,
+    first_in,
+    second_in,
     pot_out,
     lanes_out,
     own_out,
     prev_out,
+    first_out,
+    second_out,
     left,
     ext,
     own,
-    following,
-    before,
     back,
+    first_part,
+    second_part,
     pot,
     lanes,
     own_sum,
     prev_sum,
+    first_sum,
+    second_sum,
     pot_lanes,
     sums,
     raw,
@@ -353,7 +393,7 @@
     half = prev_low_in.shape[1]
     scale = log2_scale(channels)
     fetches = copies_of(
-        ((own_in, own), (next_in, following), (before_in, before), (back_in, back)), sems
+        ((own_in, own), (back_in, back), (first_in, first_part), (second_in, second_part)), sems
     )
     begin_copies(fetches)
     pairs = feature_pairs(left_in, right_in, prev_low_in, prev_high_in, left, ext)
@@ -361,8 +401,10 @@
         begin_copies(line_copies(pairs, line_sems, line, lines_here))
     wait(fetches)
 
-    def parts(ref, first, stop):
-        return ref[:lines_here, first:stop], ref[lines_here:, first:stop]
+    following, before = by_parity(first_part[...], second_part[...])
+
+    def parts(part, first, stop):
+        return part[:lines_here, first:stop], part[lines_here:, first:stop]
 
     rest = seg_len - half
     pot[:, seg_len : seg_len + half] = potential(*parts(own, 0, half))
@@ -423,39 +465,43 @@
         return carry
 
     lax.fori_loop(0, lines_here, one_line, 0)
+    first_sum[...], second_sum[...] = by_parity(own_sum[...], prev_sum[...])
     sends = copies_of(
-        ((own_sum, own_out), (prev_sum, prev_out), (pot, pot_out), (lanes, lanes_out)), sems
+        (
+            (first_sum, first_out),
+            (second_sum, second_out),
+            (own_sum, own_out),
+            (prev_sum, prev_out),
+            (pot, pot_out),
+            (lanes, lanes_out),
+        ),
+        sems,
     )
     begin_copies(sends)
     wait(sends)
 
 
-def row_pass(left, right, prev_low, prev_high, own, following, before, back, block):
+def row_pass(left, right, prev_low, prev_high, own, back, first, second, block):
     lines_here, seg_len, channels = left.shape
     bf16, f32 = jnp.bfloat16, jnp.float32
+    part = (own.shape, f32)
     marginal = ((lines_here, seg_len), f32)
     pot = ((lines_here, 2 * seg_len), f32)
     lanes = (left.shape, bf16)
     return kernel_call(
         functools.partial(row_kernel, block),
-        (left, right, prev_low, prev_high, own, following, before, back),
-        (pot, lanes, marginal, marginal),
-        (
-            (left.shape, bf16),
-            ((lines_here, 2 * seg_len, channels), bf16),
-            (own.shape, f32),
-            (following.shape, f32),
-            (before.shape, f32),
-            (back.shape, f32),
-            pot,
-            lanes,
-            marginal,
-            marginal,
+        (left, right, prev_low, prev_high, own, back, first, second),
+        (pot, lanes) + (marginal,) * 4,
+        ((left.shape, bf16), ((lines_here, 2 * seg_len, channels), bf16))
+        + (part,) * 4
+        + (pot, lanes)
+        + (marginal,) * 4
+        + (
             ((2 * seg_len, channels), bf16),
             ((8, 2 * seg_len), f32),
             ((2, 2 * block, seg_len + 2 * block), f32),
         ),
-        (4 * lines_here, 4),
+        (4 * lines_here, 6),
         "row_pass",
     )
 
@@ -469,25 +515,27 @@
     prev_low_in,
     prev_high_in,
     own_in,
-    next_in,
-    before_in,
     back_in,
+    first_in,
+    second_in,
     state_out,
     disp_out,
     first_out,
     last_out,
-    low_out,
-    high_out,
+    first_px_out,
+    second_px_out,
     pot,
     lanes,
     left,
     ext,
     own,
-    following,
-    before,
     back,
+    first_part,
+    second_part,
     state,
     disp,
+    first_px,
+    second_px,
     pot_lanes,
     marks,
     raw,
@@ -502,7 +550,13 @@
     big = 2 * block
     window = seg_len + big
     fetches = copies_of(
-        ((pot_in, pot), (own_in, own), (next_in, following), (before_in, before), (back_in, back)),
+        (
+            (pot_in, pot),
+            (own_in, own),
+            (back_in, back),
+            (first_in, first_part),
+            (second_in, second_part),
+        ),
         sems,
     )
     begin_copies(fetches)
@@ -521,13 +575,13 @@
     )
     marks[...] = values.astype(jnp.float32).astype(jnp.bfloat16)
     wait(fetches)
-    total = jnp.concatenate([before[...] + back[...], own[...] + following[...]], axis=1)
+    following, before = by_parity(first_part[...], second_part[...])
+    total = jnp.concatenate([before + back[...], own[...] + following], axis=1)
     final = jnp.where(total > 0, pot[...] - jnp.log2(total), NEG)
     pot_lanes[...] = potential_lanes(final * (1.0 / scale), channels)
     offsets = lax.broadcasted_iota(jnp.int32, (1, big), 1).astype(jnp.float32)
     corner = jnp.zeros((block, block), jnp.bfloat16)
     steps = seg_len // big
-    edges = ((state.at[:, pl.ds(0, EDGE)], low_out), (state.at[:, pl.ds(seg_len - EDGE, EDGE)], high_out))
 
     def one_line(line, carry):
         wait(line_copies(pairs, line_sems, line, lines_here))
@@ -570,7 +624,11 @@
             if 1 <= index <= steps:
                 weigh(index - 1)
         disp[pl.ds(line, 1), :] = jnp.concatenate(disparity, axis=1)
-        begin_copies(line_copies(((state, state_out),) + edges, send_sems, line, lines_here))
+        begin_copies(line_copies(((state, state_out),), send_sems, line, lines_here))
+        high = state[line, seg_len - EDGE :].astype(jnp.float32)
+        first, second = by_parity(high, state[line, :EDGE].astype(jnp.float32))
+        first_px[line] = first.astype(jnp.bfloat16)
+        second_px[line] = second.astype(jnp.bfloat16)
 
         @pl.when(line < layers)
         def _():
@@ -586,18 +644,21 @@
         return carry
 
     lax.fori_loop(0, lines_here, one_line, 0)
-    send = pltpu.make_async_copy(disp, disp_out, sems.at[2 * layers])
-    send.start()
+    sends = copies_of(
+        ((first_px, first_px_out), (second_px, second_px_out), (disp, disp_out)),
+        send_sems.at[pl.ds(lines_here, 3)],
+    )
+    begin_copies(sends)
     for line in range(layers):
         pltpu.make_async_copy(state.at[line], first_out.at[line], sems.at[line]).wait()
         source = line + lines_here - layers
         pltpu.make_async_copy(state.at[source], last_out.at[line], sems.at[layers + line]).wait()
     for line in range(lines_here):
-        wait(line_copies(((state, state_out),) + edges, send_sems, line, lines_here))
-    send.wait()
-
-
-def transport(pot, lanes, left, right, prev_low, prev_high, own, following, before, back, block, layers):
+        wait(line_copies(((state, state_out),), send_sems, line, lines_here))
+    wait(sends)
+
+
+def transport(pot, lanes, left, right, prev_low, prev_high, own, back, first, second, block, layers):
     lines_here, seg_len, channels = left.shape
     bf16, f32 = jnp.bfloat16, jnp.float32
     edge = ((layers, seg_len, channels), bf16)
@@ -607,25 +668,19 @@
     window = seg_len + 2 * block
     return kernel_call(
         functools.partial(transport_kernel, block),
-        (pot, lanes, left, right, prev_low, prev_high, own, following, before, back),
+        (pot, lanes, left, right, prev_low, prev_high, own, back, first, second),
         (state, marginal, edge, edge, side, side),
-        (
-            (pot.shape, f32),
-            (lanes.shape, bf16),
-            state,
-            ((lines_here, 2 * seg_len, channels), bf16),
-            marginal,
-            marginal,
-            marginal,
-            marginal,
-            state,
-            marginal,
+        ((pot.shape, f32), (lanes.shape, bf16), state)
+        + (((lines_here, 2 * seg_len, channels), bf16),)
+        + (marginal,) * 4
+        + (state, marginal, side, side)
+        + (
             ((2 * seg_len, channels), bf16),
             ((window, channels), bf16),
             ((2, 2 * block, window), f32),
             ((2, 2 * block, window), bf16),
         ),
-        (5 * lines_here, max(5, 2 * layers + 1), 3 * lines_here),
+        (5 * lines_here, max(5, 2 * layers), lines_here + 3),
         "transport",
     )
 
@@ -648,8 +703,8 @@
     state_in,
     top_in,
     bottom_in,
-    left_in,
-    right_in,
+    first_in,
+    second_in,
     corner_top_in,
     corner_bottom_in,
     weight_in,
@@ -658,8 +713,8 @@
     state_ref,
     top_ref,
     bottom_ref,
-    left_ref,
-    right_ref,
+    first_ref,
+    second_ref,
     corner_top_ref,
     corner_bottom_ref,
     weight_ref,
@@ -673,8 +728,8 @@
     fetches = copies_of(
         (
             (state_in, state_ref),
-            (left_in, left_ref),
-            (right_in, right_ref),
+            (first_in, first_ref),
+            (second_in, second_ref),
             (corner_top_in, corner_top_ref),
             (corner_bottom_in, corner_bottom_ref),
             (top_in, top_ref),
@@ -695,11 +750,14 @@
     wait(fetches[1:])
     first_image[:layers, EDGE:right] = top_ref[...].astype(f32)
     first_image[after:, EDGE:right] = bottom_ref[...].astype(f32)
-    first_image[layers:after, :EDGE] = left_ref[...].astype(f32)
-    first_image[layers:after, right:] = right_ref[...].astype(f32)
-    for rows, corner_ref in ((slice(0, layers), corner_top_ref), (slice(after, None), corner_bottom_ref)):
-        first_image[rows, :EDGE] = corner_ref[:, :EDGE].astype(f32)
-        first_image[rows, right:] = corner_ref[:, EDGE:].astype(f32)
+    for rows, first_px, second_px in (
+        (slice(layers, after), first_ref[...], second_ref[...]),
+        (slice(0, layers), corner_top_ref[:, :EDGE], corner_top_ref[:, EDGE:]),
+        (slice(after, None), corner_bottom_ref[:, :EDGE], corner_bottom_ref[:, EDGE:]),
+    ):
+        following, before = by_parity(first_px.astype(f32), second_px.astype(f32))
+        first_image[rows, :EDGE] = before
+        first_image[rows, right:] = following
     line0 = lax.axis_index("lines") * lines_here - layers
     all_lines = lax.axis_size("lines") * lines_here
     px0 = lax.axis_index("seg") * seg_len - EDGE
@@ -772,27 +830,28 @@
     next_low = shifted(left_features[:, :half], "seg", -1)
     prev_low = shifted(right_features[:, :half], "seg", 1)
     stacked, own = own_partials(left_features, right_features, conv_weight)
-    own, back = cross_partials(left_features, prev_high, next_low, right_features, own)
-    before = shifted(own, "seg", 1)
-    following = shifted(back, "seg", -1)
+    own = next_partials(next_low, right_features, own)
+    back, first, second = cross_partials(left_features, prev_high, own)
+    first = exchanged(first, "seg", 0)
+    second = exchanged(second, "seg", 1)
     block = min(128, half)
-    pot, lanes, own, back = row_pass(
-        left_features, right_features, prev_low, prev_high, own, following, before, back, block
-    )
-    before = shifted(own, "seg", 1)
-    following = shifted(back, "seg", -1)
-    state, disparity, first, last, low, high = transport(
-        pot, lanes, left_features, right_features, prev_low, prev_high, own, following, before, back, block, layers
-    )
-    bottom = shifted(first, "lines", -1)
-    top = shifted(last, "lines", 1)
-    left_px = shifted(high, "seg", 1)
-    right_px = shifted(low, "seg", -1)
-    edges = jnp.concatenate([left_px, right_px], axis=1)
+    pot, lanes, own, back, first, second = row_pass(
+        left_features, right_features, prev_low, prev_high, own, back, first, second, block
+    )
+    first = exchanged(first, "seg", 0)
+    second = exchanged(second, "seg", 1)
+    state, disparity, first_lines, last_lines, first, second = transport(
+        pot, lanes, left_features, right_features, prev_low, prev_high, own, back, first, second, block, layers
+    )
+    bottom = shifted(first_lines, "lines", -1)
+    top = shifted(last_lines, "lines", 1)
+    first = exchanged(first, "seg", 0)
+    second = exchanged(second, "seg", 1)
+    edges = jnp.concatenate([first, second], axis=1)
     corners_bottom = shifted(edges[:layers], "lines", -1)
     corners_top = shifted(edges[-layers:], "lines", 1)
     refined = conv_layers(
-        state, top, bottom, left_px, right_px, corners_top, corners_bottom, stacked, conv_bias
+        state, top, bottom, first, second, corners_top, corners_bottom, stacked, conv_bias
     )
     return (refined, disparity)
 

time: 102 us -> 95 us (0.931)
  the two profiles are of different devices: /device:TPU:1 before, /device:TPU:19 now
where the time goes in v5:
time: 95 us; the launch traced here: 94.6 us
  Pallas kernels  42.4 us (45%)
  starting transfers between devices  31.3 us (33%)
  waiting for transfers between devices  17.5 us (18%)
  local copies, waits for them, and re-layouts  2.55 us (3%)
    pallas_call x6, Pallas kernels, kernel_call(): pl.pallas_call(kernel, in_specs=[ANYWHERE] * len(operands), out_specs=[AN...  42.4 us
    ppermute x7, starting transfers between devices, shifted(): return lax.ppermute(block, axis, route)  22.7 us
    ppermute x7, waiting for transfers between devices, shifted(): return lax.ppermute(block, axis, route)  11.4 us
    ppermute x6, starting transfers between devices, exchanged(): return lax.ppermute(block, axis, route)  8.6 us
    ppermute x6, waiting for transfers between devices, exchanged(): return lax.ppermute(block, axis, route)  6.14 us
  transfers between devices with their start and end apart: 13, of which 7 were waited for; matrix products, arithmetic and copies ran while one was open for 1% of the time, Pallas kernels for 12%

profile of v5, /device:TPU:19, one launch (start us, length us, event | category | flops | bytes accessed | tf_op | source)
XLA Modules:
  0.0 94.6 jit_solution(9154645837727898932)
XLA Ops:
  0.6 0.0 copy-start
  0.7 1.2 %slice.17 = bf16[4,512,128]{2,1,0:T(8,128)(2,1)S(1)} slice(bf16[4,1024,128]{2,1,0:T(8,128)(2,1)} %left_in.7), slice={[0:4], [0:512], [0:128]} | slice | bytes 1048576 | tf_op jit(solution)/shard_map/slice | solution.py:830
  1.9 2.1 %collective-permute-start.2 = (bf16[4,512,128]{2,1,0:T(8,128)(2,1)S(1)}, bf16[4,512,128]{2,1,0:T(8,128)(2,1)S(1)}, u32[]{:S(2)}, u32[]{:S(2)}) collective-permute-start(bf16[4,512,128]{2,1,0:T(8,128)(2,1)S(1)} %slice.17), channel_id=1, source_target_pairs={{8,0},{16,8},{24,16},{9,1},{17,9},{25,17},{10,2},{18,10},{26,18},{... | collective-permute-start | bytes 1572872 | tf_op jit(solution)/shard_map/ppermute | solution.py:20
  4.0 1.3 %fusion = (bf16[4,512,128]{2,1,0:T(8,128)(2,1)S(1)}, bf16[4,512,128]{2,1,0:T(8,128)(2,1)S(1)}) fusion(bf16[4,1024,128]{2,1,0:T(8,128)(2,1)} %right_in.7), kind=kLoop, calls=%fused_computation.2 | loop fusion | bytes 2097152 | tf_op jit(solution)/shard_map/slice | solution.py:829
  5.3 3.2 %collective-permute-start.1 = (bf16[4,512,128]{2,1,0:T(8,128)(2,1)S(1)}, bf16[4,512,128]{2,1,0:T(8,128)(2,1)S(1)}, u32[]{:S(2)}, u32[]{:S(2)}) collective-permute-start(bf16[4,512,128]{2,1,0:T(8,128)(2,1)S(1)} %get-tuple-element.36), channel_id=1, source_target_pairs={{0,8},{8,16},{16,24},{1,9},{9,17},{17,25},{2,10},{10,18},{18,26},{... | collective-permute-start | bytes 1572872 | tf_op jit(solution)/shard_map/ppermute | solution.py:20
  8.5 1.9 %collective-permute-start = (bf16[4,512,128]{2,1,0:T(8,128)(2,1)S(1)}, bf16[4,512,128]{2,1,0:T(8,128)(2,1)S(1)}, u32[]{:S(2)}, u32[]{:S(2)}) collective-permute-start(bf16[4,512,128]{2,1,0:T(8,128)(2,1)S(1)} %get-tuple-element.37), channel_id=1, source_target_pairs={{0,8},{8,16},{16,24},{1,9},{9,17},{17,25},{2,10},{10,18},{18,26},{... | collective-permute-start | bytes 1572872 | tf_op jit(solution)/shard_map/ppermute | solution.py:20
  10.5 4.4 %column_own.1 = (bf16[3,1536,256]{2,1,0:T(8,128)(2,1)S(1)}, f32[8,1024]{1,0:T(8,128)S(1)}) custom-call(bf16[4,1024,128]{2,1,0:T(8,128)(2,1)S(1)} %copy-done.1, bf16[4,1024,128]{2,1,0:T(8,128)(2,1)S(1)} %copy-done, bf16[3,3,3,128,128]{4,3,2,1,0:T(8,128)(2,1)S(1)} %copy-done.3), custom_call_target="tpu_custom_call" | custom-call | flops 1073741824 | bytes 4194304 | tf_op jit(solution)/shard_map/column_own/pallas_call | solution.py:47
  14.9 1.7 %collective-permute-done.2.next_in = bf16[4,512,128]{2,1,0:T(8,128)(2,1)S(1)} collective-permute-done((bf16[4,512,128]{2,1,0:T(8,128)(2,1)S(1)}, bf16[4,512,128]{2,1,0:T(8,128)(2,1)S(1)}, u32[]{:S(2)}, u32[]{:S(2)}) %collective-permute-start.2) | collective-permute-done | bytes 524320 | tf_op jit(solution)/shard_map/ppermute | solution.py:20
  16.6 3.0 %column_next.1.own_in = f32[8,1024]{1,0:T(8,128)S(1)} custom-call(bf16[4,512,128]{2,1,0:T(8,128)(2,1)S(1)} %collective-permute-done.2.next_in, bf16[4,1024,128]{2,1,0:T(8,128)(2,1)S(1)} %copy-done, f32[8,1024]{1,0:T(8,128)S(1)} %get-tuple-element.19.own_in), custom_call_target="tpu_custom_call" | custom-call | flops 268435456 | bytes 2097152 | tf_op jit(solution)/shard_map/column_next/pallas_call | solution.py:47
  19.6 0.0 collective-permute-done.1.prev_in.prev_high_in
  19.6 3.7 %column_cross.1 = (f32[8,1024]{1,0:T(8,128)S(1)}, f32[8,1024]{1,0:T(8,128)S(1)}, f32[8,1024]{1,0:T(8,128)S(1)}) custom-call(bf16[4,1024,128]{2,1,0:T(8,128)(2,1)S(1)} %copy-done.1, bf16[4,512,128]{2,1,0:T(8,128)(2,1)S(1)} %collective-permute-done.1.prev_in.prev_high_in, f32[8,1024]{1,0:T(8,128)S(1)} %column_next.1.own_in), custom_call_target="tpu_custom_call" | custom-call | flops 1073741824 | bytes 4194304 | tf_op jit(solution)/shard_map/column_cross/pallas_call | solution.py:47
  23.3 1.4 %collective-permute-start.3 = (f32[8,1024]{1,0:T(8,128)S(1)}, f32[8,1024]{1,0:T(8,128)S(1)}, u32[]{:S(2)}, u32[]{:S(2)}) collective-permute-start(f32[8,1024]{1,0:T(8,128)S(1)} %get-tuple-element.21), channel_id=1, source_target_pairs={{0,8},{8,0},{16,24},{24,16},{1,9},{9,1},{17,25},{25,17},{2,10},{10... | collective-permute-start | bytes 98312 | tf_op jit(solution)/shard_map/ppermute | solution.py:27
  24.7 1.9 %collective-permute-start.4 = (f32[8,1024]{1,0:T(8,128)S(1)}, f32[8,1024]{1,0:T(8,128)S(1)}, u32[]{:S(2)}, u32[]{:S(2)}) collective-permute-start(f32[8,1024]{1,0:T(8,128)S(1)} %get-tuple-element.22), channel_id=1, source_target_pairs={{8,16},{16,8},{9,17},{17,9},{10,18},{18,10},{11,19},{19,11},{12,20... | collective-permute-start | bytes 98312 | tf_op jit(solution)/shard_map/ppermute | solution.py:27
  26.6 4.3 %collective-permute-done.prev_low_in = bf16[4,512,128]{2,1,0:T(8,128)(2,1)S(1)} collective-permute-done((bf16[4,512,128]{2,1,0:T(8,128)(2,1)S(1)}, bf16[4,512,128]{2,1,0:T(8,128)(2,1)S(1)}, u32[]{:S(2)}, u32[]{:S(2)}) %collective-permute-start) | collective-permute-done | bytes 524320 | tf_op jit(solution)/shard_map/ppermute | solution.py:20
  30.9 0.0 collective-permute-done.3.first_in
  30.9 0.7 collective-permute-done.4.second_in
  31.6 9.4 %row_pass.1 = (f32[4,2048]{1,0:T(4,128)S(1)}, bf16[4,1024,128]{2,1,0:T(8,128)(2,1)S(1)}, f32[4,1024]{1,0:T(4,128)S(1)}, f32[4,1024]{1,0:T(4,128)S(1)}, f32[4,1024]{1,0:T(4,128)S(1)}, /*index=5*/f32[4,1024]{1,0:T(4,128)S(1)}) custom-call(bf16[4,1024,128]{2,1,0:T(8,128)(2,1)S(1)} %copy-done.1, bf16[4,1024,128]{2,1,0:T(8,128)(2,1)S(1)} %copy-done, ...), custom_call_target="tpu_custom_call" | custom-call | tf_op jit(solution)/shard_map/row_pass/pallas_call | solution.py:47
  41.0 0.0 copy-start.2
  41.0 1.4 %collective-permute-start.5 = (f32[4,1024]{1,0:T(4,128)S(1)}, f32[4,1024]{1,0:T(4,128)S(1)}, u32[]{:S(2)}, u32[]{:S(2)}) collective-permute-start(f32[4,1024]{1,0:T(4,128)S(1)} %get-tuple-element.27), channel_id=1, source_target_pairs={{0,8},{8,0},{16,24},{24,16},{1,9},{9,1},{17,25},{25,17},{2,10},{10... | collective-permute-start | bytes 49160 | tf_op jit(solution)/shard_map/ppermute | solution.py:27
  42.4 1.9 %collective-permute-start.6 = (f32[4,1024]{1,0:T(4,128)S(1)}, f32[4,1024]{1,0:T(4,128)S(1)}, u32[]{:S(2)}, u32[]{:S(2)}) collective-permute-start(f32[4,1024]{1,0:T(4,128)S(1)} %get-tuple-element.28), channel_id=1, source_target_pairs={{8,16},{16,8},{9,17},{17,9},{10,18},{18,10},{11,19},{19,11},{12,20... | collective-permute-start | bytes 49160 | tf_op jit(solution)/shard_map/ppermute | solution.py:27
  44.4 2.6 %collective-permute-done.6.second_in = f32[4,1024]{1,0:T(4,128)S(1)} collective-permute-done((f32[4,1024]{1,0:T(4,128)S(1)}, f32[4,1024]{1,0:T(4,128)S(1)}, u32[]{:S(2)}, u32[]{:S(2)}) %collective-permute-start.6) | collective-permute-done | bytes 16416 | tf_op jit(solution)/shard_map/ppermute | solution.py:27
  46.9 10.3 %transport.1 = (bf16[4,1024,128]{2,1,0:T(8,128)(2,1)S(1)}, f32[4,1024]{1,0:T(4,128)}, bf16[3,1024,128]{2,1,0:T(8,128)(2,1)S(1)}, bf16[3,1024,128]{2,1,0:T(8,128)...) custom-call(f32[4,2048]{1,0:T(4,128)S(1)} %get-tuple-element.23.pot_in, ...), custom_call_target="tpu_custom_call" | custom-call | tf_op jit(solution)/shard_map/transport/pallas_call | solution.py:47
  57.2 6.2 %collective-permute-start.7 = (bf16[3,1024,128]{2,1,0:T(8,128)(2,1)S(1)}, bf16[3,1024,128]{2,1,0:T(8,128)(2,1)S(1)}, u32[]{:S(2)}, u32[]{:S(2)}) collective-permute-start(bf16[3,1024,128]{2,1,0:T(8,128)(2,1)S(1)} %get-tuple-element.30), channel_id=1, source_target_pairs={{0,1},{1,2},{2,3},{3,4},{4,5},{5,6},{6,7},{8,9},{9,10},{10,11},{11... | collective-permute-start | bytes 2359304 | tf_op jit(solution)/shard_map/ppermute | solution.py:20
  63.5 1.9 %collective-permute-start.8 = (bf16[3,1024,128]{2,1,0:T(8,128)(2,1)S(1)}, bf16[3,1024,128]{2,1,0:T(8,128)(2,1)S(1)}, u32[]{:S(2)}, u32[]{:S(2)}) collective-permute-start(bf16[3,1024,128]{2,1,0:T(8,128)(2,1)S(1)} %get-tuple-element.31), channel_id=1, source_target_pairs={{1,0},{2,1},{3,2},{4,3},{5,4},{6,5},{7,6},{9,8},{10,9},{11,10},{12... | collective-permute-start | bytes 2359304 | tf_op jit(solution)/shard_map/ppermute | solution.py:20
  65.4 0.1 collective-permute-start.9
  65.5 1.9 %collective-permute-start.10 = (bf16[4,16,128]{2,1,0:T(8,128)(2,1)S(1)}, bf16[4,16,128]{2,1,0:T(8,128)(2,1)S(1)}, u32[]{:S(2)}, u32[]{:S(2)}) collective-permute-start(bf16[4,16,128]{2,1,0:T(8,128)(2,1)S(1)} %get-tuple-element.33), channel_id=1, source_target_pairs={{8,16},{16,8},{9,17},{17,9},{10,18},{18,10},{11,19},{19,11},{12,20... | collective-permute-start | bytes 49160 | tf_op jit(solution)/shard_map/ppermute | solution.py:27
  67.4 0.9 collective-permute-done.9.first_in
  68.4 1.9 %collective-permute-done.10.second_in = bf16[4,16,128]{2,1,0:T(8,128)(2,1)S(1)} collective-permute-done((bf16[4,16,128]{2,1,0:T(8,128)(2,1)S(1)}, bf16[4,16,128]{2,1,0:T(8,128)(2,1)S(1)}, u32[]{:S(2)}, u32[]{:S(2)}) %collective-permute-start.10) | collective-permute-done | bytes 16416 | tf_op jit(solution)/shard_map/ppermute | solution.py:27
  70.3 3.4 %collective-permute-start.12 = (bf16[3,32,128]{2,1,0:T(8,128)(2,1)S(1)}, bf16[3,32,128]{2,1,0:T(8,128)(2,1)S(1)}, u32[]{:S(2)}, u32[]{:S(2)}) collective-permute-start(bf16[3,32,128]{2,1,0:T(8,128)(2,1)S(1)} %get-tuple-element.38), channel_id=1, source_target_pairs={{1,0},{2,1},{3,2},{4,3},{5,4},{6,5},{7,6},{9,8},{10,9},{11,10},{12... | collective-permute-start | bytes 73736 | tf_op jit(solution)/shard_map/ppermute | solution.py:20
  73.7 3.9 %collective-permute-start.11 = (bf16[3,32,128]{2,1,0:T(8,128)(2,1)S(1)}, bf16[3,32,128]{2,1,0:T(8,128)(2,1)S(1)}, u32[]{:S(2)}, u32[]{:S(2)}) collective-permute-start(bf16[3,32,128]{2,1,0:T(8,128)(2,1)S(1)} %get-tuple-element.39), channel_id=1, source_target_pairs={{0,1},{1,2},{2,3},{3,4},{4,5},{5,6},{6,7},{8,9},{9,10},{10,11},{11... | collective-permute-start | bytes 73736 | tf_op jit(solution)/shard_map/ppermute | solution.py:20
  77.6 5.4 %collective-permute-done.12.corner_bottom_in = bf16[3,32,128]{2,1,0:T(8,128)(2,1)S(1)} collective-permute-done((bf16[3,32,128]{2,1,0:T(8,128)(2,1)S(1)}, bf16[3,32,128]{2,1,0:T(8,128)(2,1)S(1)}, u32[]{:S(2)}, u32[]{:S(2)}) %collective-permute-start.12) | collective-permute-done | bytes 24608 | tf_op jit(solution)/shard_map/ppermute | solution.py:20
  83.0 11.6 %conv_layers.1 = bf16[4,1024,128]{2,1,0:T(8,128)(2,1)} custom-call(bf16[4,1024,128]{2,1,0:T(8,128)(2,1)S(1)} %get-tuple-element.29.state_in, bf16[3,1024,128]{2,1,0:T(8,128)(2,1)S(1)} %collective-permute-done.7.top_in, bf16[3,1024,128]{2,1,0:T(8,128)(2,1)S(1)} %collective-permute-done.8.bottom_in, bf16[4,16,128]{2,1,0:T(8,128)(2,1)S(1)} %collective-permute-done.9.first_in, ...), custom_call_target="tpu_custom_call" | custom-call | tf_op jit(solution)/shard_map/conv_layers/pallas_call | solution.py:47
  (13 shorter events, 0.0 us)
Async XLA Ops:
  0.6 9.8 %copy-start.1 = (bf16[4,1024,128]{2,1,0:T(8,128)(2,1)S(1)}, bf16[4,1024,128]{2,1,0:T(8,128)(2,1)}, u32[]{:S(2)}) copy-start(bf16[4,1024,128]{2,1,0:T(8,128)(2,1)} %left_in.7) | copy-start | bytes 3145732
  0.6 9.8 %copy-start = (bf16[4,1024,128]{2,1,0:T(8,128)(2,1)S(1)}, bf16[4,1024,128]{2,1,0:T(8,128)(2,1)}, u32[]{:S(2)}) copy-start(bf16[4,1024,128]{2,1,0:T(8,128)(2,1)} %right_in.7) | copy-start | bytes 3145732
  0.7 9.8 %copy-start.3 = (bf16[3,3,3,128,128]{4,3,2,1,0:T(8,128)(2,1)S(1)}, bf16[3,3,3,128,128]{4,3,2,1,0:T(8,128)(2,1)}, u32[]{:S(2)}) copy-start(bf16[3,3,3,128,128]{4,3,2,1,0:T(8,128)(2,1)} %weight_in.1) | copy-start | bytes 2654212
  1.9 14.7 %collective-permute-start.2 = (bf16[4,512,128]{2,1,0:T(8,128)(2,1)S(1)}, bf16[4,512,128]{2,1,0:T(8,128)(2,1)S(1)}, u32[]{:S(2)}, u32[]{:S(2)}) collective-permute-start(bf16[4,512,128]{2,1,0:T(8,128)(2,1)S(1)} %slice.17), channel_id=1, source_target_pairs={{8,0},{16,8},{24,16},{9,1},{17,9},{25,17},{10,2},{18,10},{26,18},{... | collective-permute-start | bytes 1572872 | tf_op jit(solution)/shard_map/ppermute | solution.py:20
  5.3 14.4 %collective-permute-start.1 = (bf16[4,512,128]{2,1,0:T(8,128)(2,1)S(1)}, bf16[4,512,128]{2,1,0:T(8,128)(2,1)S(1)}, u32[]{:S(2)}, u32[]{:S(2)}) collective-permute-start(bf16[4,512,128]{2,1,0:T(8,128)(2,1)S(1)} %get-tuple-element.36), channel_id=1, source_target_pairs={{0,8},{8,16},{16,24},{1,9},{9,17},{17,25},{2,10},{10,18},{18,26},{... | collective-permute-start | bytes 1572872 | tf_op jit(solution)/shard_map/ppermute | solution.py:20
  8.5 22.4 %collective-permute-start = (bf16[4,512,128]{2,1,0:T(8,128)(2,1)S(1)}, bf16[4,512,128]{2,1,0:T(8,128)(2,1)S(1)}, u32[]{:S(2)}, u32[]{:S(2)}) collective-permute-start(bf16[4,512,128]{2,1,0:T(8,128)(2,1)S(1)} %get-tuple-element.37), channel_id=1, source_target_pairs={{0,8},{8,16},{16,24},{1,9},{9,17},{17,25},{2,10},{10,18},{18,26},{... | collective-permute-start | bytes 1572872 | tf_op jit(solution)/shard_map/ppermute | solution.py:20
  23.3 7.6 %collective-permute-start.3 = (f32[8,1024]{1,0:T(8,128)S(1)}, f32[8,1024]{1,0:T(8,128)S(1)}, u32[]{:S(2)}, u32[]{:S(2)}) collective-permute-start(f32[8,1024]{1,0:T(8,128)S(1)} %get-tuple-element.21), channel_id=1, source_target_pairs={{0,8},{8,0},{16,24},{24,16},{1,9},{9,1},{17,25},{25,17},{2,10},{10... | collective-permute-start | bytes 98312 | tf_op jit(solution)/shard_map/ppermute | solution.py:27
  24.7 6.9 %collective-permute-start.4 = (f32[8,1024]{1,0:T(8,128)S(1)}, f32[8,1024]{1,0:T(8,128)S(1)}, u32[]{:S(2)}, u32[]{:S(2)}) collective-permute-start(f32[8,1024]{1,0:T(8,128)S(1)} %get-tuple-element.22), channel_id=1, source_target_pairs={{8,16},{16,8},{9,17},{17,9},{10,18},{18,10},{11,19},{19,11},{12,20... | collective-permute-start | bytes 98312 | tf_op jit(solution)/shard_map/ppermute | solution.py:27
  41.0 42.0 %copy-start.2 = (f32[3,128]{1,0:T(4,128)S(1)}, f32[3,128]{1,0:T(4,128)}, u32[]{:S(2)}) copy-start(f32[3,128]{1,0:T(4,128)} %bias_in.1) | copy-start | bytes 4612
  41.0 3.3 %collective-permute-start.5 = (f32[4,1024]{1,0:T(4,128)S(1)}, f32[4,1024]{1,0:T(4,128)S(1)}, u32[]{:S(2)}, u32[]{:S(2)}) collective-permute-start(f32[4,1024]{1,0:T(4,128)S(1)} %get-tuple-element.27), channel_id=1, source_target_pairs={{0,8},{8,0},{16,24},{24,16},{1,9},{9,1},{17,25},{25,17},{2,10},{10... | collective-permute-start | bytes 49160 | tf_op jit(solution)/shard_map/ppermute | solution.py:27
  42.4 4.5 %collective-permute-start.6 = (f32[4,1024]{1,0:T(4,128)S(1)}, f32[4,1024]{1,0:T(4,128)S(1)}, u32[]{:S(2)}, u32[]{:S(2)}) collective-permute-start(f32[4,1024]{1,0:T(4,128)S(1)} %get-tuple-element.28), channel_id=1, source_target_pairs={{8,16},{16,8},{9,17},{17,9},{10,18},{18,10},{11,19},{19,11},{12,20... | collective-permute-start | bytes 49160 | tf_op jit(solution)/shard_map/ppermute | solution.py:27
  57.2 25.8 %collective-permute-start.7 = (bf16[3,1024,128]{2,1,0:T(8,128)(2,1)S(1)}, bf16[3,1024,128]{2,1,0:T(8,128)(2,1)S(1)}, u32[]{:S(2)}, u32[]{:S(2)}) collective-permute-start(bf16[3,1024,128]{2,1,0:T(8,128)(2,1)S(1)} %get-tuple-element.30), channel_id=1, source_target_pairs={{0,1},{1,2},{2,3},{3,4},{4,5},{5,6},{6,7},{8,9},{9,10},{10,11},{11... | collective-permute-start | bytes 2359304 | tf_op jit(solution)/shard_map/ppermute | solution.py:20
  63.5 19.5 %collective-permute-start.8 = (bf16[3,1024,128]{2,1,0:T(8,128)(2,1)S(1)}, bf16[3,1024,128]{2,1,0:T(8,128)(2,1)S(1)}, u32[]{:S(2)}, u32[]{:S(2)}) collective-permute-start(bf16[3,1024,128]{2,1,0:T(8,128)(2,1)S(1)} %get-tuple-element.31), channel_id=1, source_target_pairs={{1,0},{2,1},{3,2},{4,3},{5,4},{6,5},{7,6},{9,8},{10,9},{11,10},{12... | collective-permute-start | bytes 2359304 | tf_op jit(solution)/shard_map/ppermute | solution.py:20
  65.4 2.9 %collective-permute-start.9 = (bf16[4,16,128]{2,1,0:T(8,128)(2,1)S(1)}, bf16[4,16,128]{2,1,0:T(8,128)(2,1)S(1)}, u32[]{:S(2)}, u32[]{:S(2)}) collective-permute-start(bf16[4,16,128]{2,1,0:T(8,128)(2,1)S(1)} %get-tuple-element.32), channel_id=1, source_target_pairs={{0,8},{8,0},{16,24},{24,16},{1,9},{9,1},{17,25},{25,17},{2,10},{10... | collective-permute-start | bytes 49160 | tf_op jit(solution)/shard_map/ppermute | solution.py:27
  65.5 4.8 %collective-permute-start.10 = (bf16[4,16,128]{2,1,0:T(8,128)(2,1)S(1)}, bf16[4,16,128]{2,1,0:T(8,128)(2,1)S(1)}, u32[]{:S(2)}, u32[]{:S(2)}) collective-permute-start(bf16[4,16,128]{2,1,0:T(8,128)(2,1)S(1)} %get-tuple-element.33), channel_id=1, source_target_pairs={{8,16},{16,8},{9,17},{17,9},{10,18},{18,10},{11,19},{19,11},{12,20... | collective-permute-start | bytes 49160 | tf_op jit(solution)/shard_map/ppermute | solution.py:27
  70.3 12.7 %collective-permute-start.12 = (bf16[3,32,128]{2,1,0:T(8,128)(2,1)S(1)}, bf16[3,32,128]{2,1,0:T(8,128)(2,1)S(1)}, u32[]{:S(2)}, u32[]{:S(2)}) collective-permute-start(bf16[3,32,128]{2,1,0:T(8,128)(2,1)S(1)} %get-tuple-element.38), channel_id=1, source_target_pairs={{1,0},{2,1},{3,2},{4,3},{5,4},{6,5},{7,6},{9,8},{10,9},{11,10},{12... | collective-permute-start | bytes 73736 | tf_op jit(solution)/shard_map/ppermute | solution.py:20
  73.7 9.3 %collective-permute-start.11 = (bf16[3,32,128]{2,1,0:T(8,128)(2,1)S(1)}, bf16[3,32,128]{2,1,0:T(8,128)(2,1)S(1)}, u32[]{:S(2)}, u32[]{:S(2)}) collective-permute-start(bf16[3,32,128]{2,1,0:T(8,128)(2,1)S(1)} %get-tuple-element.39), channel_id=1, source_target_pairs={{0,1},{1,2},{2,3},{3,4},{4,5},{5,6},{6,7},{8,9},{9,10},{10,11},{11... | collective-permute-start | bytes 73736 | tf_op jit(solution)/shard_map/ppermute | solution.py:20

commit v6 on v5

--- a/solution.py
+++ b/solution.py
@@ -182,15 +182,34 @@
 
 
 def next_kernel(
-    block, next_in, right_in, own_in, merged_out, following, right, merged, line_sems, sems
+    block,
+    next_in,
+    right_in,
+    own_in,
+    back_in,
+    merged_out,
+    first_out,
+    second_out,
+    following,
+    right,
+    merged,
+    back,
+    first_part,
+    second_part,
+    line_sems,
+    sems,
 ):
     lines_here, half = following.shape[:2]
     pairs = ((next_in, following), (right_in.at[:, pl.ds(0, half)], right))
-    fetch, send = copies_of(((own_in, merged), (merged, merged_out)), sems)
-    fetch.start()
+    fetches = copies_of(((own_in, merged), (back_in, back)), sems)
+    sends = copies_of(
+        ((first_part, first_out), (second_part, second_out), (merged, merged_out)),
+        sems.at[pl.ds(2, 3)],
+    )
+    begin_copies(fetches)
     for line in range(lines_here):
         begin_copies(line_copies(pairs, line_sems, line, lines_here))
-    fetch.wait()
+    wait(fetches)
     last = lax.axis_index("seg") == lax.axis_size("seg") - 1
 
     def one_line(line, carry):
@@ -210,52 +229,33 @@
         return carry
 
     lax.fori_loop(0, lines_here, one_line, 0)
-    send.start()
-    send.wait()
-
-
-def next_partials(next_low, right, own):
+    first_part[...], second_part[...] = by_parity(merged[...], back[...])
+    begin_copies(sends)
+    wait(sends)
+
+
+def next_partials(next_low, right, own, back):
     lines_here, half, channels = next_low.shape
-    merged = (own.shape, jnp.float32)
+    part = (own.shape, jnp.float32)
     features = (next_low.shape, jnp.bfloat16)
     return kernel_call(
         functools.partial(next_kernel, min(256, half)),
-        (next_low, right, own),
-        (merged,),
-        (features, features, merged),
-        (2 * lines_here, 2),
+        (next_low, right, own, back),
+        (part,) * 3,
+        (features, features) + (part,) * 4,
+        (2 * lines_here, 5),
         "column_next",
         column_cost(lines_here, half, channels),
-    )[0]
-
-
-def cross_kernel(
-    block,
-    left_in,
-    prev_in,
-    own_in,
-    back_out,
-    first_out,
-    second_out,
-    left,
-    prev,
-    own,
-    back,
-    first_part,
-    second_part,
-    line_sems,
-    sems,
-):
+    )
+
+
+def cross_kernel(block, left_in, prev_in, back_out, left, prev, back, line_sems, sems):
     lines_here, seg_len = left.shape[:2]
     half = seg_len - prev.shape[1]
     pairs = ((left_in, left), (prev_in, prev))
-    fetch, *sends = copies_of(
-        ((own_in, own), (back, back_out), (first_part, first_out), (second_part, second_out)), sems
-    )
-    fetch.start()
     for line in range(lines_here):
         begin_copies(line_copies(pairs, line_sems, line, lines_here))
-    fetch.wait()
+    (send,) = copies_of(((back, back_out),), sems)
     back[...] = jnp.zeros_like(back)
 
     def one_line(line, carry):
@@ -271,23 +271,22 @@
         return carry
 
     lax.fori_loop(0, lines_here, one_line, 0)
-    first_part[...], second_part[...] = by_parity(own[...], back[...])
-    begin_copies(sends)
-    wait(sends)
-
-
-def cross_partials(left, prev_high, own):
+    send.start()
+    send.wait()
+
+
+def cross_partials(left, prev_high):
     lines_here, seg_len, channels = left.shape
-    part = (own.shape, jnp.float32)
+    part = ((2 * lines_here, seg_len), jnp.float32)
     return kernel_call(
         functools.partial(cross_kernel, min(256, prev_high.shape[1])),
-        (left, prev_high, own),
-        (part,) * 3,
-        ((left.shape, jnp.bfloat16), (prev_high.shape, jnp.bfloat16)) + (part,) * 4,
-        (2 * lines_here, 4),
+        (left, prev_high),
+        (part,),
+        ((left.shape, jnp.bfloat16), (prev_high.shape, jnp.bfloat16), part),
+        (2 * lines_here, 1),
         "column_cross",
         column_cost(*left.shape),
-    )
+    )[0]
 
 
 def potential(peak, total):
@@ -766,13 +765,13 @@
     for layer in range(layers):
         reach = layers - 1 - layer
         begin, end = (EDGE // 2, right + EDGE // 2) if reach else (EDGE, right)
-        pieces = 5 if reach else 4
-        size = (end - begin) // pieces
-
-        def pair(index, carry, layer=layer, reach=reach, begin=begin, pieces=pieces, size=size, source=source, target=target):
+        middle = begin + seg_len // 2
+        pieces = ((begin, middle), (middle, end))
+
+        def pair(index, carry, layer=layer, reach=reach, pieces=pieces, source=source, target=target):
             base = layer + 2 * index
-            for piece in range(pieces):
-                start = begin + piece * size
+            for start, stop in pieces:
+                size = stop - start
                 taps = [
                     source[base + line, start + col_tap - 1 : start + col_tap - 1 + size].astype(jnp.bfloat16)
                     for col_tap in range(3)
@@ -790,7 +789,7 @@
                         continue
                     image_line = line0 + line
                     inside = (image_line >= 0) & (image_line < all_lines)
-                    if piece in (0, pieces - 1):
+                    if reach:
                         px = px0 + start + lax.broadcasted_iota(jnp.int32, updated.shape, 0)
                         inside = inside & (px >= 0) & (px < all_px)
                     updated = jnp.where(inside, updated, 0.0)
@@ -828,10 +827,11 @@
     layers = conv_weight.shape[0]
     prev_high = shifted(right_features[:, half:], "seg", 1)
     next_low = shifted(left_features[:, :half], "seg", -1)
-    prev_low = shifted(right_features[:, :half], "seg", 1)
     stacked, own = own_partials(left_features, right_features, conv_weight)
-    own = next_partials(next_low, right_features, own)
-    back, first, second = cross_partials(left_features, prev_high, own)
+    right_low, own = lax.optimization_barrier((right_features[:, :half], own))
+    prev_low = shifted(right_low, "seg", 1)
+    back = cross_partials(left_features, prev_high)
+    own, first, second = next_partials(next_low, right_features, own, back)
     first = exchanged(first, "seg", 0)
     second = exchanged(second, "seg", 1)
     block = min(128, half)

time: 95 us -> 94 us (0.989)
  waiting for transfers between devices: 17.5 us -> 15.4 us
  starting transfers between devices: 31.3 us -> 33 us
  local copies, waits for them, and re-layouts: 2.55 us -> 1.5 us
    ppermute x7, waiting for transfers between devices: 11.4 us -> 8.23 us  [shifted(): return lax.ppermute(block, axis, route)]
    ppermute x7, starting transfers between devices: 22.7 us -> 25.6 us  [shifted(): return lax.ppermute(block, axis, route)]
    slice x1, local copies, waits for them, and re-layouts: 1.23 us -> 0.04 us  [shards(): next_low = shifted(left_features[:, :half], 'seg', -1)]
    ppermute x6, starting transfers between devices: 8.6 us -> 7.46 us  [exchanged(): return lax.ppermute(block, axis, route)]
    ppermute x6, waiting for transfers between devices: 6.14 us -> 7.18 us  [exchanged(): return lax.ppermute(block, axis, route)]
  transfers between devices with their start and end apart: 13 -> 13, of which waited for: 7 -> 8; matrix products, arithmetic and copies ran while one was open for 1% -> 0% of each run, Pallas kernels for 12% -> 12%
where the time goes in v6:
time: 94 us; the launch traced here: 93.6 us
  Pallas kernels  42.9 us (46%)
  starting transfers between devices  33 us (35%)
  waiting for transfers between devices  15.4 us (16%)
  local copies, waits for them, and re-layouts  1.5 us (2%)
    pallas_call x6, Pallas kernels, kernel_call(): pl.pallas_call(kernel, in_specs=[ANYWHERE] * len(operands), out_specs=[AN...  42.9 us
    ppermute x7, starting transfers between devices, shifted(): return lax.ppermute(block, axis, route)  25.6 us
    ppermute x7, waiting for transfers between devices, shifted(): return lax.ppermute(block, axis, route)  8.23 us
    ppermute x6, starting transfers between devices, exchanged(): return lax.ppermute(block, axis, route)  7.46 us
    ppermute x6, waiting for transfers between devices, exchanged(): return lax.ppermute(block, axis, route)  7.18 us
  transfers between devices with their start and end apart: 13, of which 8 were waited for; matrix products, arithmetic and copies ran while one was open for 0% of the time, Pallas kernels for 12%

profile of v6, /device:TPU:19, one launch (start us, length us, event | category | flops | bytes accessed | tf_op | source)
XLA Modules:
  0.0 93.6 jit_solution(306680424811266116)
XLA Ops:
  0.7 1.4 %fusion = (bf16[4,512,128]{2,1,0:T(8,128)(2,1)S(1)}, bf16[4,512,128]{2,1,0:T(8,128)(2,1)S(1)}) fusion(bf16[4,1024,128]{2,1,0:T(8,128)(2,1)} %right_in.7), kind=kLoop, calls=%fused_computation.2 | loop fusion | bytes 2097152 | tf_op jit(solution)/shard_map/slice | solution.py:828
  2.1 3.2 %collective-permute-start.1 = (bf16[4,512,128]{2,1,0:T(8,128)(2,1)S(1)}, bf16[4,512,128]{2,1,0:T(8,128)(2,1)S(1)}, u32[]{:S(2)}, u32[]{:S(2)}) collective-permute-start(bf16[4,512,128]{2,1,0:T(8,128)(2,1)S(1)} %get-tuple-element.40), channel_id=1, source_target_pairs={{0,8},{8,16},{16,24},{1,9},{9,17},{17,25},{2,10},{10,18},{18,26},{... | collective-permute-start | bytes 1572872 | tf_op jit(solution)/shard_map/ppermute | solution.py:20
  5.4 2.1 %collective-permute-start.2 = (bf16[4,512,128]{2,1,0:T(8,128)(2,1)S(1)}, bf16[4,512,128]{2,1,0:T(8,128)(2,1)S(1)}, u32[]{:S(2)}, u32[]{:S(2)}) collective-permute-start(bf16[4,512,128]{2,1,0:T(8,128)(2,1)S(1)} %slice.17), channel_id=1, source_target_pairs={{8,0},{16,8},{24,16},{9,1},{17,9},{25,17},{10,2},{18,10},{26,18},{... | collective-permute-start | bytes 1572872 | tf_op jit(solution)/shard_map/ppermute | solution.py:20
  7.5 4.4 %column_own.1 = (bf16[3,1536,256]{2,1,0:T(8,128)(2,1)S(1)}, f32[8,1024]{1,0:T(8,128)S(1)}) custom-call(bf16[4,1024,128]{2,1,0:T(8,128)(2,1)S(1)} %copy-done.1, bf16[4,1024,128]{2,1,0:T(8,128)(2,1)S(1)} %copy-done, bf16[3,3,3,128,128]{4,3,2,1,0:T(8,128)(2,1)S(1)} %copy-done.3), custom_call_target="tpu_custom_call" | custom-call | flops 1073741824 | bytes 4194304 | tf_op jit(solution)/shard_map/column_own/pallas_call | solution.py:47
  11.9 3.2 %collective-permute-start = (bf16[4,512,128]{2,1,0:T(8,128)(2,1)S(1)}, bf16[4,512,128]{2,1,0:T(8,128)(2,1)S(1)}, u32[]{:S(2)}, u32[]{:S(2)}) collective-permute-start(bf16[4,512,128]{2,1,0:T(8,128)(2,1)S(1)} %get-tuple-element.22), channel_id=1, source_target_pairs={{0,8},{8,16},{16,24},{1,9},{9,17},{17,25},{2,10},{10,18},{18,26},{... | collective-permute-start | bytes 1572872 | tf_op jit(solution)/shard_map/ppermute | solution.py:20
  15.2 1.6 %collective-permute-done.1.prev_in.prev_high_in = bf16[4,512,128]{2,1,0:T(8,128)(2,1)S(1)} collective-permute-done((bf16[4,512,128]{2,1,0:T(8,128)(2,1)S(1)}, bf16[4,512,128]{2,1,0:T(8,128)(2,1)S(1)}, u32[]{:S(2)}, u32[]{:S(2)}) %collective-permute-start.1) | collective-permute-done | bytes 524320 | tf_op jit(solution)/shard_map/ppermute | solution.py:20
  16.8 3.5 %column_cross.1.back_in = f32[8,1024]{1,0:T(8,128)S(1)} custom-call(bf16[4,1024,128]{2,1,0:T(8,128)(2,1)S(1)} %copy-done.1, bf16[4,512,128]{2,1,0:T(8,128)(2,1)S(1)} %collective-permute-done.1.prev_in.prev_high_in), custom_call_target="tpu_custom_call" | custom-call | flops 1073741824 | bytes 4194304 | tf_op jit(solution)/shard_map/column_cross/pallas_call | solution.py:47
  20.3 0.0 collective-permute-done.2.next_in
  20.3 3.2 %column_next.1 = (f32[8,1024]{1,0:T(8,128)S(1)}, f32[8,1024]{1,0:T(8,128)S(1)}, f32[8,1024]{1,0:T(8,128)S(1)}) custom-call(bf16[4,512,128]{2,1,0:T(8,128)(2,1)S(1)} %collective-permute-done.2.next_in, bf16[4,1024,128]{2,1,0:T(8,128)(2,1)S(1)} %copy-done, f32[8,1024]{1,0:T(8,128)S(1)} %get-tuple-element.23.own_in, f32[8,1024]{1,0:T(8,128)S(1)} %column_cross.1.back_in), custom_call_target="tpu_custom_call" | custom-call | flops 268435456 | bytes 2097152 | tf_op jit(solution)/shard_map/column_next/pallas_call | solution.py:47
  23.5 1.4 %collective-permute-start.3 = (f32[8,1024]{1,0:T(8,128)S(1)}, f32[8,1024]{1,0:T(8,128)S(1)}, u32[]{:S(2)}, u32[]{:S(2)}) collective-permute-start(f32[8,1024]{1,0:T(8,128)S(1)} %get-tuple-element.25), channel_id=1, source_target_pairs={{0,8},{8,0},{16,24},{24,16},{1,9},{9,1},{17,25},{25,17},{2,10},{10... | collective-permute-start | bytes 98312 | tf_op jit(solution)/shard_map/ppermute | solution.py:27
  24.9 1.9 %collective-permute-start.4 = (f32[8,1024]{1,0:T(8,128)S(1)}, f32[8,1024]{1,0:T(8,128)S(1)}, u32[]{:S(2)}, u32[]{:S(2)}) collective-permute-start(f32[8,1024]{1,0:T(8,128)S(1)} %get-tuple-element.26), channel_id=1, source_target_pairs={{8,16},{16,8},{9,17},{17,9},{10,18},{18,10},{11,19},{19,11},{12,20... | collective-permute-start | bytes 98312 | tf_op jit(solution)/shard_map/ppermute | solution.py:27
  26.8 1.2 %collective-permute-done.prev_low_in = bf16[4,512,128]{2,1,0:T(8,128)(2,1)S(1)} collective-permute-done((bf16[4,512,128]{2,1,0:T(8,128)(2,1)S(1)}, bf16[4,512,128]{2,1,0:T(8,128)(2,1)S(1)}, u32[]{:S(2)}, u32[]{:S(2)}) %collective-permute-start) | collective-permute-done | bytes 524320 | tf_op jit(solution)/shard_map/ppermute | solution.py:20
  28.0 0.0 collective-permute-done.3.first_in
  28.0 1.8 %collective-permute-done.4.second_in = f32[8,1024]{1,0:T(8,128)S(1)} collective-permute-done((f32[8,1024]{1,0:T(8,128)S(1)}, f32[8,1024]{1,0:T(8,128)S(1)}, u32[]{:S(2)}, u32[]{:S(2)}) %collective-permute-start.4) | collective-permute-done | bytes 32800 | tf_op jit(solution)/shard_map/ppermute | solution.py:27
  29.8 9.4 %row_pass.1 = (f32[4,2048]{1,0:T(4,128)S(1)}, bf16[4,1024,128]{2,1,0:T(8,128)(2,1)S(1)}, f32[4,1024]{1,0:T(4,128)S(1)}, f32[4,1024]{1,0:T(4,128)S(1)}, f32[4,1024]{1,0:T(4,128)S(1)}, /*index=5*/f32[4,1024]{1,0:T(4,128)S(1)}) custom-call(bf16[4,1024,128]{2,1,0:T(8,128)(2,1)S(1)} %copy-done.1, bf16[4,1024,128]{2,1,0:T(8,128)(2,1)S(1)} %copy-done, ...), custom_call_target="tpu_custom_call" | custom-call | tf_op jit(solution)/shard_map/row_pass/pallas_call | solution.py:47
  39.2 0.0 copy-start.2
  39.2 0.3 collective-permute-start.5
  39.5 1.9 %collective-permute-start.6 = (f32[4,1024]{1,0:T(4,128)S(1)}, f32[4,1024]{1,0:T(4,128)S(1)}, u32[]{:S(2)}, u32[]{:S(2)}) collective-permute-start(f32[4,1024]{1,0:T(4,128)S(1)} %get-tuple-element.32), channel_id=1, source_target_pairs={{8,16},{16,8},{9,17},{17,9},{10,18},{18,10},{11,19},{19,11},{12,20... | collective-permute-start | bytes 49160 | tf_op jit(solution)/shard_map/ppermute | solution.py:27
  41.5 0.4 collective-permute-done.5.first_in
  41.9 2.1 %collective-permute-done.6.second_in = f32[4,1024]{1,0:T(4,128)S(1)} collective-permute-done((f32[4,1024]{1,0:T(4,128)S(1)}, f32[4,1024]{1,0:T(4,128)S(1)}, u32[]{:S(2)}, u32[]{:S(2)}) %collective-permute-start.6) | collective-permute-done | bytes 16416 | tf_op jit(solution)/shard_map/ppermute | solution.py:27
  44.0 10.3 %transport.1 = (bf16[4,1024,128]{2,1,0:T(8,128)(2,1)S(1)}, f32[4,1024]{1,0:T(4,128)}, bf16[3,1024,128]{2,1,0:T(8,128)(2,1)S(1)}, bf16[3,1024,128]{2,1,0:T(8,128)...) custom-call(f32[4,2048]{1,0:T(4,128)S(1)} %get-tuple-element.27.pot_in, ...), custom_call_target="tpu_custom_call" | custom-call | tf_op jit(solution)/shard_map/transport/pallas_call | solution.py:47
  54.3 7.8 %collective-permute-start.7 = (bf16[3,1024,128]{2,1,0:T(8,128)(2,1)S(1)}, bf16[3,1024,128]{2,1,0:T(8,128)(2,1)S(1)}, u32[]{:S(2)}, u32[]{:S(2)}) collective-permute-start(bf16[3,1024,128]{2,1,0:T(8,128)(2,1)S(1)} %get-tuple-element.34), channel_id=1, source_target_pairs={{0,1},{1,2},{2,3},{3,4},{4,5},{5,6},{6,7},{8,9},{9,10},{10,11},{11... | collective-permute-start | bytes 2359304 | tf_op jit(solution)/shard_map/ppermute | solution.py:20
  62.1 1.9 %collective-permute-start.8 = (bf16[3,1024,128]{2,1,0:T(8,128)(2,1)S(1)}, bf16[3,1024,128]{2,1,0:T(8,128)(2,1)S(1)}, u32[]{:S(2)}, u32[]{:S(2)}) collective-permute-start(bf16[3,1024,128]{2,1,0:T(8,128)(2,1)S(1)} %get-tuple-element.35), channel_id=1, source_target_pairs={{1,0},{2,1},{3,2},{4,3},{5,4},{6,5},{7,6},{9,8},{10,9},{11,10},{12... | collective-permute-start | bytes 2359304 | tf_op jit(solution)/shard_map/ppermute | solution.py:20
  64.0 0.1 collective-permute-start.9
  64.1 1.9 %collective-permute-start.10 = (bf16[4,16,128]{2,1,0:T(8,128)(2,1)S(1)}, bf16[4,16,128]{2,1,0:T(8,128)(2,1)S(1)}, u32[]{:S(2)}, u32[]{:S(2)}) collective-permute-start(bf16[4,16,128]{2,1,0:T(8,128)(2,1)S(1)} %get-tuple-element.37), channel_id=1, source_target_pairs={{8,16},{16,8},{9,17},{17,9},{10,18},{18,10},{11,19},{19,11},{12,20... | collective-permute-start | bytes 49160 | tf_op jit(solution)/shard_map/ppermute | solution.py:27
  66.0 0.9 %collective-permute-done.9.first_in = bf16[4,16,128]{2,1,0:T(8,128)(2,1)S(1)} collective-permute-done((bf16[4,16,128]{2,1,0:T(8,128)(2,1)S(1)}, bf16[4,16,128]{2,1,0:T(8,128)(2,1)S(1)}, u32[]{:S(2)}, u32[]{:S(2)}) %collective-permute-start.9) | collective-permute-done | bytes 16416 | tf_op jit(solution)/shard_map/ppermute | solution.py:27
  67.0 1.9 %collective-permute-done.10.second_in = bf16[4,16,128]{2,1,0:T(8,128)(2,1)S(1)} collective-permute-done((bf16[4,16,128]{2,1,0:T(8,128)(2,1)S(1)}, bf16[4,16,128]{2,1,0:T(8,128)(2,1)S(1)}, u32[]{:S(2)}, u32[]{:S(2)}) %collective-permute-start.10) | collective-permute-done | bytes 16416 | tf_op jit(solution)/shard_map/ppermute | solution.py:27
  68.9 3.4 %collective-permute-start.12 = (bf16[3,32,128]{2,1,0:T(8,128)(2,1)S(1)}, bf16[3,32,128]{2,1,0:T(8,128)(2,1)S(1)}, u32[]{:S(2)}, u32[]{:S(2)}) collective-permute-start(bf16[3,32,128]{2,1,0:T(8,128)(2,1)S(1)} %get-tuple-element.42), channel_id=1, source_target_pairs={{1,0},{2,1},{3,2},{4,3},{5,4},{6,5},{7,6},{9,8},{10,9},{11,10},{12... | collective-permute-start | bytes 73736 | tf_op jit(solution)/shard_map/ppermute | solution.py:20
  72.3 3.9 %collective-permute-start.11 = (bf16[3,32,128]{2,1,0:T(8,128)(2,1)S(1)}, bf16[3,32,128]{2,1,0:T(8,128)(2,1)S(1)}, u32[]{:S(2)}, u32[]{:S(2)}) collective-permute-start(bf16[3,32,128]{2,1,0:T(8,128)(2,1)S(1)} %get-tuple-element.43), channel_id=1, source_target_pairs={{0,1},{1,2},{2,3},{3,4},{4,5},{5,6},{6,7},{8,9},{9,10},{10,11},{11... | collective-permute-start | bytes 73736 | tf_op jit(solution)/shard_map/ppermute | solution.py:20
  76.2 5.4 %collective-permute-done.12.corner_bottom_in = bf16[3,32,128]{2,1,0:T(8,128)(2,1)S(1)} collective-permute-done((bf16[3,32,128]{2,1,0:T(8,128)(2,1)S(1)}, bf16[3,32,128]{2,1,0:T(8,128)(2,1)S(1)}, u32[]{:S(2)}, u32[]{:S(2)}) %collective-permute-start.12) | collective-permute-done | bytes 24608 | tf_op jit(solution)/shard_map/ppermute | solution.py:20
  81.6 0.0 collective-permute-done.11.corner_top_in
  81.6 12.0 %conv_layers.1 = bf16[4,1024,128]{2,1,0:T(8,128)(2,1)} custom-call(bf16[4,1024,128]{2,1,0:T(8,128)(2,1)S(1)} %get-tuple-element.33.state_in, bf16[3,1024,128]{2,1,0:T(8,128)(2,1)S(1)} %collective-permute-done.7.top_in, bf16[3,1024,128]{2,1,0:T(8,128)(2,1)S(1)} %collective-permute-done.8.bottom_in, bf16[4,16,128]{2,1,0:T(8,128)(2,1)S(1)} %collective-permute-done.9.first_in, ...), custom_call_target="tpu_custom_call" | custom-call | tf_op jit(solution)/shard_map/conv_layers/pallas_call | solution.py:47
  (13 shorter events, 0.1 us)
Async XLA Ops:
  0.6 6.8 %copy-start = (bf16[4,1024,128]{2,1,0:T(8,128)(2,1)S(1)}, bf16[4,1024,128]{2,1,0:T(8,128)(2,1)}, u32[]{:S(2)}) copy-start(bf16[4,1024,128]{2,1,0:T(8,128)(2,1)} %right_in.7) | copy-start | bytes 3145732
  0.6 4.7 %copy-start.1 = (bf16[4,1024,128]{2,1,0:T(8,128)(2,1)S(1)}, bf16[4,1024,128]{2,1,0:T(8,128)(2,1)}, u32[]{:S(2)}) copy-start(bf16[4,1024,128]{2,1,0:T(8,128)(2,1)} %left_in.7) | copy-start | bytes 3145732
  0.6 6.8 %copy-start.3 = (bf16[3,3,3,128,128]{4,3,2,1,0:T(8,128)(2,1)S(1)}, bf16[3,3,3,128,128]{4,3,2,1,0:T(8,128)(2,1)}, u32[]{:S(2)}) copy-start(bf16[3,3,3,128,128]{4,3,2,1,0:T(8,128)(2,1)} %weight_in.1) | copy-start | bytes 2654212
  2.1 14.7 %collective-permute-start.1 = (bf16[4,512,128]{2,1,0:T(8,128)(2,1)S(1)}, bf16[4,512,128]{2,1,0:T(8,128)(2,1)S(1)}, u32[]{:S(2)}, u32[]{:S(2)}) collective-permute-start(bf16[4,512,128]{2,1,0:T(8,128)(2,1)S(1)} %get-tuple-element.40), channel_id=1, source_target_pairs={{0,8},{8,16},{16,24},{1,9},{9,17},{17,25},{2,10},{10,18},{18,26},{... | collective-permute-start | bytes 1572872 | tf_op jit(solution)/shard_map/ppermute | solution.py:20
  5.4 14.9 %collective-permute-start.2 = (bf16[4,512,128]{2,1,0:T(8,128)(2,1)S(1)}, bf16[4,512,128]{2,1,0:T(8,128)(2,1)S(1)}, u32[]{:S(2)}, u32[]{:S(2)}) collective-permute-start(bf16[4,512,128]{2,1,0:T(8,128)(2,1)S(1)} %slice.17), channel_id=1, source_target_pairs={{8,0},{16,8},{24,16},{9,1},{17,9},{25,17},{10,2},{18,10},{26,18},{... | collective-permute-start | bytes 1572872 | tf_op jit(solution)/shard_map/ppermute | solution.py:20
  11.9 16.1 %collective-permute-start = (bf16[4,512,128]{2,1,0:T(8,128)(2,1)S(1)}, bf16[4,512,128]{2,1,0:T(8,128)(2,1)S(1)}, u32[]{:S(2)}, u32[]{:S(2)}) collective-permute-start(bf16[4,512,128]{2,1,0:T(8,128)(2,1)S(1)} %get-tuple-element.22), channel_id=1, source_target_pairs={{0,8},{8,16},{16,24},{1,9},{9,17},{17,25},{2,10},{10,18},{18,26},{... | collective-permute-start | bytes 1572872 | tf_op jit(solution)/shard_map/ppermute | solution.py:20
  23.5 4.5 %collective-permute-start.3 = (f32[8,1024]{1,0:T(8,128)S(1)}, f32[8,1024]{1,0:T(8,128)S(1)}, u32[]{:S(2)}, u32[]{:S(2)}) collective-permute-start(f32[8,1024]{1,0:T(8,128)S(1)} %get-tuple-element.25), channel_id=1, source_target_pairs={{0,8},{8,0},{16,24},{24,16},{1,9},{9,1},{17,25},{25,17},{2,10},{10... | collective-permute-start | bytes 98312 | tf_op jit(solution)/shard_map/ppermute | solution.py:27
  24.9 4.9 %collective-permute-start.4 = (f32[8,1024]{1,0:T(8,128)S(1)}, f32[8,1024]{1,0:T(8,128)S(1)}, u32[]{:S(2)}, u32[]{:S(2)}) collective-permute-start(f32[8,1024]{1,0:T(8,128)S(1)} %get-tuple-element.26), channel_id=1, source_target_pairs={{8,16},{16,8},{9,17},{17,9},{10,18},{18,10},{11,19},{19,11},{12,20... | collective-permute-start | bytes 98312 | tf_op jit(solution)/shard_map/ppermute | solution.py:27
  39.2 42.4 %copy-start.2 = (f32[3,128]{1,0:T(4,128)S(1)}, f32[3,128]{1,0:T(4,128)}, u32[]{:S(2)}) copy-start(f32[3,128]{1,0:T(4,128)} %bias_in.1) | copy-start | bytes 4612
  39.2 2.7 %collective-permute-start.5 = (f32[4,1024]{1,0:T(4,128)S(1)}, f32[4,1024]{1,0:T(4,128)S(1)}, u32[]{:S(2)}, u32[]{:S(2)}) collective-permute-start(f32[4,1024]{1,0:T(4,128)S(1)} %get-tuple-element.31), channel_id=1, source_target_pairs={{0,8},{8,0},{16,24},{24,16},{1,9},{9,1},{17,25},{25,17},{2,10},{10... | collective-permute-start | bytes 49160 | tf_op jit(solution)/shard_map/ppermute | solution.py:27
  39.5 4.5 %collective-permute-start.6 = (f32[4,1024]{1,0:T(4,128)S(1)}, f32[4,1024]{1,0:T(4,128)S(1)}, u32[]{:S(2)}, u32[]{:S(2)}) collective-permute-start(f32[4,1024]{1,0:T(4,128)S(1)} %get-tuple-element.32), channel_id=1, source_target_pairs={{8,16},{16,8},{9,17},{17,9},{10,18},{18,10},{11,19},{19,11},{12,20... | collective-permute-start | bytes 49160 | tf_op jit(solution)/shard_map/ppermute | solution.py:27
  54.3 27.3 %collective-permute-start.7 = (bf16[3,1024,128]{2,1,0:T(8,128)(2,1)S(1)}, bf16[3,1024,128]{2,1,0:T(8,128)(2,1)S(1)}, u32[]{:S(2)}, u32[]{:S(2)}) collective-permute-start(bf16[3,1024,128]{2,1,0:T(8,128)(2,1)S(1)} %get-tuple-element.34), channel_id=1, source_target_pairs={{0,1},{1,2},{2,3},{3,4},{4,5},{5,6},{6,7},{8,9},{9,10},{10,11},{11... | collective-permute-start | bytes 2359304 | tf_op jit(solution)/shard_map/ppermute | solution.py:20
  62.1 19.5 %collective-permute-start.8 = (bf16[3,1024,128]{2,1,0:T(8,128)(2,1)S(1)}, bf16[3,1024,128]{2,1,0:T(8,128)(2,1)S(1)}, u32[]{:S(2)}, u32[]{:S(2)}) collective-permute-start(bf16[3,1024,128]{2,1,0:T(8,128)(2,1)S(1)} %get-tuple-element.35), channel_id=1, source_target_pairs={{1,0},{2,1},{3,2},{4,3},{5,4},{6,5},{7,6},{9,8},{10,9},{11,10},{12... | collective-permute-start | bytes 2359304 | tf_op jit(solution)/shard_map/ppermute | solution.py:20
  64.0 2.9 %collective-permute-start.9 = (bf16[4,16,128]{2,1,0:T(8,128)(2,1)S(1)}, bf16[4,16,128]{2,1,0:T(8,128)(2,1)S(1)}, u32[]{:S(2)}, u32[]{:S(2)}) collective-permute-start(bf16[4,16,128]{2,1,0:T(8,128)(2,1)S(1)} %get-tuple-element.36), channel_id=1, source_target_pairs={{0,8},{8,0},{16,24},{24,16},{1,9},{9,1},{17,25},{25,17},{2,10},{10... | collective-permute-start | bytes 49160 | tf_op jit(solution)/shard_map/ppermute | solution.py:27
  64.1 4.8 %collective-permute-start.10 = (bf16[4,16,128]{2,1,0:T(8,128)(2,1)S(1)}, bf16[4,16,128]{2,1,0:T(8,128)(2,1)S(1)}, u32[]{:S(2)}, u32[]{:S(2)}) collective-permute-start(bf16[4,16,128]{2,1,0:T(8,128)(2,1)S(1)} %get-tuple-element.37), channel_id=1, source_target_pairs={{8,16},{16,8},{9,17},{17,9},{10,18},{18,10},{11,19},{19,11},{12,20... | collective-permute-start | bytes 49160 | tf_op jit(solution)/shard_map/ppermute | solution.py:27
  68.9 12.7 %collective-permute-start.12 = (bf16[3,32,128]{2,1,0:T(8,128)(2,1)S(1)}, bf16[3,32,128]{2,1,0:T(8,128)(2,1)S(1)}, u32[]{:S(2)}, u32[]{:S(2)}) collective-permute-start(bf16[3,32,128]{2,1,0:T(8,128)(2,1)S(1)} %get-tuple-element.42), channel_id=1, source_target_pairs={{1,0},{2,1},{3,2},{4,3},{5,4},{6,5},{7,6},{9,8},{10,9},{11,10},{12... | collective-permute-start | bytes 73736 | tf_op jit(solution)/shard_map/ppermute | solution.py:20
  72.3 9.3 %collective-permute-start.11 = (bf16[3,32,128]{2,1,0:T(8,128)(2,1)S(1)}, bf16[3,32,128]{2,1,0:T(8,128)(2,1)S(1)}, u32[]{:S(2)}, u32[]{:S(2)}) collective-permute-start(bf16[3,32,128]{2,1,0:T(8,128)(2,1)S(1)} %get-tuple-element.43), channel_id=1, source_target_pairs={{0,1},{1,2},{2,3},{3,4},{4,5},{5,6},{6,7},{8,9},{9,10},{10,11},{11... | collective-permute-start | bytes 73736 | tf_op jit(solution)/shard_map/ppermute | solution.py:20

commit v7 on v6

--- a/solution.py
+++ b/solution.py
@@ -799,7 +799,7 @@
                     begin_copies(line_copies(((out_ref, result_out),), send_sems, line - layers, lines_here))
             return carry
 
-        lax.fori_loop(0, (lines_here + 2 * reach) // 2, pair, 0)
+        lax.fori_loop(0, (lines_here + 2 * reach) // 2, pair, 0, unroll=True)
         source, target = target, source
     for line in range(lines_here):
         wait(line_copies(((out_ref, result_out),), send_sems, line, lines_here))

time: 94 us -> 92.2 us (0.981)
  Pallas kernels: 42.9 us -> 40.9 us
    pallas_call x6, Pallas kernels: 42.9 us -> 40.9 us  [kernel_call(): pl.pallas_call(kernel, in_specs=[ANYWHERE] * len(operands), out_specs=[AN...]
where the time goes in v7:
time: 92.2 us; the launch traced here: 91.8 us
  Pallas kernels  40.9 us (44%)
  starting transfers between devices  33.2 us (36%)
  waiting for transfers between devices  15.2 us (16%)
  local copies, waits for them, and re-layouts  1.5 us (2%)
  between operations  1.02 us (1%)
    pallas_call x6, Pallas kernels, kernel_call(): pl.pallas_call(kernel, in_specs=[ANYWHERE] * len(operands), out_specs=[AN...  40.9 us
    ppermute x7, starting transfers between devices, shifted(): return lax.ppermute(block, axis, route)  25.7 us
    ppermute x7, waiting for transfers between devices, shifted(): return lax.ppermute(block, axis, route)  8.05 us
    ppermute x6, starting transfers between devices, exchanged(): return lax.ppermute(block, axis, route)  7.47 us
    ppermute x6, waiting for transfers between devices, exchanged(): return lax.ppermute(block, axis, route)  7.18 us
  transfers between devices with their start and end apart: 13, of which 8 were waited for; matrix products, arithmetic and copies ran while one was open for 0% of the time, Pallas kernels for 12%

profile of v7, /device:TPU:19, one launch (start us, length us, event | category | flops | bytes accessed | tf_op | source)
XLA Modules:
  0.0 91.8 jit_solution(14724842168556686441)
XLA Ops:
  0.7 1.4 %fusion = (bf16[4,512,128]{2,1,0:T(8,128)(2,1)S(1)}, bf16[4,512,128]{2,1,0:T(8,128)(2,1)S(1)}) fusion(bf16[4,1024,128]{2,1,0:T(8,128)(2,1)} %right_in.7), kind=kLoop, calls=%fused_computation.2 | loop fusion | bytes 2097152 | tf_op jit(solution)/shard_map/slice | solution.py:828
  2.1 3.2 %collective-permute-start.1 = (bf16[4,512,128]{2,1,0:T(8,128)(2,1)S(1)}, bf16[4,512,128]{2,1,0:T(8,128)(2,1)S(1)}, u32[]{:S(2)}, u32[]{:S(2)}) collective-permute-start(bf16[4,512,128]{2,1,0:T(8,128)(2,1)S(1)} %get-tuple-element.40), channel_id=1, source_target_pairs={{0,8},{8,16},{16,24},{1,9},{9,17},{17,25},{2,10},{10,18},{18,26},{... | collective-permute-start | bytes 1572872 | tf_op jit(solution)/shard_map/ppermute | solution.py:20
  5.4 2.1 %collective-permute-start.2 = (bf16[4,512,128]{2,1,0:T(8,128)(2,1)S(1)}, bf16[4,512,128]{2,1,0:T(8,128)(2,1)S(1)}, u32[]{:S(2)}, u32[]{:S(2)}) collective-permute-start(bf16[4,512,128]{2,1,0:T(8,128)(2,1)S(1)} %slice.17), channel_id=1, source_target_pairs={{8,0},{16,8},{24,16},{9,1},{17,9},{25,17},{10,2},{18,10},{26,18},{... | collective-permute-start | bytes 1572872 | tf_op jit(solution)/shard_map/ppermute | solution.py:20
  7.5 4.4 %column_own.1 = (bf16[3,1536,256]{2,1,0:T(8,128)(2,1)S(1)}, f32[8,1024]{1,0:T(8,128)S(1)}) custom-call(bf16[4,1024,128]{2,1,0:T(8,128)(2,1)S(1)} %copy-done.1, bf16[4,1024,128]{2,1,0:T(8,128)(2,1)S(1)} %copy-done, bf16[3,3,3,128,128]{4,3,2,1,0:T(8,128)(2,1)S(1)} %copy-done.3), custom_call_target="tpu_custom_call" | custom-call | flops 1073741824 | bytes 4194304 | tf_op jit(solution)/shard_map/column_own/pallas_call | solution.py:47
  11.9 3.2 %collective-permute-start = (bf16[4,512,128]{2,1,0:T(8,128)(2,1)S(1)}, bf16[4,512,128]{2,1,0:T(8,128)(2,1)S(1)}, u32[]{:S(2)}, u32[]{:S(2)}) collective-permute-start(bf16[4,512,128]{2,1,0:T(8,128)(2,1)S(1)} %get-tuple-element.22), channel_id=1, source_target_pairs={{0,8},{8,16},{16,24},{1,9},{9,17},{17,25},{2,10},{10,18},{18,26},{... | collective-permute-start | bytes 1572872 | tf_op jit(solution)/shard_map/ppermute | solution.py:20
  15.2 1.6 %collective-permute-done.1.prev_in.prev_high_in = bf16[4,512,128]{2,1,0:T(8,128)(2,1)S(1)} collective-permute-done((bf16[4,512,128]{2,1,0:T(8,128)(2,1)S(1)}, bf16[4,512,128]{2,1,0:T(8,128)(2,1)S(1)}, u32[]{:S(2)}, u32[]{:S(2)}) %collective-permute-start.1) | collective-permute-done | bytes 524320 | tf_op jit(solution)/shard_map/ppermute | solution.py:20
  16.8 3.5 %column_cross.1.back_in = f32[8,1024]{1,0:T(8,128)S(1)} custom-call(bf16[4,1024,128]{2,1,0:T(8,128)(2,1)S(1)} %copy-done.1, bf16[4,512,128]{2,1,0:T(8,128)(2,1)S(1)} %collective-permute-done.1.prev_in.prev_high_in), custom_call_target="tpu_custom_call" | custom-call | flops 1073741824 | bytes 4194304 | tf_op jit(solution)/shard_map/column_cross/pallas_call | solution.py:47
  20.3 3.2 %column_next.1 = (f32[8,1024]{1,0:T(8,128)S(1)}, f32[8,1024]{1,0:T(8,128)S(1)}, f32[8,1024]{1,0:T(8,128)S(1)}) custom-call(bf16[4,512,128]{2,1,0:T(8,128)(2,1)S(1)} %collective-permute-done.2.next_in, bf16[4,1024,128]{2,1,0:T(8,128)(2,1)S(1)} %copy-done, f32[8,1024]{1,0:T(8,128)S(1)} %get-tuple-element.23.own_in, f32[8,1024]{1,0:T(8,128)S(1)} %column_cross.1.back_in), custom_call_target="tpu_custom_call" | custom-call | flops 268435456 | bytes 2097152 | tf_op jit(solution)/shard_map/column_next/pallas_call | solution.py:47
  23.5 1.4 %collective-permute-start.3 = (f32[8,1024]{1,0:T(8,128)S(1)}, f32[8,1024]{1,0:T(8,128)S(1)}, u32[]{:S(2)}, u32[]{:S(2)}) collective-permute-start(f32[8,1024]{1,0:T(8,128)S(1)} %get-tuple-element.25), channel_id=1, source_target_pairs={{0,8},{8,0},{16,24},{24,16},{1,9},{9,1},{17,25},{25,17},{2,10},{10... | collective-permute-start | bytes 98312 | tf_op jit(solution)/shard_map/ppermute | solution.py:27
  24.9 1.9 %collective-permute-start.4 = (f32[8,1024]{1,0:T(8,128)S(1)}, f32[8,1024]{1,0:T(8,128)S(1)}, u32[]{:S(2)}, u32[]{:S(2)}) collective-permute-start(f32[8,1024]{1,0:T(8,128)S(1)} %get-tuple-element.26), channel_id=1, source_target_pairs={{8,16},{16,8},{9,17},{17,9},{10,18},{18,10},{11,19},{19,11},{12,20... | collective-permute-start | bytes 98312 | tf_op jit(solution)/shard_map/ppermute | solution.py:27
  26.8 1.2 %collective-permute-done.prev_low_in = bf16[4,512,128]{2,1,0:T(8,128)(2,1)S(1)} collective-permute-done((bf16[4,512,128]{2,1,0:T(8,128)(2,1)S(1)}, bf16[4,512,128]{2,1,0:T(8,128)(2,1)S(1)}, u32[]{:S(2)}, u32[]{:S(2)}) %collective-permute-start) | collective-permute-done | bytes 524320 | tf_op jit(solution)/shard_map/ppermute | solution.py:20
  28.0 0.0 collective-permute-done.3.first_in
  28.0 1.8 %collective-permute-done.4.second_in = f32[8,1024]{1,0:T(8,128)S(1)} collective-permute-done((f32[8,1024]{1,0:T(8,128)S(1)}, f32[8,1024]{1,0:T(8,128)S(1)}, u32[]{:S(2)}, u32[]{:S(2)}) %collective-permute-start.4) | collective-permute-done | bytes 32800 | tf_op jit(solution)/shard_map/ppermute | solution.py:27
  29.8 9.4 %row_pass.1 = (f32[4,2048]{1,0:T(4,128)S(1)}, bf16[4,1024,128]{2,1,0:T(8,128)(2,1)S(1)}, f32[4,1024]{1,0:T(4,128)S(1)}, f32[4,1024]{1,0:T(4,128)S(1)}, f32[4,1024]{1,0:T(4,128)S(1)}, /*index=5*/f32[4,1024]{1,0:T(4,128)S(1)}) custom-call(bf16[4,1024,128]{2,1,0:T(8,128)(2,1)S(1)} %copy-done.1, bf16[4,1024,128]{2,1,0:T(8,128)(2,1)S(1)} %copy-done, ...), custom_call_target="tpu_custom_call" | custom-call | tf_op jit(solution)/shard_map/row_pass/pallas_call | solution.py:47
  39.2 0.0 copy-start.2
  39.2 0.3 collective-permute-start.5
  39.5 1.9 %collective-permute-start.6 = (f32[4,1024]{1,0:T(4,128)S(1)}, f32[4,1024]{1,0:T(4,128)S(1)}, u32[]{:S(2)}, u32[]{:S(2)}) collective-permute-start(f32[4,1024]{1,0:T(4,128)S(1)} %get-tuple-element.32), channel_id=1, source_target_pairs={{8,16},{16,8},{9,17},{17,9},{10,18},{18,10},{11,19},{19,11},{12,20... | collective-permute-start | bytes 49160 | tf_op jit(solution)/shard_map/ppermute | solution.py:27
  41.5 0.4 collective-permute-done.5.first_in
  41.9 2.1 %collective-permute-done.6.second_in = f32[4,1024]{1,0:T(4,128)S(1)} collective-permute-done((f32[4,1024]{1,0:T(4,128)S(1)}, f32[4,1024]{1,0:T(4,128)S(1)}, u32[]{:S(2)}, u32[]{:S(2)}) %collective-permute-start.6) | collective-permute-done | bytes 16416 | tf_op jit(solution)/shard_map/ppermute | solution.py:27
  44.0 10.3 %transport.1 = (bf16[4,1024,128]{2,1,0:T(8,128)(2,1)S(1)}, f32[4,1024]{1,0:T(4,128)}, bf16[3,1024,128]{2,1,0:T(8,128)(2,1)S(1)}, bf16[3,1024,128]{2,1,0:T(8,128)...) custom-call(f32[4,2048]{1,0:T(4,128)S(1)} %get-tuple-element.27.pot_in, ...), custom_call_target="tpu_custom_call" | custom-call | tf_op jit(solution)/shard_map/transport/pallas_call | solution.py:47
  54.3 7.8 %collective-permute-start.7 = (bf16[3,1024,128]{2,1,0:T(8,128)(2,1)S(1)}, bf16[3,1024,128]{2,1,0:T(8,128)(2,1)S(1)}, u32[]{:S(2)}, u32[]{:S(2)}) collective-permute-start(bf16[3,1024,128]{2,1,0:T(8,128)(2,1)S(1)} %get-tuple-element.34), channel_id=1, source_target_pairs={{0,1},{1,2},{2,3},{3,4},{4,5},{5,6},{6,7},{8,9},{9,10},{10,11},{11... | collective-permute-start | bytes 2359304 | tf_op jit(solution)/shard_map/ppermute | solution.py:20
  62.1 1.9 %collective-permute-start.8 = (bf16[3,1024,128]{2,1,0:T(8,128)(2,1)S(1)}, bf16[3,1024,128]{2,1,0:T(8,128)(2,1)S(1)}, u32[]{:S(2)}, u32[]{:S(2)}) collective-permute-start(bf16[3,1024,128]{2,1,0:T(8,128)(2,1)S(1)} %get-tuple-element.35), channel_id=1, source_target_pairs={{1,0},{2,1},{3,2},{4,3},{5,4},{6,5},{7,6},{9,8},{10,9},{11,10},{12... | collective-permute-start | bytes 2359304 | tf_op jit(solution)/shard_map/ppermute | solution.py:20
  64.0 0.1 collective-permute-start.9
  64.1 1.9 %collective-permute-start.10 = (bf16[4,16,128]{2,1,0:T(8,128)(2,1)S(1)}, bf16[4,16,128]{2,1,0:T(8,128)(2,1)S(1)}, u32[]{:S(2)}, u32[]{:S(2)}) collective-permute-start(bf16[4,16,128]{2,1,0:T(8,128)(2,1)S(1)} %get-tuple-element.37), channel_id=1, source_target_pairs={{8,16},{16,8},{9,17},{17,9},{10,18},{18,10},{11,19},{19,11},{12,20... | collective-permute-start | bytes 49160 | tf_op jit(solution)/shard_map/ppermute | solution.py:27
  66.0 0.9 %collective-permute-done.9.first_in = bf16[4,16,128]{2,1,0:T(8,128)(2,1)S(1)} collective-permute-done((bf16[4,16,128]{2,1,0:T(8,128)(2,1)S(1)}, bf16[4,16,128]{2,1,0:T(8,128)(2,1)S(1)}, u32[]{:S(2)}, u32[]{:S(2)}) %collective-permute-start.9) | collective-permute-done | bytes 16416 | tf_op jit(solution)/shard_map/ppermute | solution.py:27
  67.0 1.9 %collective-permute-done.10.second_in = bf16[4,16,128]{2,1,0:T(8,128)(2,1)S(1)} collective-permute-done((bf16[4,16,128]{2,1,0:T(8,128)(2,1)S(1)}, bf16[4,16,128]{2,1,0:T(8,128)(2,1)S(1)}, u32[]{:S(2)}, u32[]{:S(2)}) %collective-permute-start.10) | collective-permute-done | bytes 16416 | tf_op jit(solution)/shard_map/ppermute | solution.py:27
  68.9 3.4 %collective-permute-start.12 = (bf16[3,32,128]{2,1,0:T(8,128)(2,1)S(1)}, bf16[3,32,128]{2,1,0:T(8,128)(2,1)S(1)}, u32[]{:S(2)}, u32[]{:S(2)}) collective-permute-start(bf16[3,32,128]{2,1,0:T(8,128)(2,1)S(1)} %get-tuple-element.42), channel_id=1, source_target_pairs={{1,0},{2,1},{3,2},{4,3},{5,4},{6,5},{7,6},{9,8},{10,9},{11,10},{12... | collective-permute-start | bytes 73736 | tf_op jit(solution)/shard_map/ppermute | solution.py:20
  72.3 4.1 %collective-permute-start.11 = (bf16[3,32,128]{2,1,0:T(8,128)(2,1)S(1)}, bf16[3,32,128]{2,1,0:T(8,128)(2,1)S(1)}, u32[]{:S(2)}, u32[]{:S(2)}) collective-permute-start(bf16[3,32,128]{2,1,0:T(8,128)(2,1)S(1)} %get-tuple-element.43), channel_id=1, source_target_pairs={{0,1},{1,2},{2,3},{3,4},{4,5},{5,6},{6,7},{8,9},{9,10},{10,11},{11... | collective-permute-start | bytes 73736 | tf_op jit(solution)/shard_map/ppermute | solution.py:20
  76.4 5.2 %collective-permute-done.12.corner_bottom_in = bf16[3,32,128]{2,1,0:T(8,128)(2,1)S(1)} collective-permute-done((bf16[3,32,128]{2,1,0:T(8,128)(2,1)S(1)}, bf16[3,32,128]{2,1,0:T(8,128)(2,1)S(1)}, u32[]{:S(2)}, u32[]{:S(2)}) %collective-permute-start.12) | collective-permute-done | bytes 24608 | tf_op jit(solution)/shard_map/ppermute | solution.py:20
  81.6 0.0 collective-permute-done.11.corner_top_in
  81.6 0.0 collective-permute-done.7.top_in
  81.6 10.0 %conv_layers.1 = bf16[4,1024,128]{2,1,0:T(8,128)(2,1)} custom-call(bf16[4,1024,128]{2,1,0:T(8,128)(2,1)S(1)} %get-tuple-element.33.state_in, bf16[3,1024,128]{2,1,0:T(8,128)(2,1)S(1)} %collective-permute-done.7.top_in, bf16[3,1024,128]{2,1,0:T(8,128)(2,1)S(1)} %collective-permute-done.8.bottom_in, bf16[4,16,128]{2,1,0:T(8,128)(2,1)S(1)} %collective-permute-done.9.first_in, ...), custom_call_target="tpu_custom_call" | custom-call | tf_op jit(solution)/shard_map/conv_layers/pallas_call | solution.py:47
  (13 shorter events, 0.1 us)
Async XLA Ops:
  0.6 6.8 %copy-start = (bf16[4,1024,128]{2,1,0:T(8,128)(2,1)S(1)}, bf16[4,1024,128]{2,1,0:T(8,128)(2,1)}, u32[]{:S(2)}) copy-start(bf16[4,1024,128]{2,1,0:T(8,128)(2,1)} %right_in.7) | copy-start | bytes 3145732
  0.6 4.7 %copy-start.1 = (bf16[4,1024,128]{2,1,0:T(8,128)(2,1)S(1)}, bf16[4,1024,128]{2,1,0:T(8,128)(2,1)}, u32[]{:S(2)}) copy-start(bf16[4,1024,128]{2,1,0:T(8,128)(2,1)} %left_in.7) | copy-start | bytes 3145732
  0.6 6.8 %copy-start.3 = (bf16[3,3,3,128,128]{4,3,2,1,0:T(8,128)(2,1)S(1)}, bf16[3,3,3,128,128]{4,3,2,1,0:T(8,128)(2,1)}, u32[]{:S(2)}) copy-start(bf16[3,3,3,128,128]{4,3,2,1,0:T(8,128)(2,1)} %weight_in.1) | copy-start | bytes 2654212
  2.1 14.7 %collective-permute-start.1 = (bf16[4,512,128]{2,1,0:T(8,128)(2,1)S(1)}, bf16[4,512,128]{2,1,0:T(8,128)(2,1)S(1)}, u32[]{:S(2)}, u32[]{:S(2)}) collective-permute-start(bf16[4,512,128]{2,1,0:T(8,128)(2,1)S(1)} %get-tuple-element.40), channel_id=1, source_target_pairs={{0,8},{8,16},{16,24},{1,9},{9,17},{17,25},{2,10},{10,18},{18,26},{... | collective-permute-start | bytes 1572872 | tf_op jit(solution)/shard_map/ppermute | solution.py:20
  5.4 14.9 %collective-permute-start.2 = (bf16[4,512,128]{2,1,0:T(8,128)(2,1)S(1)}, bf16[4,512,128]{2,1,0:T(8,128)(2,1)S(1)}, u32[]{:S(2)}, u32[]{:S(2)}) collective-permute-start(bf16[4,512,128]{2,1,0:T(8,128)(2,1)S(1)} %slice.17), channel_id=1, source_target_pairs={{8,0},{16,8},{24,16},{9,1},{17,9},{25,17},{10,2},{18,10},{26,18},{... | collective-permute-start | bytes 1572872 | tf_op jit(solution)/shard_map/ppermute | solution.py:20
  11.9 16.1 %collective-permute-start = (bf16[4,512,128]{2,1,0:T(8,128)(2,1)S(1)}, bf16[4,512,128]{2,1,0:T(8,128)(2,1)S(1)}, u32[]{:S(2)}, u32[]{:S(2)}) collective-permute-start(bf16[4,512,128]{2,1,0:T(8,128)(2,1)S(1)} %get-tuple-element.22), channel_id=1, source_target_pairs={{0,8},{8,16},{16,24},{1,9},{9,17},{17,25},{2,10},{10,18},{18,26},{... | collective-permute-start | bytes 1572872 | tf_op jit(solution)/shard_map/ppermute | solution.py:20
  23.5 4.5 %collective-permute-start.3 = (f32[8,1024]{1,0:T(8,128)S(1)}, f32[8,1024]{1,0:T(8,128)S(1)}, u32[]{:S(2)}, u32[]{:S(2)}) collective-permute-start(f32[8,1024]{1,0:T(8,128)S(1)} %get-tuple-element.25), channel_id=1, source_target_pairs={{0,8},{8,0},{16,24},{24,16},{1,9},{9,1},{17,25},{25,17},{2,10},{10... | collective-permute-start | bytes 98312 | tf_op jit(solution)/shard_map/ppermute | solution.py:27
  24.9 4.9 %collective-permute-start.4 = (f32[8,1024]{1,0:T(8,128)S(1)}, f32[8,1024]{1,0:T(8,128)S(1)}, u32[]{:S(2)}, u32[]{:S(2)}) collective-permute-start(f32[8,1024]{1,0:T(8,128)S(1)} %get-tuple-element.26), channel_id=1, source_target_pairs={{8,16},{16,8},{9,17},{17,9},{10,18},{18,10},{11,19},{19,11},{12,20... | collective-permute-start | bytes 98312 | tf_op jit(solution)/shard_map/ppermute | solution.py:27
  39.2 42.4 %copy-start.2 = (f32[3,128]{1,0:T(4,128)S(1)}, f32[3,128]{1,0:T(4,128)}, u32[]{:S(2)}) copy-start(f32[3,128]{1,0:T(4,128)} %bias_in.1) | copy-start | bytes 4612
  39.2 2.7 %collective-permute-start.5 = (f32[4,1024]{1,0:T(4,128)S(1)}, f32[4,1024]{1,0:T(4,128)S(1)}, u32[]{:S(2)}, u32[]{:S(2)}) collective-permute-start(f32[4,1024]{1,0:T(4,128)S(1)} %get-tuple-element.31), channel_id=1, source_target_pairs={{0,8},{8,0},{16,24},{24,16},{1,9},{9,1},{17,25},{25,17},{2,10},{10... | collective-permute-start | bytes 49160 | tf_op jit(solution)/shard_map/ppermute | solution.py:27
  39.5 4.5 %collective-permute-start.6 = (f32[4,1024]{1,0:T(4,128)S(1)}, f32[4,1024]{1,0:T(4,128)S(1)}, u32[]{:S(2)}, u32[]{:S(2)}) collective-permute-start(f32[4,1024]{1,0:T(4,128)S(1)} %get-tuple-element.32), channel_id=1, source_target_pairs={{8,16},{16,8},{9,17},{17,9},{10,18},{18,10},{11,19},{19,11},{12,20... | collective-permute-start | bytes 49160 | tf_op jit(solution)/shard_map/ppermute | solution.py:27
  54.3 27.3 %collective-permute-start.7 = (bf16[3,1024,128]{2,1,0:T(8,128)(2,1)S(1)}, bf16[3,1024,128]{2,1,0:T(8,128)(2,1)S(1)}, u32[]{:S(2)}, u32[]{:S(2)}) collective-permute-start(bf16[3,1024,128]{2,1,0:T(8,128)(2,1)S(1)} %get-tuple-element.34), channel_id=1, source_target_pairs={{0,1},{1,2},{2,3},{3,4},{4,5},{5,6},{6,7},{8,9},{9,10},{10,11},{11... | collective-permute-start | bytes 2359304 | tf_op jit(solution)/shard_map/ppermute | solution.py:20
  62.1 19.5 %collective-permute-start.8 = (bf16[3,1024,128]{2,1,0:T(8,128)(2,1)S(1)}, bf16[3,1024,128]{2,1,0:T(8,128)(2,1)S(1)}, u32[]{:S(2)}, u32[]{:S(2)}) collective-permute-start(bf16[3,1024,128]{2,1,0:T(8,128)(2,1)S(1)} %get-tuple-element.35), channel_id=1, source_target_pairs={{1,0},{2,1},{3,2},{4,3},{5,4},{6,5},{7,6},{9,8},{10,9},{11,10},{12... | collective-permute-start | bytes 2359304 | tf_op jit(solution)/shard_map/ppermute | solution.py:20
  64.0 2.9 %collective-permute-start.9 = (bf16[4,16,128]{2,1,0:T(8,128)(2,1)S(1)}, bf16[4,16,128]{2,1,0:T(8,128)(2,1)S(1)}, u32[]{:S(2)}, u32[]{:S(2)}) collective-permute-start(bf16[4,16,128]{2,1,0:T(8,128)(2,1)S(1)} %get-tuple-element.36), channel_id=1, source_target_pairs={{0,8},{8,0},{16,24},{24,16},{1,9},{9,1},{17,25},{25,17},{2,10},{10... | collective-permute-start | bytes 49160 | tf_op jit(solution)/shard_map/ppermute | solution.py:27
  64.1 4.8 %collective-permute-start.10 = (bf16[4,16,128]{2,1,0:T(8,128)(2,1)S(1)}, bf16[4,16,128]{2,1,0:T(8,128)(2,1)S(1)}, u32[]{:S(2)}, u32[]{:S(2)}) collective-permute-start(bf16[4,16,128]{2,1,0:T(8,128)(2,1)S(1)} %get-tuple-element.37), channel_id=1, source_target_pairs={{8,16},{16,8},{9,17},{17,9},{10,18},{18,10},{11,19},{19,11},{12,20... | collective-permute-start | bytes 49160 | tf_op jit(solution)/shard_map/ppermute | solution.py:27
  68.9 12.7 %collective-permute-start.12 = (bf16[3,32,128]{2,1,0:T(8,128)(2,1)S(1)}, bf16[3,32,128]{2,1,0:T(8,128)(2,1)S(1)}, u32[]{:S(2)}, u32[]{:S(2)}) collective-permute-start(bf16[3,32,128]{2,1,0:T(8,128)(2,1)S(1)} %get-tuple-element.42), channel_id=1, source_target_pairs={{1,0},{2,1},{3,2},{4,3},{5,4},{6,5},{7,6},{9,8},{10,9},{11,10},{12... | collective-permute-start | bytes 73736 | tf_op jit(solution)/shard_map/ppermute | solution.py:20
  72.3 9.3 %collective-permute-start.11 = (bf16[3,32,128]{2,1,0:T(8,128)(2,1)S(1)}, bf16[3,32,128]{2,1,0:T(8,128)(2,1)S(1)}, u32[]{:S(2)}, u32[]{:S(2)}) collective-permute-start(bf16[3,32,128]{2,1,0:T(8,128)(2,1)S(1)} %get-tuple-element.43), channel_id=1, source_target_pairs={{0,1},{1,2},{2,3},{3,4},{4,5},{5,6},{6,7},{8,9},{9,10},{10,11},{11... | collective-permute-start | bytes 73736 | tf_op jit(solution)/shard_map/ppermute | solution.py:20

commit v8 on v7

--- a/solution.py
+++ b/solution.py
@@ -505,46 +505,35 @@
     )
 
 
-def transport_kernel(
-    block,
-    pot_in,
-    lanes_in,
-    left_in,
-    right_in,
-    prev_low_in,
-    prev_high_in,
-    own_in,
-    back_in,
-    first_in,
-    second_in,
-    state_out,
-    disp_out,
-    first_out,
-    last_out,
-    first_px_out,
-    second_px_out,
-    pot,
-    lanes,
-    left,
-    ext,
-    own,
-    back,
-    first_part,
-    second_part,
-    state,
-    disp,
-    first_px,
-    second_px,
-    pot_lanes,
-    marks,
-    raw,
-    weights,
-    line_sems,
-    sems,
-    send_sems,
-):
+def transport_kernel(block, targets, outs, earlier, *refs):
+    pot_in, lanes_in, left_in, right_in, prev_low_in, prev_high_in = refs[:6]
+    own_in, back_in, first_in, second_in = refs[6:10]
+    earlier_in = refs[10 : 10 + earlier]
+    refs = refs[10 + earlier :]
+    state_outs = refs[:outs]
+    disp_out, first_px_out, second_px_out = refs[outs : outs + 3]
+    (
+        pot,
+        lanes,
+        left,
+        ext,
+        own,
+        back,
+        first_part,
+        second_part,
+        state,
+        disp,
+        first_px,
+        second_px,
+        pot_lanes,
+        marks,
+        raw,
+        weights,
+        line_sems,
+        sems,
+        send_sems,
+    ) = refs[outs + 3 :]
     lines_here, seg_len, channels = left.shape
-    layers = first_out.shape[0]
     scale = log2_scale(channels)
     big = 2 * block
     window = seg_len + big
@@ -555,14 +544,15 @@
             (back_in, back),
             (first_in, first_part),
             (second_in, second_part),
-        ),
+        )
+        + tuple(zip(earlier_in, (disp, first_px, second_px))),
         sems,
     )
     begin_copies(fetches)
     pairs = feature_pairs(left_in, right_in, prev_low_in, prev_high_in, left, ext) + (
         (lanes_in, lanes),
     )
-    for line in range(lines_here):
+    for line, _, _ in targets:
         begin_copies(line_copies(pairs, line_sems, line, lines_here))
     lane = lax.broadcasted_iota(jnp.int32, (window, channels), 1)
     distance = seg_len - lax.broadcasted_iota(jnp.int32, (window, channels), 0)
@@ -581,8 +571,9 @@
     offsets = lax.broadcasted_iota(jnp.int32, (1, big), 1).astype(jnp.float32)
     corner = jnp.zeros((block, block), jnp.bfloat16)
     steps = seg_len // big
-
-    def one_line(line, carry):
+    sends = []
+
+    def one_line(line):
         wait(line_copies(pairs, line_sems, line, lines_here))
 
         def score(index):
@@ -622,53 +613,41 @@
                 disparity.append(gather(index - 2))
             if 1 <= index <= steps:
                 weigh(index - 1)
-        disp[pl.ds(line, 1), :] = jnp.concatenate(disparity, axis=1)
-        begin_copies(line_copies(((state, state_out),), send_sems, line, lines_here))
+        disp[line : line + 1, :] = jnp.concatenate(disparity, axis=1)
         high = state[line, seg_len - EDGE :].astype(jnp.float32)
         first, second = by_parity(high, state[line, :EDGE].astype(jnp.float32))
         first_px[line] = first.astype(jnp.bfloat16)
         second_px[line] = second.astype(jnp.bfloat16)
 
-        @pl.when(line < layers)
-        def _():
-            pltpu.make_async_copy(state.at[line], first_out.at[line], sems.at[line]).start()
-
-        @pl.when(line >= lines_here - layers)
-        def _():
-            target = line - (lines_here - layers)
-            pltpu.make_async_copy(
-                state.at[line], last_out.at[target], sems.at[layers + target]
-            ).start()
-
-        return carry
-
-    lax.fori_loop(0, lines_here, one_line, 0)
-    sends = copies_of(
+    for index, (line, out, place) in enumerate(targets):
+        one_line(line)
+        sends.append(
+            pltpu.make_async_copy(state.at[line], state_outs[out].at[place], send_sems.at[index])
+        )
+        sends[-1].start()
+    last = copies_of(
         ((first_px, first_px_out), (second_px, second_px_out), (disp, disp_out)),
-        send_sems.at[pl.ds(lines_here, 3)],
-    )
-    begin_copies(sends)
-    for line in range(layers):
-        pltpu.make_async_copy(state.at[line], first_out.at[line], sems.at[line]).wait()
-        source = line + lines_here - layers
-        pltpu.make_async_copy(state.at[source], last_out.at[line], sems.at[layers + line]).wait()
-    for line in range(lines_here):
-        wait(line_copies(((state, state_out),), send_sems, line, lines_here))
-    wait(sends)
-
-
-def transport(pot, lanes, left, right, prev_low, prev_high, own, back, first, second, block, layers):
+        send_sems.at[pl.ds(len(targets), 3)],
+    )
+    begin_copies(last)
+    wait(sends + last)
+
+
+def transport(groups, earlier, pot, lanes, left, right, prev_low, prev_high, own, back, first, second, block):
     lines_here, seg_len, channels = left.shape
     bf16, f32 = jnp.bfloat16, jnp.float32
-    edge = ((layers, seg_len, channels), bf16)
     side = ((lines_here, EDGE, channels), bf16)
     state = (left.shape, bf16)
     marginal = ((lines_here, seg_len), f32)
     window = seg_len + 2 * block
+    targets = tuple(
+        (line, out, place) for out, group in enumerate(groups) for place, line in enumerate(group)
+    )
     return kernel_call(
-        functools.partial(transport_kernel, block),
-        (pot, lanes, left, right, prev_low, prev_high, own, back, first, second),
-        (state, marginal, edge, edge, side, side),
+        functools.partial(transport_kernel, block, targets, len(groups), len(earlier)),
+        (pot, lanes, left, right, prev_low, prev_high, own, back, first, second) + earlier,
+        tuple(((len(group), seg_len, channels), bf16) for group in groups)
+        + (marginal, side, side),
         ((pot.shape, f32), (lanes.shape, bf16), state)
         + (((lines_here, 2 * seg_len, channels), bf16),)
         + (marginal,) * 4
@@ -679,8 +658,13 @@
             ((2, 2 * block, window), f32),
             ((2, 2 * block, window), bf16),
         ),
-        (5 * lines_here, max(5, 2 * layers), lines_here + 3),
+        (5 * lines_here, 8, len(targets) + 3),
         "transport",
+        pl.CostEstimate(
+            flops=len(targets) * 4 * seg_len * seg_len * channels,
+            bytes_accessed=len(targets) * 8 * seg_len * channels,
+            transcendentals=len(targets) * seg_len * seg_len,
+        ),
     )
 
 
@@ -699,9 +683,13 @@
 
 
 def conv_kernel(
-    state_in,
-    top_in,
-    bottom_in,
+    first_line_in,
+    middle_in,
+    last_line_in,
+    top_middle_in,
+    top_last_in,
+    bottom_first_in,
+    bottom_middle_in,
     first_in,
     second_in,
     corner_top_in,
@@ -709,9 +697,13 @@
     weight_in,
     bias_in,
     result_out,
-    state_ref,
-    top_ref,
-    bottom_ref,
+    first_line_ref,
+    middle_ref,
+    last_line_ref,
+    top_middle_ref,
+    top_last_ref,
+    bottom_first_ref,
+    bottom_middle_ref,
     first_ref,
     second_ref,
     corner_top_ref,
@@ -726,29 +718,41 @@
 ):
     fetches = copies_of(
         (
-            (state_in, state_ref),
+            (first_line_in, first_line_ref),
+            (middle_in, middle_ref),
+            (last_line_in, last_line_ref),
             (first_in, first_ref),
             (second_in, second_ref),
             (corner_top_in, corner_top_ref),
             (corner_bottom_in, corner_bottom_ref),
-            (top_in, top_ref),
-            (bottom_in, bottom_ref),
+            (top_middle_in, top_middle_ref),
+            (top_last_in, top_last_ref),
+            (bottom_first_in, bottom_first_ref),
+            (bottom_middle_in, bottom_middle_ref),
             (weight_in, weight_ref),
             (bias_in, bias_ref),
         ),
         sems,
     )
     begin_copies(fetches)
-    lines_here, seg_len, channels = state_ref.shape
+    lines_here, seg_len, channels = out_ref.shape
     layers = weight_ref.shape[0]
     after = layers + lines_here
     right = EDGE + seg_len
     f32 = jnp.float32
-    wait(fetches[:1])
-    first_image[layers:after, EDGE:right] = state_ref[...].astype(f32)
-    wait(fetches[1:])
-    first_image[:layers, EDGE:right] = top_ref[...].astype(f32)
-    first_image[after:, EDGE:right] = bottom_ref[...].astype(f32)
+    wait(fetches)
+    line = 0
+    for part in (
+        top_middle_ref,
+        top_last_ref,
+        first_line_ref,
+        middle_ref,
+        last_line_ref,
+        bottom_first_ref,
+        bottom_middle_ref,
+    ):
+        first_image[line : line + part.shape[0], EDGE:right] = part[...].astype(f32)
+        line += part.shape[0]
     for rows, first_px, second_px in (
         (slice(layers, after), first_ref[...], second_ref[...]),
         (slice(0, layers), corner_top_ref[:, :EDGE], corner_top_ref[:, EDGE:]),
@@ -805,12 +809,12 @@
         wait(line_copies(((out_ref, result_out),), send_sems, line, lines_here))
 
 
-def conv_layers(state, top, bottom, left_px, right_px, corners_top, corners_bottom, weight, bias):
+def conv_layers(lines_here, lines, edges, weight, bias):
     layers = weight.shape[0]
-    lines_here, seg_len, channels = state.shape
+    seg_len, channels = lines[0].shape[1:]
     image = ((lines_here + 2 * layers, seg_len + 2 * EDGE, channels), jnp.float32)
-    operands = (state, top, bottom, left_px, right_px, corners_top, corners_bottom, weight, bias)
-    result = (state.shape, state.dtype)
+    operands = lines + edges + (weight, bias)
+    result = ((lines_here, seg_len, channels), jnp.bfloat16)
     return kernel_call(
         conv_kernel,
         operands,
@@ -824,7 +828,6 @@
 def shards(left_features, right_features, conv_weight, conv_bias):
     seg_len = left_features.shape[1]
     half = seg_len // 2
-    layers = conv_weight.shape[0]
     prev_high = shifted(right_features[:, half:], "seg", 1)
     next_low = shifted(left_features[:, :half], "seg", -1)
     stacked, own = own_partials(left_features, right_features, conv_weight)
@@ -840,18 +843,29 @@
     )
     first = exchanged(first, "seg", 0)
     second = exchanged(second, "seg", 1)
-    state, disparity, first_lines, last_lines, first, second = transport(
-        pot, lanes, left_features, right_features, prev_low, prev_high, own, back, first, second, block, layers
-    )
-    bottom = shifted(first_lines, "lines", -1)
-    top = shifted(last_lines, "lines", 1)
+    lines_here, layers = left_features.shape[0], conv_weight.shape[0]
+    low, high = tuple(range(lines_here - layers)), tuple(range(layers, lines_here))
+    shared = tuple(range(lines_here - layers, layers))
+    given = (
+        pot, lanes, left_features, right_features, prev_low, prev_high, own, back, first, second, block
+    )
+    middle, *earlier = transport((shared,), (), *given)
+    bottom_middle = shifted(middle, "lines", -1)
+    top_middle = shifted(middle, "lines", 1)
+    first_line, last_line, disparity, first, second = transport((low, high), tuple(earlier), *given)
+    bottom_first = shifted(first_line, "lines", -1)
+    top_last = shifted(last_line, "lines", 1)
     first = exchanged(first, "seg", 0)
     second = exchanged(second, "seg", 1)
     edges = jnp.concatenate([first, second], axis=1)
     corners_bottom = shifted(edges[:layers], "lines", -1)
     corners_top = shifted(edges[-layers:], "lines", 1)
     refined = conv_layers(
-        state, top, bottom, first, second, corners_top, corners_bottom, stacked, conv_bias
+        lines_here,
+        (first_line, middle, last_line, top_middle, top_last, bottom_first, bottom_middle),
+        (first, second, corners_top, corners_bottom),
+        stacked,
+        conv_bias,
     )
     return (refined, disparity)
 

time: 92.2 us -> 96.2 us (1.043)
  the two profiles are of different devices: /device:TPU:19 before, /device:TPU:12 now
where the time goes in v8:
time: 96.2 us; the launch traced here: 95.8 us
  Pallas kernels  42.1 us (44%)
  starting transfers between devices  39.2 us (41%)
  waiting for transfers between devices  11.9 us (12%)
  local copies, waits for them, and re-layouts  1.5 us (2%)
  between operations  1.12 us (1%)
    pallas_call x7, Pallas kernels, kernel_call(): pl.pallas_call(kernel, in_specs=[ANYWHERE] * len(operands), out_specs=[AN...  42.1 us
    ppermute x9, starting transfers between devices, shifted(): return lax.ppermute(block, axis, route)  26 us
    ppermute x6, starting transfers between devices, exchanged(): return lax.ppermute(block, axis, route)  13.1 us
    ppermute x9, waiting for transfers between devices, shifted(): return lax.ppermute(block, axis, route)  8.39 us
    ppermute x6, waiting for transfers between devices, exchanged(): return lax.ppermute(block, axis, route)  3.56 us
  transfers between devices with their start and end apart: 15, of which 5 were waited for; matrix products, arithmetic and copies ran while one was open for 0% of the time, Pallas kernels for 18%

profile of v8, /device:TPU:12, one launch (start us, length us, event | category | flops | bytes accessed | tf_op | source)
XLA Modules:
  0.0 95.8 jit_solution(7821984942898721424)
XLA Ops:
  0.7 1.4 %fusion = (bf16[4,512,128]{2,1,0:T(8,128)(2,1)S(1)}, bf16[4,512,128]{2,1,0:T(8,128)(2,1)S(1)}) fusion(bf16[4,1024,128]{2,1,0:T(8,128)(2,1)} %refs_3_.3), kind=kLoop, calls=%fused_computation.2 | loop fusion | bytes 2097152 | tf_op jit(solution)/shard_map/slice | solution.py:831
  2.1 3.5 %collective-permute-start.1 = (bf16[4,512,128]{2,1,0:T(8,128)(2,1)S(1)}, bf16[4,512,128]{2,1,0:T(8,128)(2,1)S(1)}, u32[]{:S(2)}, u32[]{:S(2)}) collective-permute-start(bf16[4,512,128]{2,1,0:T(8,128)(2,1)S(1)} %get-tuple-element.46), channel_id=1, source_target_pairs={{0,8},{8,16},{16,24},{1,9},{9,17},{17,25},{2,10},{10,18},{18,26},{... | collective-permute-start | bytes 1572872 | tf_op jit(solution)/shard_map/ppermute | solution.py:20
  5.6 2.4 %collective-permute-start.2 = (bf16[4,512,128]{2,1,0:T(8,128)(2,1)S(1)}, bf16[4,512,128]{2,1,0:T(8,128)(2,1)S(1)}, u32[]{:S(2)}, u32[]{:S(2)}) collective-permute-start(bf16[4,512,128]{2,1,0:T(8,128)(2,1)S(1)} %slice.17), channel_id=1, source_target_pairs={{8,0},{16,8},{24,16},{9,1},{17,9},{25,17},{10,2},{18,10},{26,18},{... | collective-permute-start | bytes 1572872 | tf_op jit(solution)/shard_map/ppermute | solution.py:20
  8.1 4.4 %column_own.1 = (bf16[3,1536,256]{2,1,0:T(8,128)(2,1)S(1)}, f32[8,1024]{1,0:T(8,128)S(1)}) custom-call(bf16[4,1024,128]{2,1,0:T(8,128)(2,1)S(1)} %copy-done.1, bf16[4,1024,128]{2,1,0:T(8,128)(2,1)S(1)} %copy-done, bf16[3,3,3,128,128]{4,3,2,1,0:T(8,128)(2,1)S(1)} %copy-done.3), custom_call_target="tpu_custom_call" | custom-call | flops 1073741824 | bytes 4194304 | tf_op jit(solution)/shard_map/column_own/pallas_call | solution.py:47
  12.5 3.5 %collective-permute-start = (bf16[4,512,128]{2,1,0:T(8,128)(2,1)S(1)}, bf16[4,512,128]{2,1,0:T(8,128)(2,1)S(1)}, u32[]{:S(2)}, u32[]{:S(2)}) collective-permute-start(bf16[4,512,128]{2,1,0:T(8,128)(2,1)S(1)} %get-tuple-element.25), channel_id=1, source_target_pairs={{0,8},{8,16},{16,24},{1,9},{9,17},{17,25},{2,10},{10,18},{18,26},{... | collective-permute-start | bytes 1572872 | tf_op jit(solution)/shard_map/ppermute | solution.py:20
  16.0 2.8 %collective-permute-done.1.prev_in.prev_high_in.refs_5_ = bf16[4,512,128]{2,1,0:T(8,128)(2,1)S(1)} collective-permute-done((bf16[4,512,128]{2,1,0:T(8,128)(2,1)S(1)}, bf16[4,512,128]{2,1,0:T(8,128)(2,1)S(1)}, u32[]{:S(2)}, u32[]{:S(2)}) %collective-permute-start.1) | collective-permute-done | bytes 524320 | tf_op jit(solution)/shard_map/ppermute | solution.py:20
  18.8 3.5 %column_cross.1.back_in = f32[8,1024]{1,0:T(8,128)S(1)} custom-call(bf16[4,1024,128]{2,1,0:T(8,128)(2,1)S(1)} %copy-done.1, bf16[4,512,128]{2,1,0:T(8,128)(2,1)S(1)} %collective-permute-done.1.prev_in.prev_high_in.refs_5_), custom_call_target="tpu_custom_call" | custom-call | flops 1073741824 | bytes 4194304 | tf_op jit(solution)/shard_map/column_cross/pallas_call | solution.py:47
  22.3 0.0 collective-permute-done.2.next_in
  22.3 3.2 %column_next.1 = (f32[8,1024]{1,0:T(8,128)S(1)}, f32[8,1024]{1,0:T(8,128)S(1)}, f32[8,1024]{1,0:T(8,128)S(1)}) custom-call(bf16[4,512,128]{2,1,0:T(8,128)(2,1)S(1)} %collective-permute-done.2.next_in, bf16[4,1024,128]{2,1,0:T(8,128)(2,1)S(1)} %copy-done, f32[8,1024]{1,0:T(8,128)S(1)} %get-tuple-element.26.own_in, f32[8,1024]{1,0:T(8,128)S(1)} %column_cross.1.back_in), custom_call_target="tpu_custom_call" | custom-call | flops 268435456 | bytes 2097152 | tf_op jit(solution)/shard_map/column_next/pallas_call | solution.py:47
  25.5 0.1 collective-permute-start.3
  25.6 5.0 %collective-permute-start.4 = (f32[8,1024]{1,0:T(8,128)S(1)}, f32[8,1024]{1,0:T(8,128)S(1)}, u32[]{:S(2)}, u32[]{:S(2)}) collective-permute-start(f32[8,1024]{1,0:T(8,128)S(1)} %get-tuple-element.29), channel_id=1, source_target_pairs={{8,16},{16,8},{9,17},{17,9},{10,18},{18,10},{11,19},{19,11},{12,20... | collective-permute-start | bytes 98312 | tf_op jit(solution)/shard_map/ppermute | solution.py:27
  30.7 0.0 collective-permute-done.prev_low_in.refs_4_
  30.7 1.9 %collective-permute-done.4.second_in = f32[8,1024]{1,0:T(8,128)S(1)} collective-permute-done((f32[8,1024]{1,0:T(8,128)S(1)}, f32[8,1024]{1,0:T(8,128)S(1)}, u32[]{:S(2)}, u32[]{:S(2)}) %collective-permute-start.4) | collective-permute-done | bytes 32800 | tf_op jit(solution)/shard_map/ppermute | solution.py:27
  32.5 9.4 %row_pass.1 = (f32[4,2048]{1,0:T(4,128)S(1)}, bf16[4,1024,128]{2,1,0:T(8,128)(2,1)S(1)}, f32[4,1024]{1,0:T(4,128)S(1)}, f32[4,1024]{1,0:T(4,128)S(1)}, f32[4,1024]{1,0:T(4,128)S(1)}, /*index=5*/f32[4,1024]{1,0:T(4,128)S(1)}) custom-call(bf16[4,1024,128]{2,1,0:T(8,128)(2,1)S(1)} %copy-done.1, bf16[4,1024,128]{2,1,0:T(8,128)(2,1)S(1)} %copy-done, ...), custom_call_target="tpu_custom_call" | custom-call | tf_op jit(solution)/shard_map/row_pass/pallas_call | solution.py:47
  42.0 0.1 collective-permute-start.5
  42.1 3.9 %collective-permute-start.6 = (f32[4,1024]{1,0:T(4,128)S(1)}, f32[4,1024]{1,0:T(4,128)S(1)}, u32[]{:S(2)}, u32[]{:S(2)}) collective-permute-start(f32[4,1024]{1,0:T(4,128)S(1)} %get-tuple-element.35), channel_id=1, source_target_pairs={{8,16},{16,8},{9,17},{17,9},{10,18},{18,10},{11,19},{19,11},{12,20... | collective-permute-start | bytes 49160 | tf_op jit(solution)/shard_map/ppermute | solution.py:27
  46.0 0.0 collective-permute-done.5.refs_8_
  46.0 1.7 %collective-permute-done.6.refs_9_ = f32[4,1024]{1,0:T(4,128)S(1)} collective-permute-done((f32[4,1024]{1,0:T(4,128)S(1)}, f32[4,1024]{1,0:T(4,128)S(1)}, u32[]{:S(2)}, u32[]{:S(2)}) %collective-permute-start.6) | collective-permute-done | bytes 16416 | tf_op jit(solution)/shard_map/ppermute | solution.py:27
  47.7 5.4 %transport.2 = (bf16[2,1024,128]{2,1,0:T(8,128)(2,1)S(1)}, f32[4,1024]{1,0:T(4,128)S(1)}, bf16[4,16,128]{2,1,0:T(8,128)(2,1)S(1)}, bf16[4,16,128]{2,1,0:T(8,128)(2,1)S(1)}) custom-call(f32[4,2048]{1,0:T(4,128)S(1)} %get-tuple-element.30.refs_0_, bf16[4,1024,128]{2,1,0:T(8,128)(2,1)S(1)} %get-tuple-element.31.refs_1_, bf16[4,1024,128]{2,1,0:T(8,128)(2,1)S(1)} %copy-done.1, ...), custom_call_target="tpu_custom_call" | custom-call | flops 1073741824 | bytes 2097152 | tf_op jit(solution)/shard_map/transport/pallas_call | solution.py:47
  53.1 0.0 copy-start.2
  53.1 1.9 %collective-permute-start.10 = (bf16[2,1024,128]{2,1,0:T(8,128)(2,1)S(1)}, bf16[2,1024,128]{2,1,0:T(8,128)(2,1)S(1)}, u32[]{:S(2)}, u32[]{:S(2)}) collective-permute-start(bf16[2,1024,128]{2,1,0:T(8,128)(2,1)S(1)} %get-tuple-element.40.middle_in), channel_id=1, source_target_pairs={{1,0},{2,1},{3,2},{4,3},{5,4},{6,5},{7,6},{9,8},{10,9},{11,10},{12... | collective-permute-start | bytes 1572872 | tf_op jit(solution)/shard_map/ppermute | solution.py:20
  55.0 2.6 %collective-permute-start.7 = (bf16[2,1024,128]{2,1,0:T(8,128)(2,1)S(1)}, bf16[2,1024,128]{2,1,0:T(8,128)(2,1)S(1)}, u32[]{:S(2)}, u32[]{:S(2)}) collective-permute-start(bf16[2,1024,128]{2,1,0:T(8,128)(2,1)S(1)} %get-tuple-element.40.middle_in), channel_id=1, source_target_pairs={{0,1},{1,2},{2,3},{3,4},{4,5},{5,6},{6,7},{8,9},{9,10},{10,11},{11... | collective-permute-start | bytes 1572872 | tf_op jit(solution)/shard_map/ppermute | solution.py:20
  57.6 6.1 %transport.3 = (bf16[1,1024,128]{2,1,0:T(8,128)(2,1)S(1)}, bf16[1,1024,128]{2,1,0:T(8,128)(2,1)S(1)}, f32[4,1024]{1,0:T(4,128)}, bf16[4,16,128]{2,1,0:T(8,128)(2,1)S(1)}, bf16[4,16,128]{2,1,0:T(8,128)(2,1)S(1)}) custom-call(f32[4,2048]{1,0:T(4,128)S(1)} %get-tuple-element.30.refs_0_, bf16[4,1024,128]{2,1,0:T(8,128)(2,1)S(1)} %get-tuple-element.31.refs_1_, ...), custom_call_target="tpu_custom_call" | custom-call | flops 1073741824 | bytes 2097152 | tf_op jit(solution)/shard_map/transport/pallas_call | solution.py:47
  63.7 0.1 collective-permute-start.11
  63.8 3.9 %collective-permute-start.12 = (bf16[4,16,128]{2,1,0:T(8,128)(2,1)S(1)}, bf16[4,16,128]{2,1,0:T(8,128)(2,1)S(1)}, u32[]{:S(2)}, u32[]{:S(2)}) collective-permute-start(bf16[4,16,128]{2,1,0:T(8,128)(2,1)S(1)} %get-tuple-element.43), channel_id=1, source_target_pairs={{8,16},{16,8},{9,17},{17,9},{10,18},{18,10},{11,19},{19,11},{12,20... | collective-permute-start | bytes 49160 | tf_op jit(solution)/shard_map/ppermute | solution.py:27
  67.8 3.8 %collective-permute-start.9 = (bf16[1,1024,128]{2,1,0:T(8,128)(2,1)S(1)}, bf16[1,1024,128]{2,1,0:T(8,128)(2,1)S(1)}, u32[]{:S(2)}, u32[]{:S(2)}) collective-permute-start(bf16[1,1024,128]{2,1,0:T(8,128)(2,1)S(1)} %get-tuple-element.39.first_line_in), channel_id=1, source_target_pairs={{1,0},{2,1},{3,2},{4,3},{5,4},{6,5},{7,6},{9,8},{10,9},{11,10},{12... | collective-permute-start | bytes 786440 | tf_op jit(solution)/shard_map/ppermute | solution.py:20
  71.6 1.9 %collective-permute-start.8 = (bf16[1,1024,128]{2,1,0:T(8,128)(2,1)S(1)}, bf16[1,1024,128]{2,1,0:T(8,128)(2,1)S(1)}, u32[]{:S(2)}, u32[]{:S(2)}) collective-permute-start(bf16[1,1024,128]{2,1,0:T(8,128)(2,1)S(1)} %get-tuple-element.41.last_line_in), channel_id=1, source_target_pairs={{0,1},{1,2},{2,3},{3,4},{4,5},{5,6},{6,7},{8,9},{9,10},{10,11},{11... | collective-permute-start | bytes 786440 | tf_op jit(solution)/shard_map/ppermute | solution.py:20
  73.5 4.5 %collective-permute-start.14 = (bf16[3,32,128]{2,1,0:T(8,128)(2,1)S(1)}, bf16[3,32,128]{2,1,0:T(8,128)(2,1)S(1)}, u32[]{:S(2)}, u32[]{:S(2)}) collective-permute-start(bf16[3,32,128]{2,1,0:T(8,128)(2,1)S(1)} %get-tuple-element.48), channel_id=1, source_target_pairs={{1,0},{2,1},{3,2},{4,3},{5,4},{6,5},{7,6},{9,8},{10,9},{11,10},{12... | collective-permute-start | bytes 73736 | tf_op jit(solution)/shard_map/ppermute | solution.py:20
  78.1 1.5 %collective-permute-done.14.corner_bottom_in = bf16[3,32,128]{2,1,0:T(8,128)(2,1)S(1)} collective-permute-done((bf16[3,32,128]{2,1,0:T(8,128)(2,1)S(1)}, bf16[3,32,128]{2,1,0:T(8,128)(2,1)S(1)}, u32[]{:S(2)}, u32[]{:S(2)}) %collective-permute-start.14) | collective-permute-done | bytes 24608 | tf_op jit(solution)/shard_map/ppermute | solution.py:20
  79.6 2.0 %collective-permute-start.13 = (bf16[3,32,128]{2,1,0:T(8,128)(2,1)S(1)}, bf16[3,32,128]{2,1,0:T(8,128)(2,1)S(1)}, u32[]{:S(2)}, u32[]{:S(2)}) collective-permute-start(bf16[3,32,128]{2,1,0:T(8,128)(2,1)S(1)} %get-tuple-element.49), channel_id=1, source_target_pairs={{0,1},{1,2},{2,3},{3,4},{4,5},{5,6},{6,7},{8,9},{9,10},{10,11},{11... | collective-permute-start | bytes 73736 | tf_op jit(solution)/shard_map/ppermute | solution.py:20
  81.6 4.0 %collective-permute-done.13.corner_top_in = bf16[3,32,128]{2,1,0:T(8,128)(2,1)S(1)} collective-permute-done((bf16[3,32,128]{2,1,0:T(8,128)(2,1)S(1)}, bf16[3,32,128]{2,1,0:T(8,128)(2,1)S(1)}, u32[]{:S(2)}, u32[]{:S(2)}) %collective-permute-start.13) | collective-permute-done | bytes 24608 | tf_op jit(solution)/shard_map/ppermute | solution.py:20
  85.6 10.0 %conv_layers.1 = bf16[4,1024,128]{2,1,0:T(8,128)(2,1)} custom-call(bf16[1,1024,128]{2,1,0:T(8,128)(2,1)S(1)} %get-tuple-element.39.first_line_in, bf16[2,1024,128]{2,1,0:T(8,128)(2,1)S(1)} %get-tuple-element.40.middle_in, bf16[1,1024,128]{2,1,0:T(8,128)(2,1)S(1)} %get-tuple-element.41.last_line_in, ...), custom_call_target="tpu_custom_call" | custom-call | tf_op jit(solution)/shard_map/conv_layers/pallas_call | solution.py:47
  (18 shorter events, 0.1 us)
Async XLA Ops:
  0.6 7.4 %copy-start = (bf16[4,1024,128]{2,1,0:T(8,128)(2,1)S(1)}, bf16[4,1024,128]{2,1,0:T(8,128)(2,1)}, u32[]{:S(2)}) copy-start(bf16[4,1024,128]{2,1,0:T(8,128)(2,1)} %refs_3_.3) | copy-start | bytes 3145732
  0.6 4.9 %copy-start.1 = (bf16[4,1024,128]{2,1,0:T(8,128)(2,1)S(1)}, bf16[4,1024,128]{2,1,0:T(8,128)(2,1)}, u32[]{:S(2)}) copy-start(bf16[4,1024,128]{2,1,0:T(8,128)(2,1)} %refs_2_.3) | copy-start | bytes 3145732
  0.6 7.4 %copy-start.3 = (bf16[3,3,3,128,128]{4,3,2,1,0:T(8,128)(2,1)S(1)}, bf16[3,3,3,128,128]{4,3,2,1,0:T(8,128)(2,1)}, u32[]{:S(2)}) copy-start(bf16[3,3,3,128,128]{4,3,2,1,0:T(8,128)(2,1)} %weight_in.1) | copy-start | bytes 2654212
  2.1 16.7 %collective-permute-start.1 = (bf16[4,512,128]{2,1,0:T(8,128)(2,1)S(1)}, bf16[4,512,128]{2,1,0:T(8,128)(2,1)S(1)}, u32[]{:S(2)}, u32[]{:S(2)}) collective-permute-start(bf16[4,512,128]{2,1,0:T(8,128)(2,1)S(1)} %get-tuple-element.46), channel_id=1, source_target_pairs={{0,8},{8,16},{16,24},{1,9},{9,17},{17,25},{2,10},{10,18},{18,26},{... | collective-permute-start | bytes 1572872 | tf_op jit(solution)/shard_map/ppermute | solution.py:20
  5.6 16.7 %collective-permute-start.2 = (bf16[4,512,128]{2,1,0:T(8,128)(2,1)S(1)}, bf16[4,512,128]{2,1,0:T(8,128)(2,1)S(1)}, u32[]{:S(2)}, u32[]{:S(2)}) collective-permute-start(bf16[4,512,128]{2,1,0:T(8,128)(2,1)S(1)} %slice.17), channel_id=1, source_target_pairs={{8,0},{16,8},{24,16},{9,1},{17,9},{25,17},{10,2},{18,10},{26,18},{... | collective-permute-start | bytes 1572872 | tf_op jit(solution)/shard_map/ppermute | solution.py:20
  12.5 18.2 %collective-permute-start = (bf16[4,512,128]{2,1,0:T(8,128)(2,1)S(1)}, bf16[4,512,128]{2,1,0:T(8,128)(2,1)S(1)}, u32[]{:S(2)}, u32[]{:S(2)}) collective-permute-start(bf16[4,512,128]{2,1,0:T(8,128)(2,1)S(1)} %get-tuple-element.25), channel_id=1, source_target_pairs={{0,8},{8,16},{16,24},{1,9},{9,17},{17,25},{2,10},{10,18},{18,26},{... | collective-permute-start | bytes 1572872 | tf_op jit(solution)/shard_map/ppermute | solution.py:20
  25.5 5.1 %collective-permute-start.3 = (f32[8,1024]{1,0:T(8,128)S(1)}, f32[8,1024]{1,0:T(8,128)S(1)}, u32[]{:S(2)}, u32[]{:S(2)}) collective-permute-start(f32[8,1024]{1,0:T(8,128)S(1)} %get-tuple-element.28), channel_id=1, source_target_pairs={{0,8},{8,0},{16,24},{24,16},{1,9},{9,1},{17,25},{25,17},{2,10},{10... | collective-permute-start | bytes 98312 | tf_op jit(solution)/shard_map/ppermute | solution.py:27
  25.6 6.9 %collective-permute-start.4 = (f32[8,1024]{1,0:T(8,128)S(1)}, f32[8,1024]{1,0:T(8,128)S(1)}, u32[]{:S(2)}, u32[]{:S(2)}) collective-permute-start(f32[8,1024]{1,0:T(8,128)S(1)} %get-tuple-element.29), channel_id=1, source_target_pairs={{8,16},{16,8},{9,17},{17,9},{10,18},{18,10},{11,19},{19,11},{12,20... | collective-permute-start | bytes 98312 | tf_op jit(solution)/shard_map/ppermute | solution.py:27
  42.0 4.0 %collective-permute-start.5 = (f32[4,1024]{1,0:T(4,128)S(1)}, f32[4,1024]{1,0:T(4,128)S(1)}, u32[]{:S(2)}, u32[]{:S(2)}) collective-permute-start(f32[4,1024]{1,0:T(4,128)S(1)} %get-tuple-element.34), channel_id=1, source_target_pairs={{0,8},{8,0},{16,24},{24,16},{1,9},{9,1},{17,25},{25,17},{2,10},{10... | collective-permute-start | bytes 49160 | tf_op jit(solution)/shard_map/ppermute | solution.py:27
  42.1 5.6 %collective-permute-start.6 = (f32[4,1024]{1,0:T(4,128)S(1)}, f32[4,1024]{1,0:T(4,128)S(1)}, u32[]{:S(2)}, u32[]{:S(2)}) collective-permute-start(f32[4,1024]{1,0:T(4,128)S(1)} %get-tuple-element.35), channel_id=1, source_target_pairs={{8,16},{16,8},{9,17},{17,9},{10,18},{18,10},{11,19},{19,11},{12,20... | collective-permute-start | bytes 49160 | tf_op jit(solution)/shard_map/ppermute | solution.py:27
  53.1 32.6 %copy-start.2 = (f32[3,128]{1,0:T(4,128)S(1)}, f32[3,128]{1,0:T(4,128)}, u32[]{:S(2)}) copy-start(f32[3,128]{1,0:T(4,128)} %bias_in.1) | copy-start | bytes 4612
  53.1 32.5 %collective-permute-start.10 = (bf16[2,1024,128]{2,1,0:T(8,128)(2,1)S(1)}, bf16[2,1024,128]{2,1,0:T(8,128)(2,1)S(1)}, u32[]{:S(2)}, u32[]{:S(2)}) collective-permute-start(bf16[2,1024,128]{2,1,0:T(8,128)(2,1)S(1)} %get-tuple-element.40.middle_in), channel_id=1, source_target_pairs={{1,0},{2,1},{3,2},{4,3},{5,4},{6,5},{7,6},{9,8},{10,9},{11,10},{12... | collective-permute-start | bytes 1572872 | tf_op jit(solution)/shard_map/ppermute | solution.py:20
  55.0 30.6 %collective-permute-start.7 = (bf16[2,1024,128]{2,1,0:T(8,128)(2,1)S(1)}, bf16[2,1024,128]{2,1,0:T(8,128)(2,1)S(1)}, u32[]{:S(2)}, u32[]{:S(2)}) collective-permute-start(bf16[2,1024,128]{2,1,0:T(8,128)(2,1)S(1)} %get-tuple-element.40.middle_in), channel_id=1, source_target_pairs={{0,1},{1,2},{2,3},{3,4},{4,5},{5,6},{6,7},{8,9},{9,10},{10,11},{11... | collective-permute-start | bytes 1572872 | tf_op jit(solution)/shard_map/ppermute | solution.py:20
  63.7 7.8 %collective-permute-start.11 = (bf16[4,16,128]{2,1,0:T(8,128)(2,1)S(1)}, bf16[4,16,128]{2,1,0:T(8,128)(2,1)S(1)}, u32[]{:S(2)}, u32[]{:S(2)}) collective-permute-start(bf16[4,16,128]{2,1,0:T(8,128)(2,1)S(1)} %get-tuple-element.42), channel_id=1, source_target_pairs={{0,8},{8,0},{16,24},{24,16},{1,9},{9,1},{17,25},{25,17},{2,10},{10... | collective-permute-start | bytes 49160 | tf_op jit(solution)/shard_map/ppermute | solution.py:27
  63.8 9.7 %collective-permute-start.12 = (bf16[4,16,128]{2,1,0:T(8,128)(2,1)S(1)}, bf16[4,16,128]{2,1,0:T(8,128)(2,1)S(1)}, u32[]{:S(2)}, u32[]{:S(2)}) collective-permute-start(bf16[4,16,128]{2,1,0:T(8,128)(2,1)S(1)} %get-tuple-element.43), channel_id=1, source_target_pairs={{8,16},{16,8},{9,17},{17,9},{10,18},{18,10},{11,19},{19,11},{12,20... | collective-permute-start | bytes 49160 | tf_op jit(solution)/shard_map/ppermute | solution.py:27
  67.8 17.9 %collective-permute-start.9 = (bf16[1,1024,128]{2,1,0:T(8,128)(2,1)S(1)}, bf16[1,1024,128]{2,1,0:T(8,128)(2,1)S(1)}, u32[]{:S(2)}, u32[]{:S(2)}) collective-permute-start(bf16[1,1024,128]{2,1,0:T(8,128)(2,1)S(1)} %get-tuple-element.39.first_line_in), channel_id=1, source_target_pairs={{1,0},{2,1},{3,2},{4,3},{5,4},{6,5},{7,6},{9,8},{10,9},{11,10},{12... | collective-permute-start | bytes 786440 | tf_op jit(solution)/shard_map/ppermute | solution.py:20
  71.6 14.1 %collective-permute-start.8 = (bf16[1,1024,128]{2,1,0:T(8,128)(2,1)S(1)}, bf16[1,1024,128]{2,1,0:T(8,128)(2,1)S(1)}, u32[]{:S(2)}, u32[]{:S(2)}) collective-permute-start(bf16[1,1024,128]{2,1,0:T(8,128)(2,1)S(1)} %get-tuple-element.41.last_line_in), channel_id=1, source_target_pairs={{0,1},{1,2},{2,3},{3,4},{4,5},{5,6},{6,7},{8,9},{9,10},{10,11},{11... | collective-permute-start | bytes 786440 | tf_op jit(solution)/shard_map/ppermute | solution.py:20
  73.5 6.0 %collective-permute-start.14 = (bf16[3,32,128]{2,1,0:T(8,128)(2,1)S(1)}, bf16[3,32,128]{2,1,0:T(8,128)(2,1)S(1)}, u32[]{:S(2)}, u32[]{:S(2)}) collective-permute-start(bf16[3,32,128]{2,1,0:T(8,128)(2,1)S(1)} %get-tuple-element.48), channel_id=1, source_target_pairs={{1,0},{2,1},{3,2},{4,3},{5,4},{6,5},{7,6},{9,8},{10,9},{11,10},{12... | collective-permute-start | bytes 73736 | tf_op jit(solution)/shard_map/ppermute | solution.py:20
  79.6 6.0 %collective-permute-start.13 = (bf16[3,32,128]{2,1,0:T(8,128)(2,1)S(1)}, bf16[3,32,128]{2,1,0:T(8,128)(2,1)S(1)}, u32[]{:S(2)}, u32[]{:S(2)}) collective-permute-start(bf16[3,32,128]{2,1,0:T(8,128)(2,1)S(1)} %get-tuple-element.49), channel_id=1, source_target_pairs={{0,1},{1,2},{2,3},{3,4},{4,5},{5,6},{6,7},{8,9},{9,10},{10,11},{11... | collective-permute-start | bytes 73736 | tf_op jit(solution)/shard_map/ppermute | solution.py:20

commit v9 on v7

--- a/solution.py
+++ b/solution.py
@@ -387,6 +387,7 @@
     raw,
     line_sems,
     sems,
+    lane_sems,
 ):
     lines_here, seg_len, channels = left.shape
     half = prev_low_in.shape[1]
@@ -459,6 +460,7 @@
                     lanes[line, first + row : first + row + strip] = marked.astype(jnp.bfloat16)
                 sums[:, first : first + window] += column_sum
         totals = jnp.sum(sums[...], axis=0, keepdims=True)
+        begin_copies(line_copies(((lanes, lanes_out),), lane_sems, line, lines_here))
         prev_sum[pl.ds(line, 1), :] = totals[:, :seg_len]
         own_sum[pl.ds(line, 1), :] = totals[:, seg_len:]
         return carry
@@ -472,12 +474,13 @@
             (own_sum, own_out),
             (prev_sum, prev_out),
             (pot, pot_out),
-            (lanes, lanes_out),
         ),
         sems,
     )
     begin_copies(sends)
     wait(sends)
+    for line in range(lines_here):
+        wait(line_copies(((lanes, lanes_out),), lane_sems, line, lines_here))
 
 
 def row_pass(left, right, prev_low, prev_high, own, back, first, second, block):
@@ -500,7 +503,7 @@
             ((8, 2 * seg_len), f32),
             ((2, 2 * block, seg_len + 2 * block), f32),
         ),
-        (4 * lines_here, 6),
+        (4 * lines_here, 5, lines_here),
         "row_pass",
     )
 
@@ -746,7 +749,7 @@
     f32 = jnp.float32
     wait(fetches[:1])
     first_image[layers:after, EDGE:right] = state_ref[...].astype(f32)
-    wait(fetches[1:])
+    wait(fetches[1:-2])
     first_image[:layers, EDGE:right] = top_ref[...].astype(f32)
     first_image[after:, EDGE:right] = bottom_ref[...].astype(f32)
     for rows, first_px, second_px in (
@@ -757,6 +760,7 @@
         following, before = by_parity(first_px.astype(f32), second_px.astype(f32))
         first_image[rows, :EDGE] = before
         first_image[rows, right:] = following
+    wait(fetches[-2:])
     line0 = lax.axis_index("lines") * lines_here - layers
     all_lines = lax.axis_size("lines") * lines_here
     px0 = lax.axis_index("seg") * seg_len - EDGE

time: 92.2 us -> 92.4 us (level)
  no operation moved by 1% of the time
where the time goes in v9:
time: 92.4 us; the launch traced here: 92.1 us
  Pallas kernels  41.1 us (44%)
  starting transfers between devices  33.2 us (36%)
  waiting for transfers between devices  15.2 us (16%)
  local copies, waits for them, and re-layouts  1.5 us (2%)
  between operations  1.02 us (1%)
    pallas_call x6, Pallas kernels, kernel_call(): pl.pallas_call(kernel, in_specs=[ANYWHERE] * len(operands), out_specs=[AN...  41.1 us
    ppermute x7, starting transfers between devices, shifted(): return lax.ppermute(block, axis, route)  25.7 us
    ppermute x7, waiting for transfers between devices, shifted(): return lax.ppermute(block, axis, route)  8.05 us
    ppermute x6, starting transfers between devices, exchanged(): return lax.ppermute(block, axis, route)  7.47 us
    ppermute x6, waiting for transfers between devices, exchanged(): return lax.ppermute(block, axis, route)  7.18 us
  transfers between devices with their start and end apart: 13, of which 8 were waited for; matrix products, arithmetic and copies ran while one was open for 0% of the time, Pallas kernels for 12%

profile of v9, /device:TPU:19, one launch (start us, length us, event | category | flops | bytes accessed | tf_op | source)
XLA Modules:
  0.0 92.1 jit_solution(2952671218413448987)
XLA Ops:
  0.7 1.4 %fusion = (bf16[4,512,128]{2,1,0:T(8,128)(2,1)S(1)}, bf16[4,512,128]{2,1,0:T(8,128)(2,1)S(1)}) fusion(bf16[4,1024,128]{2,1,0:T(8,128)(2,1)} %right_in.7), kind=kLoop, calls=%fused_computation.2 | loop fusion | bytes 2097152 | tf_op jit(solution)/shard_map/slice | solution.py:832
  2.1 3.2 %collective-permute-start.1 = (bf16[4,512,128]{2,1,0:T(8,128)(2,1)S(1)}, bf16[4,512,128]{2,1,0:T(8,128)(2,1)S(1)}, u32[]{:S(2)}, u32[]{:S(2)}) collective-permute-start(bf16[4,512,128]{2,1,0:T(8,128)(2,1)S(1)} %get-tuple-element.40), channel_id=1, source_target_pairs={{0,8},{8,16},{16,24},{1,9},{9,17},{17,25},{2,10},{10,18},{18,26},{... | collective-permute-start | bytes 1572872 | tf_op jit(solution)/shard_map/ppermute | solution.py:20
  5.4 2.1 %collective-permute-start.2 = (bf16[4,512,128]{2,1,0:T(8,128)(2,1)S(1)}, bf16[4,512,128]{2,1,0:T(8,128)(2,1)S(1)}, u32[]{:S(2)}, u32[]{:S(2)}) collective-permute-start(bf16[4,512,128]{2,1,0:T(8,128)(2,1)S(1)} %slice.17), channel_id=1, source_target_pairs={{8,0},{16,8},{24,16},{9,1},{17,9},{25,17},{10,2},{18,10},{26,18},{... | collective-permute-start | bytes 1572872 | tf_op jit(solution)/shard_map/ppermute | solution.py:20
  7.5 4.4 %column_own.1 = (bf16[3,1536,256]{2,1,0:T(8,128)(2,1)S(1)}, f32[8,1024]{1,0:T(8,128)S(1)}) custom-call(bf16[4,1024,128]{2,1,0:T(8,128)(2,1)S(1)} %copy-done.1, bf16[4,1024,128]{2,1,0:T(8,128)(2,1)S(1)} %copy-done, bf16[3,3,3,128,128]{4,3,2,1,0:T(8,128)(2,1)S(1)} %copy-done.3), custom_call_target="tpu_custom_call" | custom-call | flops 1073741824 | bytes 4194304 | tf_op jit(solution)/shard_map/column_own/pallas_call | solution.py:47
  11.9 3.2 %collective-permute-start = (bf16[4,512,128]{2,1,0:T(8,128)(2,1)S(1)}, bf16[4,512,128]{2,1,0:T(8,128)(2,1)S(1)}, u32[]{:S(2)}, u32[]{:S(2)}) collective-permute-start(bf16[4,512,128]{2,1,0:T(8,128)(2,1)S(1)} %get-tuple-element.22), channel_id=1, source_target_pairs={{0,8},{8,16},{16,24},{1,9},{9,17},{17,25},{2,10},{10,18},{18,26},{... | collective-permute-start | bytes 1572872 | tf_op jit(solution)/shard_map/ppermute | solution.py:20
  15.2 1.6 %collective-permute-done.1.prev_in.prev_high_in = bf16[4,512,128]{2,1,0:T(8,128)(2,1)S(1)} collective-permute-done((bf16[4,512,128]{2,1,0:T(8,128)(2,1)S(1)}, bf16[4,512,128]{2,1,0:T(8,128)(2,1)S(1)}, u32[]{:S(2)}, u32[]{:S(2)}) %collective-permute-start.1) | collective-permute-done | bytes 524320 | tf_op jit(solution)/shard_map/ppermute | solution.py:20
  16.8 3.5 %column_cross.1.back_in = f32[8,1024]{1,0:T(8,128)S(1)} custom-call(bf16[4,1024,128]{2,1,0:T(8,128)(2,1)S(1)} %copy-done.1, bf16[4,512,128]{2,1,0:T(8,128)(2,1)S(1)} %collective-permute-done.1.prev_in.prev_high_in), custom_call_target="tpu_custom_call" | custom-call | flops 1073741824 | bytes 4194304 | tf_op jit(solution)/shard_map/column_cross/pallas_call | solution.py:47
  20.3 0.0 collective-permute-done.2.next_in
  20.3 3.2 %column_next.1 = (f32[8,1024]{1,0:T(8,128)S(1)}, f32[8,1024]{1,0:T(8,128)S(1)}, f32[8,1024]{1,0:T(8,128)S(1)}) custom-call(bf16[4,512,128]{2,1,0:T(8,128)(2,1)S(1)} %collective-permute-done.2.next_in, bf16[4,1024,128]{2,1,0:T(8,128)(2,1)S(1)} %copy-done, f32[8,1024]{1,0:T(8,128)S(1)} %get-tuple-element.23.own_in, f32[8,1024]{1,0:T(8,128)S(1)} %column_cross.1.back_in), custom_call_target="tpu_custom_call" | custom-call | flops 268435456 | bytes 2097152 | tf_op jit(solution)/shard_map/column_next/pallas_call | solution.py:47
  23.5 1.4 %collective-permute-start.3 = (f32[8,1024]{1,0:T(8,128)S(1)}, f32[8,1024]{1,0:T(8,128)S(1)}, u32[]{:S(2)}, u32[]{:S(2)}) collective-permute-start(f32[8,1024]{1,0:T(8,128)S(1)} %get-tuple-element.25), channel_id=1, source_target_pairs={{0,8},{8,0},{16,24},{24,16},{1,9},{9,1},{17,25},{25,17},{2,10},{10... | collective-permute-start | bytes 98312 | tf_op jit(solution)/shard_map/ppermute | solution.py:27
  24.9 1.9 %collective-permute-start.4 = (f32[8,1024]{1,0:T(8,128)S(1)}, f32[8,1024]{1,0:T(8,128)S(1)}, u32[]{:S(2)}, u32[]{:S(2)}) collective-permute-start(f32[8,1024]{1,0:T(8,128)S(1)} %get-tuple-element.26), channel_id=1, source_target_pairs={{8,16},{16,8},{9,17},{17,9},{10,18},{18,10},{11,19},{19,11},{12,20... | collective-permute-start | bytes 98312 | tf_op jit(solution)/shard_map/ppermute | solution.py:27
  26.8 1.2 %collective-permute-done.prev_low_in = bf16[4,512,128]{2,1,0:T(8,128)(2,1)S(1)} collective-permute-done((bf16[4,512,128]{2,1,0:T(8,128)(2,1)S(1)}, bf16[4,512,128]{2,1,0:T(8,128)(2,1)S(1)}, u32[]{:S(2)}, u32[]{:S(2)}) %collective-permute-start) | collective-permute-done | bytes 524320 | tf_op jit(solution)/shard_map/ppermute | solution.py:20
  28.0 0.0 collective-permute-done.3.first_in
  28.0 1.8 %collective-permute-done.4.second_in = f32[8,1024]{1,0:T(8,128)S(1)} collective-permute-done((f32[8,1024]{1,0:T(8,128)S(1)}, f32[8,1024]{1,0:T(8,128)S(1)}, u32[]{:S(2)}, u32[]{:S(2)}) %collective-permute-start.4) | collective-permute-done | bytes 32800 | tf_op jit(solution)/shard_map/ppermute | solution.py:27
  29.8 9.5 %row_pass.1 = (f32[4,2048]{1,0:T(4,128)S(1)}, bf16[4,1024,128]{2,1,0:T(8,128)(2,1)S(1)}, f32[4,1024]{1,0:T(4,128)S(1)}, f32[4,1024]{1,0:T(4,128)S(1)}, f32[4,1024]{1,0:T(4,128)S(1)}, /*index=5*/f32[4,1024]{1,0:T(4,128)S(1)}) custom-call(bf16[4,1024,128]{2,1,0:T(8,128)(2,1)S(1)} %copy-done.1, bf16[4,1024,128]{2,1,0:T(8,128)(2,1)S(1)} %copy-done, ...), custom_call_target="tpu_custom_call" | custom-call | tf_op jit(solution)/shard_map/row_pass/pallas_call | solution.py:47
  39.3 0.0 copy-start.2
  39.3 0.3 collective-permute-start.5
  39.6 1.9 %collective-permute-start.6 = (f32[4,1024]{1,0:T(4,128)S(1)}, f32[4,1024]{1,0:T(4,128)S(1)}, u32[]{:S(2)}, u32[]{:S(2)}) collective-permute-start(f32[4,1024]{1,0:T(4,128)S(1)} %get-tuple-element.32), channel_id=1, source_target_pairs={{8,16},{16,8},{9,17},{17,9},{10,18},{18,10},{11,19},{19,11},{12,20... | collective-permute-start | bytes 49160 | tf_op jit(solution)/shard_map/ppermute | solution.py:27
  41.5 0.4 collective-permute-done.5.first_in
  42.0 2.1 %collective-permute-done.6.second_in = f32[4,1024]{1,0:T(4,128)S(1)} collective-permute-done((f32[4,1024]{1,0:T(4,128)S(1)}, f32[4,1024]{1,0:T(4,128)S(1)}, u32[]{:S(2)}, u32[]{:S(2)}) %collective-permute-start.6) | collective-permute-done | bytes 16416 | tf_op jit(solution)/shard_map/ppermute | solution.py:27
  44.1 10.3 %transport.1 = (bf16[4,1024,128]{2,1,0:T(8,128)(2,1)S(1)}, f32[4,1024]{1,0:T(4,128)}, bf16[3,1024,128]{2,1,0:T(8,128)(2,1)S(1)}, bf16[3,1024,128]{2,1,0:T(8,128)...) custom-call(f32[4,2048]{1,0:T(4,128)S(1)} %get-tuple-element.27.pot_in, ...), custom_call_target="tpu_custom_call" | custom-call | tf_op jit(solution)/shard_map/transport/pallas_call | solution.py:47
  54.4 7.8 %collective-permute-start.7 = (bf16[3,1024,128]{2,1,0:T(8,128)(2,1)S(1)}, bf16[3,1024,128]{2,1,0:T(8,128)(2,1)S(1)}, u32[]{:S(2)}, u32[]{:S(2)}) collective-permute-start(bf16[3,1024,128]{2,1,0:T(8,128)(2,1)S(1)} %get-tuple-element.34), channel_id=1, source_target_pairs={{0,1},{1,2},{2,3},{3,4},{4,5},{5,6},{6,7},{8,9},{9,10},{10,11},{11... | collective-permute-start | bytes 2359304 | tf_op jit(solution)/shard_map/ppermute | solution.py:20
  62.2 1.9 %collective-permute-start.8 = (bf16[3,1024,128]{2,1,0:T(8,128)(2,1)S(1)}, bf16[3,1024,128]{2,1,0:T(8,128)(2,1)S(1)}, u32[]{:S(2)}, u32[]{:S(2)}) collective-permute-start(bf16[3,1024,128]{2,1,0:T(8,128)(2,1)S(1)} %get-tuple-element.35), channel_id=1, source_target_pairs={{1,0},{2,1},{3,2},{4,3},{5,4},{6,5},{7,6},{9,8},{10,9},{11,10},{12... | collective-permute-start | bytes 2359304 | tf_op jit(solution)/shard_map/ppermute | solution.py:20
  64.1 0.1 collective-permute-start.9
  64.2 1.9 %collective-permute-start.10 = (bf16[4,16,128]{2,1,0:T(8,128)(2,1)S(1)}, bf16[4,16,128]{2,1,0:T(8,128)(2,1)S(1)}, u32[]{:S(2)}, u32[]{:S(2)}) collective-permute-start(bf16[4,16,128]{2,1,0:T(8,128)(2,1)S(1)} %get-tuple-element.37), channel_id=1, source_target_pairs={{8,16},{16,8},{9,17},{17,9},{10,18},{18,10},{11,19},{19,11},{12,20... | collective-permute-start | bytes 49160 | tf_op jit(solution)/shard_map/ppermute | solution.py:27
  66.1 0.9 %collective-permute-done.9.first_in = bf16[4,16,128]{2,1,0:T(8,128)(2,1)S(1)} collective-permute-done((bf16[4,16,128]{2,1,0:T(8,128)(2,1)S(1)}, bf16[4,16,128]{2,1,0:T(8,128)(2,1)S(1)}, u32[]{:S(2)}, u32[]{:S(2)}) %collective-permute-start.9) | collective-permute-done | bytes 16416 | tf_op jit(solution)/shard_map/ppermute | solution.py:27
  67.1 1.9 %collective-permute-done.10.second_in = bf16[4,16,128]{2,1,0:T(8,128)(2,1)S(1)} collective-permute-done((bf16[4,16,128]{2,1,0:T(8,128)(2,1)S(1)}, bf16[4,16,128]{2,1,0:T(8,128)(2,1)S(1)}, u32[]{:S(2)}, u32[]{:S(2)}) %collective-permute-start.10) | collective-permute-done | bytes 16416 | tf_op jit(solution)/shard_map/ppermute | solution.py:27
  69.0 3.4 %collective-permute-start.12 = (bf16[3,32,128]{2,1,0:T(8,128)(2,1)S(1)}, bf16[3,32,128]{2,1,0:T(8,128)(2,1)S(1)}, u32[]{:S(2)}, u32[]{:S(2)}) collective-permute-start(bf16[3,32,128]{2,1,0:T(8,128)(2,1)S(1)} %get-tuple-element.42), channel_id=1, source_target_pairs={{1,0},{2,1},{3,2},{4,3},{5,4},{6,5},{7,6},{9,8},{10,9},{11,10},{12... | collective-permute-start | bytes 73736 | tf_op jit(solution)/shard_map/ppermute | solution.py:20
  72.4 4.1 %collective-permute-start.11 = (bf16[3,32,128]{2,1,0:T(8,128)(2,1)S(1)}, bf16[3,32,128]{2,1,0:T(8,128)(2,1)S(1)}, u32[]{:S(2)}, u32[]{:S(2)}) collective-permute-start(bf16[3,32,128]{2,1,0:T(8,128)(2,1)S(1)} %get-tuple-element.43), channel_id=1, source_target_pairs={{0,1},{1,2},{2,3},{3,4},{4,5},{5,6},{6,7},{8,9},{9,10},{10,11},{11... | collective-permute-start | bytes 73736 | tf_op jit(solution)/shard_map/ppermute | solution.py:20
  76.5 5.2 %collective-permute-done.12.corner_bottom_in = bf16[3,32,128]{2,1,0:T(8,128)(2,1)S(1)} collective-permute-done((bf16[3,32,128]{2,1,0:T(8,128)(2,1)S(1)}, bf16[3,32,128]{2,1,0:T(8,128)(2,1)S(1)}, u32[]{:S(2)}, u32[]{:S(2)}) %collective-permute-start.12) | collective-permute-done | bytes 24608 | tf_op jit(solution)/shard_map/ppermute | solution.py:20
  81.7 0.0 collective-permute-done.8.bottom_in
  81.7 10.2 %conv_layers.1 = bf16[4,1024,128]{2,1,0:T(8,128)(2,1)} custom-call(bf16[4,1024,128]{2,1,0:T(8,128)(2,1)S(1)} %get-tuple-element.33.state_in, bf16[3,1024,128]{2,1,0:T(8,128)(2,1)S(1)} %collective-permute-done.7.top_in, bf16[3,1024,128]{2,1,0:T(8,128)(2,1)S(1)} %collective-permute-done.8.bottom_in, bf16[4,16,128]{2,1,0:T(8,128)(2,1)S(1)} %collective-permute-done.9.first_in, ...), custom_call_target="tpu_custom_call" | custom-call | tf_op jit(solution)/shard_map/conv_layers/pallas_call | solution.py:47
  (13 shorter events, 0.1 us)
Async XLA Ops:
  0.6 6.8 %copy-start = (bf16[4,1024,128]{2,1,0:T(8,128)(2,1)S(1)}, bf16[4,1024,128]{2,1,0:T(8,128)(2,1)}, u32[]{:S(2)}) copy-start(bf16[4,1024,128]{2,1,0:T(8,128)(2,1)} %right_in.7) | copy-start | bytes 3145732
  0.6 4.7 %copy-start.1 = (bf16[4,1024,128]{2,1,0:T(8,128)(2,1)S(1)}, bf16[4,1024,128]{2,1,0:T(8,128)(2,1)}, u32[]{:S(2)}) copy-start(bf16[4,1024,128]{2,1,0:T(8,128)(2,1)} %left_in.7) | copy-start | bytes 3145732
  0.6 6.8 %copy-start.3 = (bf16[3,3,3,128,128]{4,3,2,1,0:T(8,128)(2,1)S(1)}, bf16[3,3,3,128,128]{4,3,2,1,0:T(8,128)(2,1)}, u32[]{:S(2)}) copy-start(bf16[3,3,3,128,128]{4,3,2,1,0:T(8,128)(2,1)} %weight_in.1) | copy-start | bytes 2654212
  2.1 14.7 %collective-permute-start.1 = (bf16[4,512,128]{2,1,0:T(8,128)(2,1)S(1)}, bf16[4,512,128]{2,1,0:T(8,128)(2,1)S(1)}, u32[]{:S(2)}, u32[]{:S(2)}) collective-permute-start(bf16[4,512,128]{2,1,0:T(8,128)(2,1)S(1)} %get-tuple-element.40), channel_id=1, source_target_pairs={{0,8},{8,16},{16,24},{1,9},{9,17},{17,25},{2,10},{10,18},{18,26},{... | collective-permute-start | bytes 1572872 | tf_op jit(solution)/shard_map/ppermute | solution.py:20
  5.4 14.9 %collective-permute-start.2 = (bf16[4,512,128]{2,1,0:T(8,128)(2,1)S(1)}, bf16[4,512,128]{2,1,0:T(8,128)(2,1)S(1)}, u32[]{:S(2)}, u32[]{:S(2)}) collective-permute-start(bf16[4,512,128]{2,1,0:T(8,128)(2,1)S(1)} %slice.17), channel_id=1, source_target_pairs={{8,0},{16,8},{24,16},{9,1},{17,9},{25,17},{10,2},{18,10},{26,18},{... | collective-permute-start | bytes 1572872 | tf_op jit(solution)/shard_map/ppermute | solution.py:20
  11.9 16.1 %collective-permute-start = (bf16[4,512,128]{2,1,0:T(8,128)(2,1)S(1)}, bf16[4,512,128]{2,1,0:T(8,128)(2,1)S(1)}, u32[]{:S(2)}, u32[]{:S(2)}) collective-permute-start(bf16[4,512,128]{2,1,0:T(8,128)(2,1)S(1)} %get-tuple-element.22), channel_id=1, source_target_pairs={{0,8},{8,16},{16,24},{1,9},{9,17},{17,25},{2,10},{10,18},{18,26},{... | collective-permute-start | bytes 1572872 | tf_op jit(solution)/shard_map/ppermute | solution.py:20
  23.5 4.5 %collective-permute-start.3 = (f32[8,1024]{1,0:T(8,128)S(1)}, f32[8,1024]{1,0:T(8,128)S(1)}, u32[]{:S(2)}, u32[]{:S(2)}) collective-permute-start(f32[8,1024]{1,0:T(8,128)S(1)} %get-tuple-element.25), channel_id=1, source_target_pairs={{0,8},{8,0},{16,24},{24,16},{1,9},{9,1},{17,25},{25,17},{2,10},{10... | collective-permute-start | bytes 98312 | tf_op jit(solution)/shard_map/ppermute | solution.py:27
  24.9 4.9 %collective-permute-start.4 = (f32[8,1024]{1,0:T(8,128)S(1)}, f32[8,1024]{1,0:T(8,128)S(1)}, u32[]{:S(2)}, u32[]{:S(2)}) collective-permute-start(f32[8,1024]{1,0:T(8,128)S(1)} %get-tuple-element.26), channel_id=1, source_target_pairs={{8,16},{16,8},{9,17},{17,9},{10,18},{18,10},{11,19},{19,11},{12,20... | collective-permute-start | bytes 98312 | tf_op jit(solution)/shard_map/ppermute | solution.py:27
  39.3 42.4 %copy-start.2 = (f32[3,128]{1,0:T(4,128)S(1)}, f32[3,128]{1,0:T(4,128)}, u32[]{:S(2)}) copy-start(f32[3,128]{1,0:T(4,128)} %bias_in.1) | copy-start | bytes 4612
  39.3 2.7 %collective-permute-start.5 = (f32[4,1024]{1,0:T(4,128)S(1)}, f32[4,1024]{1,0:T(4,128)S(1)}, u32[]{:S(2)}, u32[]{:S(2)}) collective-permute-start(f32[4,1024]{1,0:T(4,128)S(1)} %get-tuple-element.31), channel_id=1, source_target_pairs={{0,8},{8,0},{16,24},{24,16},{1,9},{9,1},{17,25},{25,17},{2,10},{10... | collective-permute-start | bytes 49160 | tf_op jit(solution)/shard_map/ppermute | solution.py:27
  39.6 4.5 %collective-permute-start.6 = (f32[4,1024]{1,0:T(4,128)S(1)}, f32[4,1024]{1,0:T(4,128)S(1)}, u32[]{:S(2)}, u32[]{:S(2)}) collective-permute-start(f32[4,1024]{1,0:T(4,128)S(1)} %get-tuple-element.32), channel_id=1, source_target_pairs={{8,16},{16,8},{9,17},{17,9},{10,18},{18,10},{11,19},{19,11},{12,20... | collective-permute-start | bytes 49160 | tf_op jit(solution)/shard_map/ppermute | solution.py:27
  54.4 27.3 %collective-permute-start.7 = (bf16[3,1024,128]{2,1,0:T(8,128)(2,1)S(1)}, bf16[3,1024,128]{2,1,0:T(8,128)(2,1)S(1)}, u32[]{:S(2)}, u32[]{:S(2)}) collective-permute-start(bf16[3,1024,128]{2,1,0:T(8,128)(2,1)S(1)} %get-tuple-element.34), channel_id=1, source_target_pairs={{0,1},{1,2},{2,3},{3,4},{4,5},{5,6},{6,7},{8,9},{9,10},{10,11},{11... | collective-permute-start | bytes 2359304 | tf_op jit(solution)/shard_map/ppermute | solution.py:20
  62.2 19.5 %collective-permute-start.8 = (bf16[3,1024,128]{2,1,0:T(8,128)(2,1)S(1)}, bf16[3,1024,128]{2,1,0:T(8,128)(2,1)S(1)}, u32[]{:S(2)}, u32[]{:S(2)}) collective-permute-start(bf16[3,1024,128]{2,1,0:T(8,128)(2,1)S(1)} %get-tuple-element.35), channel_id=1, source_target_pairs={{1,0},{2,1},{3,2},{4,3},{5,4},{6,5},{7,6},{9,8},{10,9},{11,10},{12... | collective-permute-start | bytes 2359304 | tf_op jit(solution)/shard_map/ppermute | solution.py:20
  64.1 2.9 %collective-permute-start.9 = (bf16[4,16,128]{2,1,0:T(8,128)(2,1)S(1)}, bf16[4,16,128]{2,1,0:T(8,128)(2,1)S(1)}, u32[]{:S(2)}, u32[]{:S(2)}) collective-permute-start(bf16[4,16,128]{2,1,0:T(8,128)(2,1)S(1)} %get-tuple-element.36), channel_id=1, source_target_pairs={{0,8},{8,0},{16,24},{24,16},{1,9},{9,1},{17,25},{25,17},{2,10},{10... | collective-permute-start | bytes 49160 | tf_op jit(solution)/shard_map/ppermute | solution.py:27
  64.2 4.8 %collective-permute-start.10 = (bf16[4,16,128]{2,1,0:T(8,128)(2,1)S(1)}, bf16[4,16,128]{2,1,0:T(8,128)(2,1)S(1)}, u32[]{:S(2)}, u32[]{:S(2)}) collective-permute-start(bf16[4,16,128]{2,1,0:T(8,128)(2,1)S(1)} %get-tuple-element.37), channel_id=1, source_target_pairs={{8,16},{16,8},{9,17},{17,9},{10,18},{18,10},{11,19},{19,11},{12,20... | collective-permute-start | bytes 49160 | tf_op jit(solution)/shard_map/ppermute | solution.py:27
  69.0 12.7 %collective-permute-start.12 = (bf16[3,32,128]{2,1,0:T(8,128)(2,1)S(1)}, bf16[3,32,128]{2,1,0:T(8,128)(2,1)S(1)}, u32[]{:S(2)}, u32[]{:S(2)}) collective-permute-start(bf16[3,32,128]{2,1,0:T(8,128)(2,1)S(1)} %get-tuple-element.42), channel_id=1, source_target_pairs={{1,0},{2,1},{3,2},{4,3},{5,4},{6,5},{7,6},{9,8},{10,9},{11,10},{12... | collective-permute-start | bytes 73736 | tf_op jit(solution)/shard_map/ppermute | solution.py:20
  72.4 9.3 %collective-permute-start.11 = (bf16[3,32,128]{2,1,0:T(8,128)(2,1)S(1)}, bf16[3,32,128]{2,1,0:T(8,128)(2,1)S(1)}, u32[]{:S(2)}, u32[]{:S(2)}) collective-permute-start(bf16[3,32,128]{2,1,0:T(8,128)(2,1)S(1)} %get-tuple-element.43), channel_id=1, source_target_pairs={{0,1},{1,2},{2,3},{3,4},{4,5},{5,6},{6,7},{8,9},{9,10},{10,11},{11... | collective-permute-start | bytes 73736 | tf_op jit(solution)/shard_map/ppermute | solution.py:20

commit v10 on v9

--- a/solution.py
+++ b/solution.py
@@ -832,8 +832,8 @@
     prev_high = shifted(right_features[:, half:], "seg", 1)
     next_low = shifted(left_features[:, :half], "seg", -1)
     stacked, own = own_partials(left_features, right_features, conv_weight)
-    right_low, own = lax.optimization_barrier((right_features[:, :half], own))
-    prev_low = shifted(right_low, "seg", 1)
+    right_later, own = lax.optimization_barrier((right_features, own))
+    prev_low = shifted(right_later[:, :half], "seg", 1)
     back = cross_partials(left_features, prev_high)
     own, first, second = next_partials(next_low, right_features, own, back)
     first = exchanged(first, "seg", 0)

time: 92.4 us -> 93.9 us (1.016)
  local copies, waits for them, and re-layouts: 1.5 us -> 5.84 us
  starting transfers between devices: 33.2 us -> 31.5 us
  waiting for transfers between devices: 15.2 us -> 13.9 us
    unnamed x9 -> x11, local copies, waits for them, and re-layouts: 0.02 us -> 3.63 us
    ppermute x7, starting transfers between devices: 25.7 us -> 24.5 us  [shifted(): return lax.ppermute(block, axis, route)]
    ppermute x7, waiting for transfers between devices: 8.05 us -> 6.94 us  [shifted(): return lax.ppermute(block, axis, route)]
    slice x1, local copies, waits for them, and re-layouts: 0.04 us -> 1.08 us  [shards(): next_low = shifted(left_features[:, :half], 'seg', -1)]
  transfers between devices with their start and end apart: 13 -> 13, of which waited for: 8 -> 6; matrix products, arithmetic and copies ran while one was open for 0% -> 1% of each run, Pallas kernels for 12% -> 12%
where the time goes in v10:
time: 93.9 us; the launch traced here: 93.3 us
  Pallas kernels  41.1 us (44%)
  starting transfers between devices  31.5 us (34%)
  waiting for transfers between devices  13.9 us (15%)
  local copies, waits for them, and re-layouts  5.84 us (6%)
  between operations  1.01 us (1%)
    pallas_call x6, Pallas kernels, kernel_call(): pl.pallas_call(kernel, in_specs=[ANYWHERE] * len(operands), out_specs=[AN...  41.1 us
    ppermute x7, starting transfers between devices, shifted(): return lax.ppermute(block, axis, route)  24.5 us
    ppermute x6, starting transfers between devices, exchanged(): return lax.ppermute(block, axis, route)  6.96 us
    ppermute x7, waiting for transfers between devices, shifted(): return lax.ppermute(block, axis, route)  6.94 us
    ppermute x6, waiting for transfers between devices, exchanged(): return lax.ppermute(block, axis, route)  6.94 us
    unnamed x11, local copies, waits for them, and re-layouts  3.63 us
  transfers between devices with their start and end apart: 13, of which 6 were waited for; matrix products, arithmetic and copies ran while one was open for 1% of the time, Pallas kernels for 12%

profile of v10, /device:TPU:19, one launch (start us, length us, event | category | flops | bytes accessed | tf_op | source)
XLA Modules:
  0.0 93.3 jit_solution(9401105533707849659)
XLA Ops:
  0.6 1.1 %slice.16 = bf16[4,512,128]{2,1,0:T(8,128)(2,1)S(1)} slice(bf16[4,1024,128]{2,1,0:T(8,128)(2,1)} %right_in.7), slice={[0:4], [512:1024], [0:128]} | slice | bytes 1048576 | tf_op jit(solution)/shard_map/slice | solution.py:832
  1.7 3.2 %collective-permute-start.1 = (bf16[4,512,128]{2,1,0:T(8,128)(2,1)S(1)}, bf16[4,512,128]{2,1,0:T(8,128)(2,1)S(1)}, u32[]{:S(2)}, u32[]{:S(2)}) collective-permute-start(bf16[4,512,128]{2,1,0:T(8,128)(2,1)S(1)} %slice.16), channel_id=1, source_target_pairs={{0,8},{8,16},{16,24},{1,9},{9,17},{17,25},{2,10},{10,18},{18,26},{... | collective-permute-start | bytes 1572872 | tf_op jit(solution)/shard_map/ppermute | solution.py:20
  4.9 1.1 %slice.17 = bf16[4,512,128]{2,1,0:T(8,128)(2,1)S(1)} slice(bf16[4,1024,128]{2,1,0:T(8,128)(2,1)} %left_in.7), slice={[0:4], [0:512], [0:128]} | slice | bytes 1048576 | tf_op jit(solution)/shard_map/slice | solution.py:833
  6.0 2.1 %collective-permute-start.2 = (bf16[4,512,128]{2,1,0:T(8,128)(2,1)S(1)}, bf16[4,512,128]{2,1,0:T(8,128)(2,1)S(1)}, u32[]{:S(2)}, u32[]{:S(2)}) collective-permute-start(bf16[4,512,128]{2,1,0:T(8,128)(2,1)S(1)} %slice.17), channel_id=1, source_target_pairs={{8,0},{16,8},{24,16},{9,1},{17,9},{25,17},{10,2},{18,10},{26,18},{... | collective-permute-start | bytes 1572872 | tf_op jit(solution)/shard_map/ppermute | solution.py:20
  8.1 0.0 copy-start
  8.1 1.2 %copy-done = bf16[4,1024,128]{2,1,0:T(8,128)(2,1)S(1)} copy-done((bf16[4,1024,128]{2,1,0:T(8,128)(2,1)S(1)}, bf16[4,1024,128]{2,1,0:T(8,128)(2,1)}, u32[]{:S(2)}) %copy-start) | copy-done | bytes 1048600
  9.3 1.2 %copy-done.2 = bf16[4,1024,128]{2,1,0:T(8,128)(2,1)S(1)} copy-done((bf16[4,1024,128]{2,1,0:T(8,128)(2,1)S(1)}, bf16[4,1024,128]{2,1,0:T(8,128)(2,1)}, u32[]{:S(2)}) %copy-start.2) | copy-done | bytes 1048600
  10.6 1.2 %copy-done.4 = bf16[3,3,3,128,128]{4,3,2,1,0:T(8,128)(2,1)S(1)} copy-done((bf16[3,3,3,128,128]{4,3,2,1,0:T(8,128)(2,1)S(1)}, bf16[3,3,3,128,128]{4,3,2,1,0:T(8,128)(2,1)}, u32[]{:S(2)}) %copy-start.4) | copy-done | bytes 884760
  11.7 4.4 %column_own.1 = (bf16[3,1536,256]{2,1,0:T(8,128)(2,1)S(1)}, f32[8,1024]{1,0:T(8,128)S(1)}) custom-call(bf16[4,1024,128]{2,1,0:T(8,128)(2,1)S(1)} %copy-done.2, bf16[4,1024,128]{2,1,0:T(8,128)(2,1)S(1)} %copy-done, bf16[3,3,3,128,128]{4,3,2,1,0:T(8,128)(2,1)S(1)} %copy-done.4), custom_call_target="tpu_custom_call" | custom-call | flops 1073741824 | bytes 4194304 | tf_op jit(solution)/shard_map/column_own/pallas_call | solution.py:47
  16.2 0.0 copy-start.1
  16.2 3.4 %collective-permute-start = (bf16[4,512,128]{2,1,0:T(8,128)(2,1)S(1)}, bf16[4,512,128]{2,1,0:T(8,128)(2,1)S(1)}, u32[]{:S(2)}, u32[]{:S(2)}) collective-permute-start(bf16[4,512,128]{2,1,0:T(8,128)(2,1)S(1)} %slice.15), channel_id=1, source_target_pairs={{0,8},{8,16},{16,24},{1,9},{9,17},{17,25},{2,10},{10,18},{18,26},{... | collective-permute-start | bytes 1572872 | tf_op jit(solution)/shard_map/ppermute | solution.py:20
  19.6 3.5 %column_cross.1.back_in = f32[8,1024]{1,0:T(8,128)S(1)} custom-call(bf16[4,1024,128]{2,1,0:T(8,128)(2,1)S(1)} %copy-done.2, bf16[4,512,128]{2,1,0:T(8,128)(2,1)S(1)} %collective-permute-done.1.prev_in.prev_high_in), custom_call_target="tpu_custom_call" | custom-call | flops 1073741824 | bytes 4194304 | tf_op jit(solution)/shard_map/column_cross/pallas_call | solution.py:47
  23.1 3.2 %column_next.1 = (f32[8,1024]{1,0:T(8,128)S(1)}, f32[8,1024]{1,0:T(8,128)S(1)}, f32[8,1024]{1,0:T(8,128)S(1)}) custom-call(bf16[4,512,128]{2,1,0:T(8,128)(2,1)S(1)} %collective-permute-done.2.next_in, bf16[4,1024,128]{2,1,0:T(8,128)(2,1)S(1)} %copy-done.1, f32[8,1024]{1,0:T(8,128)S(1)} %get-tuple-element.23.own_in, f32[8,1024]{1,0:T(8,128)S(1)} %column_cross.1.back_in), custom_call_target="tpu_custom_call" | custom-call | flops 268435456 | bytes 2097152 | tf_op jit(solution)/shard_map/column_next/pallas_call | solution.py:47
  26.4 0.1 collective-permute-start.3
  26.4 2.3 %collective-permute-start.4 = (f32[8,1024]{1,0:T(8,128)S(1)}, f32[8,1024]{1,0:T(8,128)S(1)}, u32[]{:S(2)}, u32[]{:S(2)}) collective-permute-start(f32[8,1024]{1,0:T(8,128)S(1)} %get-tuple-element.26), channel_id=1, source_target_pairs={{8,16},{16,8},{9,17},{17,9},{10,18},{18,10},{11,19},{19,11},{12,20... | collective-permute-start | bytes 98312 | tf_op jit(solution)/shard_map/ppermute | solution.py:27
  28.7 1.7 %collective-permute-done.prev_low_in = bf16[4,512,128]{2,1,0:T(8,128)(2,1)S(1)} collective-permute-done((bf16[4,512,128]{2,1,0:T(8,128)(2,1)S(1)}, bf16[4,512,128]{2,1,0:T(8,128)(2,1)S(1)}, u32[]{:S(2)}, u32[]{:S(2)}) %collective-permute-start) | collective-permute-done | bytes 524320 | tf_op jit(solution)/shard_map/ppermute | solution.py:20
  30.4 1.4 %collective-permute-done.4.second_in = f32[8,1024]{1,0:T(8,128)S(1)} collective-permute-done((f32[8,1024]{1,0:T(8,128)S(1)}, f32[8,1024]{1,0:T(8,128)S(1)}, u32[]{:S(2)}, u32[]{:S(2)}) %collective-permute-start.4) | collective-permute-done | bytes 32800 | tf_op jit(solution)/shard_map/ppermute | solution.py:27
  31.8 9.5 %row_pass.1 = (f32[4,2048]{1,0:T(4,128)S(1)}, bf16[4,1024,128]{2,1,0:T(8,128)(2,1)S(1)}, f32[4,1024]{1,0:T(4,128)S(1)}, f32[4,1024]{1,0:T(4,128)S(1)}, f32[4,1024]{1,0:T(4,128)S(1)}, /*index=5*/f32[4,1024]{1,0:T(4,128)S(1)}) custom-call(bf16[4,1024,128]{2,1,0:T(8,128)(2,1)S(1)} %copy-done.2, bf16[4,1024,128]{2,1,0:T(8,128)(2,1)S(1)} %copy-done.1, ...), custom_call_target="tpu_custom_call" | custom-call | tf_op jit(solution)/shard_map/row_pass/pallas_call | solution.py:47
  41.3 0.7 collective-permute-start.5
  42.1 1.9 %collective-permute-start.6 = (f32[4,1024]{1,0:T(4,128)S(1)}, f32[4,1024]{1,0:T(4,128)S(1)}, u32[]{:S(2)}, u32[]{:S(2)}) collective-permute-start(f32[4,1024]{1,0:T(4,128)S(1)} %get-tuple-element.32), channel_id=1, source_target_pairs={{8,16},{16,8},{9,17},{17,9},{10,18},{18,10},{11,19},{19,11},{12,20... | collective-permute-start | bytes 49160 | tf_op jit(solution)/shard_map/ppermute | solution.py:27
  44.0 2.7 %collective-permute-done.6.second_in = f32[4,1024]{1,0:T(4,128)S(1)} collective-permute-done((f32[4,1024]{1,0:T(4,128)S(1)}, f32[4,1024]{1,0:T(4,128)S(1)}, u32[]{:S(2)}, u32[]{:S(2)}) %collective-permute-start.6) | collective-permute-done | bytes 16416 | tf_op jit(solution)/shard_map/ppermute | solution.py:27
  46.7 10.3 %transport.1 = (bf16[4,1024,128]{2,1,0:T(8,128)(2,1)S(1)}, f32[4,1024]{1,0:T(4,128)}, bf16[3,1024,128]{2,1,0:T(8,128)(2,1)S(1)}, bf16[3,1024,128]{2,1,0:T(8,128)...) custom-call(f32[4,2048]{1,0:T(4,128)S(1)} %get-tuple-element.27.pot_in, ...), custom_call_target="tpu_custom_call" | custom-call | tf_op jit(solution)/shard_map/transport/pallas_call | solution.py:47
  57.0 6.4 %collective-permute-start.7 = (bf16[3,1024,128]{2,1,0:T(8,128)(2,1)S(1)}, bf16[3,1024,128]{2,1,0:T(8,128)(2,1)S(1)}, u32[]{:S(2)}, u32[]{:S(2)}) collective-permute-start(bf16[3,1024,128]{2,1,0:T(8,128)(2,1)S(1)} %get-tuple-element.34), channel_id=1, source_target_pairs={{0,1},{1,2},{2,3},{3,4},{4,5},{5,6},{6,7},{8,9},{9,10},{10,11},{11... | collective-permute-start | bytes 2359304 | tf_op jit(solution)/shard_map/ppermute | solution.py:20
  63.4 1.9 %collective-permute-start.8 = (bf16[3,1024,128]{2,1,0:T(8,128)(2,1)S(1)}, bf16[3,1024,128]{2,1,0:T(8,128)(2,1)S(1)}, u32[]{:S(2)}, u32[]{:S(2)}) collective-permute-start(bf16[3,1024,128]{2,1,0:T(8,128)(2,1)S(1)} %get-tuple-element.35), channel_id=1, source_target_pairs={{1,0},{2,1},{3,2},{4,3},{5,4},{6,5},{7,6},{9,8},{10,9},{11,10},{12... | collective-permute-start | bytes 2359304 | tf_op jit(solution)/shard_map/ppermute | solution.py:20
  65.3 0.1 collective-permute-start.9
  65.4 1.9 %collective-permute-start.10 = (bf16[4,16,128]{2,1,0:T(8,128)(2,1)S(1)}, bf16[4,16,128]{2,1,0:T(8,128)(2,1)S(1)}, u32[]{:S(2)}, u32[]{:S(2)}) collective-permute-start(bf16[4,16,128]{2,1,0:T(8,128)(2,1)S(1)} %get-tuple-element.37), channel_id=1, source_target_pairs={{8,16},{16,8},{9,17},{17,9},{10,18},{18,10},{11,19},{19,11},{12,20... | collective-permute-start | bytes 49160 | tf_op jit(solution)/shard_map/ppermute | solution.py:27
  67.4 0.9 %collective-permute-done.9.first_in = bf16[4,16,128]{2,1,0:T(8,128)(2,1)S(1)} collective-permute-done((bf16[4,16,128]{2,1,0:T(8,128)(2,1)S(1)}, bf16[4,16,128]{2,1,0:T(8,128)(2,1)S(1)}, u32[]{:S(2)}, u32[]{:S(2)}) %collective-permute-start.9) | collective-permute-done | bytes 16416 | tf_op jit(solution)/shard_map/ppermute | solution.py:27
  68.3 1.9 %collective-permute-done.10.second_in = bf16[4,16,128]{2,1,0:T(8,128)(2,1)S(1)} collective-permute-done((bf16[4,16,128]{2,1,0:T(8,128)(2,1)S(1)}, bf16[4,16,128]{2,1,0:T(8,128)(2,1)S(1)}, u32[]{:S(2)}, u32[]{:S(2)}) %collective-permute-start.10) | collective-permute-done | bytes 16416 | tf_op jit(solution)/shard_map/ppermute | solution.py:27
  70.2 3.4 %collective-permute-start.12 = (bf16[3,32,128]{2,1,0:T(8,128)(2,1)S(1)}, bf16[3,32,128]{2,1,0:T(8,128)(2,1)S(1)}, u32[]{:S(2)}, u32[]{:S(2)}) collective-permute-start(bf16[3,32,128]{2,1,0:T(8,128)(2,1)S(1)} %get-tuple-element.40), channel_id=1, source_target_pairs={{1,0},{2,1},{3,2},{4,3},{5,4},{6,5},{7,6},{9,8},{10,9},{11,10},{12... | collective-permute-start | bytes 73736 | tf_op jit(solution)/shard_map/ppermute | solution.py:20
  73.6 4.1 %collective-permute-start.11 = (bf16[3,32,128]{2,1,0:T(8,128)(2,1)S(1)}, bf16[3,32,128]{2,1,0:T(8,128)(2,1)S(1)}, u32[]{:S(2)}, u32[]{:S(2)}) collective-permute-start(bf16[3,32,128]{2,1,0:T(8,128)(2,1)S(1)} %get-tuple-element.41), channel_id=1, source_target_pairs={{0,1},{1,2},{2,3},{3,4},{4,5},{5,6},{6,7},{8,9},{9,10},{10,11},{11... | collective-permute-start | bytes 73736 | tf_op jit(solution)/shard_map/ppermute | solution.py:20
  77.7 5.2 %collective-permute-done.12.corner_bottom_in = bf16[3,32,128]{2,1,0:T(8,128)(2,1)S(1)} collective-permute-done((bf16[3,32,128]{2,1,0:T(8,128)(2,1)S(1)}, bf16[3,32,128]{2,1,0:T(8,128)(2,1)S(1)}, u32[]{:S(2)}, u32[]{:S(2)}) %collective-permute-start.12) | collective-permute-done | bytes 24608 | tf_op jit(solution)/shard_map/ppermute | solution.py:20
  83.0 10.2 %conv_layers.1 = bf16[4,1024,128]{2,1,0:T(8,128)(2,1)} custom-call(bf16[4,1024,128]{2,1,0:T(8,128)(2,1)S(1)} %get-tuple-element.33.state_in, bf16[3,1024,128]{2,1,0:T(8,128)(2,1)S(1)} %collective-permute-done.7.top_in, bf16[3,1024,128]{2,1,0:T(8,128)(2,1)S(1)} %collective-permute-done.8.bottom_in, bf16[4,16,128]{2,1,0:T(8,128)(2,1)S(1)} %collective-permute-done.9.first_in, ...), custom_call_target="tpu_custom_call" | custom-call | tf_op jit(solution)/shard_map/conv_layers/pallas_call | solution.py:47
  (16 shorter events, 0.1 us)
Async XLA Ops:
  1.7 17.9 %collective-permute-start.1 = (bf16[4,512,128]{2,1,0:T(8,128)(2,1)S(1)}, bf16[4,512,128]{2,1,0:T(8,128)(2,1)S(1)}, u32[]{:S(2)}, u32[]{:S(2)}) collective-permute-start(bf16[4,512,128]{2,1,0:T(8,128)(2,1)S(1)} %slice.16), channel_id=1, source_target_pairs={{0,8},{8,16},{16,24},{1,9},{9,17},{17,25},{2,10},{10,18},{18,26},{... | collective-permute-start | bytes 1572872 | tf_op jit(solution)/shard_map/ppermute | solution.py:20
  6.0 17.1 %collective-permute-start.2 = (bf16[4,512,128]{2,1,0:T(8,128)(2,1)S(1)}, bf16[4,512,128]{2,1,0:T(8,128)(2,1)S(1)}, u32[]{:S(2)}, u32[]{:S(2)}) collective-permute-start(bf16[4,512,128]{2,1,0:T(8,128)(2,1)S(1)} %slice.17), channel_id=1, source_target_pairs={{8,0},{16,8},{24,16},{9,1},{17,9},{25,17},{10,2},{18,10},{26,18},{... | collective-permute-start | bytes 1572872 | tf_op jit(solution)/shard_map/ppermute | solution.py:20
  8.1 1.2 %copy-start = (bf16[4,1024,128]{2,1,0:T(8,128)(2,1)S(1)}, bf16[4,1024,128]{2,1,0:T(8,128)(2,1)}, u32[]{:S(2)}) copy-start(bf16[4,1024,128]{2,1,0:T(8,128)(2,1)} %right_in.7) | copy-start | bytes 3145732
  9.3 1.2 %copy-start.2 = (bf16[4,1024,128]{2,1,0:T(8,128)(2,1)S(1)}, bf16[4,1024,128]{2,1,0:T(8,128)(2,1)}, u32[]{:S(2)}) copy-start(bf16[4,1024,128]{2,1,0:T(8,128)(2,1)} %left_in.7) | copy-start | bytes 3145732
  10.6 1.2 %copy-start.4 = (bf16[3,3,3,128,128]{4,3,2,1,0:T(8,128)(2,1)S(1)}, bf16[3,3,3,128,128]{4,3,2,1,0:T(8,128)(2,1)}, u32[]{:S(2)}) copy-start(bf16[3,3,3,128,128]{4,3,2,1,0:T(8,128)(2,1)} %weight_in.1) | copy-start | bytes 2654212
  16.2 7.0 %copy-start.1 = (bf16[4,1024,128]{2,1,0:T(8,128)(2,1)S(1)}, bf16[4,1024,128]{2,1,0:T(8,128)(2,1)}, u32[]{:S(2)}) copy-start(bf16[4,1024,128]{2,1,0:T(8,128)(2,1)} %right_in.7) | copy-start | bytes 3145732
  16.2 14.2 %collective-permute-start = (bf16[4,512,128]{2,1,0:T(8,128)(2,1)S(1)}, bf16[4,512,128]{2,1,0:T(8,128)(2,1)S(1)}, u32[]{:S(2)}, u32[]{:S(2)}) collective-permute-start(bf16[4,512,128]{2,1,0:T(8,128)(2,1)S(1)} %slice.15), channel_id=1, source_target_pairs={{0,8},{8,16},{16,24},{1,9},{9,17},{17,25},{2,10},{10,18},{18,26},{... | collective-permute-start | bytes 1572872 | tf_op jit(solution)/shard_map/ppermute | solution.py:20
  26.4 4.1 %collective-permute-start.3 = (f32[8,1024]{1,0:T(8,128)S(1)}, f32[8,1024]{1,0:T(8,128)S(1)}, u32[]{:S(2)}, u32[]{:S(2)}) collective-permute-start(f32[8,1024]{1,0:T(8,128)S(1)} %get-tuple-element.25), channel_id=1, source_target_pairs={{0,8},{8,0},{16,24},{24,16},{1,9},{9,1},{17,25},{25,17},{2,10},{10... | collective-permute-start | bytes 98312 | tf_op jit(solution)/shard_map/ppermute | solution.py:27
  26.4 5.4 %collective-permute-start.4 = (f32[8,1024]{1,0:T(8,128)S(1)}, f32[8,1024]{1,0:T(8,128)S(1)}, u32[]{:S(2)}, u32[]{:S(2)}) collective-permute-start(f32[8,1024]{1,0:T(8,128)S(1)} %get-tuple-element.26), channel_id=1, source_target_pairs={{8,16},{16,8},{9,17},{17,9},{10,18},{18,10},{11,19},{19,11},{12,20... | collective-permute-start | bytes 98312 | tf_op jit(solution)/shard_map/ppermute | solution.py:27
  41.3 41.6 %copy-start.3 = (f32[3,128]{1,0:T(4,128)S(1)}, f32[3,128]{1,0:T(4,128)}, u32[]{:S(2)}) copy-start(f32[3,128]{1,0:T(4,128)} %bias_in.1) | copy-start | bytes 4612
  41.3 2.7 %collective-permute-start.5 = (f32[4,1024]{1,0:T(4,128)S(1)}, f32[4,1024]{1,0:T(4,128)S(1)}, u32[]{:S(2)}, u32[]{:S(2)}) collective-permute-start(f32[4,1024]{1,0:T(4,128)S(1)} %get-tuple-element.31), channel_id=1, source_target_pairs={{0,8},{8,0},{16,24},{24,16},{1,9},{9,1},{17,25},{25,17},{2,10},{10... | collective-permute-start | bytes 49160 | tf_op jit(solution)/shard_map/ppermute | solution.py:27
  42.1 4.6 %collective-permute-start.6 = (f32[4,1024]{1,0:T(4,128)S(1)}, f32[4,1024]{1,0:T(4,128)S(1)}, u32[]{:S(2)}, u32[]{:S(2)}) collective-permute-start(f32[4,1024]{1,0:T(4,128)S(1)} %get-tuple-element.32), channel_id=1, source_target_pairs={{8,16},{16,8},{9,17},{17,9},{10,18},{18,10},{11,19},{19,11},{12,20... | collective-permute-start | bytes 49160 | tf_op jit(solution)/shard_map/ppermute | solution.py:27
  57.0 26.0 %collective-permute-start.7 = (bf16[3,1024,128]{2,1,0:T(8,128)(2,1)S(1)}, bf16[3,1024,128]{2,1,0:T(8,128)(2,1)S(1)}, u32[]{:S(2)}, u32[]{:S(2)}) collective-permute-start(bf16[3,1024,128]{2,1,0:T(8,128)(2,1)S(1)} %get-tuple-element.34), channel_id=1, source_target_pairs={{0,1},{1,2},{2,3},{3,4},{4,5},{5,6},{6,7},{8,9},{9,10},{10,11},{11... | collective-permute-start | bytes 2359304 | tf_op jit(solution)/shard_map/ppermute | solution.py:20
  63.4 19.5 %collective-permute-start.8 = (bf16[3,1024,128]{2,1,0:T(8,128)(2,1)S(1)}, bf16[3,1024,128]{2,1,0:T(8,128)(2,1)S(1)}, u32[]{:S(2)}, u32[]{:S(2)}) collective-permute-start(bf16[3,1024,128]{2,1,0:T(8,128)(2,1)S(1)} %get-tuple-element.35), channel_id=1, source_target_pairs={{1,0},{2,1},{3,2},{4,3},{5,4},{6,5},{7,6},{9,8},{10,9},{11,10},{12... | collective-permute-start | bytes 2359304 | tf_op jit(solution)/shard_map/ppermute | solution.py:20
  65.3 2.9 %collective-permute-start.9 = (bf16[4,16,128]{2,1,0:T(8,128)(2,1)S(1)}, bf16[4,16,128]{2,1,0:T(8,128)(2,1)S(1)}, u32[]{:S(2)}, u32[]{:S(2)}) collective-permute-start(bf16[4,16,128]{2,1,0:T(8,128)(2,1)S(1)} %get-tuple-element.36), channel_id=1, source_target_pairs={{0,8},{8,0},{16,24},{24,16},{1,9},{9,1},{17,25},{25,17},{2,10},{10... | collective-permute-start | bytes 49160 | tf_op jit(solution)/shard_map/ppermute | solution.py:27
  65.4 4.8 %collective-permute-start.10 = (bf16[4,16,128]{2,1,0:T(8,128)(2,1)S(1)}, bf16[4,16,128]{2,1,0:T(8,128)(2,1)S(1)}, u32[]{:S(2)}, u32[]{:S(2)}) collective-permute-start(bf16[4,16,128]{2,1,0:T(8,128)(2,1)S(1)} %get-tuple-element.37), channel_id=1, source_target_pairs={{8,16},{16,8},{9,17},{17,9},{10,18},{18,10},{11,19},{19,11},{12,20... | collective-permute-start | bytes 49160 | tf_op jit(solution)/shard_map/ppermute | solution.py:27
  70.2 12.7 %collective-permute-start.12 = (bf16[3,32,128]{2,1,0:T(8,128)(2,1)S(1)}, bf16[3,32,128]{2,1,0:T(8,128)(2,1)S(1)}, u32[]{:S(2)}, u32[]{:S(2)}) collective-permute-start(bf16[3,32,128]{2,1,0:T(8,128)(2,1)S(1)} %get-tuple-element.40), channel_id=1, source_target_pairs={{1,0},{2,1},{3,2},{4,3},{5,4},{6,5},{7,6},{9,8},{10,9},{11,10},{12... | collective-permute-start | bytes 73736 | tf_op jit(solution)/shard_map/ppermute | solution.py:20
  73.6 9.3 %collective-permute-start.11 = (bf16[3,32,128]{2,1,0:T(8,128)(2,1)S(1)}, bf16[3,32,128]{2,1,0:T(8,128)(2,1)S(1)}, u32[]{:S(2)}, u32[]{:S(2)}) collective-permute-start(bf16[3,32,128]{2,1,0:T(8,128)(2,1)S(1)} %get-tuple-element.41), channel_id=1, source_target_pairs={{0,1},{1,2},{2,3},{3,4},{4,5},{5,6},{6,7},{8,9},{9,10},{10,11},{11... | collective-permute-start | bytes 73736 | tf_op jit(solution)/shard_map/ppermute | solution.py:20

commit v11 on v9

--- a/solution.py
+++ b/solution.py
@@ -228,7 +228,7 @@
             merged[top, cols] = joint
         return carry
 
-    lax.fori_loop(0, lines_here, one_line, 0)
+    lax.fori_loop(0, lines_here, one_line, 0, unroll=True)
     first_part[...], second_part[...] = by_parity(merged[...], back[...])
     begin_copies(sends)
     wait(sends)
@@ -270,7 +270,7 @@
             back[bottom, cols] = total
         return carry
 
-    lax.fori_loop(0, lines_here, one_line, 0)
+    lax.fori_loop(0, lines_here, one_line, 0, unroll=True)
     send.start()
     send.wait()
 

time: 92.4 us -> 92.9 us (level)
  transfers between devices with their start and end apart: 13 -> 13, of which waited for: 8 -> 8; matrix products, arithmetic and copies ran while one was open for 0% -> 0% of each run, Pallas kernels for 12% -> 13%
where the time goes in v11:
time: 92.9 us; the launch traced here: 92.5 us
  Pallas kernels  41.6 us (45%)
  starting transfers between devices  33.2 us (36%)
  waiting for transfers between devices  15.2 us (16%)
  local copies, waits for them, and re-layouts  1.5 us (2%)
  between operations  1.02 us (1%)
    pallas_call x6, Pallas kernels, kernel_call(): pl.pallas_call(kernel, in_specs=[ANYWHERE] * len(operands), out_specs=[AN...  41.6 us
    ppermute x7, starting transfers between devices, shifted(): return lax.ppermute(block, axis, route)  25.9 us
    ppermute x7, waiting for transfers between devices, shifted(): return lax.ppermute(block, axis, route)  7.62 us
    ppermute x6, waiting for transfers between devices, exchanged(): return lax.ppermute(block, axis, route)  7.58 us
    ppermute x6, starting transfers between devices, exchanged(): return lax.ppermute(block, axis, route)  7.3 us
  transfers between devices with their start and end apart: 13, of which 8 were waited for; matrix products, arithmetic and copies ran while one was open for 0% of the time, Pallas kernels for 13%

profile of v11, /device:TPU:19, one launch (start us, length us, event | category | flops | bytes accessed | tf_op | source)
XLA Modules:
  0.0 92.5 jit_solution(1069961717213701614)
XLA Ops:
  0.7 1.4 %fusion = (bf16[4,512,128]{2,1,0:T(8,128)(2,1)S(1)}, bf16[4,512,128]{2,1,0:T(8,128)(2,1)S(1)}) fusion(bf16[4,1024,128]{2,1,0:T(8,128)(2,1)} %right_in.7), kind=kLoop, calls=%fused_computation.2 | loop fusion | bytes 2097152 | tf_op jit(solution)/shard_map/slice | solution.py:832
  2.1 3.2 %collective-permute-start.1 = (bf16[4,512,128]{2,1,0:T(8,128)(2,1)S(1)}, bf16[4,512,128]{2,1,0:T(8,128)(2,1)S(1)}, u32[]{:S(2)}, u32[]{:S(2)}) collective-permute-start(bf16[4,512,128]{2,1,0:T(8,128)(2,1)S(1)} %get-tuple-element.40), channel_id=1, source_target_pairs={{0,8},{8,16},{16,24},{1,9},{9,17},{17,25},{2,10},{10,18},{18,26},{... | collective-permute-start | bytes 1572872 | tf_op jit(solution)/shard_map/ppermute | solution.py:20
  5.4 2.1 %collective-permute-start.2 = (bf16[4,512,128]{2,1,0:T(8,128)(2,1)S(1)}, bf16[4,512,128]{2,1,0:T(8,128)(2,1)S(1)}, u32[]{:S(2)}, u32[]{:S(2)}) collective-permute-start(bf16[4,512,128]{2,1,0:T(8,128)(2,1)S(1)} %slice.17), channel_id=1, source_target_pairs={{8,0},{16,8},{24,16},{9,1},{17,9},{25,17},{10,2},{18,10},{26,18},{... | collective-permute-start | bytes 1572872 | tf_op jit(solution)/shard_map/ppermute | solution.py:20
  7.5 4.4 %column_own.1 = (bf16[3,1536,256]{2,1,0:T(8,128)(2,1)S(1)}, f32[8,1024]{1,0:T(8,128)S(1)}) custom-call(bf16[4,1024,128]{2,1,0:T(8,128)(2,1)S(1)} %copy-done.1, bf16[4,1024,128]{2,1,0:T(8,128)(2,1)S(1)} %copy-done, bf16[3,3,3,128,128]{4,3,2,1,0:T(8,128)(2,1)S(1)} %copy-done.3), custom_call_target="tpu_custom_call" | custom-call | flops 1073741824 | bytes 4194304 | tf_op jit(solution)/shard_map/column_own/pallas_call | solution.py:47
  11.9 3.2 %collective-permute-start = (bf16[4,512,128]{2,1,0:T(8,128)(2,1)S(1)}, bf16[4,512,128]{2,1,0:T(8,128)(2,1)S(1)}, u32[]{:S(2)}, u32[]{:S(2)}) collective-permute-start(bf16[4,512,128]{2,1,0:T(8,128)(2,1)S(1)} %get-tuple-element.22), channel_id=1, source_target_pairs={{0,8},{8,16},{16,24},{1,9},{9,17},{17,25},{2,10},{10,18},{18,26},{... | collective-permute-start | bytes 1572872 | tf_op jit(solution)/shard_map/ppermute | solution.py:20
  15.2 1.6 %collective-permute-done.1.prev_in.prev_high_in = bf16[4,512,128]{2,1,0:T(8,128)(2,1)S(1)} collective-permute-done((bf16[4,512,128]{2,1,0:T(8,128)(2,1)S(1)}, bf16[4,512,128]{2,1,0:T(8,128)(2,1)S(1)}, u32[]{:S(2)}, u32[]{:S(2)}) %collective-permute-start.1) | collective-permute-done | bytes 524320 | tf_op jit(solution)/shard_map/ppermute | solution.py:20
  16.8 3.7 %column_cross.1.back_in = f32[8,1024]{1,0:T(8,128)S(1)} custom-call(bf16[4,1024,128]{2,1,0:T(8,128)(2,1)S(1)} %copy-done.1, bf16[4,512,128]{2,1,0:T(8,128)(2,1)S(1)} %collective-permute-done.1.prev_in.prev_high_in), custom_call_target="tpu_custom_call" | custom-call | flops 1073741824 | bytes 4194304 | tf_op jit(solution)/shard_map/column_cross/pallas_call | solution.py:47
  20.5 0.0 collective-permute-done.2.next_in
  20.5 3.4 %column_next.1 = (f32[8,1024]{1,0:T(8,128)S(1)}, f32[8,1024]{1,0:T(8,128)S(1)}, f32[8,1024]{1,0:T(8,128)S(1)}) custom-call(bf16[4,512,128]{2,1,0:T(8,128)(2,1)S(1)} %collective-permute-done.2.next_in, bf16[4,1024,128]{2,1,0:T(8,128)(2,1)S(1)} %copy-done, f32[8,1024]{1,0:T(8,128)S(1)} %get-tuple-element.23.own_in, f32[8,1024]{1,0:T(8,128)S(1)} %column_cross.1.back_in), custom_call_target="tpu_custom_call" | custom-call | flops 268435456 | bytes 2097152 | tf_op jit(solution)/shard_map/column_next/pallas_call | solution.py:47
  24.0 1.4 %collective-permute-start.3 = (f32[8,1024]{1,0:T(8,128)S(1)}, f32[8,1024]{1,0:T(8,128)S(1)}, u32[]{:S(2)}, u32[]{:S(2)}) collective-permute-start(f32[8,1024]{1,0:T(8,128)S(1)} %get-tuple-element.25), channel_id=1, source_target_pairs={{0,8},{8,0},{16,24},{24,16},{1,9},{9,1},{17,25},{25,17},{2,10},{10... | collective-permute-start | bytes 98312 | tf_op jit(solution)/shard_map/ppermute | solution.py:27
  25.3 1.9 %collective-permute-start.4 = (f32[8,1024]{1,0:T(8,128)S(1)}, f32[8,1024]{1,0:T(8,128)S(1)}, u32[]{:S(2)}, u32[]{:S(2)}) collective-permute-start(f32[8,1024]{1,0:T(8,128)S(1)} %get-tuple-element.26), channel_id=1, source_target_pairs={{8,16},{16,8},{9,17},{17,9},{10,18},{18,10},{11,19},{19,11},{12,20... | collective-permute-start | bytes 98312 | tf_op jit(solution)/shard_map/ppermute | solution.py:27
  27.2 0.8 collective-permute-done.prev_low_in
  28.0 0.0 collective-permute-done.3.first_in
  28.0 2.2 %collective-permute-done.4.second_in = f32[8,1024]{1,0:T(8,128)S(1)} collective-permute-done((f32[8,1024]{1,0:T(8,128)S(1)}, f32[8,1024]{1,0:T(8,128)S(1)}, u32[]{:S(2)}, u32[]{:S(2)}) %collective-permute-start.4) | collective-permute-done | bytes 32800 | tf_op jit(solution)/shard_map/ppermute | solution.py:27
  30.2 9.5 %row_pass.1 = (f32[4,2048]{1,0:T(4,128)S(1)}, bf16[4,1024,128]{2,1,0:T(8,128)(2,1)S(1)}, f32[4,1024]{1,0:T(4,128)S(1)}, f32[4,1024]{1,0:T(4,128)S(1)}, f32[4,1024]{1,0:T(4,128)S(1)}, /*index=5*/f32[4,1024]{1,0:T(4,128)S(1)}) custom-call(bf16[4,1024,128]{2,1,0:T(8,128)(2,1)S(1)} %copy-done.1, bf16[4,1024,128]{2,1,0:T(8,128)(2,1)S(1)} %copy-done, ...), custom_call_target="tpu_custom_call" | custom-call | tf_op jit(solution)/shard_map/row_pass/pallas_call | solution.py:47
  39.7 0.0 copy-start.2
  39.8 0.1 collective-permute-start.5
  39.8 2.0 %collective-permute-start.6 = (f32[4,1024]{1,0:T(4,128)S(1)}, f32[4,1024]{1,0:T(4,128)S(1)}, u32[]{:S(2)}, u32[]{:S(2)}) collective-permute-start(f32[4,1024]{1,0:T(4,128)S(1)} %get-tuple-element.32), channel_id=1, source_target_pairs={{8,16},{16,8},{9,17},{17,9},{10,18},{18,10},{11,19},{19,11},{12,20... | collective-permute-start | bytes 49160 | tf_op jit(solution)/shard_map/ppermute | solution.py:27
  41.8 0.6 collective-permute-done.5.first_in
  42.4 1.9 %collective-permute-done.6.second_in = f32[4,1024]{1,0:T(4,128)S(1)} collective-permute-done((f32[4,1024]{1,0:T(4,128)S(1)}, f32[4,1024]{1,0:T(4,128)S(1)}, u32[]{:S(2)}, u32[]{:S(2)}) %collective-permute-start.6) | collective-permute-done | bytes 16416 | tf_op jit(solution)/shard_map/ppermute | solution.py:27
  44.3 10.3 %transport.1 = (bf16[4,1024,128]{2,1,0:T(8,128)(2,1)S(1)}, f32[4,1024]{1,0:T(4,128)}, bf16[3,1024,128]{2,1,0:T(8,128)(2,1)S(1)}, bf16[3,1024,128]{2,1,0:T(8,128)...) custom-call(f32[4,2048]{1,0:T(4,128)S(1)} %get-tuple-element.27.pot_in, ...), custom_call_target="tpu_custom_call" | custom-call | tf_op jit(solution)/shard_map/transport/pallas_call | solution.py:47
  54.6 8.0 %collective-permute-start.7 = (bf16[3,1024,128]{2,1,0:T(8,128)(2,1)S(1)}, bf16[3,1024,128]{2,1,0:T(8,128)(2,1)S(1)}, u32[]{:S(2)}, u32[]{:S(2)}) collective-permute-start(bf16[3,1024,128]{2,1,0:T(8,128)(2,1)S(1)} %get-tuple-element.34), channel_id=1, source_target_pairs={{0,1},{1,2},{2,3},{3,4},{4,5},{5,6},{6,7},{8,9},{9,10},{10,11},{11... | collective-permute-start | bytes 2359304 | tf_op jit(solution)/shard_map/ppermute | solution.py:20
  62.6 1.9 %collective-permute-start.8 = (bf16[3,1024,128]{2,1,0:T(8,128)(2,1)S(1)}, bf16[3,1024,128]{2,1,0:T(8,128)(2,1)S(1)}, u32[]{:S(2)}, u32[]{:S(2)}) collective-permute-start(bf16[3,1024,128]{2,1,0:T(8,128)(2,1)S(1)} %get-tuple-element.35), channel_id=1, source_target_pairs={{1,0},{2,1},{3,2},{4,3},{5,4},{6,5},{7,6},{9,8},{10,9},{11,10},{12... | collective-permute-start | bytes 2359304 | tf_op jit(solution)/shard_map/ppermute | solution.py:20
  64.5 0.1 collective-permute-start.9
  64.6 1.9 %collective-permute-start.10 = (bf16[4,16,128]{2,1,0:T(8,128)(2,1)S(1)}, bf16[4,16,128]{2,1,0:T(8,128)(2,1)S(1)}, u32[]{:S(2)}, u32[]{:S(2)}) collective-permute-start(bf16[4,16,128]{2,1,0:T(8,128)(2,1)S(1)} %get-tuple-element.37), channel_id=1, source_target_pairs={{8,16},{16,8},{9,17},{17,9},{10,18},{18,10},{11,19},{19,11},{12,20... | collective-permute-start | bytes 49160 | tf_op jit(solution)/shard_map/ppermute | solution.py:27
  66.5 0.9 %collective-permute-done.9.first_in = bf16[4,16,128]{2,1,0:T(8,128)(2,1)S(1)} collective-permute-done((bf16[4,16,128]{2,1,0:T(8,128)(2,1)S(1)}, bf16[4,16,128]{2,1,0:T(8,128)(2,1)S(1)}, u32[]{:S(2)}, u32[]{:S(2)}) %collective-permute-start.9) | collective-permute-done | bytes 16416 | tf_op jit(solution)/shard_map/ppermute | solution.py:27
  67.5 1.9 %collective-permute-done.10.second_in = bf16[4,16,128]{2,1,0:T(8,128)(2,1)S(1)} collective-permute-done((bf16[4,16,128]{2,1,0:T(8,128)(2,1)S(1)}, bf16[4,16,128]{2,1,0:T(8,128)(2,1)S(1)}, u32[]{:S(2)}, u32[]{:S(2)}) %collective-permute-start.10) | collective-permute-done | bytes 16416 | tf_op jit(solution)/shard_map/ppermute | solution.py:27
  69.4 3.4 %collective-permute-start.12 = (bf16[3,32,128]{2,1,0:T(8,128)(2,1)S(1)}, bf16[3,32,128]{2,1,0:T(8,128)(2,1)S(1)}, u32[]{:S(2)}, u32[]{:S(2)}) collective-permute-start(bf16[3,32,128]{2,1,0:T(8,128)(2,1)S(1)} %get-tuple-element.42), channel_id=1, source_target_pairs={{1,0},{2,1},{3,2},{4,3},{5,4},{6,5},{7,6},{9,8},{10,9},{11,10},{12... | collective-permute-start | bytes 73736 | tf_op jit(solution)/shard_map/ppermute | solution.py:20
  72.8 4.1 %collective-permute-start.11 = (bf16[3,32,128]{2,1,0:T(8,128)(2,1)S(1)}, bf16[3,32,128]{2,1,0:T(8,128)(2,1)S(1)}, u32[]{:S(2)}, u32[]{:S(2)}) collective-permute-start(bf16[3,32,128]{2,1,0:T(8,128)(2,1)S(1)} %get-tuple-element.43), channel_id=1, source_target_pairs={{0,1},{1,2},{2,3},{3,4},{4,5},{5,6},{6,7},{8,9},{9,10},{10,11},{11... | collective-permute-start | bytes 73736 | tf_op jit(solution)/shard_map/ppermute | solution.py:20
  76.9 5.2 %collective-permute-done.12.corner_bottom_in = bf16[3,32,128]{2,1,0:T(8,128)(2,1)S(1)} collective-permute-done((bf16[3,32,128]{2,1,0:T(8,128)(2,1)S(1)}, bf16[3,32,128]{2,1,0:T(8,128)(2,1)S(1)}, u32[]{:S(2)}, u32[]{:S(2)}) %collective-permute-start.12) | collective-permute-done | bytes 24608 | tf_op jit(solution)/shard_map/ppermute | solution.py:20
  82.1 0.0 collective-permute-done.11.corner_top_in
  82.2 10.2 %conv_layers.1 = bf16[4,1024,128]{2,1,0:T(8,128)(2,1)} custom-call(bf16[4,1024,128]{2,1,0:T(8,128)(2,1)S(1)} %get-tuple-element.33.state_in, bf16[3,1024,128]{2,1,0:T(8,128)(2,1)S(1)} %collective-permute-done.7.top_in, bf16[3,1024,128]{2,1,0:T(8,128)(2,1)S(1)} %collective-permute-done.8.bottom_in, bf16[4,16,128]{2,1,0:T(8,128)(2,1)S(1)} %collective-permute-done.9.first_in, ...), custom_call_target="tpu_custom_call" | custom-call | tf_op jit(solution)/shard_map/conv_layers/pallas_call | solution.py:47
  (13 shorter events, 0.1 us)
Async XLA Ops:
  0.6 6.8 %copy-start = (bf16[4,1024,128]{2,1,0:T(8,128)(2,1)S(1)}, bf16[4,1024,128]{2,1,0:T(8,128)(2,1)}, u32[]{:S(2)}) copy-start(bf16[4,1024,128]{2,1,0:T(8,128)(2,1)} %right_in.7) | copy-start | bytes 3145732
  0.6 4.7 %copy-start.1 = (bf16[4,1024,128]{2,1,0:T(8,128)(2,1)S(1)}, bf16[4,1024,128]{2,1,0:T(8,128)(2,1)}, u32[]{:S(2)}) copy-start(bf16[4,1024,128]{2,1,0:T(8,128)(2,1)} %left_in.7) | copy-start | bytes 3145732
  0.6 6.8 %copy-start.3 = (bf16[3,3,3,128,128]{4,3,2,1,0:T(8,128)(2,1)S(1)}, bf16[3,3,3,128,128]{4,3,2,1,0:T(8,128)(2,1)}, u32[]{:S(2)}) copy-start(bf16[3,3,3,128,128]{4,3,2,1,0:T(8,128)(2,1)} %weight_in.1) | copy-start | bytes 2654212
  2.1 14.7 %collective-permute-start.1 = (bf16[4,512,128]{2,1,0:T(8,128)(2,1)S(1)}, bf16[4,512,128]{2,1,0:T(8,128)(2,1)S(1)}, u32[]{:S(2)}, u32[]{:S(2)}) collective-permute-start(bf16[4,512,128]{2,1,0:T(8,128)(2,1)S(1)} %get-tuple-element.40), channel_id=1, source_target_pairs={{0,8},{8,16},{16,24},{1,9},{9,17},{17,25},{2,10},{10,18},{18,26},{... | collective-permute-start | bytes 1572872 | tf_op jit(solution)/shard_map/ppermute | solution.py:20
  5.4 15.2 %collective-permute-start.2 = (bf16[4,512,128]{2,1,0:T(8,128)(2,1)S(1)}, bf16[4,512,128]{2,1,0:T(8,128)(2,1)S(1)}, u32[]{:S(2)}, u32[]{:S(2)}) collective-permute-start(bf16[4,512,128]{2,1,0:T(8,128)(2,1)S(1)} %slice.17), channel_id=1, source_target_pairs={{8,0},{16,8},{24,16},{9,1},{17,9},{25,17},{10,2},{18,10},{26,18},{... | collective-permute-start | bytes 1572872 | tf_op jit(solution)/shard_map/ppermute | solution.py:20
  11.9 16.1 %collective-permute-start = (bf16[4,512,128]{2,1,0:T(8,128)(2,1)S(1)}, bf16[4,512,128]{2,1,0:T(8,128)(2,1)S(1)}, u32[]{:S(2)}, u32[]{:S(2)}) collective-permute-start(bf16[4,512,128]{2,1,0:T(8,128)(2,1)S(1)} %get-tuple-element.22), channel_id=1, source_target_pairs={{0,8},{8,16},{16,24},{1,9},{9,17},{17,25},{2,10},{10,18},{18,26},{... | collective-permute-start | bytes 1572872 | tf_op jit(solution)/shard_map/ppermute | solution.py:20
  24.0 4.1 %collective-permute-start.3 = (f32[8,1024]{1,0:T(8,128)S(1)}, f32[8,1024]{1,0:T(8,128)S(1)}, u32[]{:S(2)}, u32[]{:S(2)}) collective-permute-start(f32[8,1024]{1,0:T(8,128)S(1)} %get-tuple-element.25), channel_id=1, source_target_pairs={{0,8},{8,0},{16,24},{24,16},{1,9},{9,1},{17,25},{25,17},{2,10},{10... | collective-permute-start | bytes 98312 | tf_op jit(solution)/shard_map/ppermute | solution.py:27
  25.3 4.9 %collective-permute-start.4 = (f32[8,1024]{1,0:T(8,128)S(1)}, f32[8,1024]{1,0:T(8,128)S(1)}, u32[]{:S(2)}, u32[]{:S(2)}) collective-permute-start(f32[8,1024]{1,0:T(8,128)S(1)} %get-tuple-element.26), channel_id=1, source_target_pairs={{8,16},{16,8},{9,17},{17,9},{10,18},{18,10},{11,19},{19,11},{12,20... | collective-permute-start | bytes 98312 | tf_op jit(solution)/shard_map/ppermute | solution.py:27
  39.7 42.4 %copy-start.2 = (f32[3,128]{1,0:T(4,128)S(1)}, f32[3,128]{1,0:T(4,128)}, u32[]{:S(2)}) copy-start(f32[3,128]{1,0:T(4,128)} %bias_in.1) | copy-start | bytes 4612
  39.8 2.7 %collective-permute-start.5 = (f32[4,1024]{1,0:T(4,128)S(1)}, f32[4,1024]{1,0:T(4,128)S(1)}, u32[]{:S(2)}, u32[]{:S(2)}) collective-permute-start(f32[4,1024]{1,0:T(4,128)S(1)} %get-tuple-element.31), channel_id=1, source_target_pairs={{0,8},{8,0},{16,24},{24,16},{1,9},{9,1},{17,25},{25,17},{2,10},{10... | collective-permute-start | bytes 49160 | tf_op jit(solution)/shard_map/ppermute | solution.py:27
  39.8 4.5 %collective-permute-start.6 = (f32[4,1024]{1,0:T(4,128)S(1)}, f32[4,1024]{1,0:T(4,128)S(1)}, u32[]{:S(2)}, u32[]{:S(2)}) collective-permute-start(f32[4,1024]{1,0:T(4,128)S(1)} %get-tuple-element.32), channel_id=1, source_target_pairs={{8,16},{16,8},{9,17},{17,9},{10,18},{18,10},{11,19},{19,11},{12,20... | collective-permute-start | bytes 49160 | tf_op jit(solution)/shard_map/ppermute | solution.py:27
  54.6 27.5 %collective-permute-start.7 = (bf16[3,1024,128]{2,1,0:T(8,128)(2,1)S(1)}, bf16[3,1024,128]{2,1,0:T(8,128)(2,1)S(1)}, u32[]{:S(2)}, u32[]{:S(2)}) collective-permute-start(bf16[3,1024,128]{2,1,0:T(8,128)(2,1)S(1)} %get-tuple-element.34), channel_id=1, source_target_pairs={{0,1},{1,2},{2,3},{3,4},{4,5},{5,6},{6,7},{8,9},{9,10},{10,11},{11... | collective-permute-start | bytes 2359304 | tf_op jit(solution)/shard_map/ppermute | solution.py:20
  62.6 19.5 %collective-permute-start.8 = (bf16[3,1024,128]{2,1,0:T(8,128)(2,1)S(1)}, bf16[3,1024,128]{2,1,0:T(8,128)(2,1)S(1)}, u32[]{:S(2)}, u32[]{:S(2)}) collective-permute-start(bf16[3,1024,128]{2,1,0:T(8,128)(2,1)S(1)} %get-tuple-element.35), channel_id=1, source_target_pairs={{1,0},{2,1},{3,2},{4,3},{5,4},{6,5},{7,6},{9,8},{10,9},{11,10},{12... | collective-permute-start | bytes 2359304 | tf_op jit(solution)/shard_map/ppermute | solution.py:20
  64.5 2.9 %collective-permute-start.9 = (bf16[4,16,128]{2,1,0:T(8,128)(2,1)S(1)}, bf16[4,16,128]{2,1,0:T(8,128)(2,1)S(1)}, u32[]{:S(2)}, u32[]{:S(2)}) collective-permute-start(bf16[4,16,128]{2,1,0:T(8,128)(2,1)S(1)} %get-tuple-element.36), channel_id=1, source_target_pairs={{0,8},{8,0},{16,24},{24,16},{1,9},{9,1},{17,25},{25,17},{2,10},{10... | collective-permute-start | bytes 49160 | tf_op jit(solution)/shard_map/ppermute | solution.py:27
  64.6 4.8 %collective-permute-start.10 = (bf16[4,16,128]{2,1,0:T(8,128)(2,1)S(1)}, bf16[4,16,128]{2,1,0:T(8,128)(2,1)S(1)}, u32[]{:S(2)}, u32[]{:S(2)}) collective-permute-start(bf16[4,16,128]{2,1,0:T(8,128)(2,1)S(1)} %get-tuple-element.37), channel_id=1, source_target_pairs={{8,16},{16,8},{9,17},{17,9},{10,18},{18,10},{11,19},{19,11},{12,20... | collective-permute-start | bytes 49160 | tf_op jit(solution)/shard_map/ppermute | solution.py:27
  69.4 12.7 %collective-permute-start.12 = (bf16[3,32,128]{2,1,0:T(8,128)(2,1)S(1)}, bf16[3,32,128]{2,1,0:T(8,128)(2,1)S(1)}, u32[]{:S(2)}, u32[]{:S(2)}) collective-permute-start(bf16[3,32,128]{2,1,0:T(8,128)(2,1)S(1)} %get-tuple-element.42), channel_id=1, source_target_pairs={{1,0},{2,1},{3,2},{4,3},{5,4},{6,5},{7,6},{9,8},{10,9},{11,10},{12... | collective-permute-start | bytes 73736 | tf_op jit(solution)/shard_map/ppermute | solution.py:20
  72.8 9.3 %collective-permute-start.11 = (bf16[3,32,128]{2,1,0:T(8,128)(2,1)S(1)}, bf16[3,32,128]{2,1,0:T(8,128)(2,1)S(1)}, u32[]{:S(2)}, u32[]{:S(2)}) collective-permute-start(bf16[3,32,128]{2,1,0:T(8,128)(2,1)S(1)} %get-tuple-element.43), channel_id=1, source_target_pairs={{0,1},{1,2},{2,3},{3,4},{4,5},{5,6},{6,7},{8,9},{9,10},{10,11},{11... | collective-permute-start | bytes 73736 | tf_op jit(solution)/shard_map/ppermute | solution.py:20
